TPU v7x, 32 devices: a whole 2x2x4 slice. The times are simulated.
32 devices in a mesh: groups: 2 (over x), seq: 16 (over z, y, core).
Axes of the slice: x: 2, y: 2, z: 4, core: 2. Of those that a mesh axis runs over, the one named last changes fastest.
Arguments:
- query_states: bfloat16 [3584, 16, 128], P(('groups', 'seq')), parts along dimension 0, may hold values from -6 to 6
- key_states: bfloat16 [3584, 8, 128], P(('groups', 'seq')), parts along dimension 0, may hold values from -6 to 6
- value_states: bfloat16 [3584, 8, 128], P(('groups', 'seq')), parts along dimension 0, may hold values from -6 to 6
- query_gain: float32 [128], replicated, may hold values from 0.5 to 5.5
- key_gain: float32 [128], replicated, may hold values from 0.5 to 5.5
Outputs:
- attended: bfloat16 [3584, 16, 128], P(('groups', 'seq')), parts along dimension 0
There are 2 independent parts, one for each index of `groups`. A program takes and returns all parts, laid end to end along the dimension named above; an argument that names none is the same for every part. Nothing has to cross between parts.
All inputs are finite; a program needn't handle non-finite values.
Results may differ from a plain program's by a relative error of at most 0.0025.
The roundings to bfloat16 on the way count: a program that leaves them out, or rounds other values in their place, can miss the bound.
Values may be sent and summed in bfloat16 or wider, within the bound.
No kernel may reach another device: no remote copies, remote signals or barrier semaphores. Data moves between devices by JAX's collectives and lax.ppermute only.
A program may use at most 64 MiB of HBM per device.

v0:
```python
import math

import jax
import jax.numpy as jnp
from jax import lax
from jax.sharding import PartitionSpec as P

BLOCK = 896


ROPE_BASE = 1000000.0
EPSILON = 1e-06
MASKED = -1e30


def rotate(tensor, norm_gain, positions):
    floats = tensor.astype(jnp.float32)
    mean_square = jnp.mean(floats * floats, axis=-1, keepdims=True)
    normed = floats * lax.rsqrt(mean_square + EPSILON) * norm_gain
    halfway = tensor.shape[-1] // 2
    frequency = ROPE_BASE ** (-(jnp.arange(halfway, dtype=jnp.float32) * 2.0 / tensor.shape[-1]))
    angles = positions.astype(jnp.float32)[:, None] * frequency[None, :]
    cosine = jnp.cos(angles)[:, None, :]
    sine_vals = jnp.sin(angles)[:, None, :]
    first_half = normed[..., :halfway]
    second_half = normed[..., halfway:]
    rotated = jnp.concatenate(
        [
            first_half * cosine - second_half * sine_vals,
            second_half * cosine + first_half * sine_vals,
        ],
        axis=-1,
    )
    return rotated.astype(jnp.bfloat16)


def update_block(carried, scores, allowed, value_block):
    running_max, running_sum, weighted = carried
    scores = jnp.where(allowed[None], scores, MASKED)
    new_max = jnp.maximum(running_max, jnp.max(scores, axis=-1))
    probs = jnp.where(allowed[None], jnp.exp(scores - new_max[..., None]), 0.0)
    factor = jnp.exp(running_max - new_max)
    running_sum = running_sum * factor + jnp.sum(probs, axis=-1)
    summed = jnp.einsum(
        "hbk,khd->hbd", probs.astype(jnp.bfloat16), value_block, preferred_element_type=jnp.float32
    )
    weighted = weighted * factor[..., None] + summed
    return (new_max, running_sum, weighted)


def causal_blocks(queries, keys_local, values_local):
    length, head_count, head_width = queries.shape
    block_count = length // BLOCK
    factor = 1.0 / math.sqrt(head_width)
    row_ids = jnp.arange(BLOCK, dtype=jnp.int32)

    def query_block_out(block_index):
        query_block = lax.dynamic_slice_in_dim(queries, block_index * BLOCK, BLOCK, 0)

        def advance(key_index, carried):
            key_block = lax.dynamic_slice_in_dim(keys_local, key_index * BLOCK, BLOCK, 0)
            value_block = lax.dynamic_slice_in_dim(values_local, key_index * BLOCK, BLOCK, 0)
            scores = (
                jnp.einsum(
                    "bhd,khd->hbk", query_block, key_block, preferred_element_type=jnp.float32
                )
                * factor
            )
            allowed = (key_index * BLOCK + row_ids)[None, :] <= (block_index * BLOCK + row_ids)[
                :, None
            ]
            return update_block(carried, scores, allowed, value_block)

        initial = (
            jnp.full((head_count, BLOCK), MASKED, jnp.float32),
            jnp.zeros((head_count, BLOCK), jnp.float32),
            jnp.zeros((head_count, BLOCK, head_width), jnp.float32),
        )
        running_max, running_sum, weighted = lax.fori_loop(0, block_index + 1, advance, initial)
        return weighted / running_sum[..., None]

    result = lax.map(query_block_out, jnp.arange(block_count, dtype=jnp.int32))
    return jnp.transpose(result, (0, 2, 1, 3)).reshape(length, head_count, head_width)


def on_device(query_states, key_states, value_states, query_gain, key_gain):
    tok_count = query_states.shape[0]
    offset = lax.axis_index("seq") * tok_count
    positions = offset + jnp.arange(tok_count, dtype=jnp.int32)
    query_rot = rotate(query_states, query_gain, positions)
    group_size = query_states.shape[1] // key_states.shape[1]
    key_rot = rotate(key_states, key_gain, positions)
    key_wide = jnp.repeat(key_rot, group_size, axis=1)
    value_wide = jnp.repeat(value_states, group_size, axis=1)
    query_all, key_all, value_all = (
        lax.all_to_all(query_rot, "seq", split_axis=1, concat_axis=0, tiled=True),
        lax.all_to_all(key_wide, "seq", split_axis=1, concat_axis=0, tiled=True),
        lax.all_to_all(value_wide, "seq", split_axis=1, concat_axis=0, tiled=True),
    )
    attended = causal_blocks(query_all, key_all, value_all)
    return lax.all_to_all(
        attended.astype(jnp.bfloat16), "seq", split_axis=0, concat_axis=1, tiled=True
    )


def solution(mesh):
    placed = (
        P(("groups", "seq"), None, None),
        P(("groups", "seq"), None, None),
        P(("groups", "seq"), None, None),
        P(),
        P(),
    )
    return jax.shard_map(
        on_device,
        mesh=mesh,
        in_specs=placed,
        out_specs=P(("groups", "seq"), None, None),
        check_vma=False,
    )
```

profile of v0, /device:TPU:0, one launch (start us, length us, event | category | flops | bytes accessed | tf_op | source)
XLA Modules:
  0.0 94.2 jit_solution(4159948933605750573)
XLA Ops:
  0.0 1.4 %fusion.25 = f32[112,16]{0,1:T(8,128)S(1)} fusion(bf16[112,16,128]{2,1,0:T(8,128)(2,1)} %param.9), kind=kLoop, calls=%fused_computation.30 | loop fusion | flops 686336 | bytes 465920 | tf_op jit(solution)/shard_map/reduce_sum | solution.py:18
  1.4 0.0 copy-start
  1.4 0.0 copy-start.2
  1.4 1.4 %fusion.26 = f32[112,16,128]{2,0,1:T(8,128)S(1)} fusion(f32[128]{0:T(128)} %param.12, f32[112,16]{0,1:T(8,128)S(1)} %add_rsqrt_fusion, bf16[112,16,128]{2,1,0:T(8,128)(2,1)} %param.9), kind=kLoop, calls=%fused_computation.31 | loop fusion | flops 688128 | bytes 1383936 | tf_op jit(solution)/shard_map/mul | solution.py:19
  2.8 0.3 multiply_cosine_fusion
  3.1 0.4 subtract_convert_fusion
  3.5 1.0 %pad_maximum_fusion = bf16[112,16,128]{2,0,1:T(8,128)(2,1)} fusion(bf16[112,16,64]{2,0,1:T(8,128)(2,1)S(1)} %get-tuple-element.270, bf16[112,16,64]{2,0,1:T(8,128)(2,1)S(1)} %get-tuple-element.269), kind=kLoop, calls=%fused_computation.39 | loop fusion | flops 917504 | bytes 917504 | tf_op jit(solution)/shard_map/concatenate | solution.py:27
  4.5 0.0 copy-start.1
  4.5 7.5 %all-to-all-start = ((bf16[112,16,128]{2,0,1:T(8,128)(2,1)}), bf16[112,16,128]{2,0,1:T(8,128)(2,1)S(1)}, u32[]{:S(2)}, u32[]{:S(2)}) async-start(bf16[112,16,128]{2,0,1:T(8,128)(2,1)} %pad_maximum_fusion), calls=%async_computation | async-start | bytes 917504 | tf_op jit(solution)/shard_map/all_to_all | solution.py:96
  12.1 0.0 copy-done
  12.1 0.2 fusion.27
  12.3 0.1 copy.31
  12.3 0.1 copy.32
  12.4 0.0 copy-done.2
  12.4 0.2 fusion.28
  12.6 0.3 subtract_convert_fusion.1
  12.9 0.1 pad_maximum_fusion.1
  13.1 12.2 %all-to-all-done = bf16[112,16,128]{2,0,1:T(8,128)(2,1)S(1)} async-done(((bf16[112,16,128]{2,0,1:T(8,128)(2,1)}), bf16[112,16,128]{2,0,1:T(8,128)(2,1)S(1)}, u32[]{:S(2)}, u32[]{:S(2)}) %all-to-all-start) | async-done | bytes 458784 | tf_op jit(solution)/shard_map/all_to_all | solution.py:96
  25.3 0.8 broadcast_in_dim.16
  26.1 3.9 %all-to-all-start.1 = ((bf16[112,16,128]{2,0,1:T(8,128)(2,1)}), bf16[112,16,128]{2,0,1:T(8,128)(2,1)S(1)}, u32[]{:S(2)}, u32[]{:S(2)}) async-start(bf16[112,16,128]{2,0,1:T(8,128)(2,1)} %bitcast.3), calls=%async_computation.1 | async-start | bytes 917504 | tf_op jit(solution)/shard_map/all_to_all | solution.py:97
  30.0 0.0 copy-done.1
  30.1 13.2 %all-to-all-done.1 = bf16[112,16,128]{2,0,1:T(8,128)(2,1)S(1)} async-done(((bf16[112,16,128]{2,0,1:T(8,128)(2,1)}), bf16[112,16,128]{2,0,1:T(8,128)(2,1)S(1)}, u32[]{:S(2)}, u32[]{:S(2)}) %all-to-all-start.1) | async-done | bytes 458784 | tf_op jit(solution)/shard_map/all_to_all | solution.py:97
  43.3 0.8 broadcast_in_dim.17
  44.1 3.9 %all-to-all-start.2 = ((bf16[112,16,128]{2,0,1:T(8,128)(2,1)}), bf16[112,16,128]{2,0,1:T(8,128)(2,1)S(1)}, u32[]{:S(2)}, u32[]{:S(2)}) async-start(bf16[112,16,128]{2,0,1:T(8,128)(2,1)} %bitcast.7), calls=%async_computation.2 | async-start | bytes 917504 | tf_op jit(solution)/shard_map/all_to_all | solution.py:98
  48.0 13.2 %all-to-all-done.2 = bf16[112,16,128]{2,0,1:T(8,128)(2,1)S(1)} async-done(((bf16[112,16,128]{2,0,1:T(8,128)(2,1)}), bf16[112,16,128]{2,0,1:T(8,128)(2,1)S(1)}, u32[]{:S(2)}, u32[]{:S(2)}) %all-to-all-start.2) | async-done | bytes 458784 | tf_op jit(solution)/shard_map/all_to_all | solution.py:98
  61.3 13.1 %while.32 = (s32[]{:T(128)}, bf16[2,1,896,128]{3,2,1,0:T(8,128)(2,1)S(1)}, s32[2]{0:T(128)S(1)}, bf16[1792,1,128]{2,0,1:T(8,128)(2,1)S(1)}, bf16[1792,1,128]{2,0...) while((s32[]{:T(128)}, ...), condition=%wide.region_7.8_spmd.clone.clone, body=%wide.region_2.7_spmd.clone.clone.sunk | while | flops 424235392 | bytes 13193294 | solution.py:82
  61.3 0.6 dynamic_slice.39
  63.1 3.0 %while.33 = (s32[]{:T(128)}, f32[1,896]{1,0:T(1,128)S(1)}, f32[1,896]{1,0:T(1,128)S(1)}, f32[1,896,128]{2,1,0:T(8,128)S(1)}, s32[]{:T(128)}, /*index=5*/s32[896]...) while((s32[]{:T(128)}, f32[1,896]{1,0:T(1,128)S(1)}, ...), condition=%wide.region_6.6_spmd.clone, body=%wide.region_3.5_spmd.clone.sunk | while | flops 424120704 | bytes 11335883 | solution.py:79
  63.1 0.6 fusion.37
  63.8 0.9 fusion.39
  64.8 1.3 %fusion.40 = f32[1,896,128]{2,1,0:T(8,128)S(1)} fusion(f32[896,896]{1,0:T(8,128)S(1)} %get-tuple-element.410, f32[896]{0:T(1024)S(1)} %get-tuple-element.411, s32[896]{0:T(1024)S(1)} %get-tuple-element.406, s32[896]{0:T(1024)S(1)} %get-tuple-element.407, f32[1,896,128]{2,1,0:T(8,128)S(1)} %get-tuple-element.430, ...), kind=kOutput, calls=%fused_computation.8.clone.1 | convolution fusion | flops 210567168 | bytes 4374532 | tf_op jit(solution)/shard_map/while/body/eval_jaxpr/while/body/hbk,khd->hbd/dot_general | solution.py:44
  66.1 0.2 bitcast_dynamic-update-slice_fusion.2
  66.3 0.6 dynamic_slice.39
  68.2 5.9 %while.33 = (s32[]{:T(128)}, f32[1,896]{1,0:T(1,128)S(1)}, f32[1,896]{1,0:T(1,128)S(1)}, f32[1,896,128]{2,1,0:T(8,128)S(1)}, s32[]{:T(128)}, /*index=5*/s32[896]...) while((s32[]{:T(128)}, f32[1,896]{1,0:T(1,128)S(1)}, ...), condition=%wide.region_6.6_spmd.clone, body=%wide.region_3.5_spmd.clone.sunk | while | flops 424120704 | bytes 11335883 | solution.py:79
  68.2 0.6 fusion.37
  68.9 0.9 fusion.39
  69.8 1.3 %fusion.40 = f32[1,896,128]{2,1,0:T(8,128)S(1)} fusion(f32[896,896]{1,0:T(8,128)S(1)} %get-tuple-element.410, f32[896]{0:T(1024)S(1)} %get-tuple-element.411, s32[896]{0:T(1024)S(1)} %get-tuple-element.406, s32[896]{0:T(1024)S(1)} %get-tuple-element.407, f32[1,896,128]{2,1,0:T(8,128)S(1)} %get-tuple-element.430, ...), kind=kOutput, calls=%fused_computation.8.clone.1 | convolution fusion | flops 210567168 | bytes 4374532 | tf_op jit(solution)/shard_map/while/body/eval_jaxpr/while/body/hbk,khd->hbd/dot_general | solution.py:44
  71.2 0.6 fusion.37
  71.8 0.9 fusion.39
  72.8 1.3 %fusion.40 = f32[1,896,128]{2,1,0:T(8,128)S(1)} fusion(f32[896,896]{1,0:T(8,128)S(1)} %get-tuple-element.410, f32[896]{0:T(1024)S(1)} %get-tuple-element.411, s32[896]{0:T(1024)S(1)} %get-tuple-element.406, s32[896]{0:T(1024)S(1)} %get-tuple-element.407, f32[1,896,128]{2,1,0:T(8,128)S(1)} %get-tuple-element.430, ...), kind=kOutput, calls=%fused_computation.8.clone.1 | convolution fusion | flops 210567168 | bytes 4374532 | tf_op jit(solution)/shard_map/while/body/eval_jaxpr/while/body/hbk,khd->hbd/dot_general | solution.py:44
  74.1 0.2 bitcast_dynamic-update-slice_fusion.2
  74.4 0.5 broadcast.135
  74.9 1.0 %reduce.13 = bf16[1792,128]{1,0:T(8,128)(2,1)S(1)} reduce(bf16[1792,1,128]{2,0,1:T(8,128)(2,1)S(1)} %bitcast.86, bf16[]{:T(256)} %broadcast.135), dimensions={1}, to_apply=%copy.36.reduce_sub_computation | reduce | bytes 917506 | tf_op jit(solution)/shard_map/convert_element_type | solution.py:102
  75.8 0.1 reshape.161
  76.0 16.9 %all_to_all.72 = bf16[16,2,7168]{2,1,0:T(2,128)(2,1)S(1)} all-to-all(bf16[16,2,7168]{2,1,0:T(2,128)(2,1)S(1)} %reshape.161), channel_id=1, replica_groups=mesh['groups'=2,'seq'=16] {'seq'}, dimensions={0} | all-to-all | bytes 917504 | tf_op jit(solution)/shard_map/all_to_all | solution.py:101
  92.9 0.4 reshape.162
  93.3 0.1 copy.38
  93.3 0.9 copy.37
  (32 shorter events, 0.4 us)
Async XLA Ops:
  1.4 10.6 %copy-start = (bf16[112,8,128]{2,1,0:T(8,128)(2,1)S(1)}, bf16[112,8,128]{2,1,0:T(8,128)(2,1)}, u32[]{:S(2)}) copy-start(bf16[112,8,128]{2,1,0:T(8,128)(2,1)} %param.10) | copy-start | bytes 688132
  1.4 11.0 %copy-start.2 = (f32[128]{0:T(128)S(1)}, f32[128]{0:T(128)}, u32[]{:S(2)}) copy-start(f32[128]{0:T(128)} %param.13) | copy-start | bytes 1540
  4.5 25.5 %copy-start.1 = (bf16[112,8,128]{2,1,0:T(8,128)(2,1)S(1)}, bf16[112,8,128]{2,1,0:T(8,128)(2,1)}, u32[]{:S(2)}) copy-start(bf16[112,8,128]{2,1,0:T(8,128)(2,1)} %param.11) | copy-start | bytes 688132
  4.5 20.8 %all-to-all-start = ((bf16[112,16,128]{2,0,1:T(8,128)(2,1)}), bf16[112,16,128]{2,0,1:T(8,128)(2,1)S(1)}, u32[]{:S(2)}, u32[]{:S(2)}) async-start(bf16[112,16,128]{2,0,1:T(8,128)(2,1)} %pad_maximum_fusion), calls=%async_computation | async-start | bytes 917504 | tf_op jit(solution)/shard_map/all_to_all | solution.py:96
  26.1 17.2 %all-to-all-start.1 = ((bf16[112,16,128]{2,0,1:T(8,128)(2,1)}), bf16[112,16,128]{2,0,1:T(8,128)(2,1)S(1)}, u32[]{:S(2)}, u32[]{:S(2)}) async-start(bf16[112,16,128]{2,0,1:T(8,128)(2,1)} %bitcast.3), calls=%async_computation.1 | async-start | bytes 917504 | tf_op jit(solution)/shard_map/all_to_all | solution.py:97
  44.1 17.2 %all-to-all-start.2 = ((bf16[112,16,128]{2,0,1:T(8,128)(2,1)}), bf16[112,16,128]{2,0,1:T(8,128)(2,1)S(1)}, u32[]{:S(2)}, u32[]{:S(2)}) async-start(bf16[112,16,128]{2,0,1:T(8,128)(2,1)} %bitcast.7), calls=%async_computation.2 | async-start | bytes 917504 | tf_op jit(solution)/shard_map/all_to_all | solution.py:98
where the time goes:
time: 94.8 us; the launch traced here: 94.2 us
  waiting for transfers between devices  38.7 us (41%)
  blocking collectives  16.9 us (18%)
  starting transfers between devices  15.3 us (16%)
  other arithmetic  9.6 us (10%)
  matrix products  5.78 us (6%)
  local copies, waits for them, and re-layouts  5.13 us (5%)
  loops' own time  2.62 us (3%)
    all_to_all x1, blocking collectives, on_device(): lax.all_to_all(attended.astype(jnp.bfloat16), 'seq', split_axis=0, concat...  16.9 us
    all_to_all x1, waiting for transfers between devices, on_device(): lax.all_to_all(value_wide, 'seq', split_axis=1, concat_axis=0, tiled=True)  13.2 us
    all_to_all x1, waiting for transfers between devices, on_device(): lax.all_to_all(key_wide, 'seq', split_axis=1, concat_axis=0, tiled=True)  13.2 us
    all_to_all x1, waiting for transfers between devices, on_device(): lax.all_to_all(query_rot, 'seq', split_axis=1, concat_axis=0, tiled=True)  12.2 us
    all_to_all x1, starting transfers between devices, on_device(): lax.all_to_all(query_rot, 'seq', split_axis=1, concat_axis=0, tiled=True)  7.52 us
    all_to_all x1, starting transfers between devices, on_device(): lax.all_to_all(key_wide, 'seq', split_axis=1, concat_axis=0, tiled=True)  3.89 us
    all_to_all x1, starting transfers between devices, on_device(): lax.all_to_all(value_wide, 'seq', split_axis=1, concat_axis=0, tiled=True)  3.89 us
    dot_general x3, matrix products, update_block(): jnp.einsum('hbk,khd->hbd', probs.astype(jnp.bfloat16), value_block, prefe...  3.84 us
  transfers between devices with their start and end apart: 3, of which 3 were waited for; matrix products, arithmetic and copies ran while one was open for 1% of the time, Pallas kernels for 0%

commit v1 on v0

v1 whole, which is shorter than its diff:
```python
import functools
import math

import jax
import jax.numpy as jnp
import numpy as np
from jax import lax
from jax.experimental import pallas as pl
from jax.experimental.pallas import tpu as pltpu
from jax.sharding import PartitionSpec as P

ROPE_BASE = 1000000.0
EPSILON = 1e-06
MASKED = -1e30
VMEM_LIMIT = 48 * 1024 * 1024


def rope_table(length, width):
    half = width // 2
    frequency = np.float64(ROPE_BASE) ** (-(np.arange(half, dtype=np.float64) * 2.0 / width))
    angles = np.arange(length, dtype=np.float32)[:, None] * frequency.astype(np.float32)[None, :]
    wide = angles.astype(np.float64)
    return np.concatenate([np.cos(wide), np.sin(wide)], axis=-1).astype(np.float32)


def pack_kernel(rep, q_ref, k_ref, v_ref, table_ref, qg_ref, kg_ref, out_ref, qf_ref, kf_ref, vf_ref):
    tokens, heads, width = q_ref.shape
    kv_heads = k_ref.shape[1]
    chips, rows = out_ref.shape[:2]
    per_chip = rows - 2
    qf_ref[...] = q_ref[...].astype(jnp.float32).reshape(tokens * heads, width)
    kf_ref[...] = k_ref[...].astype(jnp.float32).reshape(tokens * kv_heads, width)
    vf_ref[...] = v_ref[...].astype(jnp.float32).reshape(tokens * kv_heads, width)
    table = table_ref[...]
    swapped = pltpu.roll(table, width // 2, 1)
    first = lax.broadcasted_iota(jnp.int32, table.shape, 1) < width // 2
    cosine = jnp.where(first, table, swapped)
    sine = jnp.where(first, -swapped, table)

    def rotate(floats, gain):
        mean_square = jnp.mean(floats * floats, axis=-1, keepdims=True)
        normed = floats * lax.rsqrt(mean_square + EPSILON) * gain
        turned = pltpu.roll(normed, width // 2, 1)
        return (normed * cosine + turned * sine).astype(jnp.bfloat16)

    query_gain, key_gain = qg_ref[...], kg_ref[...]
    for head in range(heads):
        floats = qf_ref[pl.ds(head, tokens, stride=heads), :]
        out_ref[head // per_chip, head % per_chip] = rotate(floats, query_gain)
    for head in range(kv_heads):
        floats = kf_ref[pl.ds(head, tokens, stride=kv_heads), :]
        rotated = rotate(floats, key_gain)
        values = vf_ref[pl.ds(head, tokens, stride=kv_heads), :].astype(jnp.bfloat16)
        for copy in range(rep):
            out_ref[head * rep + copy, per_chip] = rotated
            out_ref[head * rep + copy, per_chip + 1] = values


def attention_kernel(core_ref, x_ref, other_ref, out_ref):
    blocks, rows, tokens, width = x_ref.shape
    per_chip = rows - 2
    core = core_ref[0]
    scale = math.log2(math.e) / math.sqrt(width)
    keys_own = x_ref[:, per_chip].reshape(blocks * tokens, width)
    values_own = x_ref[:, per_chip + 1].reshape(blocks * tokens, width)
    keys_other = other_ref[:, 0].reshape(blocks * tokens, width)
    values_other = other_ref[:, 1].reshape(blocks * tokens, width)
    contract = (((1,), (1,)), ((), ()))
    for block in range(blocks):
        queries = x_ref[block, :per_chip].reshape(per_chip * tokens, width)
        reach = (block + 1) * tokens
        own = lax.dot_general(queries, keys_own[:reach], contract, preferred_element_type=jnp.float32)
        other = lax.dot_general(queries, keys_other[:reach], contract, preferred_element_type=jnp.float32)
        row = lax.broadcasted_iota(jnp.int32, (per_chip, tokens, reach), 1).reshape(per_chip * tokens, reach)
        column = lax.broadcasted_iota(jnp.int32, (per_chip * tokens, reach), 1)
        own = jnp.where(column <= row + block * tokens, own, MASKED)
        other = jnp.where(column < (block + core) * tokens, other, MASKED)
        highest = jnp.maximum(
            jnp.max(own, axis=-1, keepdims=True), jnp.max(other, axis=-1, keepdims=True)
        )
        probs_own = jnp.exp2((own - highest) * scale)
        probs_other = jnp.exp2((other - highest) * scale)
        total = jnp.sum(probs_own, axis=-1, keepdims=True) + jnp.sum(probs_other, axis=-1, keepdims=True)
        summed = jnp.dot(
            probs_own.astype(jnp.bfloat16), values_own[:reach], preferred_element_type=jnp.float32
        ) + jnp.dot(
            probs_other.astype(jnp.bfloat16), values_other[:reach], preferred_element_type=jnp.float32
        )
        out_ref[block] = (summed / total).astype(jnp.bfloat16).reshape(per_chip, tokens, width)


def looped_kernel(core_ref, x_ref, other_ref, out_ref):
    _, rows, tokens, width = x_ref.shape
    per_chip = rows - 2
    core = core_ref[0]
    block = pl.program_id(0)
    scale = math.log2(math.e) / math.sqrt(width)
    contract = (((1,), (1,)), ((), ()))
    queries = x_ref[block, :per_chip].reshape(per_chip * tokens, width)
    row = lax.broadcasted_iota(jnp.int32, (per_chip, tokens, tokens), 1).reshape(per_chip * tokens, tokens)
    column = lax.broadcasted_iota(jnp.int32, (per_chip * tokens, tokens), 1)

    def merge(carried, keys, values, allowed):
        highest, total, weighted = carried
        scores = lax.dot_general(queries, keys, contract, preferred_element_type=jnp.float32)
        scores = jnp.where(allowed, scores, MASKED)
        new = jnp.maximum(highest, jnp.max(scores, axis=-1, keepdims=True))
        probs = jnp.exp2((scores - new) * scale)
        factor = jnp.exp2((highest - new) * scale)
        total = total * factor + jnp.sum(probs, axis=-1, keepdims=True)
        summed = jnp.dot(probs.astype(jnp.bfloat16), values, preferred_element_type=jnp.float32)
        return new, total, weighted * factor + summed

    def advance(index, carried):
        behind = (block - index) * tokens
        carried = merge(carried, x_ref[index, per_chip], x_ref[index, per_chip + 1], column <= row + behind)
        return merge(carried, other_ref[index, 0], other_ref[index, 1], column < behind + core * tokens)

    initial = (
        jnp.full((per_chip * tokens, 1), MASKED, jnp.float32),
        jnp.zeros((per_chip * tokens, 1), jnp.float32),
        jnp.zeros((per_chip * tokens, width), jnp.float32),
    )
    _, total, weighted = lax.fori_loop(0, block + 1, advance, initial)
    out_ref[block] = (weighted / total).astype(jnp.bfloat16).reshape(per_chip, tokens, width)


def on_device(length, devices, query_states, key_states, value_states, query_gain, key_gain):
    tokens, heads, width = query_states.shape
    kv_heads = key_states.shape[1]
    chips = devices // 2
    per_chip = heads // chips
    rep = (heads // kv_heads) // per_chip
    me = lax.axis_index("seq")
    core = lax.rem(me, 2)
    same_core = [list(range(start, devices, 2)) for start in range(2)]
    swap = [(device, device ^ 1) for device in range(devices)]
    table = lax.dynamic_slice_in_dim(jnp.asarray(rope_table(length, width)), me * tokens, tokens, 0)
    vmem = pl.BlockSpec(memory_space=pltpu.VMEM)
    packed = pl.pallas_call(
        functools.partial(pack_kernel, rep),
        out_shape=jax.ShapeDtypeStruct((chips, per_chip + 2, tokens, width), jnp.bfloat16),
        in_specs=[vmem] * 6,
        out_specs=vmem,
        scratch_shapes=[
            pltpu.VMEM((tokens * heads, width), jnp.float32),
            pltpu.VMEM((tokens * kv_heads, width), jnp.float32),
            pltpu.VMEM((tokens * kv_heads, width), jnp.float32),
        ],
        compiler_params=pltpu.CompilerParams(vmem_limit_bytes=VMEM_LIMIT),
        name="pack",
    )(query_states, key_states, value_states, table, query_gain[None], key_gain[None])
    arrived = lax.all_to_all(
        packed, "seq", split_axis=0, concat_axis=0, axis_index_groups=same_core, tiled=True
    )
    other = lax.ppermute(arrived[:, per_chip:], "seq", swap)
    short = chips <= 8
    attended = pl.pallas_call(
        attention_kernel if short else looped_kernel,
        grid=() if short else (chips,),
        out_shape=jax.ShapeDtypeStruct((chips, per_chip, tokens, width), jnp.bfloat16),
        in_specs=[pl.BlockSpec(memory_space=pltpu.SMEM), vmem, vmem],
        out_specs=vmem,
        compiler_params=pltpu.CompilerParams(vmem_limit_bytes=VMEM_LIMIT),
        name="attention",
    )(core[None], arrived, other)
    returned = lax.all_to_all(
        attended, "seq", split_axis=0, concat_axis=0, axis_index_groups=same_core, tiled=True
    )
    return jnp.transpose(returned.reshape(heads, tokens, width), (1, 0, 2))


def solution(mesh):
    devices = mesh.shape["seq"]
    groups = mesh.shape["groups"]
    placed = P(("groups", "seq"), None, None)

    def run(query_states, key_states, value_states, query_gain, key_gain):
        length = query_states.shape[0] // groups
        return jax.shard_map(
            functools.partial(on_device, length, devices),
            mesh=mesh,
            in_specs=(placed, placed, placed, P(), P()),
            out_specs=placed,
            check_vma=False,
        )(query_states, key_states, value_states, query_gain, key_gain)

    return run
```

time: 94.8 us -> 61.5 us (0.65)
  waiting for transfers between devices: 38.7 us -> 1.8 us
  blocking collectives: 16.9 us -> 46.9 us
  starting transfers between devices: 15.3 us -> 0.07 us
  other arithmetic: 9.6 us -> 0 us
  Pallas kernels: 0 us -> 7.05 us
  matrix products: 5.78 us -> 0 us
  loops' own time: 2.62 us -> 0 us
    all_to_all x3 -> x0, waiting for transfers between devices: 38.7 us -> none  [the longest x1 13.2 us: on_device(): lax.all_to_all(value_wide, 'seq', split_axis=1, concat_axis=0, tiled=True)]
    all_to_all x1 -> x2, blocking collectives: 16.9 us -> 46.9 us  [the longest x1 30.4 us: on_device(): lax.all_to_all(packed, 'seq', split_axis=0, concat_axis=0, axis_index_gro...]
    all_to_all x3 -> x0, starting transfers between devices: 15.3 us -> none  [the longest x1 7.52 us: on_device(): lax.all_to_all(query_rot, 'seq', split_axis=1, concat_axis=0, tiled=True)]
    pallas_call x0 -> x2, Pallas kernels: none -> 7.05 us  [the longest x1 4.25 us: on_device(): pl.pallas_call(attention_kernel if short else looped_kernel, grid=() if s...]
    dot_general x6 -> x0, matrix products: 5.78 us -> none  [the longest x3 3.84 us: update_block(): jnp.einsum('hbk,khd->hbd', probs.astype(jnp.bfloat16), value_block, prefe...]
    reduce_sum x5 -> x0, other arithmetic: 4.28 us -> none  [the longest x3 2.72 us: update_block(): running_sum = running_sum * factor + jnp.sum(probs, axis=-1)]
    unnamed x10, local copies, waits for them, and re-layouts: 0.58 us -> 3.56 us
    another operation x3 -> x0, loops' own time: 2.62 us -> none  [the longest x1 2.39 us: causal_blocks(): result = lax.map(query_block_out, jnp.arange(block_count, dtype=jnp.int32))]
  transfers between devices with their start and end apart: 3 -> 1, of which waited for: 3 -> 1; matrix products, arithmetic and copies ran while one was open for 1% -> 0% of each run, Pallas kernels for 0% -> 0%
where the time goes in v1:
time: 61.5 us; the launch traced here: 61.2 us
  blocking collectives  46.9 us (76%)
  Pallas kernels  7.05 us (11%)
  local copies, waits for them, and re-layouts  5.3 us (9%)
  waiting for transfers between devices  1.8 us (3%)
    all_to_all x1, blocking collectives, on_device(): lax.all_to_all(packed, 'seq', split_axis=0, concat_axis=0, axis_index_gro...  30.4 us
    all_to_all x1, blocking collectives, on_device(): lax.all_to_all(attended, 'seq', split_axis=0, concat_axis=0, axis_index_g...  16.5 us
    pallas_call x1, Pallas kernels, on_device(): pl.pallas_call(attention_kernel if short else looped_kernel, grid=() if s...  4.25 us
    unnamed x10, local copies, waits for them, and re-layouts  3.56 us
    pallas_call x1, Pallas kernels, on_device(): pl.pallas_call(functools.partial(pack_kernel, rep), out_shape=jax.ShapeDt...  2.8 us
    ppermute x1, waiting for transfers between devices, on_device(): other = lax.ppermute(arrived[:, per_chip:], 'seq', swap)  1.8 us
  transfers between devices with their start and end apart: 1, of which 1 were waited for; matrix products, arithmetic and copies ran while one was open for 0% of the time, Pallas kernels for 0%

profile of v1, /device:TPU:0, one launch (start us, length us, event | category | flops | bytes accessed | tf_op | source)
XLA Modules:
  0.0 61.2 jit_solution(5480104955700428387)
XLA Ops:
  0.0 0.8 %constant_dynamic-slice_fusion.table_ref = f32[112,128]{1,0:T(8,128)S(1)} fusion(f32[1792,128]{1,0:T(8,128)} %constant.16.clone, s32[]{:T(128)S(6)} %select_n.3), kind=kLoop, calls=%fused_computation.1 | loop fusion | bytes 114692 | tf_op jit(solution)/shard_map/dynamic_slice | solution.py:138
  0.8 0.0 copy-start.3
  0.8 0.0 copy-start.4
  0.8 0.7 %copy-done.3 = f32[128]{0:T(128)S(1)} copy-done((f32[128]{0:T(128)S(1)}, f32[128]{0:T(128)}, u32[]{:S(2)}) %copy-start.3) | copy-done | bytes 536
  1.5 0.0 copy-done.4
  1.5 0.0 copy-start
  1.5 1.0 %copy-done = bf16[112,16,128]{2,1,0:T(8,128)(2,1)S(1)} copy-done((bf16[112,16,128]{2,1,0:T(8,128)(2,1)S(1)}, bf16[112,16,128]{2,1,0:T(8,128)(2,1)}, u32[]{:S(2)}) %copy-start) | copy-done | bytes 458776
  2.5 0.0 copy-start.1
  2.5 0.9 %copy-done.1 = bf16[112,8,128]{2,1,0:T(8,128)(2,1)S(1)} copy-done((bf16[112,8,128]{2,1,0:T(8,128)(2,1)S(1)}, bf16[112,8,128]{2,1,0:T(8,128)(2,1)}, u32[]{:S(2)}) %copy-start.1) | copy-done | bytes 229400
  3.5 0.0 copy-start.2
  3.5 0.9 %copy-done.2 = bf16[112,8,128]{2,1,0:T(8,128)(2,1)S(1)} copy-done((bf16[112,8,128]{2,1,0:T(8,128)(2,1)S(1)}, bf16[112,8,128]{2,1,0:T(8,128)(2,1)}, u32[]{:S(2)}) %copy-start.2) | copy-done | bytes 229400
  4.4 2.8 %pack.1 = bf16[8,4,112,128]{3,2,1,0:T(8,128)(2,1)S(1)} custom-call(bf16[112,16,128]{2,1,0:T(8,128)(2,1)S(1)} %copy-done, bf16[112,8,128]{2,1,0:T(8,128)(2,1)S(1)} %copy-done.1, bf16[112,8,128]{2,1,0:T(8,128)(2,1)S(1)} %copy-done.2, f32[112,128]{1,0:T(8,128)S(1)} %constant_dynamic-slice_fusion.table_ref, f32[1,128]{1,0:T(1,128)S(1)} %bitcast.7, ...), custom_call_target="tpu_custom_call" | custom-call | tf_op jit(solution)/shard_map/pack/pallas_call | solution.py:140
  7.2 30.4 %all_to_all.10.x_ref = bf16[8,4,112,128]{3,2,1,0:T(8,128)(2,1)S(1)} all-to-all(bf16[8,4,112,128]{3,2,1,0:T(8,128)(2,1)S(1)} %pack.1), channel_id=1, replica_groups={{0,2,4,6,8,10,12,14},{1,3,5,7,9,11,13,15},{16,18,20,22,24,26,28,30},{17..., dimensions={0} | all-to-all | bytes 1835008 | tf_op jit(solution)/shard_map/all_to_all | solution.py:153
  37.6 0.1 collective-permute-start
  37.7 1.8 %collective-permute-done.other_ref = bf16[8,2,112,128]{3,2,1,0:T(8,128)(2,1)S(1)} collective-permute-done((bf16[8,2,112,128]{3,2,1,0:T(8,128)(2,1)S(1)}, bf16[8,2,112,128]{3,2,1,0:T(8,128)(2,1)S(1)}, u32[]{:S(2)}, u32[]{:S(2)}) %collective-permute-start) | collective-permute-done | bytes 458784 | tf_op jit(solution)/shard_map/ppermute | solution.py:156
  39.5 4.2 %attention.1 = bf16[8,2,112,128]{3,2,1,0:T(8,128)(2,1)S(1)} custom-call(s32[1]{0:T(128)} %bitcast.core_ref, bf16[8,4,112,128]{3,2,1,0:T(8,128)(2,1)S(1)} %all_to_all.10.x_ref, bf16[8,2,112,128]{3,2,1,0:T(8,128)(2,1)S(1)} %collective-permute-done.other_ref), custom_call_target="tpu_custom_call" | custom-call | tf_op jit(solution)/shard_map/attention/pallas_call | solution.py:158
  43.8 16.5 %all_to_all.11 = bf16[8,2,112,128]{3,2,1,0:T(8,128)(2,1)S(1)} all-to-all(bf16[8,2,112,128]{3,2,1,0:T(8,128)(2,1)S(1)} %attention.1), channel_id=1, replica_groups={{0,2,4,6,8,10,12,14},{1,3,5,7,9,11,13,15},{16,18,20,22,24,26,28,30},{17..., dimensions={0} | all-to-all | bytes 917504 | tf_op jit(solution)/shard_map/all_to_all | solution.py:167
  60.3 0.9 %copy.9 = bf16[16,112,128]{2,0,1:T(8,128)(2,1)} copy(bf16[16,112,128]{2,1,0:T(8,128)(2,1)S(1)} %bitcast.9) | data formatting | bytes 917504 | tf_op jit(solution)/shard_map/reshape | solution.py:170
  (1 shorter events, 0.0 us)
Async XLA Ops:
  0.8 0.7 %copy-start.3 = (f32[128]{0:T(128)S(1)}, f32[128]{0:T(128)}, u32[]{:S(2)}) copy-start(f32[128]{0:T(128)} %param.9) | copy-start | bytes 1540
  0.8 0.7 %copy-start.4 = (f32[128]{0:T(128)S(1)}, f32[128]{0:T(128)}, u32[]{:S(2)}) copy-start(f32[128]{0:T(128)} %param.10) | copy-start | bytes 1540
  1.5 1.0 %copy-start = (bf16[112,16,128]{2,1,0:T(8,128)(2,1)S(1)}, bf16[112,16,128]{2,1,0:T(8,128)(2,1)}, u32[]{:S(2)}) copy-start(bf16[112,16,128]{2,1,0:T(8,128)(2,1)} %q_ref.1) | copy-start | bytes 1376260
  2.5 0.9 %copy-start.1 = (bf16[112,8,128]{2,1,0:T(8,128)(2,1)S(1)}, bf16[112,8,128]{2,1,0:T(8,128)(2,1)}, u32[]{:S(2)}) copy-start(bf16[112,8,128]{2,1,0:T(8,128)(2,1)} %k_ref.1) | copy-start | bytes 688132
  3.5 0.9 %copy-start.2 = (bf16[112,8,128]{2,1,0:T(8,128)(2,1)S(1)}, bf16[112,8,128]{2,1,0:T(8,128)(2,1)}, u32[]{:S(2)}) copy-start(bf16[112,8,128]{2,1,0:T(8,128)(2,1)} %v_ref.1) | copy-start | bytes 688132
  37.6 1.9 %collective-permute-start = (bf16[8,2,112,128]{3,2,1,0:T(8,128)(2,1)S(1)}, bf16[8,2,112,128]{3,2,1,0:T(8,128)(2,1)S(1)}, u32[]{:S(2)}, u32[]{:S(2)}) collective-permute-start(bf16[8,2,112,128]{3,2,1,0:T(8,128)(2,1)S(1)} %slice.4), channel_id=1, source_target_pairs={{0,1},{1,0},{2,3},{3,2},{4,5},{5,4},{6,7},{7,6},{8,9},{9,8},{10,11... | collective-permute-start | bytes 1376264 | tf_op jit(solution)/shard_map/ppermute | solution.py:156

commit v2 on v1

v2 whole, which is shorter than its diff:
```python
import functools
import math

import jax
import jax.numpy as jnp
import numpy as np
from jax import lax
from jax.experimental import pallas as pl
from jax.experimental.pallas import tpu as pltpu
from jax.sharding import PartitionSpec as P

ROPE_BASE = 1000000.0
EPSILON = 1e-06
MASKED = -1e30
PACK_VMEM = 56 * 1024 * 1024
VMEM_LIMIT = 24 * 1024 * 1024
VMEM = pl.BlockSpec(memory_space=pltpu.VMEM)
SMEM = pl.BlockSpec(memory_space=pltpu.SMEM)
ANY = pl.BlockSpec(memory_space=pl.ANY)


def rope_table(length, width):
    half = width // 2
    frequency = np.float64(ROPE_BASE) ** (-(np.arange(half, dtype=np.float64) * 2.0 / width))
    angles = np.arange(length, dtype=np.float32)[:, None] * frequency.astype(np.float32)[None, :]
    wide = angles.astype(np.float64)
    return np.concatenate([np.cos(wide), np.sin(wide)], axis=-1).astype(np.float32)


def pack_kernel(chips, me_ref, q_hbm, k_hbm, v_hbm, table_hbm, qg_ref, kg_ref, *refs):
    query_outs, pair_outs = refs[:chips], refs[chips : 2 * chips]
    q_ref, k_ref, v_ref, table_ref, qf_ref, kf_ref, vf_ref, sems = refs[2 * chips :]
    tokens, heads, width = q_ref.shape
    kv_heads = k_ref.shape[1]
    per_chip = heads // chips
    me = me_ref[0]
    chip = me // 2
    copies = [
        pltpu.make_async_copy(table_hbm.at[pl.ds(pl.multiple_of(me * tokens, 8), tokens)], table_ref, sems.at[0]),
        pltpu.make_async_copy(k_hbm, k_ref, sems.at[1]),
        pltpu.make_async_copy(v_hbm, v_ref, sems.at[2]),
        pltpu.make_async_copy(q_hbm, q_ref, sems.at[3]),
    ]
    for copy in copies:
        copy.start()
    copies[0].wait()
    table = table_ref[...]
    swapped = pltpu.roll(table, width // 2, 1)
    first = lax.broadcasted_iota(jnp.int32, table.shape, 1) < width // 2
    cosine = jnp.where(first, table, swapped)
    sine = jnp.where(first, -swapped, table)

    def rotate(floats, gain):
        mean_square = jnp.mean(floats * floats, axis=-1, keepdims=True)
        normed = floats * lax.rsqrt(mean_square + EPSILON) * gain
        turned = pltpu.roll(normed, width // 2, 1)
        return (normed * cosine + turned * sine).astype(jnp.bfloat16)

    query_gain, key_gain = qg_ref[...], kg_ref[...]
    copies[1].wait()
    kf_ref[...] = k_ref[...].astype(jnp.float32).reshape(tokens * kv_heads, width)
    copies[2].wait()
    vf_ref[...] = v_ref[...].astype(jnp.float32).reshape(tokens * kv_heads, width)
    for step in range(chips):
        head = (chip ^ step) * kv_heads // chips
        pair_outs[step][0] = rotate(kf_ref[pl.ds(head, tokens, stride=kv_heads), :], key_gain)
        pair_outs[step][1] = vf_ref[pl.ds(head, tokens, stride=kv_heads), :].astype(jnp.bfloat16)
    copies[3].wait()
    qf_ref[...] = q_ref[...].astype(jnp.float32).reshape(tokens * heads, width)
    for step in range(chips):
        for row in range(per_chip):
            head = (chip ^ step) * per_chip + row
            query_outs[step][row] = rotate(qf_ref[pl.ds(head, tokens, stride=heads), :], query_gain)


def gather_blocks(chips, me_ref, refs, scratches):
    chip = me_ref[0] // 2
    for scratch, parts in zip(scratches, refs):
        for step in range(chips):
            scratch[chip ^ step] = parts[step][...]


def scatter_blocks(chips, me_ref, scratch, outs):
    chip = me_ref[0] // 2
    for step in range(chips):
        outs[step][...] = scratch[chip ^ step]


def attention_kernel(chips, me_ref, *refs):
    outs, (q_ref, own_ref, other_ref, out_ref) = refs[3 * chips : 4 * chips], refs[4 * chips :]
    gather_blocks(chips, me_ref, [refs[i * chips : (i + 1) * chips] for i in range(3)], (q_ref, own_ref, other_ref))
    blocks, per_chip, tokens, width = q_ref.shape
    core = lax.rem(me_ref[0], 2)
    scale = math.log2(math.e) / math.sqrt(width)
    keys_own, values_own, keys_other, values_other = [
        ref[:, i].reshape(blocks * tokens, width) for ref in (own_ref, other_ref) for i in range(2)
    ]
    contract = (((1,), (1,)), ((), ()))
    for block in range(blocks):
        queries = q_ref[block].reshape(per_chip * tokens, width)
        reach = (block + 1) * tokens
        own = lax.dot_general(queries, keys_own[:reach], contract, preferred_element_type=jnp.float32)
        other = lax.dot_general(queries, keys_other[:reach], contract, preferred_element_type=jnp.float32)
        row = lax.broadcasted_iota(jnp.int32, (per_chip, tokens, reach), 1).reshape(per_chip * tokens, reach)
        column = lax.broadcasted_iota(jnp.int32, (per_chip * tokens, reach), 1)
        own = jnp.where(column <= row + block * tokens, own, MASKED)
        other = jnp.where(column < (block + core) * tokens, other, MASKED)
        highest = jnp.maximum(
            jnp.max(own, axis=-1, keepdims=True), jnp.max(other, axis=-1, keepdims=True)
        )
        probs_own = jnp.exp2((own - highest) * scale)
        probs_other = jnp.exp2((other - highest) * scale)
        total = jnp.sum(probs_own, axis=-1, keepdims=True) + jnp.sum(probs_other, axis=-1, keepdims=True)
        summed = jnp.dot(
            probs_own.astype(jnp.bfloat16), values_own[:reach], preferred_element_type=jnp.float32
        ) + jnp.dot(
            probs_other.astype(jnp.bfloat16), values_other[:reach], preferred_element_type=jnp.float32
        )
        out_ref[block] = (summed / total).astype(jnp.bfloat16).reshape(per_chip, tokens, width)
    scatter_blocks(chips, me_ref, out_ref, outs)


def looped_kernel(chips, me_ref, *refs):
    outs, (q_ref, own_ref, other_ref, out_ref) = refs[3 * chips : 4 * chips], refs[4 * chips :]
    gather_blocks(chips, me_ref, [refs[i * chips : (i + 1) * chips] for i in range(3)], (q_ref, own_ref, other_ref))
    blocks, per_chip, tokens, width = q_ref.shape
    core = lax.rem(me_ref[0], 2)
    scale = math.log2(math.e) / math.sqrt(width)
    contract = (((1,), (1,)), ((), ()))
    row = lax.broadcasted_iota(jnp.int32, (per_chip, tokens, tokens), 1).reshape(per_chip * tokens, tokens)
    column = lax.broadcasted_iota(jnp.int32, (per_chip * tokens, tokens), 1)

    def query_block(block, _):
        queries = q_ref[block].reshape(per_chip * tokens, width)

        def merge(carried, keys, values, allowed):
            highest, total, weighted = carried
            scores = lax.dot_general(queries, keys, contract, preferred_element_type=jnp.float32)
            scores = jnp.where(allowed, scores, MASKED)
            new = jnp.maximum(highest, jnp.max(scores, axis=-1, keepdims=True))
            probs = jnp.exp2((scores - new) * scale)
            factor = jnp.exp2((highest - new) * scale)
            total = total * factor + jnp.sum(probs, axis=-1, keepdims=True)
            summed = jnp.dot(probs.astype(jnp.bfloat16), values, preferred_element_type=jnp.float32)
            return new, total, weighted * factor + summed

        def advance(index, carried):
            behind = (block - index) * tokens
            carried = merge(carried, own_ref[index, 0], own_ref[index, 1], column <= row + behind)
            return merge(carried, other_ref[index, 0], other_ref[index, 1], column < behind + core * tokens)

        initial = (
            jnp.full((per_chip * tokens, 1), MASKED, jnp.float32),
            jnp.zeros((per_chip * tokens, 1), jnp.float32),
            jnp.zeros((per_chip * tokens, width), jnp.float32),
        )
        _, total, weighted = lax.fori_loop(0, block + 1, advance, initial)
        out_ref[block] = (weighted / total).astype(jnp.bfloat16).reshape(per_chip, tokens, width)
        return 0

    lax.fori_loop(0, blocks, query_block, 0)
    scatter_blocks(chips, me_ref, out_ref, outs)


def unpack_kernel(chips, me_ref, *refs):
    parts, (out_ref, floats_ref) = refs[:chips], refs[chips:]
    tokens, heads, width = out_ref.shape
    per_chip = heads // chips
    chip = me_ref[0] // 2
    for step in range(chips):
        for row in range(per_chip):
            head = (chip ^ step) * per_chip + row
            floats_ref[pl.ds(head, tokens, stride=heads), :] = parts[step][row].astype(jnp.float32)
    out_ref[...] = floats_ref[...].reshape(tokens, heads, width).astype(jnp.bfloat16)


def on_device(length, devices, query_states, key_states, value_states, query_gain, key_gain):
    tokens, heads, width = query_states.shape
    kv_heads = key_states.shape[1]
    chips = devices // 2
    per_chip = heads // chips
    me = lax.axis_index("seq")[None]
    params = pltpu.CompilerParams(vmem_limit_bytes=VMEM_LIMIT)
    bf16, f32 = jnp.bfloat16, jnp.float32
    queries_type = jax.ShapeDtypeStruct((per_chip, tokens, width), bf16)
    pair_type = jax.ShapeDtypeStruct((2, tokens, width), bf16)
    order = sorted(range(1, chips), key=lambda step: -step)

    def to_partner(step, array):
        links = [(device, ((device // 2) ^ step) * 2 + device % 2) for device in range(devices)]
        return lax.ppermute(array, "seq", links)

    packed = pl.pallas_call(
        functools.partial(pack_kernel, chips),
        out_shape=[queries_type] * chips + [pair_type] * chips,
        in_specs=[SMEM, ANY, ANY, ANY, ANY, VMEM, VMEM],
        out_specs=[VMEM] * (2 * chips),
        scratch_shapes=[
            pltpu.VMEM((tokens, heads, width), bf16),
            pltpu.VMEM((tokens, kv_heads, width), bf16),
            pltpu.VMEM((tokens, kv_heads, width), bf16),
            pltpu.VMEM((tokens, width), f32),
            pltpu.VMEM((tokens * heads, width), f32),
            pltpu.VMEM((tokens * kv_heads, width), f32),
            pltpu.VMEM((tokens * kv_heads, width), f32),
            pltpu.SemaphoreType.DMA((4,)),
        ],
        compiler_params=pltpu.CompilerParams(vmem_limit_bytes=PACK_VMEM),
        name="pack",
    )(me, query_states, key_states, value_states, rope_table(length, width), query_gain[None], key_gain[None])
    queries, own = list(packed[:chips]), list(packed[chips:])
    for step in order:
        own[step] = to_partner(step, own[step])
    for step in order:
        queries[step] = to_partner(step, queries[step])
    swap = [(device, device ^ 1) for device in range(devices)]
    other = [lax.ppermute(pair, "seq", swap) for pair in own]
    attended = pl.pallas_call(
        functools.partial(attention_kernel if chips <= 8 else looped_kernel, chips),
        out_shape=[queries_type] * chips,
        in_specs=[SMEM] + [VMEM] * (3 * chips),
        out_specs=[VMEM] * chips,
        scratch_shapes=[
            pltpu.VMEM((chips, per_chip, tokens, width), bf16),
            pltpu.VMEM((chips, 2, tokens, width), bf16),
            pltpu.VMEM((chips, 2, tokens, width), bf16),
            pltpu.VMEM((chips, per_chip, tokens, width), bf16),
        ],
        compiler_params=params,
        name="attention",
    )(me, *queries, *own, *other)
    returned = list(attended)
    for step in order:
        returned[step] = to_partner(step, returned[step])
    return pl.pallas_call(
        functools.partial(unpack_kernel, chips),
        out_shape=jax.ShapeDtypeStruct((tokens, heads, width), bf16),
        in_specs=[SMEM] + [VMEM] * chips,
        out_specs=VMEM,
        scratch_shapes=[pltpu.VMEM((tokens * heads, width), f32)],
        compiler_params=params,
        name="unpack",
    )(me, *returned)


def solution(mesh):
    devices = mesh.shape["seq"]
    groups = mesh.shape["groups"]
    placed = P(("groups", "seq"), None, None)

    def run(query_states, key_states, value_states, query_gain, key_gain):
        length = query_states.shape[0] // groups
        return jax.shard_map(
            functools.partial(on_device, length, devices),
            mesh=mesh,
            in_specs=(placed, placed, placed, P(), P()),
            out_specs=placed,
            check_vma=False,
        )(query_states, key_states, value_states, query_gain, key_gain)

    return run
```

time: 61.5 us -> 61.5 us (level)
  blocking collectives: 46.9 us -> 0 us
  starting transfers between devices: 0.07 us -> 36.1 us
  waiting for transfers between devices: 1.8 us -> 12.6 us
  Pallas kernels: 7.05 us -> 10.8 us
  local copies, waits for them, and re-layouts: 5.3 us -> 1.64 us
    all_to_all x2 -> x0, blocking collectives: 46.9 us -> none  [the longest x1 30.4 us: on_device(): lax.all_to_all(packed, 'seq', split_axis=0, concat_axis=0, axis_index_gro...]
    ppermute x1 -> x29, starting transfers between devices: 0.07 us -> 36.1 us  [the longest x21 34.1 us: to_partner(): return lax.ppermute(array, 'seq', links)]
    ppermute x1 -> x29, waiting for transfers between devices: 1.8 us -> 12.6 us  [the longest x21 11.7 us: to_partner(): return lax.ppermute(array, 'seq', links)]
    pallas_call x2 -> x3, Pallas kernels: 7.05 us -> 10.8 us  [the longest x1 5.22 us: on_device(): pl.pallas_call(functools.partial(pack_kernel, chips), out_shape=[queries_...]
    unnamed x10 -> x4, local copies, waits for them, and re-layouts: 3.56 us -> 1.64 us
    reshape x1 -> x0, local copies, waits for them, and re-layouts: 0.89 us -> none  [on_device(): return jnp.transpose(returned.reshape(heads, tokens, width), (1, 0, 2))]
    dynamic_slice x1 -> x0, local copies, waits for them, and re-layouts: 0.82 us -> none  [on_device(): lax.dynamic_slice_in_dim(jnp.asarray(rope_table(length, width)), me * tok...]
  transfers between devices with their start and end apart: 1 -> 29, of which waited for: 1 -> 10; matrix products, arithmetic and copies ran while one was open for 0% -> 0% of each run, Pallas kernels for 0% -> 0%
where the time goes in v2:
time: 61.5 us; the launch traced here: 61.3 us
  starting transfers between devices  36.1 us (59%)
  waiting for transfers between devices  12.6 us (20%)
  Pallas kernels  10.8 us (18%)
  local copies, waits for them, and re-layouts  1.64 us (3%)
    ppermute x21, starting transfers between devices, to_partner(): return lax.ppermute(array, 'seq', links)  34.1 us
    ppermute x21, waiting for transfers between devices, to_partner(): return lax.ppermute(array, 'seq', links)  11.7 us
    pallas_call x1, Pallas kernels, on_device(): pl.pallas_call(functools.partial(pack_kernel, chips), out_shape=[queries_...  5.22 us
    pallas_call x1, Pallas kernels, on_device(): pl.pallas_call(functools.partial(attention_kernel if chips <= 8 else loop...  4.34 us
    ppermute x8, starting transfers between devices, on_device(): other = [lax.ppermute(pair, 'seq', swap) for pair in own]  2.04 us
    unnamed x4, local copies, waits for them, and re-layouts  1.64 us
    pallas_call x1, Pallas kernels, on_device(): pl.pallas_call(functools.partial(unpack_kernel, chips), out_shape=jax.Sha...  1.27 us
  transfers between devices with their start and end apart: 29, of which 10 were waited for; matrix products, arithmetic and copies ran while one was open for 0% of the time, Pallas kernels for 0%

profile of v2, /device:TPU:0, one launch (start us, length us, event | category | flops | bytes accessed | tf_op | source)
XLA Modules:
  0.0 61.3 jit_solution(8330117381186107335)
XLA Ops:
  0.0 5.2 %pack.1 = (bf16[2,112,128]{2,1,0:T(8,128)(2,1)}, bf16[2,112,128]{2,1,0:T(8,128)(2,1)}, bf16[2,112,128]{2,1,0:T(8,128)(2,1)}, bf16[2,112,128]{2,1,0:T(8,128)(2,1)...) custom-call(s32[1]{0:T(128)} %bitcast.me_ref, ...), custom_call_target="tpu_custom_call" | custom-call | tf_op jit(solution)/shard_map/pack/pallas_call | solution.py:193
  5.2 3.0 %collective-permute-start = (bf16[2,112,128]{2,1,0:T(8,128)(2,1)}, bf16[2,112,128]{2,1,0:T(8,128)(2,1)S(1)}, u32[]{:S(2)}, u32[]{:S(2)}) collective-permute-start(bf16[2,112,128]{2,1,0:T(8,128)(2,1)} %get-tuple-element.30), channel_id=1, source_target_pairs={{0,2},{1,3},{2,0},{3,1},{4,6},{5,7},{6,4},{7,5},{8,10},{9,11},{10,... | collective-permute-start | bytes 172040 | tf_op jit(solution)/shard_map/ppermute | solution.py:191
  8.3 1.6 %collective-permute-start.1 = (bf16[2,112,128]{2,1,0:T(8,128)(2,1)}, bf16[2,112,128]{2,1,0:T(8,128)(2,1)S(1)}, u32[]{:S(2)}, u32[]{:S(2)}) collective-permute-start(bf16[2,112,128]{2,1,0:T(8,128)(2,1)} %get-tuple-element.31), channel_id=1, source_target_pairs={{0,4},{1,5},{2,6},{3,7},{4,0},{5,1},{6,2},{7,3},{8,12},{9,13},{10,... | collective-permute-start | bytes 172040 | tf_op jit(solution)/shard_map/ppermute | solution.py:191
  9.8 0.0 collective-permute-start.2
  9.8 3.0 %collective-permute-start.3 = (bf16[2,112,128]{2,1,0:T(8,128)(2,1)}, bf16[2,112,128]{2,1,0:T(8,128)(2,1)S(1)}, u32[]{:S(2)}, u32[]{:S(2)}) collective-permute-start(bf16[2,112,128]{2,1,0:T(8,128)(2,1)} %get-tuple-element.33), channel_id=1, source_target_pairs={{0,8},{1,9},{2,10},{3,11},{4,12},{5,13},{6,14},{7,15},{8,0},{9,1},... | collective-permute-start | bytes 172040 | tf_op jit(solution)/shard_map/ppermute | solution.py:191
  12.8 1.3 %collective-permute-start.4 = (bf16[2,112,128]{2,1,0:T(8,128)(2,1)}, bf16[2,112,128]{2,1,0:T(8,128)(2,1)S(1)}, u32[]{:S(2)}, u32[]{:S(2)}) collective-permute-start(bf16[2,112,128]{2,1,0:T(8,128)(2,1)} %get-tuple-element.34), channel_id=1, source_target_pairs={{0,10},{1,11},{2,8},{3,9},{4,14},{5,15},{6,12},{7,13},{8,2},{9,3},... | collective-permute-start | bytes 172040 | tf_op jit(solution)/shard_map/ppermute | solution.py:191
  14.1 0.0 collective-permute-done.refs_1_
  14.1 3.6 %collective-permute-start.5 = (bf16[2,112,128]{2,1,0:T(8,128)(2,1)}, bf16[2,112,128]{2,1,0:T(8,128)(2,1)S(1)}, u32[]{:S(2)}, u32[]{:S(2)}) collective-permute-start(bf16[2,112,128]{2,1,0:T(8,128)(2,1)} %get-tuple-element.35), channel_id=1, source_target_pairs={{0,12},{1,13},{2,14},{3,15},{4,8},{5,9},{6,10},{7,11},{8,4},{9,5},... | collective-permute-start | bytes 172040 | tf_op jit(solution)/shard_map/ppermute | solution.py:191
  17.7 0.0 collective-permute-done.1.refs_2_
  17.7 0.0 collective-permute-start.6
  17.7 0.0 collective-permute-done.2.refs_3_
  17.7 1.7 %collective-permute-start.7 = (bf16[2,112,128]{2,1,0:T(8,128)(2,1)}, bf16[2,112,128]{2,1,0:T(8,128)(2,1)S(1)}, u32[]{:S(2)}, u32[]{:S(2)}) collective-permute-start(bf16[2,112,128]{2,1,0:T(8,128)(2,1)} %get-tuple-element.38), channel_id=1, source_target_pairs={{0,2},{1,3},{2,0},{3,1},{4,6},{5,7},{6,4},{7,5},{8,10},{9,11},{10,... | collective-permute-start | bytes 172040 | tf_op jit(solution)/shard_map/ppermute | solution.py:191
  19.4 0.0 collective-permute-done.3.refs_4_
  19.4 0.0 collective-permute-start.8
  19.4 2.8 %collective-permute-done.4.refs_5_ = bf16[2,112,128]{2,1,0:T(8,128)(2,1)S(1)} collective-permute-done((bf16[2,112,128]{2,1,0:T(8,128)(2,1)}, bf16[2,112,128]{2,1,0:T(8,128)(2,1)S(1)}, u32[]{:S(2)}, u32[]{:S(2)}) %collective-permute-start.4) | collective-permute-done | bytes 57376 | tf_op jit(solution)/shard_map/ppermute | solution.py:191
  22.2 0.5 collective-permute-start.9
  22.7 0.0 collective-permute-done.5.refs_6_
  22.7 2.1 %collective-permute-start.10 = (bf16[2,112,128]{2,1,0:T(8,128)(2,1)}, bf16[2,112,128]{2,1,0:T(8,128)(2,1)S(1)}, u32[]{:S(2)}, u32[]{:S(2)}) collective-permute-start(bf16[2,112,128]{2,1,0:T(8,128)(2,1)} %get-tuple-element.41), channel_id=1, source_target_pairs={{0,8},{1,9},{2,10},{3,11},{4,12},{5,13},{6,14},{7,15},{8,0},{9,1},... | collective-permute-start | bytes 172040 | tf_op jit(solution)/shard_map/ppermute | solution.py:191
  24.9 0.5 collective-permute-done.6.refs_7_
  25.4 1.8 %collective-permute-start.11 = (bf16[2,112,128]{2,1,0:T(8,128)(2,1)}, bf16[2,112,128]{2,1,0:T(8,128)(2,1)S(1)}, u32[]{:S(2)}, u32[]{:S(2)}) collective-permute-start(bf16[2,112,128]{2,1,0:T(8,128)(2,1)} %get-tuple-element.42), channel_id=1, source_target_pairs={{0,10},{1,11},{2,8},{3,9},{4,14},{5,15},{6,12},{7,13},{8,2},{9,3},... | collective-permute-start | bytes 172040 | tf_op jit(solution)/shard_map/ppermute | solution.py:191
  27.2 0.0 collective-permute-done.7.refs_9_
  27.2 1.7 %collective-permute-start.12 = (bf16[2,112,128]{2,1,0:T(8,128)(2,1)}, bf16[2,112,128]{2,1,0:T(8,128)(2,1)S(1)}, u32[]{:S(2)}, u32[]{:S(2)}) collective-permute-start(bf16[2,112,128]{2,1,0:T(8,128)(2,1)} %get-tuple-element.43), channel_id=1, source_target_pairs={{0,12},{1,13},{2,14},{3,15},{4,8},{5,9},{6,10},{7,11},{8,4},{9,5},... | collective-permute-start | bytes 172040 | tf_op jit(solution)/shard_map/ppermute | solution.py:191
  28.9 0.0 collective-permute-done.8.refs_10_
  28.9 2.6 %collective-permute-start.13 = (bf16[2,112,128]{2,1,0:T(8,128)(2,1)}, bf16[2,112,128]{2,1,0:T(8,128)(2,1)S(1)}, u32[]{:S(2)}, u32[]{:S(2)}) collective-permute-start(bf16[2,112,128]{2,1,0:T(8,128)(2,1)} %get-tuple-element.44), channel_id=1, source_target_pairs={{0,14},{1,15},{2,12},{3,13},{4,10},{5,11},{6,8},{7,9},{8,6},{9,7},... | collective-permute-start | bytes 172040 | tf_op jit(solution)/shard_map/ppermute | solution.py:191
  31.5 0.0 collective-permute-done.9.refs_11_
  31.5 0.0 collective-permute-start.14
  31.5 0.0 collective-permute-done.10.refs_12_
  31.5 0.5 collective-permute-start.15
  32.0 2.1 %collective-permute-done.11.refs_13_ = bf16[2,112,128]{2,1,0:T(8,128)(2,1)S(1)} collective-permute-done((bf16[2,112,128]{2,1,0:T(8,128)(2,1)}, bf16[2,112,128]{2,1,0:T(8,128)(2,1)S(1)}, u32[]{:S(2)}, u32[]{:S(2)}) %collective-permute-start.11) | collective-permute-done | bytes 57376 | tf_op jit(solution)/shard_map/ppermute | solution.py:191
  34.2 0.0 collective-permute-start.16
  34.2 0.0 collective-permute-done.12.refs_14_
  34.2 0.5 collective-permute-start.17
  34.7 1.3 %collective-permute-done.13.refs_15_ = bf16[2,112,128]{2,1,0:T(8,128)(2,1)S(1)} collective-permute-done((bf16[2,112,128]{2,1,0:T(8,128)(2,1)}, bf16[2,112,128]{2,1,0:T(8,128)(2,1)S(1)}, u32[]{:S(2)}, u32[]{:S(2)}) %collective-permute-start.13) | collective-permute-done | bytes 57376 | tf_op jit(solution)/shard_map/ppermute | solution.py:191
  36.0 0.0 collective-permute-start.18
  36.0 0.0 collective-permute-done.14.refs_16_
  36.0 0.5 collective-permute-start.19
  36.5 0.0 collective-permute-done.15.refs_17_
  36.5 0.1 collective-permute-start.20
  36.6 0.0 collective-permute-done.16.refs_18_
  36.6 0.4 collective-permute-start.21
  37.0 0.0 collective-permute-done.17.refs_19_
  37.0 0.2 collective-permute-done.18.refs_20_
  37.2 0.2 collective-permute-done.19.refs_21_
  37.4 0.4 collective-permute-done.20.refs_22_
  37.8 0.2 collective-permute-done.21.refs_23_
  37.9 0.0 copy-start
  37.9 0.8 %copy-done = bf16[2,112,128]{2,1,0:T(8,128)(2,1)S(1)} copy-done((bf16[2,112,128]{2,1,0:T(8,128)(2,1)S(1)}, bf16[2,112,128]{2,1,0:T(8,128)(2,1)}, u32[]{:S(2)}) %copy-start) | copy-done | bytes 57368
  38.7 0.8 %copy-done.1 = bf16[2,112,128]{2,1,0:T(8,128)(2,1)S(1)} copy-done((bf16[2,112,128]{2,1,0:T(8,128)(2,1)S(1)}, bf16[2,112,128]{2,1,0:T(8,128)(2,1)}, u32[]{:S(2)}) %copy-start.1) | copy-done | bytes 57368
  39.6 4.3 %attention.1 = (bf16[2,112,128]{2,1,0:T(8,128)(2,1)S(1)}, bf16[2,112,128]{2,1,0:T(8,128)(2,1)S(1)}, bf16[2,112,128]{2,1,0:T(8,128)(2,1)S(1)}, bf16[2,112,128]{2,...) custom-call(s32[1]{0:T(128)} %bitcast.me_ref, ...), custom_call_target="tpu_custom_call" | custom-call | tf_op jit(solution)/shard_map/attention/pallas_call | solution.py:218
  43.9 1.2 %collective-permute-start.22 = (bf16[2,112,128]{2,1,0:T(8,128)(2,1)S(1)}, bf16[2,112,128]{2,1,0:T(8,128)(2,1)S(1)}, u32[]{:S(2)}, u32[]{:S(2)}) collective-permute-start(bf16[2,112,128]{2,1,0:T(8,128)(2,1)S(1)} %get-tuple-element.46), channel_id=1, source_target_pairs={{0,2},{1,3},{2,0},{3,1},{4,6},{5,7},{6,4},{7,5},{8,10},{9,11},{10,... | collective-permute-start | bytes 172040 | tf_op jit(solution)/shard_map/ppermute | solution.py:191
  45.1 0.0 collective-permute-start.23
  45.1 2.3 %collective-permute-start.24 = (bf16[2,112,128]{2,1,0:T(8,128)(2,1)S(1)}, bf16[2,112,128]{2,1,0:T(8,128)(2,1)S(1)}, u32[]{:S(2)}, u32[]{:S(2)}) collective-permute-start(bf16[2,112,128]{2,1,0:T(8,128)(2,1)S(1)} %get-tuple-element.48), channel_id=1, source_target_pairs={{0,6},{1,7},{2,4},{3,5},{4,2},{5,3},{6,0},{7,1},{8,14},{9,15},{10,... | collective-permute-start | bytes 172040 | tf_op jit(solution)/shard_map/ppermute | solution.py:191
  47.5 0.7 %collective-permute-start.25 = (bf16[2,112,128]{2,1,0:T(8,128)(2,1)S(1)}, bf16[2,112,128]{2,1,0:T(8,128)(2,1)S(1)}, u32[]{:S(2)}, u32[]{:S(2)}) collective-permute-start(bf16[2,112,128]{2,1,0:T(8,128)(2,1)S(1)} %get-tuple-element.49), channel_id=1, source_target_pairs={{0,8},{1,9},{2,10},{3,11},{4,12},{5,13},{6,14},{7,15},{8,0},{9,1},... | collective-permute-start | bytes 172040 | tf_op jit(solution)/shard_map/ppermute | solution.py:191
  48.1 2.9 %collective-permute-start.26 = (bf16[2,112,128]{2,1,0:T(8,128)(2,1)S(1)}, bf16[2,112,128]{2,1,0:T(8,128)(2,1)S(1)}, u32[]{:S(2)}, u32[]{:S(2)}) collective-permute-start(bf16[2,112,128]{2,1,0:T(8,128)(2,1)S(1)} %get-tuple-element.50), channel_id=1, source_target_pairs={{0,10},{1,11},{2,8},{3,9},{4,14},{5,15},{6,12},{7,13},{8,2},{9,3},... | collective-permute-start | bytes 172040 | tf_op jit(solution)/shard_map/ppermute | solution.py:191
  51.0 0.0 collective-permute-done.22.refs_1_
  51.0 2.0 %collective-permute-start.27 = (bf16[2,112,128]{2,1,0:T(8,128)(2,1)S(1)}, bf16[2,112,128]{2,1,0:T(8,128)(2,1)S(1)}, u32[]{:S(2)}, u32[]{:S(2)}) collective-permute-start(bf16[2,112,128]{2,1,0:T(8,128)(2,1)S(1)} %get-tuple-element.51), channel_id=1, source_target_pairs={{0,12},{1,13},{2,14},{3,15},{4,8},{5,9},{6,10},{7,11},{8,4},{9,5},... | collective-permute-start | bytes 172040 | tf_op jit(solution)/shard_map/ppermute | solution.py:191
  53.0 0.0 collective-permute-done.23.refs_2_
  53.0 2.1 %collective-permute-start.28 = (bf16[2,112,128]{2,1,0:T(8,128)(2,1)S(1)}, bf16[2,112,128]{2,1,0:T(8,128)(2,1)S(1)}, u32[]{:S(2)}, u32[]{:S(2)}) collective-permute-start(bf16[2,112,128]{2,1,0:T(8,128)(2,1)S(1)} %get-tuple-element.52), channel_id=1, source_target_pairs={{0,14},{1,15},{2,12},{3,13},{4,10},{5,11},{6,8},{7,9},{8,6},{9,7},... | collective-permute-start | bytes 172040 | tf_op jit(solution)/shard_map/ppermute | solution.py:191
  55.1 0.0 collective-permute-done.24.refs_3_
  55.1 0.0 collective-permute-done.25.refs_4_
  55.1 3.5 %collective-permute-done.26.refs_5_ = bf16[2,112,128]{2,1,0:T(8,128)(2,1)S(1)} collective-permute-done((bf16[2,112,128]{2,1,0:T(8,128)(2,1)S(1)}, bf16[2,112,128]{2,1,0:T(8,128)(2,1)S(1)}, u32[]{:S(2)}, u32[]{:S(2)}) %collective-permute-start.26) | collective-permute-done | bytes 57376 | tf_op jit(solution)/shard_map/ppermute | solution.py:191
  58.6 0.0 collective-permute-done.27.refs_6_
  58.6 1.4 %collective-permute-done.28.refs_7_ = bf16[2,112,128]{2,1,0:T(8,128)(2,1)S(1)} collective-permute-done((bf16[2,112,128]{2,1,0:T(8,128)(2,1)S(1)}, bf16[2,112,128]{2,1,0:T(8,128)(2,1)S(1)}, u32[]{:S(2)}, u32[]{:S(2)}) %collective-permute-start.28) | collective-permute-done | bytes 57376 | tf_op jit(solution)/shard_map/ppermute | solution.py:191
  60.0 1.3 %unpack.1 = bf16[112,16,128]{2,1,0:T(8,128)(2,1)} custom-call(s32[1]{0:T(128)} %bitcast.me_ref, bf16[2,112,128]{2,1,0:T(8,128)(2,1)S(1)} %get-tuple-element.45.refs_0_, bf16[2,112,128]{2,1,0:T(8,128)(2,1)S(1)} %collective-permute-done.22.refs_1_, bf16[2,112,128]{2,1,0:T(8,128)(2,1)S(1)} %collective-permute-done.23.refs_2_, ...), custom_call_target="tpu_custom_call" | custom-call | tf_op jit(solution)/shard_map/unpack/pallas_call | solution.py:235
  (1 shorter events, 0.0 us)
Async XLA Ops:
  5.2 8.9 %collective-permute-start = (bf16[2,112,128]{2,1,0:T(8,128)(2,1)}, bf16[2,112,128]{2,1,0:T(8,128)(2,1)S(1)}, u32[]{:S(2)}, u32[]{:S(2)}) collective-permute-start(bf16[2,112,128]{2,1,0:T(8,128)(2,1)} %get-tuple-element.30), channel_id=1, source_target_pairs={{0,2},{1,3},{2,0},{3,1},{4,6},{5,7},{6,4},{7,5},{8,10},{9,11},{10,... | collective-permute-start | bytes 172040 | tf_op jit(solution)/shard_map/ppermute | solution.py:191
  8.3 9.5 %collective-permute-start.1 = (bf16[2,112,128]{2,1,0:T(8,128)(2,1)}, bf16[2,112,128]{2,1,0:T(8,128)(2,1)S(1)}, u32[]{:S(2)}, u32[]{:S(2)}) collective-permute-start(bf16[2,112,128]{2,1,0:T(8,128)(2,1)} %get-tuple-element.31), channel_id=1, source_target_pairs={{0,4},{1,5},{2,6},{3,7},{4,0},{5,1},{6,2},{7,3},{8,12},{9,13},{10,... | collective-permute-start | bytes 172040 | tf_op jit(solution)/shard_map/ppermute | solution.py:191
  9.8 7.9 %collective-permute-start.2 = (bf16[2,112,128]{2,1,0:T(8,128)(2,1)}, bf16[2,112,128]{2,1,0:T(8,128)(2,1)S(1)}, u32[]{:S(2)}, u32[]{:S(2)}) collective-permute-start(bf16[2,112,128]{2,1,0:T(8,128)(2,1)} %get-tuple-element.32), channel_id=1, source_target_pairs={{0,6},{1,7},{2,4},{3,5},{4,2},{5,3},{6,0},{7,1},{8,14},{9,15},{10,... | collective-permute-start | bytes 172040 | tf_op jit(solution)/shard_map/ppermute | solution.py:191
  9.8 9.6 %collective-permute-start.3 = (bf16[2,112,128]{2,1,0:T(8,128)(2,1)}, bf16[2,112,128]{2,1,0:T(8,128)(2,1)S(1)}, u32[]{:S(2)}, u32[]{:S(2)}) collective-permute-start(bf16[2,112,128]{2,1,0:T(8,128)(2,1)} %get-tuple-element.33), channel_id=1, source_target_pairs={{0,8},{1,9},{2,10},{3,11},{4,12},{5,13},{6,14},{7,15},{8,0},{9,1},... | collective-permute-start | bytes 172040 | tf_op jit(solution)/shard_map/ppermute | solution.py:191
  12.8 9.4 %collective-permute-start.4 = (bf16[2,112,128]{2,1,0:T(8,128)(2,1)}, bf16[2,112,128]{2,1,0:T(8,128)(2,1)S(1)}, u32[]{:S(2)}, u32[]{:S(2)}) collective-permute-start(bf16[2,112,128]{2,1,0:T(8,128)(2,1)} %get-tuple-element.34), channel_id=1, source_target_pairs={{0,10},{1,11},{2,8},{3,9},{4,14},{5,15},{6,12},{7,13},{8,2},{9,3},... | collective-permute-start | bytes 172040 | tf_op jit(solution)/shard_map/ppermute | solution.py:191
  14.1 8.6 %collective-permute-start.5 = (bf16[2,112,128]{2,1,0:T(8,128)(2,1)}, bf16[2,112,128]{2,1,0:T(8,128)(2,1)S(1)}, u32[]{:S(2)}, u32[]{:S(2)}) collective-permute-start(bf16[2,112,128]{2,1,0:T(8,128)(2,1)} %get-tuple-element.35), channel_id=1, source_target_pairs={{0,12},{1,13},{2,14},{3,15},{4,8},{5,9},{6,10},{7,11},{8,4},{9,5},... | collective-permute-start | bytes 172040 | tf_op jit(solution)/shard_map/ppermute | solution.py:191
  17.7 7.6 %collective-permute-start.6 = (bf16[2,112,128]{2,1,0:T(8,128)(2,1)}, bf16[2,112,128]{2,1,0:T(8,128)(2,1)S(1)}, u32[]{:S(2)}, u32[]{:S(2)}) collective-permute-start(bf16[2,112,128]{2,1,0:T(8,128)(2,1)} %get-tuple-element.36), channel_id=1, source_target_pairs={{0,14},{1,15},{2,12},{3,13},{4,10},{5,11},{6,8},{7,9},{8,6},{9,7},... | collective-permute-start | bytes 172040 | tf_op jit(solution)/shard_map/ppermute | solution.py:191
  17.7 9.5 %collective-permute-start.7 = (bf16[2,112,128]{2,1,0:T(8,128)(2,1)}, bf16[2,112,128]{2,1,0:T(8,128)(2,1)S(1)}, u32[]{:S(2)}, u32[]{:S(2)}) collective-permute-start(bf16[2,112,128]{2,1,0:T(8,128)(2,1)} %get-tuple-element.38), channel_id=1, source_target_pairs={{0,2},{1,3},{2,0},{3,1},{4,6},{5,7},{6,4},{7,5},{8,10},{9,11},{10,... | collective-permute-start | bytes 172040 | tf_op jit(solution)/shard_map/ppermute | solution.py:191
  19.4 9.5 %collective-permute-start.8 = (bf16[2,112,128]{2,1,0:T(8,128)(2,1)}, bf16[2,112,128]{2,1,0:T(8,128)(2,1)S(1)}, u32[]{:S(2)}, u32[]{:S(2)}) collective-permute-start(bf16[2,112,128]{2,1,0:T(8,128)(2,1)} %get-tuple-element.39), channel_id=1, source_target_pairs={{0,4},{1,5},{2,6},{3,7},{4,0},{5,1},{6,2},{7,3},{8,12},{9,13},{10,... | collective-permute-start | bytes 172040 | tf_op jit(solution)/shard_map/ppermute | solution.py:191
  22.2 9.2 %collective-permute-start.9 = (bf16[2,112,128]{2,1,0:T(8,128)(2,1)}, bf16[2,112,128]{2,1,0:T(8,128)(2,1)S(1)}, u32[]{:S(2)}, u32[]{:S(2)}) collective-permute-start(bf16[2,112,128]{2,1,0:T(8,128)(2,1)} %get-tuple-element.40), channel_id=1, source_target_pairs={{0,6},{1,7},{2,4},{3,5},{4,2},{5,3},{6,0},{7,1},{8,14},{9,15},{10,... | collective-permute-start | bytes 172040 | tf_op jit(solution)/shard_map/ppermute | solution.py:191
  22.7 8.8 %collective-permute-start.10 = (bf16[2,112,128]{2,1,0:T(8,128)(2,1)}, bf16[2,112,128]{2,1,0:T(8,128)(2,1)S(1)}, u32[]{:S(2)}, u32[]{:S(2)}) collective-permute-start(bf16[2,112,128]{2,1,0:T(8,128)(2,1)} %get-tuple-element.41), channel_id=1, source_target_pairs={{0,8},{1,9},{2,10},{3,11},{4,12},{5,13},{6,14},{7,15},{8,0},{9,1},... | collective-permute-start | bytes 172040 | tf_op jit(solution)/shard_map/ppermute | solution.py:191
  25.4 8.8 %collective-permute-start.11 = (bf16[2,112,128]{2,1,0:T(8,128)(2,1)}, bf16[2,112,128]{2,1,0:T(8,128)(2,1)S(1)}, u32[]{:S(2)}, u32[]{:S(2)}) collective-permute-start(bf16[2,112,128]{2,1,0:T(8,128)(2,1)} %get-tuple-element.42), channel_id=1, source_target_pairs={{0,10},{1,11},{2,8},{3,9},{4,14},{5,15},{6,12},{7,13},{8,2},{9,3},... | collective-permute-start | bytes 172040 | tf_op jit(solution)/shard_map/ppermute | solution.py:191
  27.2 7.0 %collective-permute-start.12 = (bf16[2,112,128]{2,1,0:T(8,128)(2,1)}, bf16[2,112,128]{2,1,0:T(8,128)(2,1)S(1)}, u32[]{:S(2)}, u32[]{:S(2)}) collective-permute-start(bf16[2,112,128]{2,1,0:T(8,128)(2,1)} %get-tuple-element.43), channel_id=1, source_target_pairs={{0,12},{1,13},{2,14},{3,15},{4,8},{5,9},{6,10},{7,11},{8,4},{9,5},... | collective-permute-start | bytes 172040 | tf_op jit(solution)/shard_map/ppermute | solution.py:191
  28.9 7.1 %collective-permute-start.13 = (bf16[2,112,128]{2,1,0:T(8,128)(2,1)}, bf16[2,112,128]{2,1,0:T(8,128)(2,1)S(1)}, u32[]{:S(2)}, u32[]{:S(2)}) collective-permute-start(bf16[2,112,128]{2,1,0:T(8,128)(2,1)} %get-tuple-element.44), channel_id=1, source_target_pairs={{0,14},{1,15},{2,12},{3,13},{4,10},{5,11},{6,8},{7,9},{8,6},{9,7},... | collective-permute-start | bytes 172040 | tf_op jit(solution)/shard_map/ppermute | solution.py:191
  31.5 4.5 %collective-permute-start.14 = (bf16[2,112,128]{2,1,0:T(8,128)(2,1)}, bf16[2,112,128]{2,1,0:T(8,128)(2,1)S(1)}, u32[]{:S(2)}, u32[]{:S(2)}) collective-permute-start(bf16[2,112,128]{2,1,0:T(8,128)(2,1)} %get-tuple-element.37.refs_8_), channel_id=1, source_target_pairs={{0,1},{1,0},{2,3},{3,2},{4,5},{5,4},{6,7},{7,6},{8,9},{9,8},{10,11... | collective-permute-start | bytes 172040 | tf_op jit(solution)/shard_map/ppermute | solution.py:217
  31.5 5.0 %collective-permute-start.15 = (bf16[2,112,128]{2,1,0:T(8,128)(2,1)S(1)}, bf16[2,112,128]{2,1,0:T(8,128)(2,1)S(1)}, u32[]{:S(2)}, u32[]{:S(2)}) collective-permute-start(bf16[2,112,128]{2,1,0:T(8,128)(2,1)S(1)} %collective-permute-done.7.refs_9_), channel_id=1, source_target_pairs={{0,1},{1,0},{2,3},{3,2},{4,5},{5,4},{6,7},{7,6},{8,9},{9,8},{10,11... | collective-permute-start | bytes 172040 | tf_op jit(solution)/shard_map/ppermute | solution.py:217
  34.2 2.4 %collective-permute-start.16 = (bf16[2,112,128]{2,1,0:T(8,128)(2,1)S(1)}, bf16[2,112,128]{2,1,0:T(8,128)(2,1)S(1)}, u32[]{:S(2)}, u32[]{:S(2)}) collective-permute-start(bf16[2,112,128]{2,1,0:T(8,128)(2,1)S(1)} %collective-permute-done.8.refs_10_), channel_id=1, source_target_pairs={{0,1},{1,0},{2,3},{3,2},{4,5},{5,4},{6,7},{7,6},{8,9},{9,8},{10,11... | collective-permute-start | bytes 172040 | tf_op jit(solution)/shard_map/ppermute | solution.py:217
  34.2 2.9 %collective-permute-start.17 = (bf16[2,112,128]{2,1,0:T(8,128)(2,1)S(1)}, bf16[2,112,128]{2,1,0:T(8,128)(2,1)S(1)}, u32[]{:S(2)}, u32[]{:S(2)}) collective-permute-start(bf16[2,112,128]{2,1,0:T(8,128)(2,1)S(1)} %collective-permute-done.9.refs_11_), channel_id=1, source_target_pairs={{0,1},{1,0},{2,3},{3,2},{4,5},{5,4},{6,7},{7,6},{8,9},{9,8},{10,11... | collective-permute-start | bytes 172040 | tf_op jit(solution)/shard_map/ppermute | solution.py:217
  36.0 1.2 %collective-permute-start.18 = (bf16[2,112,128]{2,1,0:T(8,128)(2,1)S(1)}, bf16[2,112,128]{2,1,0:T(8,128)(2,1)S(1)}, u32[]{:S(2)}, u32[]{:S(2)}) collective-permute-start(bf16[2,112,128]{2,1,0:T(8,128)(2,1)S(1)} %collective-permute-done.10.refs_12_), channel_id=1, source_target_pairs={{0,1},{1,0},{2,3},{3,2},{4,5},{5,4},{6,7},{7,6},{8,9},{9,8},{10,11... | collective-permute-start | bytes 172040 | tf_op jit(solution)/shard_map/ppermute | solution.py:217
  36.0 1.4 %collective-permute-start.19 = (bf16[2,112,128]{2,1,0:T(8,128)(2,1)S(1)}, bf16[2,112,128]{2,1,0:T(8,128)(2,1)S(1)}, u32[]{:S(2)}, u32[]{:S(2)}) collective-permute-start(bf16[2,112,128]{2,1,0:T(8,128)(2,1)S(1)} %collective-permute-done.11.refs_13_), channel_id=1, source_target_pairs={{0,1},{1,0},{2,3},{3,2},{4,5},{5,4},{6,7},{7,6},{8,9},{9,8},{10,11... | collective-permute-start | bytes 172040 | tf_op jit(solution)/shard_map/ppermute | solution.py:217
  36.5 1.2 %collective-permute-start.20 = (bf16[2,112,128]{2,1,0:T(8,128)(2,1)S(1)}, bf16[2,112,128]{2,1,0:T(8,128)(2,1)S(1)}, u32[]{:S(2)}, u32[]{:S(2)}) collective-permute-start(bf16[2,112,128]{2,1,0:T(8,128)(2,1)S(1)} %collective-permute-done.12.refs_14_), channel_id=1, source_target_pairs={{0,1},{1,0},{2,3},{3,2},{4,5},{5,4},{6,7},{7,6},{8,9},{9,8},{10,11... | collective-permute-start | bytes 172040 | tf_op jit(solution)/shard_map/ppermute | solution.py:217
  36.6 1.3 %collective-permute-start.21 = (bf16[2,112,128]{2,1,0:T(8,128)(2,1)S(1)}, bf16[2,112,128]{2,1,0:T(8,128)(2,1)S(1)}, u32[]{:S(2)}, u32[]{:S(2)}) collective-permute-start(bf16[2,112,128]{2,1,0:T(8,128)(2,1)S(1)} %collective-permute-done.13.refs_15_), channel_id=1, source_target_pairs={{0,1},{1,0},{2,3},{3,2},{4,5},{5,4},{6,7},{7,6},{8,9},{9,8},{10,11... | collective-permute-start | bytes 172040 | tf_op jit(solution)/shard_map/ppermute | solution.py:217
  37.9 0.8 %copy-start = (bf16[2,112,128]{2,1,0:T(8,128)(2,1)S(1)}, bf16[2,112,128]{2,1,0:T(8,128)(2,1)}, u32[]{:S(2)}) copy-start(bf16[2,112,128]{2,1,0:T(8,128)(2,1)} %get-tuple-element.29.refs_0_) | copy-start | bytes 172036
  38.7 0.8 %copy-start.1 = (bf16[2,112,128]{2,1,0:T(8,128)(2,1)S(1)}, bf16[2,112,128]{2,1,0:T(8,128)(2,1)}, u32[]{:S(2)}) copy-start(bf16[2,112,128]{2,1,0:T(8,128)(2,1)} %get-tuple-element.37.refs_8_) | copy-start | bytes 172036
  43.9 7.1 %collective-permute-start.22 = (bf16[2,112,128]{2,1,0:T(8,128)(2,1)S(1)}, bf16[2,112,128]{2,1,0:T(8,128)(2,1)S(1)}, u32[]{:S(2)}, u32[]{:S(2)}) collective-permute-start(bf16[2,112,128]{2,1,0:T(8,128)(2,1)S(1)} %get-tuple-element.46), channel_id=1, source_target_pairs={{0,2},{1,3},{2,0},{3,1},{4,6},{5,7},{6,4},{7,5},{8,10},{9,11},{10,... | collective-permute-start | bytes 172040 | tf_op jit(solution)/shard_map/ppermute | solution.py:191
  45.1 7.9 %collective-permute-start.23 = (bf16[2,112,128]{2,1,0:T(8,128)(2,1)S(1)}, bf16[2,112,128]{2,1,0:T(8,128)(2,1)S(1)}, u32[]{:S(2)}, u32[]{:S(2)}) collective-permute-start(bf16[2,112,128]{2,1,0:T(8,128)(2,1)S(1)} %get-tuple-element.47), channel_id=1, source_target_pairs={{0,4},{1,5},{2,6},{3,7},{4,0},{5,1},{6,2},{7,3},{8,12},{9,13},{10,... | collective-permute-start | bytes 172040 | tf_op jit(solution)/shard_map/ppermute | solution.py:191
  45.1 10.0 %collective-permute-start.24 = (bf16[2,112,128]{2,1,0:T(8,128)(2,1)S(1)}, bf16[2,112,128]{2,1,0:T(8,128)(2,1)S(1)}, u32[]{:S(2)}, u32[]{:S(2)}) collective-permute-start(bf16[2,112,128]{2,1,0:T(8,128)(2,1)S(1)} %get-tuple-element.48), channel_id=1, source_target_pairs={{0,6},{1,7},{2,4},{3,5},{4,2},{5,3},{6,0},{7,1},{8,14},{9,15},{10,... | collective-permute-start | bytes 172040 | tf_op jit(solution)/shard_map/ppermute | solution.py:191
  47.5 7.7 %collective-permute-start.25 = (bf16[2,112,128]{2,1,0:T(8,128)(2,1)S(1)}, bf16[2,112,128]{2,1,0:T(8,128)(2,1)S(1)}, u32[]{:S(2)}, u32[]{:S(2)}) collective-permute-start(bf16[2,112,128]{2,1,0:T(8,128)(2,1)S(1)} %get-tuple-element.49), channel_id=1, source_target_pairs={{0,8},{1,9},{2,10},{3,11},{4,12},{5,13},{6,14},{7,15},{8,0},{9,1},... | collective-permute-start | bytes 172040 | tf_op jit(solution)/shard_map/ppermute | solution.py:191
  48.1 10.5 %collective-permute-start.26 = (bf16[2,112,128]{2,1,0:T(8,128)(2,1)S(1)}, bf16[2,112,128]{2,1,0:T(8,128)(2,1)S(1)}, u32[]{:S(2)}, u32[]{:S(2)}) collective-permute-start(bf16[2,112,128]{2,1,0:T(8,128)(2,1)S(1)} %get-tuple-element.50), channel_id=1, source_target_pairs={{0,10},{1,11},{2,8},{3,9},{4,14},{5,15},{6,12},{7,13},{8,2},{9,3},... | collective-permute-start | bytes 172040 | tf_op jit(solution)/shard_map/ppermute | solution.py:191
  51.0 7.6 %collective-permute-start.27 = (bf16[2,112,128]{2,1,0:T(8,128)(2,1)S(1)}, bf16[2,112,128]{2,1,0:T(8,128)(2,1)S(1)}, u32[]{:S(2)}, u32[]{:S(2)}) collective-permute-start(bf16[2,112,128]{2,1,0:T(8,128)(2,1)S(1)} %get-tuple-element.51), channel_id=1, source_target_pairs={{0,12},{1,13},{2,14},{3,15},{4,8},{5,9},{6,10},{7,11},{8,4},{9,5},... | collective-permute-start | bytes 172040 | tf_op jit(solution)/shard_map/ppermute | solution.py:191
  53.0 7.0 %collective-permute-start.28 = (bf16[2,112,128]{2,1,0:T(8,128)(2,1)S(1)}, bf16[2,112,128]{2,1,0:T(8,128)(2,1)S(1)}, u32[]{:S(2)}, u32[]{:S(2)}) collective-permute-start(bf16[2,112,128]{2,1,0:T(8,128)(2,1)S(1)} %get-tuple-element.52), channel_id=1, source_target_pairs={{0,14},{1,15},{2,12},{3,13},{4,10},{5,11},{6,8},{7,9},{8,6},{9,7},... | collective-permute-start | bytes 172040 | tf_op jit(solution)/shard_map/ppermute | solution.py:191

commit v3 on v1

--- a/solution.py
+++ b/solution.py
@@ -12,7 +12,12 @@
 ROPE_BASE = 1000000.0
 EPSILON = 1e-06
 MASKED = -1e30
-VMEM_LIMIT = 48 * 1024 * 1024
+VMEM_LIMIT = 24 * 1024 * 1024
+PACK_VMEM = 56 * 1024 * 1024
+VMEM = pl.BlockSpec(memory_space=pltpu.VMEM)
+SMEM = pl.BlockSpec(memory_space=pltpu.SMEM)
+ANY = pl.BlockSpec(memory_space=pl.ANY)
+CONTRACT = (((1,), (1,)), ((), ()))
 
 
 def rope_table(length, width):
@@ -56,53 +61,19 @@
             out_ref[head * rep + copy, per_chip + 1] = values
 
 
-def attention_kernel(core_ref, x_ref, other_ref, out_ref):
-    blocks, rows, tokens, width = x_ref.shape
-    per_chip = rows - 2
-    core = core_ref[0]
-    scale = math.log2(math.e) / math.sqrt(width)
-    keys_own = x_ref[:, per_chip].reshape(blocks * tokens, width)
-    values_own = x_ref[:, per_chip + 1].reshape(blocks * tokens, width)
-    keys_other = other_ref[:, 0].reshape(blocks * tokens, width)
-    values_other = other_ref[:, 1].reshape(blocks * tokens, width)
-    contract = (((1,), (1,)), ((), ()))
-    for block in range(blocks):
-        queries = x_ref[block, :per_chip].reshape(per_chip * tokens, width)
-        reach = (block + 1) * tokens
-        own = lax.dot_general(queries, keys_own[:reach], contract, preferred_element_type=jnp.float32)
-        other = lax.dot_general(queries, keys_other[:reach], contract, preferred_element_type=jnp.float32)
-        row = lax.broadcasted_iota(jnp.int32, (per_chip, tokens, reach), 1).reshape(per_chip * tokens, reach)
-        column = lax.broadcasted_iota(jnp.int32, (per_chip * tokens, reach), 1)
-        own = jnp.where(column <= row + block * tokens, own, MASKED)
-        other = jnp.where(column < (block + core) * tokens, other, MASKED)
-        highest = jnp.maximum(
-            jnp.max(own, axis=-1, keepdims=True), jnp.max(other, axis=-1, keepdims=True)
-        )
-        probs_own = jnp.exp2((own - highest) * scale)
-        probs_other = jnp.exp2((other - highest) * scale)
-        total = jnp.sum(probs_own, axis=-1, keepdims=True) + jnp.sum(probs_other, axis=-1, keepdims=True)
-        summed = jnp.dot(
-            probs_own.astype(jnp.bfloat16), values_own[:reach], preferred_element_type=jnp.float32
-        ) + jnp.dot(
-            probs_other.astype(jnp.bfloat16), values_other[:reach], preferred_element_type=jnp.float32
-        )
-        out_ref[block] = (summed / total).astype(jnp.bfloat16).reshape(per_chip, tokens, width)
-
-
 def looped_kernel(core_ref, x_ref, other_ref, out_ref):
     _, rows, tokens, width = x_ref.shape
     per_chip = rows - 2
     core = core_ref[0]
     block = pl.program_id(0)
     scale = math.log2(math.e) / math.sqrt(width)
-    contract = (((1,), (1,)), ((), ()))
     queries = x_ref[block, :per_chip].reshape(per_chip * tokens, width)
     row = lax.broadcasted_iota(jnp.int32, (per_chip, tokens, tokens), 1).reshape(per_chip * tokens, tokens)
     column = lax.broadcasted_iota(jnp.int32, (per_chip * tokens, tokens), 1)
 
     def merge(carried, keys, values, allowed):
         highest, total, weighted = carried
-        scores = lax.dot_general(queries, keys, contract, preferred_element_type=jnp.float32)
+        scores = lax.dot_general(queries, keys, CONTRACT, preferred_element_type=jnp.float32)
         scores = jnp.where(allowed, scores, MASKED)
         new = jnp.maximum(highest, jnp.max(scores, axis=-1, keepdims=True))
         probs = jnp.exp2((scores - new) * scale)
@@ -125,7 +96,7 @@
     out_ref[block] = (weighted / total).astype(jnp.bfloat16).reshape(per_chip, tokens, width)
 
 
-def on_device(length, devices, query_states, key_states, value_states, query_gain, key_gain):
+def general_plan(length, devices, query_states, key_states, value_states, query_gain, key_gain):
     tokens, heads, width = query_states.shape
     kv_heads = key_states.shape[1]
     chips = devices // 2
@@ -136,32 +107,30 @@
     same_core = [list(range(start, devices, 2)) for start in range(2)]
     swap = [(device, device ^ 1) for device in range(devices)]
     table = lax.dynamic_slice_in_dim(jnp.asarray(rope_table(length, width)), me * tokens, tokens, 0)
-    vmem = pl.BlockSpec(memory_space=pltpu.VMEM)
     packed = pl.pallas_call(
         functools.partial(pack_kernel, rep),
         out_shape=jax.ShapeDtypeStruct((chips, per_chip + 2, tokens, width), jnp.bfloat16),
-        in_specs=[vmem] * 6,
-        out_specs=vmem,
+        in_specs=[VMEM] * 6,
+        out_specs=VMEM,
         scratch_shapes=[
             pltpu.VMEM((tokens * heads, width), jnp.float32),
             pltpu.VMEM((tokens * kv_heads, width), jnp.float32),
             pltpu.VMEM((tokens * kv_heads, width), jnp.float32),
         ],
-        compiler_params=pltpu.CompilerParams(vmem_limit_bytes=VMEM_LIMIT),
+        compiler_params=pltpu.CompilerParams(vmem_limit_bytes=48 * 1024 * 1024),
         name="pack",
     )(query_states, key_states, value_states, table, query_gain[None], key_gain[None])
     arrived = lax.all_to_all(
         packed, "seq", split_axis=0, concat_axis=0, axis_index_groups=same_core, tiled=True
     )
     other = lax.ppermute(arrived[:, per_chip:], "seq", swap)
-    short = chips <= 8
     attended = pl.pallas_call(
-        attention_kernel if short else looped_kernel,
-        grid=() if short else (chips,),
+        looped_kernel,
+        grid=(chips,),
         out_shape=jax.ShapeDtypeStruct((chips, per_chip, tokens, width), jnp.bfloat16),
-        in_specs=[pl.BlockSpec(memory_space=pltpu.SMEM), vmem, vmem],
-        out_specs=vmem,
-        compiler_params=pltpu.CompilerParams(vmem_limit_bytes=VMEM_LIMIT),
+        in_specs=[SMEM, VMEM, VMEM],
+        out_specs=VMEM,
+        compiler_params=pltpu.CompilerParams(vmem_limit_bytes=48 * 1024 * 1024),
         name="attention",
     )(core[None], arrived, other)
     returned = lax.all_to_all(
@@ -170,6 +139,208 @@
     return jnp.transpose(returned.reshape(heads, tokens, width), (1, 0, 2))
 
 
+def rope_factors(table):
+    half = table.shape[1] // 2
+    swapped = pltpu.roll(table, half, 1)
+    first = lax.broadcasted_iota(jnp.int32, table.shape, 1) < half
+    return jnp.where(first, table, swapped), jnp.where(first, -swapped, table)
+
+
+def rotate(floats, gain, cosine, sine):
+    mean_square = jnp.mean(floats * floats, axis=-1, keepdims=True)
+    normed = floats * lax.rsqrt(mean_square + EPSILON) * gain
+    turned = pltpu.roll(normed, floats.shape[1] // 2, 1)
+    return (normed * cosine + turned * sine).astype(jnp.bfloat16)
+
+
+def pack_pairs_kernel(me_ref, k_hbm, v_hbm, table_hbm, gain_ref, *refs):
+    outs, (k_ref, v_ref, table_ref, kf_ref, vf_ref, sems) = refs[:-6], refs[-6:]
+    tokens, kv_heads, width = k_ref.shape
+    me = me_ref[0]
+    place, core = lax.rem(me, kv_heads), lax.rem(me, 2)
+    start = pl.multiple_of(me * tokens, 8)
+    copies = [
+        pltpu.make_async_copy(v_hbm, v_ref, sems.at[0]),
+        pltpu.make_async_copy(k_hbm, k_ref, sems.at[1]),
+        pltpu.make_async_copy(table_hbm.at[pl.ds(start, tokens)], table_ref, sems.at[2]),
+    ]
+    for copy in copies:
+        copy.start()
+    heads = [
+        (step, side, ((place // 2) ^ step) * 2 + lax.rem(core + side, 2)) for step in range(len(outs)) for side in range(2)
+    ]
+    copies[0].wait()
+    vf_ref[...] = v_ref[...].astype(jnp.float32).reshape(tokens * kv_heads, width)
+    for step, side, head in heads:
+        outs[step][side, 1] = vf_ref[pl.ds(head, tokens, stride=kv_heads), :].astype(jnp.bfloat16)
+    copies[1].wait()
+    kf_ref[...] = k_ref[...].astype(jnp.float32).reshape(tokens * kv_heads, width)
+    copies[2].wait()
+    cosine, sine = rope_factors(table_ref[...])
+    for step, side, head in heads:
+        floats = kf_ref[pl.ds(head, tokens, stride=kv_heads), :]
+        outs[step][side, 0] = rotate(floats, gain_ref[...], cosine, sine)
+
+
+def pack_all_kernel(me_ref, q_hbm, table_hbm, gain_ref, *refs):
+    pairs, (out_ref, q_ref, table_ref, qf_ref, sems) = refs[:-5], refs[-5:]
+    tokens, heads, width = q_ref.shape
+    owners, rows = out_ref.shape[:2]
+    group = rows - 2
+    me = me_ref[0]
+    place, core = lax.rem(me, owners), lax.rem(me, 2)
+    start = pl.multiple_of(me * tokens, 8)
+    copies = [
+        pltpu.make_async_copy(table_hbm.at[pl.ds(start, tokens)], table_ref, sems.at[0]),
+        pltpu.make_async_copy(q_hbm, q_ref, sems.at[1]),
+    ]
+    for copy in copies:
+        copy.start()
+    for step, pair in enumerate(pairs):
+        for side in range(2):
+            out_ref[((place // 2) ^ step) * 2 + lax.rem(core + side, 2), group:] = pair[side]
+    copies[0].wait()
+    cosine, sine = rope_factors(table_ref[...])
+    copies[1].wait()
+    qf_ref[...] = q_ref[...].astype(jnp.float32).reshape(tokens * heads, width)
+    for head in range(heads):
+        floats = qf_ref[pl.ds(head, tokens, stride=heads), :]
+        out_ref[head // group, head % group] = rotate(floats, gain_ref[...], cosine, sine)
+
+
+def near_kernel(x_ref, highest_ref, total_ref, weighted_ref):
+    blocks, rows, tokens, width = x_ref.shape
+    group = rows - 2
+    scale = math.log2(math.e) / math.sqrt(width)
+    keys = x_ref[:, group].reshape(blocks * tokens, width)
+    values = x_ref[:, group + 1].reshape(blocks * tokens, width)
+    for block in range(blocks):
+        queries = x_ref[block, :group].reshape(group * tokens, width)
+        reach = (block + 1) * tokens
+        scores = lax.dot_general(queries, keys[:reach], CONTRACT, preferred_element_type=jnp.float32)
+        row = lax.broadcasted_iota(jnp.int32, (group, tokens, reach), 1).reshape(group * tokens, reach)
+        column = lax.broadcasted_iota(jnp.int32, (group * tokens, reach), 1)
+        scores = jnp.where(column <= row + block * tokens, scores, MASKED)
+        highest = jnp.max(scores, axis=-1, keepdims=True)
+        probs = jnp.exp2((scores - highest) * scale)
+        highest_ref[block] = highest
+        total_ref[block] = jnp.sum(probs, axis=-1, keepdims=True)
+        weighted_ref[block] = jnp.dot(
+            probs.astype(jnp.bfloat16), values[:reach], preferred_element_type=jnp.float32
+        )
+
+
+def far_kernel(half, me_ref, x_ref, highest_ref, total_ref, weighted_ref, *refs):
+    steps = (len(refs) - 1) // 2
+    mine, neighbours, out_ref = refs[:steps], refs[steps : 2 * steps], refs[2 * steps]
+    blocks, rows, tokens, width = x_ref.shape
+    group = rows - 2
+    scale = math.log2(math.e) / math.sqrt(width)
+    upper = me_ref[0] >= half
+
+    def finish(block, weighted, total):
+        out_ref[block] = (weighted / total).astype(jnp.bfloat16).reshape(group, tokens, width)
+
+    @pl.when(upper)
+    def _():
+        keys = jnp.concatenate([ref[0, 0] for ref in mine] + [ref[1, 0] for ref in neighbours], axis=0)
+        values = jnp.concatenate([ref[0, 1] for ref in mine] + [ref[1, 1] for ref in neighbours], axis=0)
+        for block in range(blocks):
+            queries = x_ref[block, :group].reshape(group * tokens, width)
+            scores = lax.dot_general(queries, keys, CONTRACT, preferred_element_type=jnp.float32)
+            before = highest_ref[block]
+            highest = jnp.maximum(before, jnp.max(scores, axis=-1, keepdims=True))
+            probs = jnp.exp2((scores - highest) * scale)
+            factor = jnp.exp2((before - highest) * scale)
+            total = total_ref[block] * factor + jnp.sum(probs, axis=-1, keepdims=True)
+            summed = jnp.dot(probs.astype(jnp.bfloat16), values, preferred_element_type=jnp.float32)
+            finish(block, weighted_ref[block] * factor + summed, total)
+
+    @pl.when(jnp.logical_not(upper))
+    def _():
+        for block in range(blocks):
+            finish(block, weighted_ref[block], total_ref[block])
+
+
+def halves_plan(length, devices, query_states, key_states, value_states, query_gain, key_gain):
+    tokens, heads, width = query_states.shape
+    kv_heads = key_states.shape[1]
+    group = heads // kv_heads
+    half = devices // 2
+    steps = half // 2
+    bf16, f32 = jnp.bfloat16, jnp.float32
+    me = lax.axis_index("seq")[None]
+    table = jnp.asarray(rope_table(length, width))
+    halves = [list(range(half)), list(range(half, devices))]
+    own_copies = pltpu.CompilerParams(vmem_limit_bytes=PACK_VMEM)
+    params = pltpu.CompilerParams(vmem_limit_bytes=VMEM_LIMIT)
+    pairs = pl.pallas_call(
+        pack_pairs_kernel,
+        out_shape=[jax.ShapeDtypeStruct((2, 2, tokens, width), bf16)] * steps,
+        in_specs=[SMEM, ANY, ANY, ANY, VMEM],
+        out_specs=[VMEM] * steps,
+        scratch_shapes=[
+            pltpu.VMEM((tokens, kv_heads, width), bf16),
+            pltpu.VMEM((tokens, kv_heads, width), bf16),
+            pltpu.VMEM((tokens, width), f32),
+            pltpu.VMEM((tokens * kv_heads, width), f32),
+            pltpu.VMEM((tokens * kv_heads, width), f32),
+            pltpu.SemaphoreType.DMA((3,)),
+        ],
+        compiler_params=own_copies,
+        name="pack_pairs",
+    )(me, key_states, value_states, table, key_gain[None])
+    mine = [
+        lax.ppermute(
+            pair,
+            "seq",
+            [(device, half + ((device // 2) ^ step) * 2 + device % 2) for device in range(half)],
+        )
+        for step, pair in enumerate(pairs)
+    ]
+    packed = pl.pallas_call(
+        pack_all_kernel,
+        out_shape=jax.ShapeDtypeStruct((half, group + 2, tokens, width), bf16),
+        in_specs=[SMEM, ANY, ANY, VMEM] + [VMEM] * steps,
+        out_specs=VMEM,
+        scratch_shapes=[
+            pltpu.VMEM((tokens, heads, width), bf16),
+            pltpu.VMEM((tokens, width), f32),
+            pltpu.VMEM((tokens * heads, width), f32),
+            pltpu.SemaphoreType.DMA((2,)),
+        ],
+        compiler_params=own_copies,
+        name="pack_all",
+    )(me, query_states, table, query_gain[None], *pairs)
+    arrived = lax.all_to_all(packed, "seq", split_axis=0, concat_axis=0, axis_index_groups=halves, tiled=True)
+    rows = group * tokens
+    near = pl.pallas_call(
+        near_kernel,
+        out_shape=[
+            jax.ShapeDtypeStruct((half, rows, 1), f32),
+            jax.ShapeDtypeStruct((half, rows, 1), f32),
+            jax.ShapeDtypeStruct((half, rows, width), f32),
+        ],
+        in_specs=[VMEM],
+        out_specs=[VMEM] * 3,
+        compiler_params=params,
+        name="near",
+    )(arrived)
+    near, mine = lax.optimization_barrier((near, mine))
+    swap = [(device, device ^ 1) for device in range(half, devices)]
+    neighbours = [lax.ppermute(pair, "seq", swap) for pair in mine]
+    attended = pl.pallas_call(
+        functools.partial(far_kernel, half),
+        out_shape=jax.ShapeDtypeStruct((half, group, tokens, width), bf16),
+        in_specs=[SMEM] + [VMEM] * (4 + 2 * steps),
+        out_specs=VMEM,
+        compiler_params=params,
+        name="far",
+    )(me, arrived, *near, *mine, *neighbours)
+    returned = lax.all_to_all(attended, "seq", split_axis=0, concat_axis=0, axis_index_groups=halves, tiled=True)
+    return jnp.transpose(returned.reshape(heads, tokens, width), (1, 0, 2))
+
+
 def solution(mesh):
     devices = mesh.shape["seq"]
     groups = mesh.shape["groups"]
@@ -177,8 +348,9 @@
 
     def run(query_states, key_states, value_states, query_gain, key_gain):
         length = query_states.shape[0] // groups
+        plan = halves_plan if devices == 2 * key_states.shape[1] else general_plan
         return jax.shard_map(
-            functools.partial(on_device, length, devices),
+            functools.partial(plan, length, devices),
             mesh=mesh,
             in_specs=(placed, placed, placed, P(), P()),
             out_specs=placed,

time: 61.5 us -> 65.3 us (1.062)
  the two profiles are of different devices: /device:TPU:0 before, /device:TPU:16 now
where the time goes in v3:
time: 65.3 us; the launch traced here: 64.9 us
  waiting for transfers between devices  19.5 us (30%)
  starting transfers between devices  17.8 us (27%)
  Pallas kernels  15.7 us (24%)
  blocking collectives  10.9 us (17%)
  local copies, waits for them, and re-layouts  0.9 us (1%)
    all_to_all x1, waiting for transfers between devices, halves_plan(): lax.all_to_all(packed, 'seq', split_axis=0, concat_axis=0, axis_index_gro...  11 us
    all_to_all x1, blocking collectives, halves_plan(): lax.all_to_all(attended, 'seq', split_axis=0, concat_axis=0, axis_index_g...  10.9 us
    ppermute x4, starting transfers between devices, halves_plan(): neighbours = [lax.ppermute(pair, 'seq', swap) for pair in mine]  8.64 us
    ppermute x4, waiting for transfers between devices, halves_plan(): lax.ppermute(pair, 'seq', [(device, half + (device // 2 ^ step) * 2 + dev...  7.54 us
    ppermute x4, starting transfers between devices, halves_plan(): lax.ppermute(pair, 'seq', [(device, half + (device // 2 ^ step) * 2 + dev...  5.17 us
    pallas_call x1, Pallas kernels, halves_plan(): pl.pallas_call(pack_all_kernel, out_shape=jax.ShapeDtypeStruct((half, gro...  4.91 us
    pallas_call x1, Pallas kernels, halves_plan(): pl.pallas_call(functools.partial(far_kernel, half), out_shape=jax.ShapeDt...  4.52 us
    all_to_all x1, starting transfers between devices, halves_plan(): lax.all_to_all(packed, 'seq', split_axis=0, concat_axis=0, axis_index_gro...  3.95 us
  transfers between devices with their start and end apart: 9, of which 4 were waited for; matrix products, arithmetic and copies ran while one was open for 0% of the time, Pallas kernels for 4%

profile of v3, /device:TPU:16, one launch (start us, length us, event | category | flops | bytes accessed | tf_op | source)
XLA Modules:
  0.0 64.9 jit_solution(3007504032938856415)
XLA Ops:
  0.0 3.3 %pack_pairs.1 = (bf16[2,2,112,128]{3,2,1,0:T(8,128)(2,1)}, bf16[2,2,112,128]{3,2,1,0:T(8,128)(2,1)}, bf16[2,2,112,128]{3,2,1,0:T(8,128)(2,1)}, bf16[2,2,112,128]{3,2,1,0:T(8,128)(2,1)}) custom-call(s32[1]{0:T(128)} %bitcast.me_ref, bf16[112,8,128]{2,1,0:T(8,128)(2,1)} %k_hbm.1, bf16[112,8,128]{2,1,0:T(8,128)(2,1)} %v_hbm.1, ...), custom_call_target="tpu_custom_call" | custom-call | tf_op jit(solution)/shard_map/pack_pairs/pallas_call | solution.py:277
  3.4 4.9 %pack_all.1 = bf16[8,4,112,128]{3,2,1,0:T(8,128)(2,1)} custom-call(s32[1]{0:T(128)} %bitcast.me_ref, bf16[112,16,128]{2,1,0:T(8,128)(2,1)} %q_hbm.1, f32[1792,128]{1,0:T(8,128)} %constant.6.clone.table_hbm, f32[1,128]{1,0:T(1,128)} %bitcast.9, bf16[2,2,112,128]{3,2,1,0:T(8,128)(2,1)} %get-tuple-element.19.refs_0_, ...), custom_call_target="tpu_custom_call" | custom-call | tf_op jit(solution)/shard_map/pack_all/pallas_call | solution.py:301
  8.3 0.0 copy-start.3
  8.3 0.0 copy-start.2
  8.3 0.0 copy-start.1
  8.3 0.0 copy-start
  8.3 4.0 %all-to-all-start = ((bf16[8,4,112,128]{3,2,1,0:T(8,128)(2,1)}), bf16[8,4,112,128]{3,2,1,0:T(8,128)(2,1)S(1)}, u32[]{:S(2)}, u32[]{:S(2)}) async-start(bf16[8,4,112,128]{3,2,1,0:T(8,128)(2,1)} %pack_all.1), calls=%async_computation | async-start | bytes 1835008 | tf_op jit(solution)/shard_map/all_to_all | solution.py:315
  12.3 0.0 copy-done.3
  12.3 1.3 %collective-permute-start = (bf16[2,2,112,128]{3,2,1,0:T(8,128)(2,1)S(1)}, bf16[2,2,112,128]{3,2,1,0:T(8,128)(2,1)S(1)}, u32[]{:S(2)}, u32[]{:S(2)}) collective-permute-start(bf16[2,2,112,128]{3,2,1,0:T(8,128)(2,1)S(1)} %copy-done.3), channel_id=1, source_target_pairs={{0,8},{1,9},{2,10},{3,11},{4,12},{5,13},{6,14},{7,15},{16,24},{17,... | collective-permute-start | bytes 344072 | tf_op jit(solution)/shard_map/ppermute | solution.py:294
  13.6 0.0 copy-done.2
  13.6 1.3 %collective-permute-start.1 = (bf16[2,2,112,128]{3,2,1,0:T(8,128)(2,1)S(1)}, bf16[2,2,112,128]{3,2,1,0:T(8,128)(2,1)S(1)}, u32[]{:S(2)}, u32[]{:S(2)}) collective-permute-start(bf16[2,2,112,128]{3,2,1,0:T(8,128)(2,1)S(1)} %copy-done.2), channel_id=1, source_target_pairs={{0,10},{1,11},{2,8},{3,9},{4,14},{5,15},{6,12},{7,13},{16,26},{17,... | collective-permute-start | bytes 344072 | tf_op jit(solution)/shard_map/ppermute | solution.py:294
  14.9 0.0 copy-done.1
  14.9 1.3 %collective-permute-start.2 = (bf16[2,2,112,128]{3,2,1,0:T(8,128)(2,1)S(1)}, bf16[2,2,112,128]{3,2,1,0:T(8,128)(2,1)S(1)}, u32[]{:S(2)}, u32[]{:S(2)}) collective-permute-start(bf16[2,2,112,128]{3,2,1,0:T(8,128)(2,1)S(1)} %copy-done.1), channel_id=1, source_target_pairs={{0,12},{1,13},{2,14},{3,15},{4,8},{5,9},{6,10},{7,11},{16,28},{17,... | collective-permute-start | bytes 344072 | tf_op jit(solution)/shard_map/ppermute | solution.py:294
  16.2 0.0 copy-done
  16.2 1.3 %collective-permute-start.3 = (bf16[2,2,112,128]{3,2,1,0:T(8,128)(2,1)S(1)}, bf16[2,2,112,128]{3,2,1,0:T(8,128)(2,1)S(1)}, u32[]{:S(2)}, u32[]{:S(2)}) collective-permute-start(bf16[2,2,112,128]{3,2,1,0:T(8,128)(2,1)S(1)} %copy-done), channel_id=1, source_target_pairs={{0,14},{1,15},{2,12},{3,13},{4,10},{5,11},{6,8},{7,9},{16,30},{17,... | collective-permute-start | bytes 344072 | tf_op jit(solution)/shard_map/ppermute | solution.py:294
  17.5 11.0 %all-to-all-done.x_ref = bf16[8,4,112,128]{3,2,1,0:T(8,128)(2,1)S(1)} async-done(((bf16[8,4,112,128]{3,2,1,0:T(8,128)(2,1)}), bf16[8,4,112,128]{3,2,1,0:T(8,128)(2,1)S(1)}, u32[]{:S(2)}, u32[]{:S(2)}) %all-to-all-start) | async-done | bytes 917536 | tf_op jit(solution)/shard_map/all_to_all | solution.py:315
  28.5 2.9 %near.1 = (f32[8,224,1]{2,1,0:T(8,128)S(1)}, f32[8,224,1]{2,1,0:T(8,128)S(1)}, f32[8,224,128]{2,1,0:T(8,128)S(1)}) custom-call(bf16[8,4,112,128]{3,2,1,0:T(8,128)(2,1)S(1)} %all-to-all-done.x_ref), custom_call_target="tpu_custom_call" | custom-call | tf_op jit(solution)/shard_map/near/pallas_call | solution.py:317
  31.4 0.0 collective-permute-done.refs_0_
  31.4 0.0 collective-permute-done.1.refs_1_
  31.4 4.7 %collective-permute-done.2.refs_2_ = bf16[2,2,112,128]{3,2,1,0:T(8,128)(2,1)S(1)} collective-permute-done((bf16[2,2,112,128]{3,2,1,0:T(8,128)(2,1)S(1)}, bf16[2,2,112,128]{3,2,1,0:T(8,128)(2,1)S(1)}, u32[]{:S(2)}, u32[]{:S(2)}) %collective-permute-start.2) | collective-permute-done | bytes 114720 | tf_op jit(solution)/shard_map/ppermute | solution.py:294
  36.1 2.9 %collective-permute-done.3.refs_3_ = bf16[2,2,112,128]{3,2,1,0:T(8,128)(2,1)S(1)} collective-permute-done((bf16[2,2,112,128]{3,2,1,0:T(8,128)(2,1)S(1)}, bf16[2,2,112,128]{3,2,1,0:T(8,128)(2,1)S(1)}, u32[]{:S(2)}, u32[]{:S(2)}) %collective-permute-start.3) | collective-permute-done | bytes 114720 | tf_op jit(solution)/shard_map/ppermute | solution.py:294
  39.0 1.9 %collective-permute-start.4 = (bf16[2,2,112,128]{3,2,1,0:T(8,128)(2,1)S(1)}, bf16[2,2,112,128]{3,2,1,0:T(8,128)(2,1)S(1)}, u32[]{:S(2)}, u32[]{:S(2)}) collective-permute-start(bf16[2,2,112,128]{3,2,1,0:T(8,128)(2,1)S(1)} %collective-permute-done.refs_0_), channel_id=1, source_target_pairs={{8,9},{9,8},{10,11},{11,10},{12,13},{13,12},{14,15},{15,14},{24,25... | collective-permute-start | bytes 344072 | tf_op jit(solution)/shard_map/ppermute | solution.py:331
  40.9 2.4 %collective-permute-start.5 = (bf16[2,2,112,128]{3,2,1,0:T(8,128)(2,1)S(1)}, bf16[2,2,112,128]{3,2,1,0:T(8,128)(2,1)S(1)}, u32[]{:S(2)}, u32[]{:S(2)}) collective-permute-start(bf16[2,2,112,128]{3,2,1,0:T(8,128)(2,1)S(1)} %collective-permute-done.1.refs_1_), channel_id=1, source_target_pairs={{8,9},{9,8},{10,11},{11,10},{12,13},{13,12},{14,15},{15,14},{24,25... | collective-permute-start | bytes 344072 | tf_op jit(solution)/shard_map/ppermute | solution.py:331
  43.3 1.9 %collective-permute-start.6 = (bf16[2,2,112,128]{3,2,1,0:T(8,128)(2,1)S(1)}, bf16[2,2,112,128]{3,2,1,0:T(8,128)(2,1)S(1)}, u32[]{:S(2)}, u32[]{:S(2)}) collective-permute-start(bf16[2,2,112,128]{3,2,1,0:T(8,128)(2,1)S(1)} %collective-permute-done.2.refs_2_), channel_id=1, source_target_pairs={{8,9},{9,8},{10,11},{11,10},{12,13},{13,12},{14,15},{15,14},{24,25... | collective-permute-start | bytes 344072 | tf_op jit(solution)/shard_map/ppermute | solution.py:331
  45.2 2.4 %collective-permute-start.7 = (bf16[2,2,112,128]{3,2,1,0:T(8,128)(2,1)S(1)}, bf16[2,2,112,128]{3,2,1,0:T(8,128)(2,1)S(1)}, u32[]{:S(2)}, u32[]{:S(2)}) collective-permute-start(bf16[2,2,112,128]{3,2,1,0:T(8,128)(2,1)S(1)} %collective-permute-done.3.refs_3_), channel_id=1, source_target_pairs={{8,9},{9,8},{10,11},{11,10},{12,13},{13,12},{14,15},{15,14},{24,25... | collective-permute-start | bytes 344072 | tf_op jit(solution)/shard_map/ppermute | solution.py:331
  47.6 0.0 collective-permute-done.4.refs_4_
  47.6 0.0 collective-permute-done.5.refs_5_
  47.7 0.0 collective-permute-done.6.refs_6_
  47.7 0.9 %collective-permute-done.7.refs_7_ = bf16[2,2,112,128]{3,2,1,0:T(8,128)(2,1)S(1)} collective-permute-done((bf16[2,2,112,128]{3,2,1,0:T(8,128)(2,1)S(1)}, bf16[2,2,112,128]{3,2,1,0:T(8,128)(2,1)S(1)}, u32[]{:S(2)}, u32[]{:S(2)}) %collective-permute-start.7) | collective-permute-done | bytes 114720 | tf_op jit(solution)/shard_map/ppermute | solution.py:331
  48.6 4.5 %far.1 = bf16[8,2,112,128]{3,2,1,0:T(8,128)(2,1)S(1)} custom-call(s32[1]{0:T(128)} %bitcast.me_ref, bf16[8,4,112,128]{3,2,1,0:T(8,128)(2,1)S(1)} %all-to-all-done.x_ref, f32[8,224,1]{2,1,0:T(8,128)S(1)} %get-tuple-element.26.highest_ref, f32[8,224,1]{2,1,0:T(8,128)S(1)} %get-tuple-element.27.total_ref, f32[8,224,128]{2,1,0:T(8,128)S(1)} %get-tuple-element.28.weighted_ref, ...), custom_call_target="tpu_custom_call" | custom-call | tf_op jit(solution)/shard_map/far/pallas_call | solution.py:332
  53.1 10.9 %all_to_all.10 = bf16[8,2,112,128]{3,2,1,0:T(8,128)(2,1)S(1)} all-to-all(bf16[8,2,112,128]{3,2,1,0:T(8,128)(2,1)S(1)} %far.1), channel_id=1, replica_groups={{0,1,2,3,4,5,6,7},{8,9,10,11,12,13,14,15},{16,17,18,19,20,21,22,23},{24..., dimensions={0} | all-to-all | bytes 917504 | tf_op jit(solution)/shard_map/all_to_all | solution.py:340
  64.0 0.9 %copy.9 = bf16[16,112,128]{2,0,1:T(8,128)(2,1)} copy(bf16[16,112,128]{2,1,0:T(8,128)(2,1)S(1)} %bitcast.7) | data formatting | bytes 917504 | tf_op jit(solution)/shard_map/reshape | solution.py:341
Async XLA Ops:
  8.3 4.0 %copy-start.3 = (bf16[2,2,112,128]{3,2,1,0:T(8,128)(2,1)S(1)}, bf16[2,2,112,128]{3,2,1,0:T(8,128)(2,1)}, u32[]{:S(2)}) copy-start(bf16[2,2,112,128]{3,2,1,0:T(8,128)(2,1)} %get-tuple-element.19.refs_0_) | copy-start | bytes 344068
  8.3 5.3 %copy-start.2 = (bf16[2,2,112,128]{3,2,1,0:T(8,128)(2,1)S(1)}, bf16[2,2,112,128]{3,2,1,0:T(8,128)(2,1)}, u32[]{:S(2)}) copy-start(bf16[2,2,112,128]{3,2,1,0:T(8,128)(2,1)} %get-tuple-element.20.refs_1_) | copy-start | bytes 344068
  8.3 6.6 %copy-start.1 = (bf16[2,2,112,128]{3,2,1,0:T(8,128)(2,1)S(1)}, bf16[2,2,112,128]{3,2,1,0:T(8,128)(2,1)}, u32[]{:S(2)}) copy-start(bf16[2,2,112,128]{3,2,1,0:T(8,128)(2,1)} %get-tuple-element.21.refs_2_) | copy-start | bytes 344068
  8.3 7.9 %copy-start = (bf16[2,2,112,128]{3,2,1,0:T(8,128)(2,1)S(1)}, bf16[2,2,112,128]{3,2,1,0:T(8,128)(2,1)}, u32[]{:S(2)}) copy-start(bf16[2,2,112,128]{3,2,1,0:T(8,128)(2,1)} %get-tuple-element.22.refs_3_) | copy-start | bytes 344068
  8.3 20.2 %all-to-all-start = ((bf16[8,4,112,128]{3,2,1,0:T(8,128)(2,1)}), bf16[8,4,112,128]{3,2,1,0:T(8,128)(2,1)S(1)}, u32[]{:S(2)}, u32[]{:S(2)}) async-start(bf16[8,4,112,128]{3,2,1,0:T(8,128)(2,1)} %pack_all.1), calls=%async_computation | async-start | bytes 1835008 | tf_op jit(solution)/shard_map/all_to_all | solution.py:315
  12.3 19.1 %collective-permute-start = (bf16[2,2,112,128]{3,2,1,0:T(8,128)(2,1)S(1)}, bf16[2,2,112,128]{3,2,1,0:T(8,128)(2,1)S(1)}, u32[]{:S(2)}, u32[]{:S(2)}) collective-permute-start(bf16[2,2,112,128]{3,2,1,0:T(8,128)(2,1)S(1)} %copy-done.3), channel_id=1, source_target_pairs={{0,8},{1,9},{2,10},{3,11},{4,12},{5,13},{6,14},{7,15},{16,24},{17,... | collective-permute-start | bytes 344072 | tf_op jit(solution)/shard_map/ppermute | solution.py:294
  13.6 17.8 %collective-permute-start.1 = (bf16[2,2,112,128]{3,2,1,0:T(8,128)(2,1)S(1)}, bf16[2,2,112,128]{3,2,1,0:T(8,128)(2,1)S(1)}, u32[]{:S(2)}, u32[]{:S(2)}) collective-permute-start(bf16[2,2,112,128]{3,2,1,0:T(8,128)(2,1)S(1)} %copy-done.2), channel_id=1, source_target_pairs={{0,10},{1,11},{2,8},{3,9},{4,14},{5,15},{6,12},{7,13},{16,26},{17,... | collective-permute-start | bytes 344072 | tf_op jit(solution)/shard_map/ppermute | solution.py:294
  14.9 21.2 %collective-permute-start.2 = (bf16[2,2,112,128]{3,2,1,0:T(8,128)(2,1)S(1)}, bf16[2,2,112,128]{3,2,1,0:T(8,128)(2,1)S(1)}, u32[]{:S(2)}, u32[]{:S(2)}) collective-permute-start(bf16[2,2,112,128]{3,2,1,0:T(8,128)(2,1)S(1)} %copy-done.1), channel_id=1, source_target_pairs={{0,12},{1,13},{2,14},{3,15},{4,8},{5,9},{6,10},{7,11},{16,28},{17,... | collective-permute-start | bytes 344072 | tf_op jit(solution)/shard_map/ppermute | solution.py:294
  16.2 22.8 %collective-permute-start.3 = (bf16[2,2,112,128]{3,2,1,0:T(8,128)(2,1)S(1)}, bf16[2,2,112,128]{3,2,1,0:T(8,128)(2,1)S(1)}, u32[]{:S(2)}, u32[]{:S(2)}) collective-permute-start(bf16[2,2,112,128]{3,2,1,0:T(8,128)(2,1)S(1)} %copy-done), channel_id=1, source_target_pairs={{0,14},{1,15},{2,12},{3,13},{4,10},{5,11},{6,8},{7,9},{16,30},{17,... | collective-permute-start | bytes 344072 | tf_op jit(solution)/shard_map/ppermute | solution.py:294
  39.0 8.7 %collective-permute-start.4 = (bf16[2,2,112,128]{3,2,1,0:T(8,128)(2,1)S(1)}, bf16[2,2,112,128]{3,2,1,0:T(8,128)(2,1)S(1)}, u32[]{:S(2)}, u32[]{:S(2)}) collective-permute-start(bf16[2,2,112,128]{3,2,1,0:T(8,128)(2,1)S(1)} %collective-permute-done.refs_0_), channel_id=1, source_target_pairs={{8,9},{9,8},{10,11},{11,10},{12,13},{13,12},{14,15},{15,14},{24,25... | collective-permute-start | bytes 344072 | tf_op jit(solution)/shard_map/ppermute | solution.py:331
  40.9 6.8 %collective-permute-start.5 = (bf16[2,2,112,128]{3,2,1,0:T(8,128)(2,1)S(1)}, bf16[2,2,112,128]{3,2,1,0:T(8,128)(2,1)S(1)}, u32[]{:S(2)}, u32[]{:S(2)}) collective-permute-start(bf16[2,2,112,128]{3,2,1,0:T(8,128)(2,1)S(1)} %collective-permute-done.1.refs_1_), channel_id=1, source_target_pairs={{8,9},{9,8},{10,11},{11,10},{12,13},{13,12},{14,15},{15,14},{24,25... | collective-permute-start | bytes 344072 | tf_op jit(solution)/shard_map/ppermute | solution.py:331
  43.3 4.4 %collective-permute-start.6 = (bf16[2,2,112,128]{3,2,1,0:T(8,128)(2,1)S(1)}, bf16[2,2,112,128]{3,2,1,0:T(8,128)(2,1)S(1)}, u32[]{:S(2)}, u32[]{:S(2)}) collective-permute-start(bf16[2,2,112,128]{3,2,1,0:T(8,128)(2,1)S(1)} %collective-permute-done.2.refs_2_), channel_id=1, source_target_pairs={{8,9},{9,8},{10,11},{11,10},{12,13},{13,12},{14,15},{15,14},{24,25... | collective-permute-start | bytes 344072 | tf_op jit(solution)/shard_map/ppermute | solution.py:331
  45.2 3.4 %collective-permute-start.7 = (bf16[2,2,112,128]{3,2,1,0:T(8,128)(2,1)S(1)}, bf16[2,2,112,128]{3,2,1,0:T(8,128)(2,1)S(1)}, u32[]{:S(2)}, u32[]{:S(2)}) collective-permute-start(bf16[2,2,112,128]{3,2,1,0:T(8,128)(2,1)S(1)} %collective-permute-done.3.refs_3_), channel_id=1, source_target_pairs={{8,9},{9,8},{10,11},{11,10},{12,13},{13,12},{14,15},{15,14},{24,25... | collective-permute-start | bytes 344072 | tf_op jit(solution)/shard_map/ppermute | solution.py:331

commit v4 on v1

--- a/solution.py
+++ b/solution.py
@@ -12,7 +12,12 @@
 ROPE_BASE = 1000000.0
 EPSILON = 1e-06
 MASKED = -1e30
-VMEM_LIMIT = 48 * 1024 * 1024
+VMEM_LIMIT = 24 * 1024 * 1024
+PACK_VMEM = 56 * 1024 * 1024
+VMEM = pl.BlockSpec(memory_space=pltpu.VMEM)
+SMEM = pl.BlockSpec(memory_space=pltpu.SMEM)
+HBM = pl.BlockSpec(memory_space=pltpu.HBM)
+CONTRACT = (((1,), (1,)), ((), ()))
 
 
 def rope_table(length, width):
@@ -56,53 +61,19 @@
             out_ref[head * rep + copy, per_chip + 1] = values
 
 
-def attention_kernel(core_ref, x_ref, other_ref, out_ref):
-    blocks, rows, tokens, width = x_ref.shape
-    per_chip = rows - 2
-    core = core_ref[0]
-    scale = math.log2(math.e) / math.sqrt(width)
-    keys_own = x_ref[:, per_chip].reshape(blocks * tokens, width)
-    values_own = x_ref[:, per_chip + 1].reshape(blocks * tokens, width)
-    keys_other = other_ref[:, 0].reshape(blocks * tokens, width)
-    values_other = other_ref[:, 1].reshape(blocks * tokens, width)
-    contract = (((1,), (1,)), ((), ()))
-    for block in range(blocks):
-        queries = x_ref[block, :per_chip].reshape(per_chip * tokens, width)
-        reach = (block + 1) * tokens
-        own = lax.dot_general(queries, keys_own[:reach], contract, preferred_element_type=jnp.float32)
-        other = lax.dot_general(queries, keys_other[:reach], contract, preferred_element_type=jnp.float32)
-        row = lax.broadcasted_iota(jnp.int32, (per_chip, tokens, reach), 1).reshape(per_chip * tokens, reach)
-        column = lax.broadcasted_iota(jnp.int32, (per_chip * tokens, reach), 1)
-        own = jnp.where(column <= row + block * tokens, own, MASKED)
-        other = jnp.where(column < (block + core) * tokens, other, MASKED)
-        highest = jnp.maximum(
-            jnp.max(own, axis=-1, keepdims=True), jnp.max(other, axis=-1, keepdims=True)
-        )
-        probs_own = jnp.exp2((own - highest) * scale)
-        probs_other = jnp.exp2((other - highest) * scale)
-        total = jnp.sum(probs_own, axis=-1, keepdims=True) + jnp.sum(probs_other, axis=-1, keepdims=True)
-        summed = jnp.dot(
-            probs_own.astype(jnp.bfloat16), values_own[:reach], preferred_element_type=jnp.float32
-        ) + jnp.dot(
-            probs_other.astype(jnp.bfloat16), values_other[:reach], preferred_element_type=jnp.float32
-        )
-        out_ref[block] = (summed / total).astype(jnp.bfloat16).reshape(per_chip, tokens, width)
-
-
 def looped_kernel(core_ref, x_ref, other_ref, out_ref):
     _, rows, tokens, width = x_ref.shape
     per_chip = rows - 2
     core = core_ref[0]
     block = pl.program_id(0)
     scale = math.log2(math.e) / math.sqrt(width)
-    contract = (((1,), (1,)), ((), ()))
     queries = x_ref[block, :per_chip].reshape(per_chip * tokens, width)
     row = lax.broadcasted_iota(jnp.int32, (per_chip, tokens, tokens), 1).reshape(per_chip * tokens, tokens)
     column = lax.broadcasted_iota(jnp.int32, (per_chip * tokens, tokens), 1)
 
     def merge(carried, keys, values, allowed):
         highest, total, weighted = carried
-        scores = lax.dot_general(queries, keys, contract, preferred_element_type=jnp.float32)
+        scores = lax.dot_general(queries, keys, CONTRACT, preferred_element_type=jnp.float32)
         scores = jnp.where(allowed, scores, MASKED)
         new = jnp.maximum(highest, jnp.max(scores, axis=-1, keepdims=True))
         probs = jnp.exp2((scores - new) * scale)
@@ -125,7 +96,7 @@
     out_ref[block] = (weighted / total).astype(jnp.bfloat16).reshape(per_chip, tokens, width)
 
 
-def on_device(length, devices, query_states, key_states, value_states, query_gain, key_gain):
+def general_plan(length, devices, query_states, key_states, value_states, query_gain, key_gain):
     tokens, heads, width = query_states.shape
     kv_heads = key_states.shape[1]
     chips = devices // 2
@@ -136,32 +107,30 @@
     same_core = [list(range(start, devices, 2)) for start in range(2)]
     swap = [(device, device ^ 1) for device in range(devices)]
     table = lax.dynamic_slice_in_dim(jnp.asarray(rope_table(length, width)), me * tokens, tokens, 0)
-    vmem = pl.BlockSpec(memory_space=pltpu.VMEM)
     packed = pl.pallas_call(
         functools.partial(pack_kernel, rep),
         out_shape=jax.ShapeDtypeStruct((chips, per_chip + 2, tokens, width), jnp.bfloat16),
-        in_specs=[vmem] * 6,
-        out_specs=vmem,
+        in_specs=[VMEM] * 6,
+        out_specs=VMEM,
         scratch_shapes=[
             pltpu.VMEM((tokens * heads, width), jnp.float32),
             pltpu.VMEM((tokens * kv_heads, width), jnp.float32),
             pltpu.VMEM((tokens * kv_heads, width), jnp.float32),
         ],
-        compiler_params=pltpu.CompilerParams(vmem_limit_bytes=VMEM_LIMIT),
+        compiler_params=pltpu.CompilerParams(vmem_limit_bytes=48 * 1024 * 1024),
         name="pack",
     )(query_states, key_states, value_states, table, query_gain[None], key_gain[None])
     arrived = lax.all_to_all(
         packed, "seq", split_axis=0, concat_axis=0, axis_index_groups=same_core, tiled=True
     )
     other = lax.ppermute(arrived[:, per_chip:], "seq", swap)
-    short = chips <= 8
     attended = pl.pallas_call(
-        attention_kernel if short else looped_kernel,
-        grid=() if short else (chips,),
+        looped_kernel,
+        grid=(chips,),
         out_shape=jax.ShapeDtypeStruct((chips, per_chip, tokens, width), jnp.bfloat16),
-        in_specs=[pl.BlockSpec(memory_space=pltpu.SMEM), vmem, vmem],
-        out_specs=vmem,
-        compiler_params=pltpu.CompilerParams(vmem_limit_bytes=VMEM_LIMIT),
+        in_specs=[SMEM, VMEM, VMEM],
+        out_specs=VMEM,
+        compiler_params=pltpu.CompilerParams(vmem_limit_bytes=48 * 1024 * 1024),
         name="attention",
     )(core[None], arrived, other)
     returned = lax.all_to_all(
@@ -170,6 +139,293 @@
     return jnp.transpose(returned.reshape(heads, tokens, width), (1, 0, 2))
 
 
+def rope_factors(table):
+    half = table.shape[1] // 2
+    swapped = pltpu.roll(table, half, 1)
+    first = lax.broadcasted_iota(jnp.int32, table.shape, 1) < half
+    return jnp.where(first, table, swapped), jnp.where(first, -swapped, table)
+
+
+def normalize(rows):
+    floats = rows.astype(jnp.float32)
+    squares = floats * floats
+    large = squares.astype(jnp.bfloat16)
+    small = (squares - large.astype(jnp.float32)).astype(jnp.bfloat16)
+    width = rows.shape[1]
+    ones = jnp.ones((2 * width, width), jnp.bfloat16)
+    added = jnp.dot(jnp.concatenate([large, small], axis=1), ones, preferred_element_type=jnp.float32)
+    return floats * lax.rsqrt(added * (1.0 / width) + EPSILON)
+
+
+def turn(normed, gain, cosine, sine):
+    scaled = normed * gain
+    return (scaled * cosine + pltpu.roll(scaled, scaled.shape[1] // 2, 1) * sine).astype(jnp.bfloat16)
+
+
+def send_kernel(me_ref, q_hbm, k_hbm, v_hbm, table_hbm, query_gain_ref, key_gain_ref, *refs):
+    outs, (q_ref, k_ref, v_ref, table_ref, qf_ref, kf_ref, vf_ref, sems) = refs[:-8], refs[-8:]
+    steps = len(outs) // 2
+    pairs, fulls = outs[:steps], outs[steps:]
+    tokens, heads, width = q_ref.shape
+    kv_heads, per_chip = k_ref.shape[1], pairs[0].shape[0]
+    first, per_full = 2 * per_chip, heads // steps
+    me = me_ref[0]
+    chip = lax.rem(me // 2, steps)
+    start = pl.multiple_of(me * tokens, 8)
+    copies = [
+        pltpu.make_async_copy(k_hbm, k_ref, sems.at[0]),
+        pltpu.make_async_copy(table_hbm.at[pl.ds(start, tokens)], table_ref, sems.at[1]),
+        pltpu.make_async_copy(v_hbm, v_ref, sems.at[2]),
+        pltpu.make_async_copy(q_hbm, q_ref, sems.at[3]),
+    ]
+    for copy in copies:
+        copy.start()
+    copies[0].wait()
+    kf_ref[...] = normalize(k_ref[...].reshape(tokens * kv_heads, width))
+    copies[1].wait()
+    cosine, sine = rope_factors(table_ref[...])
+    copies[2].wait()
+    vf_ref[...] = v_ref[...].astype(jnp.float32).reshape(tokens * kv_heads, width)
+    for step in range(steps):
+        for row in range(per_chip):
+            head = (chip ^ step) * per_chip + row
+            keys = turn(kf_ref[pl.ds(head, tokens, stride=kv_heads), :], key_gain_ref[...], cosine, sine)
+            values = vf_ref[pl.ds(head, tokens, stride=kv_heads), :].astype(jnp.bfloat16)
+            pairs[step][row, 0] = keys
+            fulls[step][2 * row] = keys
+            pairs[step][row, 1] = values
+            fulls[step][2 * row + 1] = values
+    copies[3].wait()
+    qf_ref[...] = normalize(q_ref[...].reshape(tokens * heads, width))
+    for step in range(steps):
+        for row in range(per_full):
+            normed = qf_ref[pl.ds((chip ^ step) * per_full + row, tokens, stride=heads), :]
+            fulls[step][first + row] = turn(normed, query_gain_ref[...], cosine, sine)
+
+
+def order_kernel(me_ref, *refs):
+    arrays, (pair_ref, query_ref) = refs[:-2], refs[-2:]
+    steps, per_chip = pair_ref.shape[0], pair_ref.shape[1]
+    chip = lax.rem(me_ref[0] // 2, steps)
+    for step in range(steps):
+        pair_ref[chip ^ step] = arrays[step][: 2 * per_chip].reshape(pair_ref.shape[1:])
+        query_ref[chip ^ step] = arrays[step][2 * per_chip :].reshape(query_ref.shape[1:])
+
+
+def near_kernel(me_ref, q_ref, own_ref, other_ref, highest_ref, total_ref, weighted_ref):
+    blocks, kv_heads, group, tokens, width = q_ref.shape
+    core = lax.rem(me_ref[0], 2)
+    scale = math.log2(math.e) / math.sqrt(width)
+    rows = group * tokens
+    for head in range(kv_heads):
+        keys_own, values_own, keys_other, values_other = [
+            ref[:, head, i].reshape(blocks * tokens, width) for ref in (own_ref, other_ref) for i in range(2)
+        ]
+        for block in range(blocks):
+            queries = q_ref[block, head].reshape(rows, width)
+            reach = (block + 1) * tokens
+            own = lax.dot_general(queries, keys_own[:reach], CONTRACT, preferred_element_type=jnp.float32)
+            other = lax.dot_general(queries, keys_other[:reach], CONTRACT, preferred_element_type=jnp.float32)
+            row = lax.broadcasted_iota(jnp.int32, (group, tokens, reach), 1).reshape(rows, reach)
+            column = lax.broadcasted_iota(jnp.int32, (rows, reach), 1)
+            own = jnp.where(column <= row + block * tokens, own, MASKED)
+            other = jnp.where(column < (block + core) * tokens, other, MASKED)
+            highest = jnp.maximum(
+                jnp.max(own, axis=-1, keepdims=True), jnp.max(other, axis=-1, keepdims=True)
+            )
+            probs_own = jnp.exp2((own - highest) * scale)
+            probs_other = jnp.exp2((other - highest) * scale)
+            place = pl.ds(block * rows, rows)
+            highest_ref[head, place] = highest
+            total_ref[head, place] = jnp.sum(probs_own, axis=-1, keepdims=True) + jnp.sum(
+                probs_other, axis=-1, keepdims=True
+            )
+            weighted_ref[head, place] = jnp.dot(
+                probs_own.astype(jnp.bfloat16), values_own[:reach], preferred_element_type=jnp.float32
+            ) + jnp.dot(
+                probs_other.astype(jnp.bfloat16), values_other[:reach], preferred_element_type=jnp.float32
+            )
+
+
+def add_far(q_ref, highest_ref, total_ref, weighted_ref, pairs, store):
+    blocks, kv_heads, group, tokens, width = q_ref.shape
+    scale = math.log2(math.e) / math.sqrt(width)
+    rows = group * tokens
+    for head in range(kv_heads):
+        keys = jnp.concatenate([ref[head, 0] for ref in pairs], axis=0)
+        values = jnp.concatenate([ref[head, 1] for ref in pairs], axis=0)
+        for block in range(blocks):
+            queries = q_ref[block, head].reshape(rows, width)
+            place = pl.ds(block * rows, rows)
+            scores = lax.dot_general(queries, keys, CONTRACT, preferred_element_type=jnp.float32)
+            before = highest_ref[head, place]
+            highest = jnp.maximum(before, jnp.max(scores, axis=-1, keepdims=True))
+            probs = jnp.exp2((scores - highest) * scale)
+            factor = jnp.exp2((before - highest) * scale)
+            total = total_ref[head, place] * factor + jnp.sum(probs, axis=-1, keepdims=True)
+            summed = jnp.dot(probs.astype(jnp.bfloat16), values, preferred_element_type=jnp.float32)
+            store(head, block, highest, total, weighted_ref[head, place] * factor + summed)
+
+
+def far_kernel(half, me_ref, q_ref, highest_ref, total_ref, weighted_ref, *refs):
+    pairs, outs = refs[:-3], refs[-3:]
+    rows = q_ref.shape[2] * q_ref.shape[3]
+
+    def store(head, block, *values):
+        for ref, value in zip(outs, values):
+            ref[head, pl.ds(block * rows, rows)] = value
+
+    @pl.when(me_ref[0] >= half)
+    def _():
+        add_far(q_ref, highest_ref, total_ref, weighted_ref, pairs, store)
+
+    @pl.when(me_ref[0] < half)
+    def _():
+        for ref, before in zip(outs, (highest_ref, total_ref, weighted_ref)):
+            ref[...] = before[...]
+
+
+def last_kernel(half, me_ref, q_ref, highest_ref, total_ref, weighted_ref, *refs):
+    blocks, kv_heads, group, tokens, width = q_ref.shape
+    pairs, outs, out_ref = refs[: -blocks - 1], refs[-blocks - 1 : -1], refs[-1]
+    rows = group * tokens
+
+    def store(head, block, highest, total, weighted):
+        result = (weighted / total).astype(jnp.bfloat16).reshape(group, tokens, width)
+        out_ref[block, pl.ds(head * group, group)] = result
+
+    @pl.when(me_ref[0] >= half)
+    def _():
+        add_far(q_ref, highest_ref, total_ref, weighted_ref, pairs, store)
+
+    @pl.when(me_ref[0] < half)
+    def _():
+        for head in range(kv_heads):
+            for block in range(blocks):
+                place = pl.ds(block * rows, rows)
+                store(head, block, None, total_ref[head, place], weighted_ref[head, place])
+
+    chip = lax.rem(me_ref[0] // 2, blocks)
+    for step in range(blocks):
+        outs[step][...] = out_ref[chip ^ step]
+
+
+def unpack_kernel(me_ref, *refs):
+    parts, (out_ref, floats_ref) = refs[:-2], refs[-2:]
+    tokens, heads, width = out_ref.shape
+    steps = len(parts)
+    per_chip = heads // steps
+    chip = lax.rem(me_ref[0] // 2, steps)
+    for step in range(steps):
+        for row in range(per_chip):
+            head = (chip ^ step) * per_chip + row
+            floats_ref[pl.ds(head, tokens, stride=heads), :] = parts[step][row].astype(jnp.float32)
+    out_ref[...] = floats_ref[...].reshape(tokens, heads, width).astype(jnp.bfloat16)
+
+
+def halves_plan(length, devices, query_states, key_states, value_states, query_gain, key_gain):
+    tokens, heads, width = query_states.shape
+    kv_heads = key_states.shape[1]
+    group = heads // kv_heads
+    half = devices // 2
+    steps = half // 2
+    per_chip = kv_heads // steps
+    bf16, f32 = jnp.bfloat16, jnp.float32
+    me = lax.axis_index("seq")[None]
+
+    def call(kernel, name, outs, *operands, scratch=(), specs=None, limit=VMEM_LIMIT):
+        return pl.pallas_call(
+            kernel,
+            out_shape=outs,
+            in_specs=specs or [SMEM] + [VMEM] * len(operands),
+            out_specs=jax.tree.map(lambda _: VMEM, outs),
+            scratch_shapes=scratch,
+            compiler_params=pltpu.CompilerParams(vmem_limit_bytes=limit),
+            name=name,
+        )(me, *operands)
+
+    def to_upper(step, array):
+        links = [(device, half + ((device // 2) ^ step) * 2 + device % 2) for device in range(half)]
+        return lax.ppermute(array, "seq", links)
+
+    def to_chip(step, array):
+        links = [(device, ((device // 2) ^ step) * 2 + device % 2) for device in range(devices)]
+        return lax.ppermute(array, "seq", links)
+
+    def to_core(array, lowest):
+        return lax.ppermute(array, "seq", [(device, device ^ 1) for device in range(lowest, devices)])
+
+    shape = jax.ShapeDtypeStruct
+    packed = call(
+        send_kernel,
+        "send",
+        [shape((per_chip, 2, tokens, width), bf16)] * steps
+        + [shape((per_chip * (2 + group), tokens, width), bf16)] * steps,
+        query_states,
+        key_states,
+        value_states,
+        jnp.asarray(rope_table(length, width)),
+        query_gain[None],
+        key_gain[None],
+        specs=[SMEM, HBM, HBM, HBM, HBM, VMEM, VMEM],
+        scratch=[
+            pltpu.VMEM((tokens, heads, width), bf16),
+            pltpu.VMEM((tokens, kv_heads, width), bf16),
+            pltpu.VMEM((tokens, kv_heads, width), bf16),
+            pltpu.VMEM((tokens, width), f32),
+            pltpu.VMEM((tokens * heads, width), f32),
+            pltpu.VMEM((tokens * kv_heads, width), f32),
+            pltpu.VMEM((tokens * kv_heads, width), f32),
+            pltpu.SemaphoreType.DMA((4,)),
+        ],
+        limit=PACK_VMEM,
+    )
+    pairs, near = packed[:steps], packed[steps:]
+    early = steps // 2
+    far = [to_upper(step, pairs[step]) for step in range(early)]
+    near = [near[0]] + [to_chip(step, near[step]) for step in range(1, steps)]
+    near, far, late = lax.optimization_barrier((near, far, pairs[early:]))
+    far = far + [to_upper(early + i, pair) for i, pair in enumerate(late)]
+    own, queries = call(
+        order_kernel,
+        "order",
+        [shape((steps, per_chip, 2, tokens, width), bf16), shape((steps, per_chip, group, tokens, width), bf16)],
+        *near,
+    )
+    other = to_core(own, 0)
+    far_other = [to_core(pair, half) for pair in far[:early]]
+    rows = steps * group * tokens
+    state = [
+        shape((per_chip, rows, 1), f32),
+        shape((per_chip, rows, 1), f32),
+        shape((per_chip, rows, width), f32),
+    ]
+    carried = call(near_kernel, "near", state, queries, own, other)
+    carried = call(
+        functools.partial(far_kernel, half), "far", state, queries, *carried, *far[:early], *far_other
+    )
+    carried, last = lax.optimization_barrier((carried, far[early:]))
+    last_other = [to_core(pair, half) for pair in last]
+    returned = call(
+        functools.partial(last_kernel, half),
+        "last",
+        [shape((per_chip * group, tokens, width), bf16)] * steps,
+        queries,
+        *carried,
+        *last,
+        *last_other,
+        scratch=[pltpu.VMEM((steps, per_chip * group, tokens, width), bf16)],
+    )
+    returned = [returned[0]] + [to_chip(step, returned[step]) for step in range(1, steps)]
+    return call(
+        unpack_kernel,
+        "unpack",
+        shape((tokens, heads, width), bf16),
+        *returned,
+        scratch=[pltpu.VMEM((tokens * heads, width), f32)],
+    )
+
+
 def solution(mesh):
     devices = mesh.shape["seq"]
     groups = mesh.shape["groups"]
@@ -177,8 +433,9 @@
 
     def run(query_states, key_states, value_states, query_gain, key_gain):
         length = query_states.shape[0] // groups
+        plan = halves_plan if devices == 2 * key_states.shape[1] else general_plan
         return jax.shard_map(
-            functools.partial(on_device, length, devices),
+            functools.partial(plan, length, devices),
             mesh=mesh,
             in_specs=(placed, placed, placed, P(), P()),
             out_specs=placed,

time: 61.5 us -> 63.2 us (1.028)
  the two profiles are of different devices: /device:TPU:0 before, /device:TPU:16 now
where the time goes in v4:
time: 63.2 us; the launch traced here: 62.9 us
  waiting for transfers between devices  25.5 us (40%)
  starting transfers between devices  21 us (33%)
  Pallas kernels  15.3 us (24%)
  local copies, waits for them, and re-layouts  0.94 us (1%)
    ppermute x4, waiting for transfers between devices, to_upper(): return lax.ppermute(array, 'seq', links)  19 us
    pallas_call x6, Pallas kernels, call(): pl.pallas_call(kernel, out_shape=outs, in_specs=specs or [SMEM] + [VMEM]...  15.3 us
    ppermute x5, starting transfers between devices, to_core(): lax.ppermute(array, 'seq', [(device, device ^ 1) for device in range(lowe...  8.71 us
    ppermute x6, starting transfers between devices, to_chip(): return lax.ppermute(array, 'seq', links)  7.12 us
    ppermute x6, waiting for transfers between devices, to_chip(): return lax.ppermute(array, 'seq', links)  5.56 us
    ppermute x4, starting transfers between devices, to_upper(): return lax.ppermute(array, 'seq', links)  5.16 us
  transfers between devices with their start and end apart: 15, of which 8 were waited for; matrix products, arithmetic and copies ran while one was open for 0% of the time, Pallas kernels for 11%

profile of v4, /device:TPU:16, one launch (start us, length us, event | category | flops | bytes accessed | tf_op | source)
XLA Modules:
  0.0 62.9 jit_solution(16337590931934788631)
XLA Ops:
  0.0 4.2 %send.1 = (bf16[2,2,112,128]{3,2,1,0:T(8,128)(2,1)}, bf16[2,2,112,128]{3,2,1,0:T(8,128)(2,1)}, bf16[2,2,112,128]{3,2,1,0:T(8,128)(2,1)}, bf16[2,2,112,128]{3,2,1...) custom-call(s32[1]{0:T(128)} %bitcast.me_ref, ...), custom_call_target="tpu_custom_call" | custom-call | tf_op jit(solution)/shard_map/send/pallas_call | solution.py:337
  4.2 1.6 %collective-permute-start = (bf16[8,112,128]{2,1,0:T(8,128)(2,1)}, bf16[8,112,128]{2,1,0:T(8,128)(2,1)S(1)}, u32[]{:S(2)}, u32[]{:S(2)}) collective-permute-start(bf16[8,112,128]{2,1,0:T(8,128)(2,1)} %get-tuple-element.39), channel_id=1, source_target_pairs={{0,2},{1,3},{2,0},{3,1},{4,6},{5,7},{6,4},{7,5},{8,10},{9,11},{10,... | collective-permute-start | bytes 688136 | tf_op jit(solution)/shard_map/ppermute | solution.py:353
  5.8 1.6 %collective-permute-start.1 = (bf16[8,112,128]{2,1,0:T(8,128)(2,1)}, bf16[8,112,128]{2,1,0:T(8,128)(2,1)S(1)}, u32[]{:S(2)}, u32[]{:S(2)}) collective-permute-start(bf16[8,112,128]{2,1,0:T(8,128)(2,1)} %get-tuple-element.40), channel_id=1, source_target_pairs={{0,4},{1,5},{2,6},{3,7},{4,0},{5,1},{6,2},{7,3},{8,12},{9,13},{10,... | collective-permute-start | bytes 688136 | tf_op jit(solution)/shard_map/ppermute | solution.py:353
  7.4 0.4 collective-permute-start.2
  7.8 1.3 %collective-permute-start.3 = (bf16[2,2,112,128]{3,2,1,0:T(8,128)(2,1)}, bf16[2,2,112,128]{3,2,1,0:T(8,128)(2,1)S(1)}, u32[]{:S(2)}, u32[]{:S(2)}) collective-permute-start(bf16[2,2,112,128]{3,2,1,0:T(8,128)(2,1)} %get-tuple-element.42), channel_id=1, source_target_pairs={{0,8},{1,9},{2,10},{3,11},{4,12},{5,13},{6,14},{7,15},{16,24},{17,... | collective-permute-start | bytes 344072 | tf_op jit(solution)/shard_map/ppermute | solution.py:349
  9.0 1.3 %collective-permute-start.4 = (bf16[2,2,112,128]{3,2,1,0:T(8,128)(2,1)}, bf16[2,2,112,128]{3,2,1,0:T(8,128)(2,1)S(1)}, u32[]{:S(2)}, u32[]{:S(2)}) collective-permute-start(bf16[2,2,112,128]{3,2,1,0:T(8,128)(2,1)} %get-tuple-element.43), channel_id=1, source_target_pairs={{0,10},{1,11},{2,8},{3,9},{4,14},{5,15},{6,12},{7,13},{16,26},{17,... | collective-permute-start | bytes 344072 | tf_op jit(solution)/shard_map/ppermute | solution.py:349
  10.3 11.3 %collective-permute-done.3.refs_0_ = bf16[2,2,112,128]{3,2,1,0:T(8,128)(2,1)S(1)} collective-permute-done((bf16[2,2,112,128]{3,2,1,0:T(8,128)(2,1)}, bf16[2,2,112,128]{3,2,1,0:T(8,128)(2,1)S(1)}, u32[]{:S(2)}, u32[]{:S(2)}) %collective-permute-start.3) | collective-permute-done | bytes 114720 | tf_op jit(solution)/shard_map/ppermute | solution.py:349
  21.6 1.2 %collective-permute-done.4.refs_1_ = bf16[2,2,112,128]{3,2,1,0:T(8,128)(2,1)S(1)} collective-permute-done((bf16[2,2,112,128]{3,2,1,0:T(8,128)(2,1)}, bf16[2,2,112,128]{3,2,1,0:T(8,128)(2,1)S(1)}, u32[]{:S(2)}, u32[]{:S(2)}) %collective-permute-start.4) | collective-permute-done | bytes 114720 | tf_op jit(solution)/shard_map/ppermute | solution.py:349
  22.8 0.0 collective-permute-done.refs_1_
  22.8 0.0 collective-permute-done.1.refs_2_
  22.8 0.0 collective-permute-done.2.refs_3_
  22.8 0.0 copy-start
  22.8 0.9 %copy-done = bf16[8,112,128]{2,1,0:T(8,128)(2,1)S(1)} copy-done((bf16[8,112,128]{2,1,0:T(8,128)(2,1)S(1)}, bf16[8,112,128]{2,1,0:T(8,128)(2,1)}, u32[]{:S(2)}) %copy-start) | copy-done | bytes 229400
  23.8 0.0 copy-start.2
  23.8 0.0 copy-start.1
  23.8 0.1 order.1
  23.9 0.1 collective-permute-start.5
  23.9 2.4 %collective-permute-start.6 = (bf16[2,2,112,128]{3,2,1,0:T(8,128)(2,1)S(1)}, bf16[2,2,112,128]{3,2,1,0:T(8,128)(2,1)S(1)}, u32[]{:S(2)}, u32[]{:S(2)}) collective-permute-start(bf16[2,2,112,128]{3,2,1,0:T(8,128)(2,1)S(1)} %collective-permute-done.3.refs_0_), channel_id=1, source_target_pairs={{8,9},{9,8},{10,11},{11,10},{12,13},{13,12},{14,15},{15,14},{24,25... | collective-permute-start | bytes 344072 | tf_op jit(solution)/shard_map/ppermute | solution.py:356
  26.3 1.9 %collective-permute-start.7 = (bf16[2,2,112,128]{3,2,1,0:T(8,128)(2,1)S(1)}, bf16[2,2,112,128]{3,2,1,0:T(8,128)(2,1)S(1)}, u32[]{:S(2)}, u32[]{:S(2)}) collective-permute-start(bf16[2,2,112,128]{3,2,1,0:T(8,128)(2,1)S(1)} %collective-permute-done.4.refs_1_), channel_id=1, source_target_pairs={{8,9},{9,8},{10,11},{11,10},{12,13},{13,12},{14,15},{15,14},{24,25... | collective-permute-start | bytes 344072 | tf_op jit(solution)/shard_map/ppermute | solution.py:356
  28.3 0.0 copy-done.2
  28.3 1.3 %collective-permute-start.8 = (bf16[2,2,112,128]{3,2,1,0:T(8,128)(2,1)S(1)}, bf16[2,2,112,128]{3,2,1,0:T(8,128)(2,1)S(1)}, u32[]{:S(2)}, u32[]{:S(2)}) collective-permute-start(bf16[2,2,112,128]{3,2,1,0:T(8,128)(2,1)S(1)} %copy-done.2), channel_id=1, source_target_pairs={{0,12},{1,13},{2,14},{3,15},{4,8},{5,9},{6,10},{7,11},{16,28},{17,... | collective-permute-start | bytes 344072 | tf_op jit(solution)/shard_map/ppermute | solution.py:349
  29.6 0.0 copy-done.1
  29.6 1.3 %collective-permute-start.9 = (bf16[2,2,112,128]{3,2,1,0:T(8,128)(2,1)S(1)}, bf16[2,2,112,128]{3,2,1,0:T(8,128)(2,1)S(1)}, u32[]{:S(2)}, u32[]{:S(2)}) collective-permute-start(bf16[2,2,112,128]{3,2,1,0:T(8,128)(2,1)S(1)} %copy-done.1), channel_id=1, source_target_pairs={{0,14},{1,15},{2,12},{3,13},{4,10},{5,11},{6,8},{7,9},{16,30},{17,... | collective-permute-start | bytes 344072 | tf_op jit(solution)/shard_map/ppermute | solution.py:349
  30.9 0.0 collective-permute-done.5.other_ref
  30.9 3.1 %near.1 = (f32[2,896,1]{2,1,0:T(8,128)S(1)}, f32[2,896,1]{2,1,0:T(8,128)S(1)}, f32[2,896,128]{2,1,0:T(8,128)S(1)}) custom-call(s32[1]{0:T(128)} %bitcast.me_ref, bf16[4,2,2,112,128]{4,3,2,1,0:T(8,128)(2,1)S(1)} %get-tuple-element.50.q_ref, bf16[4,2,2,112,128]{4,3,2,1,0:T(8,128)(2,1)S(1)} %get-tuple-element.51.own_ref, ...), custom_call_target="tpu_custom_call" | custom-call | tf_op jit(solution)/shard_map/near/pallas_call | solution.py:337
  34.0 0.0 collective-permute-done.6.refs_2_
  34.0 0.0 collective-permute-done.7.refs_3_
  34.0 3.5 %far.1 = (f32[2,896,1]{2,1,0:T(8,128)S(1)}, f32[2,896,1]{2,1,0:T(8,128)S(1)}, f32[2,896,128]{2,1,0:T(8,128)S(1)}) custom-call(s32[1]{0:T(128)} %bitcast.me_ref, bf16[4,2,2,112,128]{4,3,2,1,0:T(8,128)(2,1)S(1)} %get-tuple-element.50.q_ref, f32[2,896,1]{2,1,0:T(8,128)S(1)} %get-tuple-element.52.highest_ref, f32[2,896,1]{2,1,0:T(8,128)S(1)} %get-tuple-element.53.total_ref, ...), custom_call_target="tpu_custom_call" | custom-call | tf_op jit(solution)/shard_map/far/pallas_call | solution.py:337
  37.6 3.2 %collective-permute-done.8.refs_0_ = bf16[2,2,112,128]{3,2,1,0:T(8,128)(2,1)S(1)} collective-permute-done((bf16[2,2,112,128]{3,2,1,0:T(8,128)(2,1)S(1)}, bf16[2,2,112,128]{3,2,1,0:T(8,128)(2,1)S(1)}, u32[]{:S(2)}, u32[]{:S(2)}) %collective-permute-start.8) | collective-permute-done | bytes 114720 | tf_op jit(solution)/shard_map/ppermute | solution.py:349
  40.7 3.3 %collective-permute-done.9.refs_1_ = bf16[2,2,112,128]{3,2,1,0:T(8,128)(2,1)S(1)} collective-permute-done((bf16[2,2,112,128]{3,2,1,0:T(8,128)(2,1)S(1)}, bf16[2,2,112,128]{3,2,1,0:T(8,128)(2,1)S(1)}, u32[]{:S(2)}, u32[]{:S(2)}) %collective-permute-start.9) | collective-permute-done | bytes 114720 | tf_op jit(solution)/shard_map/ppermute | solution.py:349
  44.0 1.9 %collective-permute-start.10 = (bf16[2,2,112,128]{3,2,1,0:T(8,128)(2,1)S(1)}, bf16[2,2,112,128]{3,2,1,0:T(8,128)(2,1)S(1)}, u32[]{:S(2)}, u32[]{:S(2)}) collective-permute-start(bf16[2,2,112,128]{3,2,1,0:T(8,128)(2,1)S(1)} %collective-permute-done.8.refs_0_), channel_id=1, source_target_pairs={{8,9},{9,8},{10,11},{11,10},{12,13},{13,12},{14,15},{15,14},{24,25... | collective-permute-start | bytes 344072 | tf_op jit(solution)/shard_map/ppermute | solution.py:356
  46.0 2.4 %collective-permute-start.11 = (bf16[2,2,112,128]{3,2,1,0:T(8,128)(2,1)S(1)}, bf16[2,2,112,128]{3,2,1,0:T(8,128)(2,1)S(1)}, u32[]{:S(2)}, u32[]{:S(2)}) collective-permute-start(bf16[2,2,112,128]{3,2,1,0:T(8,128)(2,1)S(1)} %collective-permute-done.9.refs_1_), channel_id=1, source_target_pairs={{8,9},{9,8},{10,11},{11,10},{12,13},{13,12},{14,15},{15,14},{24,25... | collective-permute-start | bytes 344072 | tf_op jit(solution)/shard_map/ppermute | solution.py:356
  48.4 0.0 collective-permute-done.10.refs_2_
  48.4 0.9 %collective-permute-done.11.refs_3_ = bf16[2,2,112,128]{3,2,1,0:T(8,128)(2,1)S(1)} collective-permute-done((bf16[2,2,112,128]{3,2,1,0:T(8,128)(2,1)S(1)}, bf16[2,2,112,128]{3,2,1,0:T(8,128)(2,1)S(1)}, u32[]{:S(2)}, u32[]{:S(2)}) %collective-permute-start.11) | collective-permute-done | bytes 114720 | tf_op jit(solution)/shard_map/ppermute | solution.py:356
  49.3 3.2 %last.1 = (bf16[4,112,128]{2,1,0:T(8,128)(2,1)S(1)}, bf16[4,112,128]{2,1,0:T(8,128)(2,1)S(1)}, bf16[4,112,128]{2,1,0:T(8,128)(2,1)S(1)}, bf16[4,112,128]{2,1,0:T(8,128)(2,1)S(1)}) custom-call(s32[1]{0:T(128)} %bitcast.me_ref, bf16[4,2,2,112,128]{4,3,2,1,0:T(8,128)(2,1)S(1)} %get-tuple-element.50.q_ref, f32[2,896,1]{2,1,0:T(8,128)S(1)} %get-tuple-element.62.highest_ref, ...), custom_call_target="tpu_custom_call" | custom-call | tf_op jit(solution)/shard_map/last/pallas_call | solution.py:337
  52.5 0.6 collective-permute-start.12
  53.1 0.0 collective-permute-start.13
  53.1 3.0 %collective-permute-start.14 = (bf16[4,112,128]{2,1,0:T(8,128)(2,1)S(1)}, bf16[4,112,128]{2,1,0:T(8,128)(2,1)S(1)}, u32[]{:S(2)}, u32[]{:S(2)}) collective-permute-start(bf16[4,112,128]{2,1,0:T(8,128)(2,1)S(1)} %get-tuple-element.70), channel_id=1, source_target_pairs={{0,6},{1,7},{2,4},{3,5},{4,2},{5,3},{6,0},{7,1},{8,14},{9,15},{10,... | collective-permute-start | bytes 344072 | tf_op jit(solution)/shard_map/ppermute | solution.py:353
  56.1 1.9 %collective-permute-done.12.refs_1_ = bf16[4,112,128]{2,1,0:T(8,128)(2,1)S(1)} collective-permute-done((bf16[4,112,128]{2,1,0:T(8,128)(2,1)S(1)}, bf16[4,112,128]{2,1,0:T(8,128)(2,1)S(1)}, u32[]{:S(2)}, u32[]{:S(2)}) %collective-permute-start.12) | collective-permute-done | bytes 114720 | tf_op jit(solution)/shard_map/ppermute | solution.py:353
  58.0 1.1 %collective-permute-done.13.refs_2_ = bf16[4,112,128]{2,1,0:T(8,128)(2,1)S(1)} collective-permute-done((bf16[4,112,128]{2,1,0:T(8,128)(2,1)S(1)}, bf16[4,112,128]{2,1,0:T(8,128)(2,1)S(1)}, u32[]{:S(2)}, u32[]{:S(2)}) %collective-permute-start.13) | collective-permute-done | bytes 114720 | tf_op jit(solution)/shard_map/ppermute | solution.py:353
  59.1 2.5 %collective-permute-done.14.refs_3_ = bf16[4,112,128]{2,1,0:T(8,128)(2,1)S(1)} collective-permute-done((bf16[4,112,128]{2,1,0:T(8,128)(2,1)S(1)}, bf16[4,112,128]{2,1,0:T(8,128)(2,1)S(1)}, u32[]{:S(2)}, u32[]{:S(2)}) %collective-permute-start.14) | collective-permute-done | bytes 114720 | tf_op jit(solution)/shard_map/ppermute | solution.py:353
  61.6 1.3 %unpack.1 = bf16[112,16,128]{2,1,0:T(8,128)(2,1)} custom-call(s32[1]{0:T(128)} %bitcast.me_ref, bf16[4,112,128]{2,1,0:T(8,128)(2,1)S(1)} %get-tuple-element.67.refs_0_, bf16[4,112,128]{2,1,0:T(8,128)(2,1)S(1)} %collective-permute-done.12.refs_1_, bf16[4,112,128]{2,1,0:T(8,128)(2,1)S(1)} %collective-permute-done.13.refs_2_, ...), custom_call_target="tpu_custom_call" | custom-call | tf_op jit(solution)/shard_map/unpack/pallas_call | solution.py:337
Async XLA Ops:
  4.2 18.6 %collective-permute-start = (bf16[8,112,128]{2,1,0:T(8,128)(2,1)}, bf16[8,112,128]{2,1,0:T(8,128)(2,1)S(1)}, u32[]{:S(2)}, u32[]{:S(2)}) collective-permute-start(bf16[8,112,128]{2,1,0:T(8,128)(2,1)} %get-tuple-element.39), channel_id=1, source_target_pairs={{0,2},{1,3},{2,0},{3,1},{4,6},{5,7},{6,4},{7,5},{8,10},{9,11},{10,... | collective-permute-start | bytes 688136 | tf_op jit(solution)/shard_map/ppermute | solution.py:353
  5.8 17.0 %collective-permute-start.1 = (bf16[8,112,128]{2,1,0:T(8,128)(2,1)}, bf16[8,112,128]{2,1,0:T(8,128)(2,1)S(1)}, u32[]{:S(2)}, u32[]{:S(2)}) collective-permute-start(bf16[8,112,128]{2,1,0:T(8,128)(2,1)} %get-tuple-element.40), channel_id=1, source_target_pairs={{0,4},{1,5},{2,6},{3,7},{4,0},{5,1},{6,2},{7,3},{8,12},{9,13},{10,... | collective-permute-start | bytes 688136 | tf_op jit(solution)/shard_map/ppermute | solution.py:353
  7.4 15.5 %collective-permute-start.2 = (bf16[8,112,128]{2,1,0:T(8,128)(2,1)}, bf16[8,112,128]{2,1,0:T(8,128)(2,1)S(1)}, u32[]{:S(2)}, u32[]{:S(2)}) collective-permute-start(bf16[8,112,128]{2,1,0:T(8,128)(2,1)} %get-tuple-element.41), channel_id=1, source_target_pairs={{0,6},{1,7},{2,4},{3,5},{4,2},{5,3},{6,0},{7,1},{8,14},{9,15},{10,... | collective-permute-start | bytes 688136 | tf_op jit(solution)/shard_map/ppermute | solution.py:353
  7.8 13.9 %collective-permute-start.3 = (bf16[2,2,112,128]{3,2,1,0:T(8,128)(2,1)}, bf16[2,2,112,128]{3,2,1,0:T(8,128)(2,1)S(1)}, u32[]{:S(2)}, u32[]{:S(2)}) collective-permute-start(bf16[2,2,112,128]{3,2,1,0:T(8,128)(2,1)} %get-tuple-element.42), channel_id=1, source_target_pairs={{0,8},{1,9},{2,10},{3,11},{4,12},{5,13},{6,14},{7,15},{16,24},{17,... | collective-permute-start | bytes 344072 | tf_op jit(solution)/shard_map/ppermute | solution.py:349
  9.0 13.8 %collective-permute-start.4 = (bf16[2,2,112,128]{3,2,1,0:T(8,128)(2,1)}, bf16[2,2,112,128]{3,2,1,0:T(8,128)(2,1)S(1)}, u32[]{:S(2)}, u32[]{:S(2)}) collective-permute-start(bf16[2,2,112,128]{3,2,1,0:T(8,128)(2,1)} %get-tuple-element.43), channel_id=1, source_target_pairs={{0,10},{1,11},{2,8},{3,9},{4,14},{5,15},{6,12},{7,13},{16,26},{17,... | collective-permute-start | bytes 344072 | tf_op jit(solution)/shard_map/ppermute | solution.py:349
  22.8 0.9 %copy-start = (bf16[8,112,128]{2,1,0:T(8,128)(2,1)S(1)}, bf16[8,112,128]{2,1,0:T(8,128)(2,1)}, u32[]{:S(2)}) copy-start(bf16[8,112,128]{2,1,0:T(8,128)(2,1)} %get-tuple-element.46.refs_0_) | copy-start | bytes 688132
  23.8 4.5 %copy-start.2 = (bf16[2,2,112,128]{3,2,1,0:T(8,128)(2,1)S(1)}, bf16[2,2,112,128]{3,2,1,0:T(8,128)(2,1)}, u32[]{:S(2)}) copy-start(bf16[2,2,112,128]{3,2,1,0:T(8,128)(2,1)} %get-tuple-element.60) | copy-start | bytes 344068
  23.8 5.8 %copy-start.1 = (bf16[2,2,112,128]{3,2,1,0:T(8,128)(2,1)S(1)}, bf16[2,2,112,128]{3,2,1,0:T(8,128)(2,1)}, u32[]{:S(2)}) copy-start(bf16[2,2,112,128]{3,2,1,0:T(8,128)(2,1)} %get-tuple-element.61) | copy-start | bytes 344068
  23.9 7.0 %collective-permute-start.5 = (bf16[4,2,2,112,128]{4,3,2,1,0:T(8,128)(2,1)S(1)}, bf16[4,2,2,112,128]{4,3,2,1,0:T(8,128)(2,1)S(1)}, u32[]{:S(2)}, u32[]{:S(2)}) collective-permute-start(bf16[4,2,2,112,128]{4,3,2,1,0:T(8,128)(2,1)S(1)} %get-tuple-element.51.own_ref), channel_id=1, source_target_pairs={{0,1},{1,0},{2,3},{3,2},{4,5},{5,4},{6,7},{7,6},{8,9},{9,8},{10,11... | collective-permute-start | bytes 1376264 | tf_op jit(solution)/shard_map/ppermute | solution.py:356
  23.9 10.1 %collective-permute-start.6 = (bf16[2,2,112,128]{3,2,1,0:T(8,128)(2,1)S(1)}, bf16[2,2,112,128]{3,2,1,0:T(8,128)(2,1)S(1)}, u32[]{:S(2)}, u32[]{:S(2)}) collective-permute-start(bf16[2,2,112,128]{3,2,1,0:T(8,128)(2,1)S(1)} %collective-permute-done.3.refs_0_), channel_id=1, source_target_pairs={{8,9},{9,8},{10,11},{11,10},{12,13},{13,12},{14,15},{15,14},{24,25... | collective-permute-start | bytes 344072 | tf_op jit(solution)/shard_map/ppermute | solution.py:356
  26.3 7.7 %collective-permute-start.7 = (bf16[2,2,112,128]{3,2,1,0:T(8,128)(2,1)S(1)}, bf16[2,2,112,128]{3,2,1,0:T(8,128)(2,1)S(1)}, u32[]{:S(2)}, u32[]{:S(2)}) collective-permute-start(bf16[2,2,112,128]{3,2,1,0:T(8,128)(2,1)S(1)} %collective-permute-done.4.refs_1_), channel_id=1, source_target_pairs={{8,9},{9,8},{10,11},{11,10},{12,13},{13,12},{14,15},{15,14},{24,25... | collective-permute-start | bytes 344072 | tf_op jit(solution)/shard_map/ppermute | solution.py:356
  28.3 12.5 %collective-permute-start.8 = (bf16[2,2,112,128]{3,2,1,0:T(8,128)(2,1)S(1)}, bf16[2,2,112,128]{3,2,1,0:T(8,128)(2,1)S(1)}, u32[]{:S(2)}, u32[]{:S(2)}) collective-permute-start(bf16[2,2,112,128]{3,2,1,0:T(8,128)(2,1)S(1)} %copy-done.2), channel_id=1, source_target_pairs={{0,12},{1,13},{2,14},{3,15},{4,8},{5,9},{6,10},{7,11},{16,28},{17,... | collective-permute-start | bytes 344072 | tf_op jit(solution)/shard_map/ppermute | solution.py:349
  29.6 14.5 %collective-permute-start.9 = (bf16[2,2,112,128]{3,2,1,0:T(8,128)(2,1)S(1)}, bf16[2,2,112,128]{3,2,1,0:T(8,128)(2,1)S(1)}, u32[]{:S(2)}, u32[]{:S(2)}) collective-permute-start(bf16[2,2,112,128]{3,2,1,0:T(8,128)(2,1)S(1)} %copy-done.1), channel_id=1, source_target_pairs={{0,14},{1,15},{2,12},{3,13},{4,10},{5,11},{6,8},{7,9},{16,30},{17,... | collective-permute-start | bytes 344072 | tf_op jit(solution)/shard_map/ppermute | solution.py:349
  44.0 4.3 %collective-permute-start.10 = (bf16[2,2,112,128]{3,2,1,0:T(8,128)(2,1)S(1)}, bf16[2,2,112,128]{3,2,1,0:T(8,128)(2,1)S(1)}, u32[]{:S(2)}, u32[]{:S(2)}) collective-permute-start(bf16[2,2,112,128]{3,2,1,0:T(8,128)(2,1)S(1)} %collective-permute-done.8.refs_0_), channel_id=1, source_target_pairs={{8,9},{9,8},{10,11},{11,10},{12,13},{13,12},{14,15},{15,14},{24,25... | collective-permute-start | bytes 344072 | tf_op jit(solution)/shard_map/ppermute | solution.py:356
  46.0 3.4 %collective-permute-start.11 = (bf16[2,2,112,128]{3,2,1,0:T(8,128)(2,1)S(1)}, bf16[2,2,112,128]{3,2,1,0:T(8,128)(2,1)S(1)}, u32[]{:S(2)}, u32[]{:S(2)}) collective-permute-start(bf16[2,2,112,128]{3,2,1,0:T(8,128)(2,1)S(1)} %collective-permute-done.9.refs_1_), channel_id=1, source_target_pairs={{8,9},{9,8},{10,11},{11,10},{12,13},{13,12},{14,15},{15,14},{24,25... | collective-permute-start | bytes 344072 | tf_op jit(solution)/shard_map/ppermute | solution.py:356
  52.5 5.5 %collective-permute-start.12 = (bf16[4,112,128]{2,1,0:T(8,128)(2,1)S(1)}, bf16[4,112,128]{2,1,0:T(8,128)(2,1)S(1)}, u32[]{:S(2)}, u32[]{:S(2)}) collective-permute-start(bf16[4,112,128]{2,1,0:T(8,128)(2,1)S(1)} %get-tuple-element.68), channel_id=1, source_target_pairs={{0,2},{1,3},{2,0},{3,1},{4,6},{5,7},{6,4},{7,5},{8,10},{9,11},{10,... | collective-permute-start | bytes 344072 | tf_op jit(solution)/shard_map/ppermute | solution.py:353
  53.1 6.0 %collective-permute-start.13 = (bf16[4,112,128]{2,1,0:T(8,128)(2,1)S(1)}, bf16[4,112,128]{2,1,0:T(8,128)(2,1)S(1)}, u32[]{:S(2)}, u32[]{:S(2)}) collective-permute-start(bf16[4,112,128]{2,1,0:T(8,128)(2,1)S(1)} %get-tuple-element.69), channel_id=1, source_target_pairs={{0,4},{1,5},{2,6},{3,7},{4,0},{5,1},{6,2},{7,3},{8,12},{9,13},{10,... | collective-permute-start | bytes 344072 | tf_op jit(solution)/shard_map/ppermute | solution.py:353
  53.1 8.5 %collective-permute-start.14 = (bf16[4,112,128]{2,1,0:T(8,128)(2,1)S(1)}, bf16[4,112,128]{2,1,0:T(8,128)(2,1)S(1)}, u32[]{:S(2)}, u32[]{:S(2)}) collective-permute-start(bf16[4,112,128]{2,1,0:T(8,128)(2,1)S(1)} %get-tuple-element.70), channel_id=1, source_target_pairs={{0,6},{1,7},{2,4},{3,5},{4,2},{5,3},{6,0},{7,1},{8,14},{9,15},{10,... | collective-permute-start | bytes 344072 | tf_op jit(solution)/shard_map/ppermute | solution.py:353

commit v5 on v1

v5 whole, which is shorter than its diff:
```python
import functools
import math

import jax
import jax.numpy as jnp
import numpy as np
from jax import lax
from jax.experimental import pallas as pl
from jax.experimental.pallas import tpu as pltpu
from jax.sharding import PartitionSpec as P

ROPE_BASE = 1000000.0
EPSILON = 1e-06
MASKED = -1e30
VMEM_LIMIT = 24 * 1024 * 1024
PACK_VMEM = 56 * 1024 * 1024
VMEM = pl.BlockSpec(memory_space=pltpu.VMEM)
SMEM = pl.BlockSpec(memory_space=pltpu.SMEM)
HBM = pl.BlockSpec(memory_space=pltpu.HBM)
CONTRACT = (((1,), (1,)), ((), ()))


def rope_table(length, width):
    half = width // 2
    frequency = np.float64(ROPE_BASE) ** (-(np.arange(half, dtype=np.float64) * 2.0 / width))
    angles = np.arange(length, dtype=np.float32)[:, None] * frequency.astype(np.float32)[None, :]
    wide = angles.astype(np.float64)
    return np.concatenate([np.cos(wide), np.sin(wide)], axis=-1).astype(np.float32)


def pack_kernel(rep, q_ref, k_ref, v_ref, table_ref, qg_ref, kg_ref, out_ref, qf_ref, kf_ref, vf_ref):
    tokens, heads, width = q_ref.shape
    kv_heads = k_ref.shape[1]
    chips, rows = out_ref.shape[:2]
    per_chip = rows - 2
    qf_ref[...] = q_ref[...].astype(jnp.float32).reshape(tokens * heads, width)
    kf_ref[...] = k_ref[...].astype(jnp.float32).reshape(tokens * kv_heads, width)
    vf_ref[...] = v_ref[...].astype(jnp.float32).reshape(tokens * kv_heads, width)
    table = table_ref[...]
    swapped = pltpu.roll(table, width // 2, 1)
    first = lax.broadcasted_iota(jnp.int32, table.shape, 1) < width // 2
    cosine = jnp.where(first, table, swapped)
    sine = jnp.where(first, -swapped, table)

    def rotate(floats, gain):
        mean_square = jnp.mean(floats * floats, axis=-1, keepdims=True)
        normed = floats * lax.rsqrt(mean_square + EPSILON) * gain
        turned = pltpu.roll(normed, width // 2, 1)
        return (normed * cosine + turned * sine).astype(jnp.bfloat16)

    query_gain, key_gain = qg_ref[...], kg_ref[...]
    for head in range(heads):
        floats = qf_ref[pl.ds(head, tokens, stride=heads), :]
        out_ref[head // per_chip, head % per_chip] = rotate(floats, query_gain)
    for head in range(kv_heads):
        floats = kf_ref[pl.ds(head, tokens, stride=kv_heads), :]
        rotated = rotate(floats, key_gain)
        values = vf_ref[pl.ds(head, tokens, stride=kv_heads), :].astype(jnp.bfloat16)
        for copy in range(rep):
            out_ref[head * rep + copy, per_chip] = rotated
            out_ref[head * rep + copy, per_chip + 1] = values


def looped_kernel(core_ref, x_ref, other_ref, out_ref):
    _, rows, tokens, width = x_ref.shape
    per_chip = rows - 2
    core = core_ref[0]
    block = pl.program_id(0)
    scale = math.log2(math.e) / math.sqrt(width)
    queries = x_ref[block, :per_chip].reshape(per_chip * tokens, width)
    row = lax.broadcasted_iota(jnp.int32, (per_chip, tokens, tokens), 1).reshape(per_chip * tokens, tokens)
    column = lax.broadcasted_iota(jnp.int32, (per_chip * tokens, tokens), 1)

    def merge(carried, keys, values, allowed):
        highest, total, weighted = carried
        scores = lax.dot_general(queries, keys, CONTRACT, preferred_element_type=jnp.float32)
        scores = jnp.where(allowed, scores, MASKED)
        new = jnp.maximum(highest, jnp.max(scores, axis=-1, keepdims=True))
        probs = jnp.exp2((scores - new) * scale)
        factor = jnp.exp2((highest - new) * scale)
        total = total * factor + jnp.sum(probs, axis=-1, keepdims=True)
        summed = jnp.dot(probs.astype(jnp.bfloat16), values, preferred_element_type=jnp.float32)
        return new, total, weighted * factor + summed

    def advance(index, carried):
        behind = (block - index) * tokens
        carried = merge(carried, x_ref[index, per_chip], x_ref[index, per_chip + 1], column <= row + behind)
        return merge(carried, other_ref[index, 0], other_ref[index, 1], column < behind + core * tokens)

    initial = (
        jnp.full((per_chip * tokens, 1), MASKED, jnp.float32),
        jnp.zeros((per_chip * tokens, 1), jnp.float32),
        jnp.zeros((per_chip * tokens, width), jnp.float32),
    )
    _, total, weighted = lax.fori_loop(0, block + 1, advance, initial)
    out_ref[block] = (weighted / total).astype(jnp.bfloat16).reshape(per_chip, tokens, width)


def general_plan(length, devices, query_states, key_states, value_states, query_gain, key_gain):
    tokens, heads, width = query_states.shape
    kv_heads = key_states.shape[1]
    chips = devices // 2
    per_chip = heads // chips
    rep = (heads // kv_heads) // per_chip
    me = lax.axis_index("seq")
    core = lax.rem(me, 2)
    same_core = [list(range(start, devices, 2)) for start in range(2)]
    swap = [(device, device ^ 1) for device in range(devices)]
    table = lax.dynamic_slice_in_dim(jnp.asarray(rope_table(length, width)), me * tokens, tokens, 0)
    packed = pl.pallas_call(
        functools.partial(pack_kernel, rep),
        out_shape=jax.ShapeDtypeStruct((chips, per_chip + 2, tokens, width), jnp.bfloat16),
        in_specs=[VMEM] * 6,
        out_specs=VMEM,
        scratch_shapes=[
            pltpu.VMEM((tokens * heads, width), jnp.float32),
            pltpu.VMEM((tokens * kv_heads, width), jnp.float32),
            pltpu.VMEM((tokens * kv_heads, width), jnp.float32),
        ],
        compiler_params=pltpu.CompilerParams(vmem_limit_bytes=48 * 1024 * 1024),
        name="pack",
    )(query_states, key_states, value_states, table, query_gain[None], key_gain[None])
    arrived = lax.all_to_all(
        packed, "seq", split_axis=0, concat_axis=0, axis_index_groups=same_core, tiled=True
    )
    other = lax.ppermute(arrived[:, per_chip:], "seq", swap)
    attended = pl.pallas_call(
        looped_kernel,
        grid=(chips,),
        out_shape=jax.ShapeDtypeStruct((chips, per_chip, tokens, width), jnp.bfloat16),
        in_specs=[SMEM, VMEM, VMEM],
        out_specs=VMEM,
        compiler_params=pltpu.CompilerParams(vmem_limit_bytes=48 * 1024 * 1024),
        name="attention",
    )(core[None], arrived, other)
    returned = lax.all_to_all(
        attended, "seq", split_axis=0, concat_axis=0, axis_index_groups=same_core, tiled=True
    )
    return jnp.transpose(returned.reshape(heads, tokens, width), (1, 0, 2))


def rope_factors(table):
    half = table.shape[1] // 2
    swapped = pltpu.roll(table, half, 1)
    first = lax.broadcasted_iota(jnp.int32, table.shape, 1) < half
    return jnp.where(first, table, swapped), jnp.where(first, -swapped, table)


def normalize(rows):
    floats = rows.astype(jnp.float32)
    squares = floats * floats
    large = squares.astype(jnp.bfloat16)
    small = (squares - large.astype(jnp.float32)).astype(jnp.bfloat16)
    width = rows.shape[1]
    ones = jnp.ones((2 * width, width), jnp.bfloat16)
    added = jnp.dot(jnp.concatenate([large, small], axis=1), ones, preferred_element_type=jnp.float32)
    return floats * lax.rsqrt(added * (1.0 / width) + EPSILON)


def turn(normed, gain, cosine, sine):
    scaled = normed * gain
    return (scaled * cosine + pltpu.roll(scaled, scaled.shape[1] // 2, 1) * sine).astype(jnp.bfloat16)


def send_kernel(me_ref, q_hbm, k_hbm, v_hbm, table_hbm, query_gain_ref, key_gain_ref, *refs):
    outs, (q_ref, k_ref, v_ref, table_ref, qf_ref, kf_ref, vf_ref, sems) = refs[:-8], refs[-8:]
    tokens, heads, width = q_ref.shape
    kv_heads = k_ref.shape[1]
    crossing, near_ref = outs[:-1], outs[-1]
    half = len(crossing)
    per_chip = near_ref.shape[1] - 2
    me = me_ref[0]
    chip = me // 2
    base = chip // half * half
    start = pl.multiple_of(me * tokens, 8)
    copies = [
        pltpu.make_async_copy(k_hbm, k_ref, sems.at[0]),
        pltpu.make_async_copy(table_hbm.at[pl.ds(start, tokens)], table_ref, sems.at[1]),
        pltpu.make_async_copy(v_hbm, v_ref, sems.at[2]),
        pltpu.make_async_copy(q_hbm, q_ref, sems.at[3]),
    ]
    for copy in copies:
        copy.start()
    targets = [(chip ^ (half + step), ref) for step, ref in enumerate(crossing)]
    targets += [(base + place, near_ref.at[place]) for place in range(half)]
    copies[0].wait()
    kf_ref[...] = normalize(k_ref[...].reshape(tokens * kv_heads, width))
    copies[1].wait()
    cosine, sine = rope_factors(table_ref[...])
    copies[2].wait()
    vf_ref[...] = v_ref[...].astype(jnp.float32).reshape(tokens * kv_heads, width)
    for target, ref in targets:
        rows = pl.ds(target, tokens, stride=kv_heads)
        ref[per_chip] = turn(kf_ref[rows, :], key_gain_ref[...], cosine, sine)
        ref[per_chip + 1] = vf_ref[rows, :].astype(jnp.bfloat16)
    copies[3].wait()
    qf_ref[...] = normalize(q_ref[...].reshape(tokens * heads, width))
    for target, ref in targets:
        for row in range(per_chip):
            normed = qf_ref[pl.ds(target * per_chip + row, tokens, stride=heads), :]
            ref[row] = turn(normed, query_gain_ref[...], cosine, sine)


def order_kernel(me_ref, *refs):
    crossed, (near_ref, query_ref, pair_ref) = refs[:-3], refs[-3:]
    half, per_chip = len(crossed), query_ref.shape[1]
    chip = me_ref[0] // 2
    base = chip // half * half
    sources = [(chip ^ (half + step), ref) for step, ref in enumerate(crossed)]
    sources += [(base + place, near_ref.at[place]) for place in range(half)]
    for source, ref in sources:
        query_ref[source] = ref[:per_chip]
        pair_ref[source] = ref[per_chip:]


def attention_kernel(me_ref, q_ref, own_ref, other_ref, *refs):
    outs, out_ref = refs[:-1], refs[-1]
    crossing, near_ref = outs[:-1], outs[-1]
    blocks, per_chip, tokens, width = q_ref.shape
    chip, core = me_ref[0] // 2, lax.rem(me_ref[0], 2)
    scale = math.log2(math.e) / math.sqrt(width)
    keys_own, values_own, keys_other, values_other = [
        ref[:, i].reshape(blocks * tokens, width) for ref in (own_ref, other_ref) for i in range(2)
    ]
    rows = per_chip * tokens
    for block in range(blocks):
        queries = q_ref[block].reshape(rows, width)
        reach = (block + 1) * tokens
        own = lax.dot_general(queries, keys_own[:reach], CONTRACT, preferred_element_type=jnp.float32)
        other = lax.dot_general(queries, keys_other[:reach], CONTRACT, preferred_element_type=jnp.float32)
        row = lax.broadcasted_iota(jnp.int32, (per_chip, tokens, reach), 1).reshape(rows, reach)
        column = lax.broadcasted_iota(jnp.int32, (rows, reach), 1)
        own = jnp.where(column <= row + block * tokens, own, MASKED)
        other = jnp.where(column < (block + core) * tokens, other, MASKED)
        highest = jnp.maximum(
            jnp.max(own, axis=-1, keepdims=True), jnp.max(other, axis=-1, keepdims=True)
        )
        probs_own = jnp.exp2((own - highest) * scale)
        probs_other = jnp.exp2((other - highest) * scale)
        total = jnp.sum(probs_own, axis=-1, keepdims=True) + jnp.sum(probs_other, axis=-1, keepdims=True)
        summed = jnp.dot(
            probs_own.astype(jnp.bfloat16), values_own[:reach], preferred_element_type=jnp.float32
        ) + jnp.dot(
            probs_other.astype(jnp.bfloat16), values_other[:reach], preferred_element_type=jnp.float32
        )
        out_ref[block] = (summed / total).astype(jnp.bfloat16).reshape(per_chip, tokens, width)
    half = len(crossing)
    base = chip // half * half
    for step, ref in enumerate(crossing):
        ref[...] = out_ref[chip ^ (half + step)]
    near_ref[...] = out_ref[pl.ds(base, half)]


def unpack_kernel(me_ref, *refs):
    crossed, (near_ref, out_ref, floats_ref) = refs[:-3], refs[-3:]
    tokens, heads, width = out_ref.shape
    half, per_chip = len(crossed), near_ref.shape[1]
    chip = me_ref[0] // 2
    base = chip // half * half
    sources = [(base + place, near_ref.at[place]) for place in range(half)]
    sources += [(chip ^ (half + step), ref) for step, ref in enumerate(crossed)]
    for source, ref in sources:
        for row in range(per_chip):
            floats_ref[pl.ds(source * per_chip + row, tokens, stride=heads), :] = ref[row].astype(jnp.float32)
    out_ref[...] = floats_ref[...].reshape(tokens, heads, width).astype(jnp.bfloat16)


def short_plan(length, devices, query_states, key_states, value_states, query_gain, key_gain):
    tokens, heads, width = query_states.shape
    kv_heads = key_states.shape[1]
    chips = devices // 2
    half = chips // 2
    per_chip = heads // chips
    bf16, f32 = jnp.bfloat16, jnp.float32
    me = lax.axis_index("seq")[None]

    def call(kernel, name, outs, *operands, scratch=(), specs=None, limit=VMEM_LIMIT):
        return pl.pallas_call(
            kernel,
            out_shape=outs,
            in_specs=specs or [SMEM] + [VMEM] * len(operands),
            out_specs=jax.tree.map(lambda _: VMEM, outs),
            scratch_shapes=scratch,
            compiler_params=pltpu.CompilerParams(vmem_limit_bytes=limit),
            name=name,
        )(me, *operands)

    def exchange(crossing, near):
        links = [
            [(device, ((device // 2) ^ (half + step)) * 2 + device % 2) for device in range(devices)]
            for step in range(half)
        ]
        groups = [[(base + place) * 2 + core for place in range(half)] for base in (0, half) for core in range(2)]
        crossed = [lax.ppermute(array, "seq", links[step]) for step, array in enumerate(crossing)]
        return crossed + [
            lax.all_to_all(near, "seq", split_axis=0, concat_axis=0, axis_index_groups=groups, tiled=True)
        ]

    shape = jax.ShapeDtypeStruct
    *crossing, near = call(
        send_kernel,
        "send",
        [shape((per_chip + 2, tokens, width), bf16)] * half + [shape((half, per_chip + 2, tokens, width), bf16)],
        query_states,
        key_states,
        value_states,
        jnp.asarray(rope_table(length, width)),
        query_gain[None],
        key_gain[None],
        specs=[SMEM, HBM, HBM, HBM, HBM, VMEM, VMEM],
        scratch=[
            pltpu.VMEM((tokens, heads, width), bf16),
            pltpu.VMEM((tokens, kv_heads, width), bf16),
            pltpu.VMEM((tokens, kv_heads, width), bf16),
            pltpu.VMEM((tokens, width), f32),
            pltpu.VMEM((tokens * heads, width), f32),
            pltpu.VMEM((tokens * kv_heads, width), f32),
            pltpu.VMEM((tokens * kv_heads, width), f32),
            pltpu.SemaphoreType.DMA((4,)),
        ],
        limit=PACK_VMEM,
    )
    queries, own = call(
        order_kernel,
        "order",
        [shape((chips, per_chip, tokens, width), bf16), shape((chips, 2, tokens, width), bf16)],
        *exchange(crossing, near),
    )
    other = lax.ppermute(own, "seq", [(device, device ^ 1) for device in range(devices)])
    *crossing, near = call(
        attention_kernel,
        "attention",
        [shape((per_chip, tokens, width), bf16)] * half + [shape((half, per_chip, tokens, width), bf16)],
        queries,
        own,
        other,
        scratch=[pltpu.VMEM((chips, per_chip, tokens, width), bf16)],
    )
    return call(
        unpack_kernel,
        "unpack",
        shape((tokens, heads, width), bf16),
        *exchange(crossing, near),
        scratch=[pltpu.VMEM((tokens * heads, width), f32)],
    )


def solution(mesh):
    devices = mesh.shape["seq"]
    groups = mesh.shape["groups"]
    placed = P(("groups", "seq"), None, None)

    def run(query_states, key_states, value_states, query_gain, key_gain):
        length = query_states.shape[0] // groups
        plan = short_plan if devices == 2 * key_states.shape[1] else general_plan
        return jax.shard_map(
            functools.partial(plan, length, devices),
            mesh=mesh,
            in_specs=(placed, placed, placed, P(), P()),
            out_specs=placed,
            check_vma=False,
        )(query_states, key_states, value_states, query_gain, key_gain)

    return run
```

time: 61.5 us -> 60.4 us (0.982)
  blocking collectives: 46.9 us -> 0 us
  starting transfers between devices: 0.07 us -> 28.2 us
  waiting for transfers between devices: 1.8 us -> 21.2 us
  local copies, waits for them, and re-layouts: 5.3 us -> 0.02 us
  Pallas kernels: 7.05 us -> 10.5 us
    all_to_all x2 -> x0, blocking collectives: 46.9 us -> none  [the longest x1 30.4 us: on_device(): lax.all_to_all(packed, 'seq', split_axis=0, concat_axis=0, axis_index_gro...]
    ppermute x1 -> x9, waiting for transfers between devices: 1.8 us -> 21.2 us  [the longest x8 19.4 us: exchange(): lax.ppermute(array, 'seq', links[step])]
    ppermute x1 -> x9, starting transfers between devices: 0.07 us -> 16.7 us  [the longest x8 16.6 us: exchange(): lax.ppermute(array, 'seq', links[step])]
    all_to_all x0 -> x2, starting transfers between devices: none -> 11.6 us  [exchange(): lax.all_to_all(near, 'seq', split_axis=0, concat_axis=0, axis_index_group...]
    unnamed x10 -> x8, local copies, waits for them, and re-layouts: 3.56 us -> 0.02 us
    pallas_call x2 -> x4, Pallas kernels: 7.05 us -> 10.5 us  [call(): pl.pallas_call(kernel, out_shape=outs, in_specs=specs or [SMEM] + [VMEM]...]
    reshape x1 -> x0, local copies, waits for them, and re-layouts: 0.89 us -> none  [on_device(): return jnp.transpose(returned.reshape(heads, tokens, width), (1, 0, 2))]
    dynamic_slice x1 -> x0, local copies, waits for them, and re-layouts: 0.82 us -> none  [on_device(): lax.dynamic_slice_in_dim(jnp.asarray(rope_table(length, width)), me * tok...]
  transfers between devices with their start and end apart: 1 -> 11, of which waited for: 1 -> 5; matrix products, arithmetic and copies ran while one was open for 0% -> 0% of each run, Pallas kernels for 0% -> 0%
where the time goes in v5:
time: 60.4 us; the launch traced here: 60.1 us
  starting transfers between devices  28.2 us (47%)
  waiting for transfers between devices  21.2 us (35%)
  Pallas kernels  10.5 us (17%)
    ppermute x8, waiting for transfers between devices, exchange(): lax.ppermute(array, 'seq', links[step])  19.4 us
    ppermute x8, starting transfers between devices, exchange(): lax.ppermute(array, 'seq', links[step])  16.6 us
    all_to_all x2, starting transfers between devices, exchange(): lax.all_to_all(near, 'seq', split_axis=0, concat_axis=0, axis_index_group...  11.6 us
    pallas_call x4, Pallas kernels, call(): pl.pallas_call(kernel, out_shape=outs, in_specs=specs or [SMEM] + [VMEM]...  10.5 us
    ppermute x1, waiting for transfers between devices, short_plan(): lax.ppermute(own, 'seq', [(device, device ^ 1) for device in range(device...  1.8 us
  transfers between devices with their start and end apart: 11, of which 5 were waited for; matrix products, arithmetic and copies ran while one was open for 0% of the time, Pallas kernels for 0%

profile of v5, /device:TPU:0, one launch (start us, length us, event | category | flops | bytes accessed | tf_op | source)
XLA Modules:
  0.0 60.1 jit_solution(9076999206471337007)
XLA Ops:
  0.0 4.2 %send.1 = (bf16[4,112,128]{2,1,0:T(8,128)(2,1)}, bf16[4,112,128]{2,1,0:T(8,128)(2,1)}, bf16[4,112,128]{2,1,0:T(8,128)(2,1)}, bf16[4,112,128]{2,1,0:T(8,128)(2,1)}, bf16[4,4,112,128]{3,2,1,0:T(8,128)(2,1)}) custom-call(s32[1]{0:T(128)} %bitcast.me_ref, bf16[112,16,128]{2,1,0:T(8,128)(2,1)} %q_hbm.1, bf16[112,8,128]{2,1,0:T(8,128)(2,1)} %k_hbm.1, ...), custom_call_target="tpu_custom_call" | custom-call | tf_op jit(solution)/shard_map/send/pallas_call | solution.py:278
  4.2 0.0 copy-start.3
  4.2 0.0 copy-start.2
  4.2 0.0 copy-start.1
  4.3 0.0 copy-start
  4.3 5.4 %all-to-all-start = ((bf16[4,4,112,128]{3,2,1,0:T(8,128)(2,1)}), bf16[4,4,112,128]{3,2,1,0:T(8,128)(2,1)S(1)}, u32[]{:S(2)}, u32[]{:S(2)}) async-start(bf16[4,4,112,128]{3,2,1,0:T(8,128)(2,1)} %get-tuple-element.21), calls=%async_computation | async-start | bytes 917504 | tf_op jit(solution)/shard_map/all_to_all | solution.py:296
  9.7 0.0 copy-done.3
  9.7 2.6 %collective-permute-start = (bf16[4,112,128]{2,1,0:T(8,128)(2,1)S(1)}, bf16[4,112,128]{2,1,0:T(8,128)(2,1)S(1)}, u32[]{:S(2)}, u32[]{:S(2)}) collective-permute-start(bf16[4,112,128]{2,1,0:T(8,128)(2,1)S(1)} %copy-done.3), channel_id=1, source_target_pairs={{0,8},{1,9},{2,10},{3,11},{4,12},{5,13},{6,14},{7,15},{8,0},{9,1},... | collective-permute-start | bytes 344072 | tf_op jit(solution)/shard_map/ppermute | solution.py:294
  12.3 0.0 copy-done.2
  12.3 1.8 %collective-permute-start.1 = (bf16[4,112,128]{2,1,0:T(8,128)(2,1)S(1)}, bf16[4,112,128]{2,1,0:T(8,128)(2,1)S(1)}, u32[]{:S(2)}, u32[]{:S(2)}) collective-permute-start(bf16[4,112,128]{2,1,0:T(8,128)(2,1)S(1)} %copy-done.2), channel_id=1, source_target_pairs={{0,10},{1,11},{2,8},{3,9},{4,14},{5,15},{6,12},{7,13},{8,2},{9,3},... | collective-permute-start | bytes 344072 | tf_op jit(solution)/shard_map/ppermute | solution.py:294
  14.1 0.0 copy-done.1
  14.1 3.5 %collective-permute-start.2 = (bf16[4,112,128]{2,1,0:T(8,128)(2,1)S(1)}, bf16[4,112,128]{2,1,0:T(8,128)(2,1)S(1)}, u32[]{:S(2)}, u32[]{:S(2)}) collective-permute-start(bf16[4,112,128]{2,1,0:T(8,128)(2,1)S(1)} %copy-done.1), channel_id=1, source_target_pairs={{0,12},{1,13},{2,14},{3,15},{4,8},{5,9},{6,10},{7,11},{8,4},{9,5},... | collective-permute-start | bytes 344072 | tf_op jit(solution)/shard_map/ppermute | solution.py:294
  17.6 0.0 copy-done
  17.6 0.1 collective-permute-start.3
  17.6 0.8 %collective-permute-done.refs_0_ = bf16[4,112,128]{2,1,0:T(8,128)(2,1)S(1)} collective-permute-done((bf16[4,112,128]{2,1,0:T(8,128)(2,1)S(1)}, bf16[4,112,128]{2,1,0:T(8,128)(2,1)S(1)}, u32[]{:S(2)}, u32[]{:S(2)}) %collective-permute-start) | collective-permute-done | bytes 114720 | tf_op jit(solution)/shard_map/ppermute | solution.py:294
  18.4 11.6 %collective-permute-done.1.refs_1_ = bf16[4,112,128]{2,1,0:T(8,128)(2,1)S(1)} collective-permute-done((bf16[4,112,128]{2,1,0:T(8,128)(2,1)S(1)}, bf16[4,112,128]{2,1,0:T(8,128)(2,1)S(1)}, u32[]{:S(2)}, u32[]{:S(2)}) %collective-permute-start.1) | collective-permute-done | bytes 114720 | tf_op jit(solution)/shard_map/ppermute | solution.py:294
  30.0 0.0 collective-permute-done.2.refs_2_
  30.0 0.0 collective-permute-done.3.refs_3_
  30.0 0.0 all-to-all-done.refs_4_
  30.1 0.1 order.1
  30.1 0.1 collective-permute-start.4
  30.2 1.8 %collective-permute-done.4.other_ref = bf16[8,2,112,128]{3,2,1,0:T(8,128)(2,1)S(1)} collective-permute-done((bf16[8,2,112,128]{3,2,1,0:T(8,128)(2,1)S(1)}, bf16[8,2,112,128]{3,2,1,0:T(8,128)(2,1)S(1)}, u32[]{:S(2)}, u32[]{:S(2)}) %collective-permute-start.4) | collective-permute-done | bytes 458784 | tf_op jit(solution)/shard_map/ppermute | solution.py:329
  32.0 5.0 %attention.1 = (bf16[2,112,128]{2,1,0:T(8,128)(2,1)S(1)}, bf16[2,112,128]{2,1,0:T(8,128)(2,1)S(1)}, bf16[2,112,128]{2,1,0:T(8,128)(2,1)S(1)}, bf16[2,112,128]{2,1,0:T(8,128)(2,1)S(1)}, bf16[4,2,112,128]{3,2,1,0:T(8,128)(2,1)}) custom-call(s32[1]{0:T(128)} %bitcast.me_ref, bf16[8,2,112,128]{3,2,1,0:T(8,128)(2,1)S(1)} %get-tuple-element.22.q_ref, ...), custom_call_target="tpu_custom_call" | custom-call | tf_op jit(solution)/shard_map/attention/pallas_call | solution.py:278
  37.0 6.2 %all-to-all-start.1 = ((bf16[4,2,112,128]{3,2,1,0:T(8,128)(2,1)}), bf16[4,2,112,128]{3,2,1,0:T(8,128)(2,1)S(1)}, u32[]{:S(2)}, u32[]{:S(2)}) async-start(bf16[4,2,112,128]{3,2,1,0:T(8,128)(2,1)} %get-tuple-element.28), calls=%async_computation.1 | async-start | bytes 458752 | tf_op jit(solution)/shard_map/all_to_all | solution.py:296
  43.1 3.5 %collective-permute-start.5 = (bf16[2,112,128]{2,1,0:T(8,128)(2,1)S(1)}, bf16[2,112,128]{2,1,0:T(8,128)(2,1)S(1)}, u32[]{:S(2)}, u32[]{:S(2)}) collective-permute-start(bf16[2,112,128]{2,1,0:T(8,128)(2,1)S(1)} %get-tuple-element.24), channel_id=1, source_target_pairs={{0,8},{1,9},{2,10},{3,11},{4,12},{5,13},{6,14},{7,15},{8,0},{9,1},... | collective-permute-start | bytes 172040 | tf_op jit(solution)/shard_map/ppermute | solution.py:294
  46.6 1.4 %collective-permute-start.6 = (bf16[2,112,128]{2,1,0:T(8,128)(2,1)S(1)}, bf16[2,112,128]{2,1,0:T(8,128)(2,1)S(1)}, u32[]{:S(2)}, u32[]{:S(2)}) collective-permute-start(bf16[2,112,128]{2,1,0:T(8,128)(2,1)S(1)} %get-tuple-element.25), channel_id=1, source_target_pairs={{0,10},{1,11},{2,8},{3,9},{4,14},{5,15},{6,12},{7,13},{8,2},{9,3},... | collective-permute-start | bytes 172040 | tf_op jit(solution)/shard_map/ppermute | solution.py:294
  48.0 3.8 %collective-permute-start.7 = (bf16[2,112,128]{2,1,0:T(8,128)(2,1)S(1)}, bf16[2,112,128]{2,1,0:T(8,128)(2,1)S(1)}, u32[]{:S(2)}, u32[]{:S(2)}) collective-permute-start(bf16[2,112,128]{2,1,0:T(8,128)(2,1)S(1)} %get-tuple-element.26), channel_id=1, source_target_pairs={{0,12},{1,13},{2,14},{3,15},{4,8},{5,9},{6,10},{7,11},{8,4},{9,5},... | collective-permute-start | bytes 172040 | tf_op jit(solution)/shard_map/ppermute | solution.py:294
  51.8 0.0 collective-permute-start.8
  51.8 0.0 collective-permute-done.5.refs_0_
  51.8 5.4 %collective-permute-done.6.refs_1_ = bf16[2,112,128]{2,1,0:T(8,128)(2,1)S(1)} collective-permute-done((bf16[2,112,128]{2,1,0:T(8,128)(2,1)S(1)}, bf16[2,112,128]{2,1,0:T(8,128)(2,1)S(1)}, u32[]{:S(2)}, u32[]{:S(2)}) %collective-permute-start.6) | collective-permute-done | bytes 57376 | tf_op jit(solution)/shard_map/ppermute | solution.py:294
  57.2 0.0 collective-permute-done.7.refs_2_
  57.2 1.5 %collective-permute-done.8.refs_3_ = bf16[2,112,128]{2,1,0:T(8,128)(2,1)S(1)} collective-permute-done((bf16[2,112,128]{2,1,0:T(8,128)(2,1)S(1)}, bf16[2,112,128]{2,1,0:T(8,128)(2,1)S(1)}, u32[]{:S(2)}, u32[]{:S(2)}) %collective-permute-start.8) | collective-permute-done | bytes 57376 | tf_op jit(solution)/shard_map/ppermute | solution.py:294
  58.8 0.0 all-to-all-done.1.refs_4_
  58.8 1.3 %unpack.1 = bf16[112,16,128]{2,1,0:T(8,128)(2,1)} custom-call(s32[1]{0:T(128)} %bitcast.me_ref, bf16[2,112,128]{2,1,0:T(8,128)(2,1)S(1)} %collective-permute-done.5.refs_0_, bf16[2,112,128]{2,1,0:T(8,128)(2,1)S(1)} %collective-permute-done.6.refs_1_, bf16[2,112,128]{2,1,0:T(8,128)(2,1)S(1)} %collective-permute-done.7.refs_2_, ...), custom_call_target="tpu_custom_call" | custom-call | tf_op jit(solution)/shard_map/unpack/pallas_call | solution.py:278
Async XLA Ops:
  4.2 5.4 %copy-start.3 = (bf16[4,112,128]{2,1,0:T(8,128)(2,1)S(1)}, bf16[4,112,128]{2,1,0:T(8,128)(2,1)}, u32[]{:S(2)}) copy-start(bf16[4,112,128]{2,1,0:T(8,128)(2,1)} %get-tuple-element.17) | copy-start | bytes 344068
  4.2 8.0 %copy-start.2 = (bf16[4,112,128]{2,1,0:T(8,128)(2,1)S(1)}, bf16[4,112,128]{2,1,0:T(8,128)(2,1)}, u32[]{:S(2)}) copy-start(bf16[4,112,128]{2,1,0:T(8,128)(2,1)} %get-tuple-element.18) | copy-start | bytes 344068
  4.2 9.8 %copy-start.1 = (bf16[4,112,128]{2,1,0:T(8,128)(2,1)S(1)}, bf16[4,112,128]{2,1,0:T(8,128)(2,1)}, u32[]{:S(2)}) copy-start(bf16[4,112,128]{2,1,0:T(8,128)(2,1)} %get-tuple-element.19) | copy-start | bytes 344068
  4.3 13.3 %copy-start = (bf16[4,112,128]{2,1,0:T(8,128)(2,1)S(1)}, bf16[4,112,128]{2,1,0:T(8,128)(2,1)}, u32[]{:S(2)}) copy-start(bf16[4,112,128]{2,1,0:T(8,128)(2,1)} %get-tuple-element.20) | copy-start | bytes 344068
  4.3 25.8 %all-to-all-start = ((bf16[4,4,112,128]{3,2,1,0:T(8,128)(2,1)}), bf16[4,4,112,128]{3,2,1,0:T(8,128)(2,1)S(1)}, u32[]{:S(2)}, u32[]{:S(2)}) async-start(bf16[4,4,112,128]{3,2,1,0:T(8,128)(2,1)} %get-tuple-element.21), calls=%async_computation | async-start | bytes 917504 | tf_op jit(solution)/shard_map/all_to_all | solution.py:296
  9.7 8.7 %collective-permute-start = (bf16[4,112,128]{2,1,0:T(8,128)(2,1)S(1)}, bf16[4,112,128]{2,1,0:T(8,128)(2,1)S(1)}, u32[]{:S(2)}, u32[]{:S(2)}) collective-permute-start(bf16[4,112,128]{2,1,0:T(8,128)(2,1)S(1)} %copy-done.3), channel_id=1, source_target_pairs={{0,8},{1,9},{2,10},{3,11},{4,12},{5,13},{6,14},{7,15},{8,0},{9,1},... | collective-permute-start | bytes 344072 | tf_op jit(solution)/shard_map/ppermute | solution.py:294
  12.3 17.8 %collective-permute-start.1 = (bf16[4,112,128]{2,1,0:T(8,128)(2,1)S(1)}, bf16[4,112,128]{2,1,0:T(8,128)(2,1)S(1)}, u32[]{:S(2)}, u32[]{:S(2)}) collective-permute-start(bf16[4,112,128]{2,1,0:T(8,128)(2,1)S(1)} %copy-done.2), channel_id=1, source_target_pairs={{0,10},{1,11},{2,8},{3,9},{4,14},{5,15},{6,12},{7,13},{8,2},{9,3},... | collective-permute-start | bytes 344072 | tf_op jit(solution)/shard_map/ppermute | solution.py:294
  14.1 16.0 %collective-permute-start.2 = (bf16[4,112,128]{2,1,0:T(8,128)(2,1)S(1)}, bf16[4,112,128]{2,1,0:T(8,128)(2,1)S(1)}, u32[]{:S(2)}, u32[]{:S(2)}) collective-permute-start(bf16[4,112,128]{2,1,0:T(8,128)(2,1)S(1)} %copy-done.1), channel_id=1, source_target_pairs={{0,12},{1,13},{2,14},{3,15},{4,8},{5,9},{6,10},{7,11},{8,4},{9,5},... | collective-permute-start | bytes 344072 | tf_op jit(solution)/shard_map/ppermute | solution.py:294
  17.6 12.5 %collective-permute-start.3 = (bf16[4,112,128]{2,1,0:T(8,128)(2,1)S(1)}, bf16[4,112,128]{2,1,0:T(8,128)(2,1)S(1)}, u32[]{:S(2)}, u32[]{:S(2)}) collective-permute-start(bf16[4,112,128]{2,1,0:T(8,128)(2,1)S(1)} %copy-done), channel_id=1, source_target_pairs={{0,14},{1,15},{2,12},{3,13},{4,10},{5,11},{6,8},{7,9},{8,6},{9,7},... | collective-permute-start | bytes 344072 | tf_op jit(solution)/shard_map/ppermute | solution.py:294
  30.1 1.9 %collective-permute-start.4 = (bf16[8,2,112,128]{3,2,1,0:T(8,128)(2,1)S(1)}, bf16[8,2,112,128]{3,2,1,0:T(8,128)(2,1)S(1)}, u32[]{:S(2)}, u32[]{:S(2)}) collective-permute-start(bf16[8,2,112,128]{3,2,1,0:T(8,128)(2,1)S(1)} %get-tuple-element.23.own_ref), channel_id=1, source_target_pairs={{0,1},{1,0},{2,3},{3,2},{4,5},{5,4},{6,7},{7,6},{8,9},{9,8},{10,11... | collective-permute-start | bytes 1376264 | tf_op jit(solution)/shard_map/ppermute | solution.py:329
  37.0 21.8 %all-to-all-start.1 = ((bf16[4,2,112,128]{3,2,1,0:T(8,128)(2,1)}), bf16[4,2,112,128]{3,2,1,0:T(8,128)(2,1)S(1)}, u32[]{:S(2)}, u32[]{:S(2)}) async-start(bf16[4,2,112,128]{3,2,1,0:T(8,128)(2,1)} %get-tuple-element.28), calls=%async_computation.1 | async-start | bytes 458752 | tf_op jit(solution)/shard_map/all_to_all | solution.py:296
  43.1 8.7 %collective-permute-start.5 = (bf16[2,112,128]{2,1,0:T(8,128)(2,1)S(1)}, bf16[2,112,128]{2,1,0:T(8,128)(2,1)S(1)}, u32[]{:S(2)}, u32[]{:S(2)}) collective-permute-start(bf16[2,112,128]{2,1,0:T(8,128)(2,1)S(1)} %get-tuple-element.24), channel_id=1, source_target_pairs={{0,8},{1,9},{2,10},{3,11},{4,12},{5,13},{6,14},{7,15},{8,0},{9,1},... | collective-permute-start | bytes 172040 | tf_op jit(solution)/shard_map/ppermute | solution.py:294
  46.6 10.6 %collective-permute-start.6 = (bf16[2,112,128]{2,1,0:T(8,128)(2,1)S(1)}, bf16[2,112,128]{2,1,0:T(8,128)(2,1)S(1)}, u32[]{:S(2)}, u32[]{:S(2)}) collective-permute-start(bf16[2,112,128]{2,1,0:T(8,128)(2,1)S(1)} %get-tuple-element.25), channel_id=1, source_target_pairs={{0,10},{1,11},{2,8},{3,9},{4,14},{5,15},{6,12},{7,13},{8,2},{9,3},... | collective-permute-start | bytes 172040 | tf_op jit(solution)/shard_map/ppermute | solution.py:294
  48.0 9.3 %collective-permute-start.7 = (bf16[2,112,128]{2,1,0:T(8,128)(2,1)S(1)}, bf16[2,112,128]{2,1,0:T(8,128)(2,1)S(1)}, u32[]{:S(2)}, u32[]{:S(2)}) collective-permute-start(bf16[2,112,128]{2,1,0:T(8,128)(2,1)S(1)} %get-tuple-element.26), channel_id=1, source_target_pairs={{0,12},{1,13},{2,14},{3,15},{4,8},{5,9},{6,10},{7,11},{8,4},{9,5},... | collective-permute-start | bytes 172040 | tf_op jit(solution)/shard_map/ppermute | solution.py:294
  51.8 7.0 %collective-permute-start.8 = (bf16[2,112,128]{2,1,0:T(8,128)(2,1)S(1)}, bf16[2,112,128]{2,1,0:T(8,128)(2,1)S(1)}, u32[]{:S(2)}, u32[]{:S(2)}) collective-permute-start(bf16[2,112,128]{2,1,0:T(8,128)(2,1)S(1)} %get-tuple-element.27), channel_id=1, source_target_pairs={{0,14},{1,15},{2,12},{3,13},{4,10},{5,11},{6,8},{7,9},{8,6},{9,7},... | collective-permute-start | bytes 172040 | tf_op jit(solution)/shard_map/ppermute | solution.py:294

commit v6 on v5

--- a/solution.py
+++ b/solution.py
@@ -163,15 +163,12 @@
 
 
 def send_kernel(me_ref, q_hbm, k_hbm, v_hbm, table_hbm, query_gain_ref, key_gain_ref, *refs):
-    outs, (q_ref, k_ref, v_ref, table_ref, qf_ref, kf_ref, vf_ref, sems) = refs[:-8], refs[-8:]
+    pairs, (near_ref, q_ref, k_ref, v_ref, table_ref, qf_ref, kf_ref, vf_ref, sems) = refs[:-9], refs[-9:]
     tokens, heads, width = q_ref.shape
     kv_heads = k_ref.shape[1]
-    crossing, near_ref = outs[:-1], outs[-1]
-    half = len(crossing)
-    per_chip = near_ref.shape[1] - 2
+    group = heads // kv_heads
     me = me_ref[0]
-    chip = me // 2
-    base = chip // half * half
+    chip, core = lax.rem(me // 2, len(pairs)), lax.rem(me, 2)
     start = pl.multiple_of(me * tokens, 8)
     copies = [
         pltpu.make_async_copy(k_hbm, k_ref, sems.at[0]),
@@ -181,96 +178,114 @@
     ]
     for copy in copies:
         copy.start()
-    targets = [(chip ^ (half + step), ref) for step, ref in enumerate(crossing)]
-    targets += [(base + place, near_ref.at[place]) for place in range(half)]
     copies[0].wait()
     kf_ref[...] = normalize(k_ref[...].reshape(tokens * kv_heads, width))
     copies[1].wait()
     cosine, sine = rope_factors(table_ref[...])
     copies[2].wait()
     vf_ref[...] = v_ref[...].astype(jnp.float32).reshape(tokens * kv_heads, width)
-    for target, ref in targets:
-        rows = pl.ds(target, tokens, stride=kv_heads)
-        ref[per_chip] = turn(kf_ref[rows, :], key_gain_ref[...], cosine, sine)
-        ref[per_chip + 1] = vf_ref[rows, :].astype(jnp.bfloat16)
+    for step, pair in enumerate(pairs):
+        for side in range(2):
+            head = (chip ^ step) * 2 + lax.rem(core + side, 2)
+            keys = turn(kf_ref[pl.ds(head, tokens, stride=kv_heads), :], key_gain_ref[...], cosine, sine)
+            values = vf_ref[pl.ds(head, tokens, stride=kv_heads), :].astype(jnp.bfloat16)
+            pair[side, 0] = keys
+            near_ref[head, group] = keys
+            pair[side, 1] = values
+            near_ref[head, group + 1] = values
     copies[3].wait()
     qf_ref[...] = normalize(q_ref[...].reshape(tokens * heads, width))
-    for target, ref in targets:
-        for row in range(per_chip):
-            normed = qf_ref[pl.ds(target * per_chip + row, tokens, stride=heads), :]
-            ref[row] = turn(normed, query_gain_ref[...], cosine, sine)
-
-
-def order_kernel(me_ref, *refs):
-    crossed, (near_ref, query_ref, pair_ref) = refs[:-3], refs[-3:]
-    half, per_chip = len(crossed), query_ref.shape[1]
-    chip = me_ref[0] // 2
-    base = chip // half * half
-    sources = [(chip ^ (half + step), ref) for step, ref in enumerate(crossed)]
-    sources += [(base + place, near_ref.at[place]) for place in range(half)]
-    for source, ref in sources:
-        query_ref[source] = ref[:per_chip]
-        pair_ref[source] = ref[per_chip:]
-
-
-def attention_kernel(me_ref, q_ref, own_ref, other_ref, *refs):
-    outs, out_ref = refs[:-1], refs[-1]
-    crossing, near_ref = outs[:-1], outs[-1]
-    blocks, per_chip, tokens, width = q_ref.shape
-    chip, core = me_ref[0] // 2, lax.rem(me_ref[0], 2)
+    for head in range(heads):
+        normed = qf_ref[pl.ds(head, tokens, stride=heads), :]
+        near_ref[head // group, head % group] = turn(normed, query_gain_ref[...], cosine, sine)
+
+
+def near_kernel(x_ref, highest_ref, total_ref, weighted_ref):
+    blocks, rows, tokens, width = x_ref.shape
+    group = rows - 2
     scale = math.log2(math.e) / math.sqrt(width)
-    keys_own, values_own, keys_other, values_other = [
-        ref[:, i].reshape(blocks * tokens, width) for ref in (own_ref, other_ref) for i in range(2)
-    ]
-    rows = per_chip * tokens
+    keys = x_ref[:, group].reshape(blocks * tokens, width)
+    values = x_ref[:, group + 1].reshape(blocks * tokens, width)
     for block in range(blocks):
-        queries = q_ref[block].reshape(rows, width)
+        queries = x_ref[block, :group].reshape(group * tokens, width)
         reach = (block + 1) * tokens
-        own = lax.dot_general(queries, keys_own[:reach], CONTRACT, preferred_element_type=jnp.float32)
-        other = lax.dot_general(queries, keys_other[:reach], CONTRACT, preferred_element_type=jnp.float32)
-        row = lax.broadcasted_iota(jnp.int32, (per_chip, tokens, reach), 1).reshape(rows, reach)
-        column = lax.broadcasted_iota(jnp.int32, (rows, reach), 1)
-        own = jnp.where(column <= row + block * tokens, own, MASKED)
-        other = jnp.where(column < (block + core) * tokens, other, MASKED)
-        highest = jnp.maximum(
-            jnp.max(own, axis=-1, keepdims=True), jnp.max(other, axis=-1, keepdims=True)
+        scores = lax.dot_general(queries, keys[:reach], CONTRACT, preferred_element_type=jnp.float32)
+        row = lax.broadcasted_iota(jnp.int32, (group, tokens, reach), 1).reshape(group * tokens, reach)
+        column = lax.broadcasted_iota(jnp.int32, (group * tokens, reach), 1)
+        scores = jnp.where(column <= row + block * tokens, scores, MASKED)
+        highest = jnp.max(scores, axis=-1, keepdims=True)
+        probs = jnp.exp2((scores - highest) * scale)
+        highest_ref[block] = highest
+        total_ref[block] = jnp.sum(probs, axis=-1, keepdims=True)
+        weighted_ref[block] = jnp.dot(
+            probs.astype(jnp.bfloat16), values[:reach], preferred_element_type=jnp.float32
         )
-        probs_own = jnp.exp2((own - highest) * scale)
-        probs_other = jnp.exp2((other - highest) * scale)
-        total = jnp.sum(probs_own, axis=-1, keepdims=True) + jnp.sum(probs_other, axis=-1, keepdims=True)
-        summed = jnp.dot(
-            probs_own.astype(jnp.bfloat16), values_own[:reach], preferred_element_type=jnp.float32
-        ) + jnp.dot(
-            probs_other.astype(jnp.bfloat16), values_other[:reach], preferred_element_type=jnp.float32
-        )
-        out_ref[block] = (summed / total).astype(jnp.bfloat16).reshape(per_chip, tokens, width)
-    half = len(crossing)
-    base = chip // half * half
-    for step, ref in enumerate(crossing):
-        ref[...] = out_ref[chip ^ (half + step)]
-    near_ref[...] = out_ref[pl.ds(base, half)]
-
-
-def unpack_kernel(me_ref, *refs):
-    crossed, (near_ref, out_ref, floats_ref) = refs[:-3], refs[-3:]
-    tokens, heads, width = out_ref.shape
-    half, per_chip = len(crossed), near_ref.shape[1]
-    chip = me_ref[0] // 2
-    base = chip // half * half
-    sources = [(base + place, near_ref.at[place]) for place in range(half)]
-    sources += [(chip ^ (half + step), ref) for step, ref in enumerate(crossed)]
-    for source, ref in sources:
-        for row in range(per_chip):
-            floats_ref[pl.ds(source * per_chip + row, tokens, stride=heads), :] = ref[row].astype(jnp.float32)
-    out_ref[...] = floats_ref[...].reshape(tokens, heads, width).astype(jnp.bfloat16)
-
-
-def short_plan(length, devices, query_states, key_states, value_states, query_gain, key_gain):
+
+
+def split_kernel(*refs):
+    for step, ref in enumerate(refs[:-2]):
+        for side in range(2):
+            refs[side - 2][step] = ref[side]
+
+
+def add_far(x_ref, state, pairs_ref, store):
+    steps, _, tokens, width = pairs_ref.shape
+    group = x_ref.shape[1] - 2
+    scale = math.log2(math.e) / math.sqrt(width)
+    highest_ref, total_ref, weighted_ref = state
+    keys = pairs_ref[:, 0].reshape(steps * tokens, width)
+    values = pairs_ref[:, 1].reshape(steps * tokens, width)
+    for block in range(x_ref.shape[0]):
+        queries = x_ref[block, :group].reshape(group * tokens, width)
+        scores = lax.dot_general(queries, keys, CONTRACT, preferred_element_type=jnp.float32)
+        before = highest_ref[block]
+        highest = jnp.maximum(before, jnp.max(scores, axis=-1, keepdims=True))
+        probs = jnp.exp2((scores - highest) * scale)
+        factor = jnp.exp2((before - highest) * scale)
+        total = total_ref[block] * factor + jnp.sum(probs, axis=-1, keepdims=True)
+        summed = jnp.dot(probs.astype(jnp.bfloat16), values, preferred_element_type=jnp.float32)
+        store(block, highest, total, weighted_ref[block] * factor + summed)
+
+
+def far_kernel(half, me_ref, x_ref, pairs_ref, *refs):
+    state, outs = refs[:3], refs[3:]
+
+    def store(block, *values):
+        for ref, value in zip(outs, values):
+            ref[block] = value
+
+    @pl.when(me_ref[0] >= half)
+    def _():
+        add_far(x_ref, state, pairs_ref, store)
+
+    @pl.when(me_ref[0] < half)
+    def _():
+        for ref, before in zip(outs, state):
+            ref[...] = before[...]
+
+
+def last_kernel(half, me_ref, x_ref, pairs_ref, *refs):
+    state, out_ref = refs[:3], refs[3]
+
+    def store(block, highest, total, weighted):
+        out_ref[block] = (weighted / total).astype(jnp.bfloat16).reshape(out_ref.shape[1:])
+
+    @pl.when(me_ref[0] >= half)
+    def _():
+        add_far(x_ref, state, pairs_ref, store)
+
+    @pl.when(me_ref[0] < half)
+    def _():
+        for block in range(out_ref.shape[0]):
+            store(block, None, state[1][block], state[2][block])
+
+
+def halves_plan(length, devices, query_states, key_states, value_states, query_gain, key_gain):
     tokens, heads, width = query_states.shape
     kv_heads = key_states.shape[1]
-    chips = devices // 2
-    half = chips // 2
-    per_chip = heads // chips
+    group = heads // kv_heads
+    half = devices // 2
+    steps = half // 2
     bf16, f32 = jnp.bfloat16, jnp.float32
     me = lax.axis_index("seq")[None]
 
@@ -283,24 +298,20 @@
             scratch_shapes=scratch,
             compiler_params=pltpu.CompilerParams(vmem_limit_bytes=limit),
             name=name,
-        )(me, *operands)
-
-    def exchange(crossing, near):
-        links = [
-            [(device, ((device // 2) ^ (half + step)) * 2 + device % 2) for device in range(devices)]
-            for step in range(half)
-        ]
-        groups = [[(base + place) * 2 + core for place in range(half)] for base in (0, half) for core in range(2)]
-        crossed = [lax.ppermute(array, "seq", links[step]) for step, array in enumerate(crossing)]
-        return crossed + [
-            lax.all_to_all(near, "seq", split_axis=0, concat_axis=0, axis_index_groups=groups, tiled=True)
-        ]
+        )(*([me] if specs is None or SMEM in specs else []), *operands)
+
+    def to_upper(step, array):
+        links = [(device, half + ((device // 2) ^ step) * 2 + device % 2) for device in range(half)]
+        return lax.ppermute(array, "seq", links)
+
+    def to_core(array, lowest):
+        return lax.ppermute(array, "seq", [(device, device ^ 1) for device in range(lowest, devices)])
 
     shape = jax.ShapeDtypeStruct
-    *crossing, near = call(
+    *pairs, near = call(
         send_kernel,
         "send",
-        [shape((per_chip + 2, tokens, width), bf16)] * half + [shape((half, per_chip + 2, tokens, width), bf16)],
+        [shape((2, 2, tokens, width), bf16)] * steps + [shape((half, group + 2, tokens, width), bf16)],
         query_states,
         key_states,
         value_states,
@@ -320,29 +331,31 @@
         ],
         limit=PACK_VMEM,
     )
-    queries, own = call(
-        order_kernel,
-        "order",
-        [shape((chips, per_chip, tokens, width), bf16), shape((chips, 2, tokens, width), bf16)],
-        *exchange(crossing, near),
-    )
-    other = lax.ppermute(own, "seq", [(device, device ^ 1) for device in range(devices)])
-    *crossing, near = call(
-        attention_kernel,
-        "attention",
-        [shape((per_chip, tokens, width), bf16)] * half + [shape((half, per_chip, tokens, width), bf16)],
-        queries,
-        own,
-        other,
-        scratch=[pltpu.VMEM((chips, per_chip, tokens, width), bf16)],
-    )
-    return call(
-        unpack_kernel,
-        "unpack",
-        shape((tokens, heads, width), bf16),
-        *exchange(crossing, near),
-        scratch=[pltpu.VMEM((tokens * heads, width), f32)],
-    )
+    groups = [list(range(half)), list(range(half, devices))]
+
+    def inside(array):
+        return lax.all_to_all(array, "seq", split_axis=0, concat_axis=0, axis_index_groups=groups, tiled=True)
+
+    far = [to_upper(step, pair) for step, pair in enumerate(pairs)]
+    arrived = inside(near)
+    rows = group * tokens
+    state = [shape((half, rows, 1), f32), shape((half, rows, 1), f32), shape((half, rows, width), f32)]
+    carried = call(near_kernel, "near", state, arrived, specs=[VMEM])
+    carried, far = lax.optimization_barrier((carried, far))
+    mine, others = call(
+        split_kernel, "split", [shape((steps, 2, tokens, width), bf16)] * 2, *far, specs=[VMEM] * steps
+    )
+    neighbours = to_core(others, half)
+    carried = call(functools.partial(far_kernel, half), "far", state, arrived, mine, *carried)
+    attended = call(
+        functools.partial(last_kernel, half),
+        "last",
+        shape((half, group, tokens, width), bf16),
+        arrived,
+        neighbours,
+        *carried,
+    )
+    return jnp.transpose(inside(attended).reshape(heads, tokens, width), (1, 0, 2))
 
 
 def solution(mesh):
@@ -352,7 +365,7 @@
 
     def run(query_states, key_states, value_states, query_gain, key_gain):
         length = query_states.shape[0] // groups
-        plan = short_plan if devices == 2 * key_states.shape[1] else general_plan
+        plan = halves_plan if devices == 2 * key_states.shape[1] else general_plan
         return jax.shard_map(
             functools.partial(plan, length, devices),
             mesh=mesh,

time: 60.4 us -> 55.6 us (0.921)
  the two profiles are of different devices: /device:TPU:0 before, /device:TPU:16 now
where the time goes in v6:
time: 55.6 us; the launch traced here: 55.2 us
  waiting for transfers between devices  18.6 us (33%)
  Pallas kernels  13.7 us (25%)
  starting transfers between devices  11 us (20%)
  blocking collectives  10.9 us (20%)
  local copies, waits for them, and re-layouts  0.9 us (2%)
    pallas_call x5, Pallas kernels, call(): pl.pallas_call(kernel, out_shape=outs, in_specs=specs or [SMEM] + [VMEM]...  13.7 us
    all_to_all x1, waiting for transfers between devices, inside(): lax.all_to_all(array, 'seq', split_axis=0, concat_axis=0, axis_index_grou...  11 us
    all_to_all x1, blocking collectives, inside(): lax.all_to_all(array, 'seq', split_axis=0, concat_axis=0, axis_index_grou...  10.9 us
    ppermute x4, waiting for transfers between devices, to_upper(): return lax.ppermute(array, 'seq', links)  7.53 us
    ppermute x4, starting transfers between devices, to_upper(): return lax.ppermute(array, 'seq', links)  5.17 us
    all_to_all x1, starting transfers between devices, inside(): lax.all_to_all(array, 'seq', split_axis=0, concat_axis=0, axis_index_grou...  3.95 us
    ppermute x1, starting transfers between devices, to_core(): lax.ppermute(array, 'seq', [(device, device ^ 1) for device in range(lowe...  1.92 us
  transfers between devices with their start and end apart: 6, of which 3 were waited for; matrix products, arithmetic and copies ran while one was open for 0% of the time, Pallas kernels for 12%

profile of v6, /device:TPU:16, one launch (start us, length us, event | category | flops | bytes accessed | tf_op | source)
XLA Modules:
  0.0 55.2 jit_solution(202056500919627908)
XLA Ops:
  0.0 4.2 %send.1 = (bf16[2,2,112,128]{3,2,1,0:T(8,128)(2,1)}, bf16[2,2,112,128]{3,2,1,0:T(8,128)(2,1)}, bf16[2,2,112,128]{3,2,1,0:T(8,128)(2,1)}, bf16[2,2,112,128]{3,2,1,0:T(8,128)(2,1)}, bf16[8,4,112,128]{3,2,1,0:T(8,128)(2,1)}) custom-call(s32[1]{0:T(128)} %bitcast.me_ref, bf16[112,16,128]{2,1,0:T(8,128)(2,1)} %q_hbm.1, bf16[112,8,128]{2,1,0:T(8,128)(2,1)} %k_hbm.1, ...), custom_call_target="tpu_custom_call" | custom-call | tf_op jit(solution)/shard_map/send/pallas_call | solution.py:293
  4.2 0.0 copy-start.3
  4.2 0.0 copy-start.2
  4.2 0.0 copy-start.1
  4.2 0.0 copy-start
  4.2 4.0 %all-to-all-start = ((bf16[8,4,112,128]{3,2,1,0:T(8,128)(2,1)}), bf16[8,4,112,128]{3,2,1,0:T(8,128)(2,1)S(1)}, u32[]{:S(2)}, u32[]{:S(2)}) async-start(bf16[8,4,112,128]{3,2,1,0:T(8,128)(2,1)} %get-tuple-element.25), calls=%async_computation | async-start | bytes 1835008 | tf_op jit(solution)/shard_map/all_to_all | solution.py:337
  8.2 0.0 copy-done.3
  8.2 1.3 %collective-permute-start = (bf16[2,2,112,128]{3,2,1,0:T(8,128)(2,1)S(1)}, bf16[2,2,112,128]{3,2,1,0:T(8,128)(2,1)S(1)}, u32[]{:S(2)}, u32[]{:S(2)}) collective-permute-start(bf16[2,2,112,128]{3,2,1,0:T(8,128)(2,1)S(1)} %copy-done.3), channel_id=1, source_target_pairs={{0,8},{1,9},{2,10},{3,11},{4,12},{5,13},{6,14},{7,15},{16,24},{17,... | collective-permute-start | bytes 344072 | tf_op jit(solution)/shard_map/ppermute | solution.py:305
  9.5 0.0 copy-done.2
  9.5 1.3 %collective-permute-start.1 = (bf16[2,2,112,128]{3,2,1,0:T(8,128)(2,1)S(1)}, bf16[2,2,112,128]{3,2,1,0:T(8,128)(2,1)S(1)}, u32[]{:S(2)}, u32[]{:S(2)}) collective-permute-start(bf16[2,2,112,128]{3,2,1,0:T(8,128)(2,1)S(1)} %copy-done.2), channel_id=1, source_target_pairs={{0,10},{1,11},{2,8},{3,9},{4,14},{5,15},{6,12},{7,13},{16,26},{17,... | collective-permute-start | bytes 344072 | tf_op jit(solution)/shard_map/ppermute | solution.py:305
  10.8 0.0 copy-done.1
  10.8 1.3 %collective-permute-start.2 = (bf16[2,2,112,128]{3,2,1,0:T(8,128)(2,1)S(1)}, bf16[2,2,112,128]{3,2,1,0:T(8,128)(2,1)S(1)}, u32[]{:S(2)}, u32[]{:S(2)}) collective-permute-start(bf16[2,2,112,128]{3,2,1,0:T(8,128)(2,1)S(1)} %copy-done.1), channel_id=1, source_target_pairs={{0,12},{1,13},{2,14},{3,15},{4,8},{5,9},{6,10},{7,11},{16,28},{17,... | collective-permute-start | bytes 344072 | tf_op jit(solution)/shard_map/ppermute | solution.py:305
  12.1 0.0 copy-done
  12.1 1.3 %collective-permute-start.3 = (bf16[2,2,112,128]{3,2,1,0:T(8,128)(2,1)S(1)}, bf16[2,2,112,128]{3,2,1,0:T(8,128)(2,1)S(1)}, u32[]{:S(2)}, u32[]{:S(2)}) collective-permute-start(bf16[2,2,112,128]{3,2,1,0:T(8,128)(2,1)S(1)} %copy-done), channel_id=1, source_target_pairs={{0,14},{1,15},{2,12},{3,13},{4,10},{5,11},{6,8},{7,9},{16,30},{17,... | collective-permute-start | bytes 344072 | tf_op jit(solution)/shard_map/ppermute | solution.py:305
  13.4 11.0 %all-to-all-done.x_ref = bf16[8,4,112,128]{3,2,1,0:T(8,128)(2,1)S(1)} async-done(((bf16[8,4,112,128]{3,2,1,0:T(8,128)(2,1)}), bf16[8,4,112,128]{3,2,1,0:T(8,128)(2,1)S(1)}, u32[]{:S(2)}, u32[]{:S(2)}) %all-to-all-start) | async-done | bytes 917536 | tf_op jit(solution)/shard_map/all_to_all | solution.py:337
  24.4 2.9 %near.1 = (f32[8,224,1]{2,1,0:T(8,128)S(1)}, f32[8,224,1]{2,1,0:T(8,128)S(1)}, f32[8,224,128]{2,1,0:T(8,128)S(1)}) custom-call(bf16[8,4,112,128]{3,2,1,0:T(8,128)(2,1)S(1)} %all-to-all-done.x_ref), custom_call_target="tpu_custom_call" | custom-call | tf_op jit(solution)/shard_map/near/pallas_call | solution.py:293
  27.3 0.0 collective-permute-done.refs_0_
  27.3 0.0 collective-permute-done.1.refs_1_
  27.3 4.7 %collective-permute-done.2.refs_2_ = bf16[2,2,112,128]{3,2,1,0:T(8,128)(2,1)S(1)} collective-permute-done((bf16[2,2,112,128]{3,2,1,0:T(8,128)(2,1)S(1)}, bf16[2,2,112,128]{3,2,1,0:T(8,128)(2,1)S(1)}, u32[]{:S(2)}, u32[]{:S(2)}) %collective-permute-start.2) | collective-permute-done | bytes 114720 | tf_op jit(solution)/shard_map/ppermute | solution.py:305
  32.0 2.9 %collective-permute-done.3.refs_3_ = bf16[2,2,112,128]{3,2,1,0:T(8,128)(2,1)S(1)} collective-permute-done((bf16[2,2,112,128]{3,2,1,0:T(8,128)(2,1)S(1)}, bf16[2,2,112,128]{3,2,1,0:T(8,128)(2,1)S(1)}, u32[]{:S(2)}, u32[]{:S(2)}) %collective-permute-start.3) | collective-permute-done | bytes 114720 | tf_op jit(solution)/shard_map/ppermute | solution.py:305
  34.9 1.9 %collective-permute-start.4 = (bf16[4,2,112,128]{3,2,1,0:T(8,128)(2,1)S(1)}, bf16[4,2,112,128]{3,2,1,0:T(8,128)(2,1)S(1)}, u32[]{:S(2)}, u32[]{:S(2)}) collective-permute-start(bf16[4,2,112,128]{3,2,1,0:T(8,128)(2,1)S(1)} %get-tuple-element.37), channel_id=1, source_target_pairs={{8,9},{9,8},{10,11},{11,10},{12,13},{13,12},{14,15},{15,14},{24,25... | collective-permute-start | bytes 688136 | tf_op jit(solution)/shard_map/ppermute | solution.py:308
  36.8 3.5 %far.1 = (f32[8,224,1]{2,1,0:T(8,128)S(1)}, f32[8,224,1]{2,1,0:T(8,128)S(1)}, f32[8,224,128]{2,1,0:T(8,128)S(1)}) custom-call(s32[1]{0:T(128)} %bitcast.me_ref, bf16[8,4,112,128]{3,2,1,0:T(8,128)(2,1)S(1)} %all-to-all-done.x_ref, bf16[4,2,112,128]{3,2,1,0:T(8,128)(2,1)S(1)} %get-tuple-element.38.pairs_ref, f32[8,224,1]{2,1,0:T(8,128)S(1)} %get-tuple-element.39.refs_0_, ...), custom_call_target="tpu_custom_call" | custom-call | tf_op jit(solution)/shard_map/far/pallas_call | solution.py:293
  40.3 0.0 collective-permute-done.4.pairs_ref
  40.3 3.1 %last.1 = bf16[8,2,112,128]{3,2,1,0:T(8,128)(2,1)S(1)} custom-call(s32[1]{0:T(128)} %bitcast.me_ref, bf16[8,4,112,128]{3,2,1,0:T(8,128)(2,1)S(1)} %all-to-all-done.x_ref, bf16[4,2,112,128]{3,2,1,0:T(8,128)(2,1)S(1)} %collective-permute-done.4.pairs_ref, f32[8,224,1]{2,1,0:T(8,128)S(1)} %get-tuple-element.42.refs_0_, ...), custom_call_target="tpu_custom_call" | custom-call | tf_op jit(solution)/shard_map/last/pallas_call | solution.py:293
  43.4 10.9 %all_to_all.10 = bf16[8,2,112,128]{3,2,1,0:T(8,128)(2,1)S(1)} all-to-all(bf16[8,2,112,128]{3,2,1,0:T(8,128)(2,1)S(1)} %last.1), channel_id=1, replica_groups={{0,1,2,3,4,5,6,7},{8,9,10,11,12,13,14,15},{16,17,18,19,20,21,22,23},{24..., dimensions={0} | all-to-all | bytes 917504 | tf_op jit(solution)/shard_map/all_to_all | solution.py:337
  54.4 0.9 %copy.9 = bf16[16,112,128]{2,0,1:T(8,128)(2,1)} copy(bf16[16,112,128]{2,1,0:T(8,128)(2,1)S(1)} %bitcast.7) | data formatting | bytes 917504 | tf_op jit(solution)/shard_map/reshape | solution.py:358
  (1 shorter events, 0.0 us)
Async XLA Ops:
  4.2 4.0 %copy-start.3 = (bf16[2,2,112,128]{3,2,1,0:T(8,128)(2,1)S(1)}, bf16[2,2,112,128]{3,2,1,0:T(8,128)(2,1)}, u32[]{:S(2)}) copy-start(bf16[2,2,112,128]{3,2,1,0:T(8,128)(2,1)} %get-tuple-element.29) | copy-start | bytes 344068
  4.2 5.3 %copy-start.2 = (bf16[2,2,112,128]{3,2,1,0:T(8,128)(2,1)S(1)}, bf16[2,2,112,128]{3,2,1,0:T(8,128)(2,1)}, u32[]{:S(2)}) copy-start(bf16[2,2,112,128]{3,2,1,0:T(8,128)(2,1)} %get-tuple-element.30) | copy-start | bytes 344068
  4.2 6.6 %copy-start.1 = (bf16[2,2,112,128]{3,2,1,0:T(8,128)(2,1)S(1)}, bf16[2,2,112,128]{3,2,1,0:T(8,128)(2,1)}, u32[]{:S(2)}) copy-start(bf16[2,2,112,128]{3,2,1,0:T(8,128)(2,1)} %get-tuple-element.31) | copy-start | bytes 344068
  4.2 7.9 %copy-start = (bf16[2,2,112,128]{3,2,1,0:T(8,128)(2,1)S(1)}, bf16[2,2,112,128]{3,2,1,0:T(8,128)(2,1)}, u32[]{:S(2)}) copy-start(bf16[2,2,112,128]{3,2,1,0:T(8,128)(2,1)} %get-tuple-element.32) | copy-start | bytes 344068
  4.2 20.2 %all-to-all-start = ((bf16[8,4,112,128]{3,2,1,0:T(8,128)(2,1)}), bf16[8,4,112,128]{3,2,1,0:T(8,128)(2,1)S(1)}, u32[]{:S(2)}, u32[]{:S(2)}) async-start(bf16[8,4,112,128]{3,2,1,0:T(8,128)(2,1)} %get-tuple-element.25), calls=%async_computation | async-start | bytes 1835008 | tf_op jit(solution)/shard_map/all_to_all | solution.py:337
  8.2 19.1 %collective-permute-start = (bf16[2,2,112,128]{3,2,1,0:T(8,128)(2,1)S(1)}, bf16[2,2,112,128]{3,2,1,0:T(8,128)(2,1)S(1)}, u32[]{:S(2)}, u32[]{:S(2)}) collective-permute-start(bf16[2,2,112,128]{3,2,1,0:T(8,128)(2,1)S(1)} %copy-done.3), channel_id=1, source_target_pairs={{0,8},{1,9},{2,10},{3,11},{4,12},{5,13},{6,14},{7,15},{16,24},{17,... | collective-permute-start | bytes 344072 | tf_op jit(solution)/shard_map/ppermute | solution.py:305
  9.5 17.8 %collective-permute-start.1 = (bf16[2,2,112,128]{3,2,1,0:T(8,128)(2,1)S(1)}, bf16[2,2,112,128]{3,2,1,0:T(8,128)(2,1)S(1)}, u32[]{:S(2)}, u32[]{:S(2)}) collective-permute-start(bf16[2,2,112,128]{3,2,1,0:T(8,128)(2,1)S(1)} %copy-done.2), channel_id=1, source_target_pairs={{0,10},{1,11},{2,8},{3,9},{4,14},{5,15},{6,12},{7,13},{16,26},{17,... | collective-permute-start | bytes 344072 | tf_op jit(solution)/shard_map/ppermute | solution.py:305
  10.8 21.2 %collective-permute-start.2 = (bf16[2,2,112,128]{3,2,1,0:T(8,128)(2,1)S(1)}, bf16[2,2,112,128]{3,2,1,0:T(8,128)(2,1)S(1)}, u32[]{:S(2)}, u32[]{:S(2)}) collective-permute-start(bf16[2,2,112,128]{3,2,1,0:T(8,128)(2,1)S(1)} %copy-done.1), channel_id=1, source_target_pairs={{0,12},{1,13},{2,14},{3,15},{4,8},{5,9},{6,10},{7,11},{16,28},{17,... | collective-permute-start | bytes 344072 | tf_op jit(solution)/shard_map/ppermute | solution.py:305
  12.1 22.8 %collective-permute-start.3 = (bf16[2,2,112,128]{3,2,1,0:T(8,128)(2,1)S(1)}, bf16[2,2,112,128]{3,2,1,0:T(8,128)(2,1)S(1)}, u32[]{:S(2)}, u32[]{:S(2)}) collective-permute-start(bf16[2,2,112,128]{3,2,1,0:T(8,128)(2,1)S(1)} %copy-done), channel_id=1, source_target_pairs={{0,14},{1,15},{2,12},{3,13},{4,10},{5,11},{6,8},{7,9},{16,30},{17,... | collective-permute-start | bytes 344072 | tf_op jit(solution)/shard_map/ppermute | solution.py:305
  34.9 5.4 %collective-permute-start.4 = (bf16[4,2,112,128]{3,2,1,0:T(8,128)(2,1)S(1)}, bf16[4,2,112,128]{3,2,1,0:T(8,128)(2,1)S(1)}, u32[]{:S(2)}, u32[]{:S(2)}) collective-permute-start(bf16[4,2,112,128]{3,2,1,0:T(8,128)(2,1)S(1)} %get-tuple-element.37), channel_id=1, source_target_pairs={{8,9},{9,8},{10,11},{11,10},{12,13},{13,12},{14,15},{15,14},{24,25... | collective-permute-start | bytes 688136 | tf_op jit(solution)/shard_map/ppermute | solution.py:308

commit v7 on v6

--- a/solution.py
+++ b/solution.py
@@ -17,6 +17,8 @@
 VMEM = pl.BlockSpec(memory_space=pltpu.VMEM)
 SMEM = pl.BlockSpec(memory_space=pltpu.SMEM)
 HBM = pl.BlockSpec(memory_space=pltpu.HBM)
+NEAR_BLOCKS = 2
+FAR_BLOCKS = 2
 CONTRACT = (((1,), (1,)), ((), ()))
 
 
@@ -200,26 +202,40 @@
         near_ref[head // group, head % group] = turn(normed, query_gain_ref[...], cosine, sine)
 
 
-def near_kernel(x_ref, highest_ref, total_ref, weighted_ref):
+def weigh(keys, values, queries, allowed, state):
+    scale = math.log2(math.e) / math.sqrt(keys.shape[1])
+    scores = lax.dot_general(keys, queries, CONTRACT, preferred_element_type=jnp.float32)
+    if allowed is not None:
+        scores = jnp.where(allowed, scores, MASKED)
+    highest = jnp.max(scores, axis=0, keepdims=True)
+    if state is not None:
+        highest = jnp.maximum(state[0], highest)
+    probs = jnp.exp2((scores - highest) * scale)
+    total = jnp.sum(probs, axis=0, keepdims=True)
+    weighted = lax.dot_general(
+        values, probs.astype(jnp.bfloat16), (((0,), (0,)), ((), ())), preferred_element_type=jnp.float32
+    )
+    if state is not None:
+        factor = jnp.exp2((state[0] - highest) * scale)
+        total, weighted = state[1] * factor + total, state[2] * factor + weighted
+    return highest, total, weighted
+
+
+def near_kernel(position_ref, x_ref, highest_ref, total_ref, weighted_ref):
     blocks, rows, tokens, width = x_ref.shape
     group = rows - 2
-    scale = math.log2(math.e) / math.sqrt(width)
     keys = x_ref[:, group].reshape(blocks * tokens, width)
     values = x_ref[:, group + 1].reshape(blocks * tokens, width)
-    for block in range(blocks):
-        queries = x_ref[block, :group].reshape(group * tokens, width)
-        reach = (block + 1) * tokens
-        scores = lax.dot_general(queries, keys[:reach], CONTRACT, preferred_element_type=jnp.float32)
-        row = lax.broadcasted_iota(jnp.int32, (group, tokens, reach), 1).reshape(group * tokens, reach)
-        column = lax.broadcasted_iota(jnp.int32, (group * tokens, reach), 1)
-        scores = jnp.where(column <= row + block * tokens, scores, MASKED)
-        highest = jnp.max(scores, axis=-1, keepdims=True)
-        probs = jnp.exp2((scores - highest) * scale)
-        highest_ref[block] = highest
-        total_ref[block] = jnp.sum(probs, axis=-1, keepdims=True)
-        weighted_ref[block] = jnp.dot(
-            probs.astype(jnp.bfloat16), values[:reach], preferred_element_type=jnp.float32
-        )
+    lanes = NEAR_BLOCKS * group * tokens
+    for first in range(0, blocks, NEAR_BLOCKS):
+        queries = x_ref[first : first + NEAR_BLOCKS, :group].reshape(lanes, width)
+        reach = (first + NEAR_BLOCKS) * tokens
+        place = slice(first * group * tokens, first * group * tokens + lanes)
+        index = lax.broadcasted_iota(jnp.int32, (reach, lanes), 0)
+        allowed = index <= position_ref[:, place]
+        results = weigh(keys[:reach], values[:reach], queries, allowed, None)
+        for ref, value in zip((highest_ref, total_ref, weighted_ref), results):
+            ref[:, place] = value
 
 
 def split_kernel(*refs):
@@ -228,35 +244,27 @@
             refs[side - 2][step] = ref[side]
 
 
-def add_far(x_ref, state, pairs_ref, store):
-    steps, _, tokens, width = pairs_ref.shape
-    group = x_ref.shape[1] - 2
-    scale = math.log2(math.e) / math.sqrt(width)
-    highest_ref, total_ref, weighted_ref = state
-    keys = pairs_ref[:, 0].reshape(steps * tokens, width)
-    values = pairs_ref[:, 1].reshape(steps * tokens, width)
-    for block in range(x_ref.shape[0]):
-        queries = x_ref[block, :group].reshape(group * tokens, width)
-        scores = lax.dot_general(queries, keys, CONTRACT, preferred_element_type=jnp.float32)
-        before = highest_ref[block]
-        highest = jnp.maximum(before, jnp.max(scores, axis=-1, keepdims=True))
-        probs = jnp.exp2((scores - highest) * scale)
-        factor = jnp.exp2((before - highest) * scale)
-        total = total_ref[block] * factor + jnp.sum(probs, axis=-1, keepdims=True)
-        summed = jnp.dot(probs.astype(jnp.bfloat16), values, preferred_element_type=jnp.float32)
-        store(block, highest, total, weighted_ref[block] * factor + summed)
+def add_far(x_ref, pairs_ref, state_refs, store):
+    blocks, rows, tokens, width = x_ref.shape
+    group = rows - 2
+    keys, values = [pairs_ref[:, i].reshape(pairs_ref.shape[0] * tokens, width) for i in range(2)]
+    lanes = FAR_BLOCKS * group * tokens
+    for first in range(0, blocks, FAR_BLOCKS):
+        queries = x_ref[first : first + FAR_BLOCKS, :group].reshape(lanes, width)
+        place = slice(first * group * tokens, first * group * tokens + lanes)
+        store(first, place, *weigh(keys, values, queries, None, [ref[:, place] for ref in state_refs]))
 
 
 def far_kernel(half, me_ref, x_ref, pairs_ref, *refs):
     state, outs = refs[:3], refs[3:]
 
-    def store(block, *values):
+    def store(first, place, *values):
         for ref, value in zip(outs, values):
-            ref[block] = value
+            ref[:, place] = value
 
     @pl.when(me_ref[0] >= half)
     def _():
-        add_far(x_ref, state, pairs_ref, store)
+        add_far(x_ref, pairs_ref, state, store)
 
     @pl.when(me_ref[0] < half)
     def _():
@@ -266,18 +274,22 @@
 
 def last_kernel(half, me_ref, x_ref, pairs_ref, *refs):
     state, out_ref = refs[:3], refs[3]
-
-    def store(block, highest, total, weighted):
-        out_ref[block] = (weighted / total).astype(jnp.bfloat16).reshape(out_ref.shape[1:])
+    blocks, group, tokens, width = out_ref.shape
+
+    def store(first, place, highest, total, weighted):
+        result = jnp.transpose(weighted * (1.0 / total)).astype(jnp.bfloat16)
+        out_ref[first : first + FAR_BLOCKS] = result.reshape(FAR_BLOCKS, group, tokens, width)
 
     @pl.when(me_ref[0] >= half)
     def _():
-        add_far(x_ref, state, pairs_ref, store)
+        add_far(x_ref, pairs_ref, state, store)
 
     @pl.when(me_ref[0] < half)
     def _():
-        for block in range(out_ref.shape[0]):
-            store(block, None, state[1][block], state[2][block])
+        lanes = FAR_BLOCKS * group * tokens
+        for first in range(0, blocks, FAR_BLOCKS):
+            place = slice(first * group * tokens, first * group * tokens + lanes)
+            store(first, place, None, state[1][:, place], state[2][:, place])
 
 
 def halves_plan(length, devices, query_states, key_states, value_states, query_gain, key_gain):
@@ -338,9 +350,11 @@
 
     far = [to_upper(step, pair) for step, pair in enumerate(pairs)]
     arrived = inside(near)
-    rows = group * tokens
-    state = [shape((half, rows, 1), f32), shape((half, rows, 1), f32), shape((half, rows, width), f32)]
-    carried = call(near_kernel, "near", state, arrived, specs=[VMEM])
+    lanes = half * group * tokens
+    state = [shape((1, lanes), f32), shape((1, lanes), f32), shape((width, lanes), f32)]
+    positions = np.broadcast_to(np.arange(half * tokens, dtype=np.int32).reshape(half, 1, tokens), (half, group, tokens))
+    carried = call(near_kernel, "near", state, jnp.asarray(positions.reshape(1, lanes)), arrived, specs=[VMEM] * 2)
+
     carried, far = lax.optimization_barrier((carried, far))
     mine, others = call(
         split_kernel, "split", [shape((steps, 2, tokens, width), bf16)] * 2, *far, specs=[VMEM] * steps

time: 55.6 us -> 54.4 us (0.978)
  Pallas kernels: 13.7 us -> 12.8 us
    pallas_call x5, Pallas kernels: 13.7 us -> 12.8 us  [call(): pl.pallas_call(kernel, out_shape=outs, in_specs=specs or [SMEM] + [VMEM]...]
  transfers between devices with their start and end apart: 6 -> 6, of which waited for: 3 -> 3; matrix products, arithmetic and copies ran while one was open for 0% -> 0% of each run, Pallas kernels for 12% -> 11%
where the time goes in v7:
time: 54.4 us; the launch traced here: 54.1 us
  waiting for transfers between devices  18.2 us (33%)
  Pallas kernels  12.8 us (24%)
  starting transfers between devices  11 us (20%)
  blocking collectives  10.9 us (20%)
  local copies, waits for them, and re-layouts  0.91 us (2%)
    pallas_call x5, Pallas kernels, call(): pl.pallas_call(kernel, out_shape=outs, in_specs=specs or [SMEM] + [VMEM]...  12.8 us
    all_to_all x1, waiting for transfers between devices, inside(): lax.all_to_all(array, 'seq', split_axis=0, concat_axis=0, axis_index_grou...  11 us
    all_to_all x1, blocking collectives, inside(): lax.all_to_all(array, 'seq', split_axis=0, concat_axis=0, axis_index_grou...  10.9 us
    ppermute x4, waiting for transfers between devices, to_upper(): return lax.ppermute(array, 'seq', links)  7.16 us
    ppermute x4, starting transfers between devices, to_upper(): return lax.ppermute(array, 'seq', links)  5.17 us
    all_to_all x1, starting transfers between devices, inside(): lax.all_to_all(array, 'seq', split_axis=0, concat_axis=0, axis_index_grou...  3.95 us
    ppermute x1, starting transfers between devices, to_core(): lax.ppermute(array, 'seq', [(device, device ^ 1) for device in range(lowe...  1.92 us
  transfers between devices with their start and end apart: 6, of which 3 were waited for; matrix products, arithmetic and copies ran while one was open for 0% of the time, Pallas kernels for 11%

profile of v7, /device:TPU:16, one launch (start us, length us, event | category | flops | bytes accessed | tf_op | source)
XLA Modules:
  0.0 54.1 jit_solution(6566208274720247076)
XLA Ops:
  0.0 4.1 %send.1 = (bf16[2,2,112,128]{3,2,1,0:T(8,128)(2,1)}, bf16[2,2,112,128]{3,2,1,0:T(8,128)(2,1)}, bf16[2,2,112,128]{3,2,1,0:T(8,128)(2,1)}, bf16[2,2,112,128]{3,2,1,0:T(8,128)(2,1)}, bf16[8,4,112,128]{3,2,1,0:T(8,128)(2,1)}) custom-call(s32[1]{0:T(128)} %bitcast.me_ref, bf16[112,16,128]{2,1,0:T(8,128)(2,1)} %q_hbm.1, bf16[112,8,128]{2,1,0:T(8,128)(2,1)} %k_hbm.1, ...), custom_call_target="tpu_custom_call" | custom-call | tf_op jit(solution)/shard_map/send/pallas_call | solution.py:305
  4.2 0.0 copy-start.4
  4.2 0.0 copy-start.3
  4.2 0.0 copy-start.2
  4.2 0.0 copy-start.1
  4.2 4.0 %all-to-all-start = ((bf16[8,4,112,128]{3,2,1,0:T(8,128)(2,1)}), bf16[8,4,112,128]{3,2,1,0:T(8,128)(2,1)S(1)}, u32[]{:S(2)}, u32[]{:S(2)}) async-start(bf16[8,4,112,128]{3,2,1,0:T(8,128)(2,1)} %get-tuple-element.25), calls=%async_computation | async-start | bytes 1835008 | tf_op jit(solution)/shard_map/all_to_all | solution.py:349
  8.2 0.0 copy-start
  8.2 0.0 copy-done.4
  8.2 1.3 %collective-permute-start = (bf16[2,2,112,128]{3,2,1,0:T(8,128)(2,1)S(1)}, bf16[2,2,112,128]{3,2,1,0:T(8,128)(2,1)S(1)}, u32[]{:S(2)}, u32[]{:S(2)}) collective-permute-start(bf16[2,2,112,128]{3,2,1,0:T(8,128)(2,1)S(1)} %copy-done.4), channel_id=1, source_target_pairs={{0,8},{1,9},{2,10},{3,11},{4,12},{5,13},{6,14},{7,15},{16,24},{17,... | collective-permute-start | bytes 344072 | tf_op jit(solution)/shard_map/ppermute | solution.py:317
  9.5 0.0 copy-done.3
  9.5 1.3 %collective-permute-start.1 = (bf16[2,2,112,128]{3,2,1,0:T(8,128)(2,1)S(1)}, bf16[2,2,112,128]{3,2,1,0:T(8,128)(2,1)S(1)}, u32[]{:S(2)}, u32[]{:S(2)}) collective-permute-start(bf16[2,2,112,128]{3,2,1,0:T(8,128)(2,1)S(1)} %copy-done.3), channel_id=1, source_target_pairs={{0,10},{1,11},{2,8},{3,9},{4,14},{5,15},{6,12},{7,13},{16,26},{17,... | collective-permute-start | bytes 344072 | tf_op jit(solution)/shard_map/ppermute | solution.py:317
  10.8 0.0 copy-done.2
  10.8 1.3 %collective-permute-start.2 = (bf16[2,2,112,128]{3,2,1,0:T(8,128)(2,1)S(1)}, bf16[2,2,112,128]{3,2,1,0:T(8,128)(2,1)S(1)}, u32[]{:S(2)}, u32[]{:S(2)}) collective-permute-start(bf16[2,2,112,128]{3,2,1,0:T(8,128)(2,1)S(1)} %copy-done.2), channel_id=1, source_target_pairs={{0,12},{1,13},{2,14},{3,15},{4,8},{5,9},{6,10},{7,11},{16,28},{17,... | collective-permute-start | bytes 344072 | tf_op jit(solution)/shard_map/ppermute | solution.py:317
  12.1 0.0 copy-done.1
  12.1 1.3 %collective-permute-start.3 = (bf16[2,2,112,128]{3,2,1,0:T(8,128)(2,1)S(1)}, bf16[2,2,112,128]{3,2,1,0:T(8,128)(2,1)S(1)}, u32[]{:S(2)}, u32[]{:S(2)}) collective-permute-start(bf16[2,2,112,128]{3,2,1,0:T(8,128)(2,1)S(1)} %copy-done.1), channel_id=1, source_target_pairs={{0,14},{1,15},{2,12},{3,13},{4,10},{5,11},{6,8},{7,9},{16,30},{17,... | collective-permute-start | bytes 344072 | tf_op jit(solution)/shard_map/ppermute | solution.py:317
  13.4 11.0 %all-to-all-done.x_ref = bf16[8,4,112,128]{3,2,1,0:T(8,128)(2,1)S(1)} async-done(((bf16[8,4,112,128]{3,2,1,0:T(8,128)(2,1)}), bf16[8,4,112,128]{3,2,1,0:T(8,128)(2,1)S(1)}, u32[]{:S(2)}, u32[]{:S(2)}) %all-to-all-start) | async-done | bytes 917536 | tf_op jit(solution)/shard_map/all_to_all | solution.py:349
  24.4 0.0 copy-done
  24.4 3.4 %near.1 = (f32[1,1792]{1,0:T(1,128)S(1)}, f32[1,1792]{1,0:T(1,128)S(1)}, f32[128,1792]{1,0:T(8,128)S(1)}) custom-call(s32[1,1792]{1,0:T(1,128)S(1)} %copy-done, bf16[8,4,112,128]{3,2,1,0:T(8,128)(2,1)S(1)} %all-to-all-done.x_ref), custom_call_target="tpu_custom_call" | custom-call | tf_op jit(solution)/shard_map/near/pallas_call | solution.py:305
  27.8 0.0 collective-permute-done.refs_0_
  27.8 0.0 collective-permute-done.1.refs_1_
  27.8 4.3 %collective-permute-done.2.refs_2_ = bf16[2,2,112,128]{3,2,1,0:T(8,128)(2,1)S(1)} collective-permute-done((bf16[2,2,112,128]{3,2,1,0:T(8,128)(2,1)S(1)}, bf16[2,2,112,128]{3,2,1,0:T(8,128)(2,1)S(1)}, u32[]{:S(2)}, u32[]{:S(2)}) %collective-permute-start.2) | collective-permute-done | bytes 114720 | tf_op jit(solution)/shard_map/ppermute | solution.py:317
  32.1 2.9 %collective-permute-done.3.refs_3_ = bf16[2,2,112,128]{3,2,1,0:T(8,128)(2,1)S(1)} collective-permute-done((bf16[2,2,112,128]{3,2,1,0:T(8,128)(2,1)S(1)}, bf16[2,2,112,128]{3,2,1,0:T(8,128)(2,1)S(1)}, u32[]{:S(2)}, u32[]{:S(2)}) %collective-permute-start.3) | collective-permute-done | bytes 114720 | tf_op jit(solution)/shard_map/ppermute | solution.py:317
  35.0 1.9 %collective-permute-start.4 = (bf16[4,2,112,128]{3,2,1,0:T(8,128)(2,1)S(1)}, bf16[4,2,112,128]{3,2,1,0:T(8,128)(2,1)S(1)}, u32[]{:S(2)}, u32[]{:S(2)}) collective-permute-start(bf16[4,2,112,128]{3,2,1,0:T(8,128)(2,1)S(1)} %get-tuple-element.37), channel_id=1, source_target_pairs={{8,9},{9,8},{10,11},{11,10},{12,13},{13,12},{14,15},{15,14},{24,25... | collective-permute-start | bytes 688136 | tf_op jit(solution)/shard_map/ppermute | solution.py:320
  37.0 2.5 %far.1 = (f32[1,1792]{1,0:T(1,128)S(1)}, f32[1,1792]{1,0:T(1,128)S(1)}, f32[128,1792]{1,0:T(8,128)S(1)}) custom-call(s32[1]{0:T(128)} %bitcast.me_ref, bf16[8,4,112,128]{3,2,1,0:T(8,128)(2,1)S(1)} %all-to-all-done.x_ref, bf16[4,2,112,128]{3,2,1,0:T(8,128)(2,1)S(1)} %get-tuple-element.38.pairs_ref, f32[1,1792]{1,0:T(1,128)S(1)} %get-tuple-element.39.refs_0_, ...), custom_call_target="tpu_custom_call" | custom-call | tf_op jit(solution)/shard_map/far/pallas_call | solution.py:305
  39.5 0.0 collective-permute-done.4.pairs_ref
  39.5 2.8 %last.1 = bf16[8,2,112,128]{3,2,1,0:T(8,128)(2,1)S(1)} custom-call(s32[1]{0:T(128)} %bitcast.me_ref, bf16[8,4,112,128]{3,2,1,0:T(8,128)(2,1)S(1)} %all-to-all-done.x_ref, bf16[4,2,112,128]{3,2,1,0:T(8,128)(2,1)S(1)} %collective-permute-done.4.pairs_ref, f32[1,1792]{1,0:T(1,128)S(1)} %get-tuple-element.42.refs_0_, f32[1,1792]{1,0:T(1,128)S(1)} %get-tuple-element.43.refs_1_, ...), custom_call_target="tpu_custom_call" | custom-call | tf_op jit(solution)/shard_map/last/pallas_call | solution.py:305
  42.3 10.9 %all_to_all.10 = bf16[8,2,112,128]{3,2,1,0:T(8,128)(2,1)S(1)} all-to-all(bf16[8,2,112,128]{3,2,1,0:T(8,128)(2,1)S(1)} %last.1), channel_id=1, replica_groups={{0,1,2,3,4,5,6,7},{8,9,10,11,12,13,14,15},{16,17,18,19,20,21,22,23},{24..., dimensions={0} | all-to-all | bytes 917504 | tf_op jit(solution)/shard_map/all_to_all | solution.py:349
  53.2 0.9 %copy.10 = bf16[16,112,128]{2,0,1:T(8,128)(2,1)} copy(bf16[16,112,128]{2,1,0:T(8,128)(2,1)S(1)} %bitcast.7) | data formatting | bytes 917504 | tf_op jit(solution)/shard_map/reshape | solution.py:372
  (1 shorter events, 0.0 us)
Async XLA Ops:
  4.2 4.0 %copy-start.4 = (bf16[2,2,112,128]{3,2,1,0:T(8,128)(2,1)S(1)}, bf16[2,2,112,128]{3,2,1,0:T(8,128)(2,1)}, u32[]{:S(2)}) copy-start(bf16[2,2,112,128]{3,2,1,0:T(8,128)(2,1)} %get-tuple-element.29) | copy-start | bytes 344068
  4.2 5.3 %copy-start.3 = (bf16[2,2,112,128]{3,2,1,0:T(8,128)(2,1)S(1)}, bf16[2,2,112,128]{3,2,1,0:T(8,128)(2,1)}, u32[]{:S(2)}) copy-start(bf16[2,2,112,128]{3,2,1,0:T(8,128)(2,1)} %get-tuple-element.30) | copy-start | bytes 344068
  4.2 6.6 %copy-start.2 = (bf16[2,2,112,128]{3,2,1,0:T(8,128)(2,1)S(1)}, bf16[2,2,112,128]{3,2,1,0:T(8,128)(2,1)}, u32[]{:S(2)}) copy-start(bf16[2,2,112,128]{3,2,1,0:T(8,128)(2,1)} %get-tuple-element.31) | copy-start | bytes 344068
  4.2 7.9 %copy-start.1 = (bf16[2,2,112,128]{3,2,1,0:T(8,128)(2,1)S(1)}, bf16[2,2,112,128]{3,2,1,0:T(8,128)(2,1)}, u32[]{:S(2)}) copy-start(bf16[2,2,112,128]{3,2,1,0:T(8,128)(2,1)} %get-tuple-element.32) | copy-start | bytes 344068
  4.2 20.2 %all-to-all-start = ((bf16[8,4,112,128]{3,2,1,0:T(8,128)(2,1)}), bf16[8,4,112,128]{3,2,1,0:T(8,128)(2,1)S(1)}, u32[]{:S(2)}, u32[]{:S(2)}) async-start(bf16[8,4,112,128]{3,2,1,0:T(8,128)(2,1)} %get-tuple-element.25), calls=%async_computation | async-start | bytes 1835008 | tf_op jit(solution)/shard_map/all_to_all | solution.py:349
  8.2 16.3 %copy-start = (s32[1,1792]{1,0:T(1,128)S(1)}, s32[1,1792]{1,0:T(1,128)}, u32[]{:S(2)}) copy-start(s32[1,1792]{1,0:T(1,128)} %constant.9.clone.position_ref) | copy-start | bytes 21508
  8.2 19.6 %collective-permute-start = (bf16[2,2,112,128]{3,2,1,0:T(8,128)(2,1)S(1)}, bf16[2,2,112,128]{3,2,1,0:T(8,128)(2,1)S(1)}, u32[]{:S(2)}, u32[]{:S(2)}) collective-permute-start(bf16[2,2,112,128]{3,2,1,0:T(8,128)(2,1)S(1)} %copy-done.4), channel_id=1, source_target_pairs={{0,8},{1,9},{2,10},{3,11},{4,12},{5,13},{6,14},{7,15},{16,24},{17,... | collective-permute-start | bytes 344072 | tf_op jit(solution)/shard_map/ppermute | solution.py:317
  9.5 18.3 %collective-permute-start.1 = (bf16[2,2,112,128]{3,2,1,0:T(8,128)(2,1)S(1)}, bf16[2,2,112,128]{3,2,1,0:T(8,128)(2,1)S(1)}, u32[]{:S(2)}, u32[]{:S(2)}) collective-permute-start(bf16[2,2,112,128]{3,2,1,0:T(8,128)(2,1)S(1)} %copy-done.3), channel_id=1, source_target_pairs={{0,10},{1,11},{2,8},{3,9},{4,14},{5,15},{6,12},{7,13},{16,26},{17,... | collective-permute-start | bytes 344072 | tf_op jit(solution)/shard_map/ppermute | solution.py:317
  10.8 21.3 %collective-permute-start.2 = (bf16[2,2,112,128]{3,2,1,0:T(8,128)(2,1)S(1)}, bf16[2,2,112,128]{3,2,1,0:T(8,128)(2,1)S(1)}, u32[]{:S(2)}, u32[]{:S(2)}) collective-permute-start(bf16[2,2,112,128]{3,2,1,0:T(8,128)(2,1)S(1)} %copy-done.2), channel_id=1, source_target_pairs={{0,12},{1,13},{2,14},{3,15},{4,8},{5,9},{6,10},{7,11},{16,28},{17,... | collective-permute-start | bytes 344072 | tf_op jit(solution)/shard_map/ppermute | solution.py:317
  12.1 22.9 %collective-permute-start.3 = (bf16[2,2,112,128]{3,2,1,0:T(8,128)(2,1)S(1)}, bf16[2,2,112,128]{3,2,1,0:T(8,128)(2,1)S(1)}, u32[]{:S(2)}, u32[]{:S(2)}) collective-permute-start(bf16[2,2,112,128]{3,2,1,0:T(8,128)(2,1)S(1)} %copy-done.1), channel_id=1, source_target_pairs={{0,14},{1,15},{2,12},{3,13},{4,10},{5,11},{6,8},{7,9},{16,30},{17,... | collective-permute-start | bytes 344072 | tf_op jit(solution)/shard_map/ppermute | solution.py:317
  35.0 4.4 %collective-permute-start.4 = (bf16[4,2,112,128]{3,2,1,0:T(8,128)(2,1)S(1)}, bf16[4,2,112,128]{3,2,1,0:T(8,128)(2,1)S(1)}, u32[]{:S(2)}, u32[]{:S(2)}) collective-permute-start(bf16[4,2,112,128]{3,2,1,0:T(8,128)(2,1)S(1)} %get-tuple-element.37), channel_id=1, source_target_pairs={{8,9},{9,8},{10,11},{11,10},{12,13},{13,12},{14,15},{15,14},{24,25... | collective-permute-start | bytes 688136 | tf_op jit(solution)/shard_map/ppermute | solution.py:320

commit v8 on v7

--- a/solution.py
+++ b/solution.py
@@ -244,10 +244,13 @@
             refs[side - 2][step] = ref[side]
 
 
-def add_far(x_ref, pairs_ref, state_refs, store):
+def add_far(x_ref, pair_refs, state_refs, store):
     blocks, rows, tokens, width = x_ref.shape
     group = rows - 2
-    keys, values = [pairs_ref[:, i].reshape(pairs_ref.shape[0] * tokens, width) for i in range(2)]
+    keys, values = [
+        jnp.concatenate([ref[:, i].reshape(ref.shape[0] * tokens, width) for ref in pair_refs], axis=0)
+        for i in range(2)
+    ]
     lanes = FAR_BLOCKS * group * tokens
     for first in range(0, blocks, FAR_BLOCKS):
         queries = x_ref[first : first + FAR_BLOCKS, :group].reshape(lanes, width)
@@ -255,24 +258,7 @@
         store(first, place, *weigh(keys, values, queries, None, [ref[:, place] for ref in state_refs]))
 
 
-def far_kernel(half, me_ref, x_ref, pairs_ref, *refs):
-    state, outs = refs[:3], refs[3:]
-
-    def store(first, place, *values):
-        for ref, value in zip(outs, values):
-            ref[:, place] = value
-
-    @pl.when(me_ref[0] >= half)
-    def _():
-        add_far(x_ref, pairs_ref, state, store)
-
-    @pl.when(me_ref[0] < half)
-    def _():
-        for ref, before in zip(outs, state):
-            ref[...] = before[...]
-
-
-def last_kernel(half, me_ref, x_ref, pairs_ref, *refs):
+def last_kernel(half, me_ref, x_ref, mine_ref, neighbours_ref, *refs):
     state, out_ref = refs[:3], refs[3]
     blocks, group, tokens, width = out_ref.shape
 
@@ -282,7 +268,7 @@
 
     @pl.when(me_ref[0] >= half)
     def _():
-        add_far(x_ref, pairs_ref, state, store)
+        add_far(x_ref, [mine_ref, neighbours_ref], state, store)
 
     @pl.when(me_ref[0] < half)
     def _():
@@ -349,23 +335,23 @@
         return lax.all_to_all(array, "seq", split_axis=0, concat_axis=0, axis_index_groups=groups, tiled=True)
 
     far = [to_upper(step, pair) for step, pair in enumerate(pairs)]
-    arrived = inside(near)
+    arrived = lax.cond(me[0] >= 0, inside, jnp.zeros_like, near)
+    arrived, far = lax.optimization_barrier((arrived, far))
+    mine, others = call(
+        split_kernel, "split", [shape((steps, 2, tokens, width), bf16)] * 2, *far, specs=[VMEM] * steps
+    )
+    neighbours = to_core(others, half)
     lanes = half * group * tokens
     state = [shape((1, lanes), f32), shape((1, lanes), f32), shape((width, lanes), f32)]
     positions = np.broadcast_to(np.arange(half * tokens, dtype=np.int32).reshape(half, 1, tokens), (half, group, tokens))
     carried = call(near_kernel, "near", state, jnp.asarray(positions.reshape(1, lanes)), arrived, specs=[VMEM] * 2)
 
-    carried, far = lax.optimization_barrier((carried, far))
-    mine, others = call(
-        split_kernel, "split", [shape((steps, 2, tokens, width), bf16)] * 2, *far, specs=[VMEM] * steps
-    )
-    neighbours = to_core(others, half)
-    carried = call(functools.partial(far_kernel, half), "far", state, arrived, mine, *carried)
     attended = call(
         functools.partial(last_kernel, half),
         "last",
         shape((half, group, tokens, width), bf16),
         arrived,
+        mine,
         neighbours,
         *carried,
     )

time: 54.4 us -> 55.7 us (1.024)
  blocking collectives: 10.9 us -> 36.7 us
  waiting for transfers between devices: 18.2 us -> 0.01 us
  starting transfers between devices: 11 us -> 7.1 us
  Pallas kernels: 12.8 us -> 10.6 us
    all_to_all x1 -> x2, blocking collectives: 10.9 us -> 36.7 us  [inside(): lax.all_to_all(array, 'seq', split_axis=0, concat_axis=0, axis_index_grou...]
    all_to_all x1 -> x0, waiting for transfers between devices: 11 us -> none  [inside(): lax.all_to_all(array, 'seq', split_axis=0, concat_axis=0, axis_index_grou...]
    ppermute x4, waiting for transfers between devices: 7.16 us -> 0.01 us  [to_upper(): return lax.ppermute(array, 'seq', links)]
    all_to_all x1 -> x0, starting transfers between devices: 3.95 us -> none  [inside(): lax.all_to_all(array, 'seq', split_axis=0, concat_axis=0, axis_index_grou...]
    pallas_call x5 -> x4, Pallas kernels: 12.8 us -> 10.6 us  [call(): pl.pallas_call(kernel, out_shape=outs, in_specs=specs or [SMEM] + [VMEM]...]
  transfers between devices with their start and end apart: 6 -> 5, of which waited for: 3 -> 0; matrix products, arithmetic and copies ran while one was open for 0% -> 0% of each run, Pallas kernels for 11% -> 6%
where the time goes in v8:
time: 55.7 us; the launch traced here: 55.4 us
  blocking collectives  36.7 us (66%)
  Pallas kernels  10.6 us (19%)
  starting transfers between devices  7.1 us (13%)
  local copies, waits for them, and re-layouts  0.89 us (2%)
    all_to_all x2, blocking collectives, inside(): lax.all_to_all(array, 'seq', split_axis=0, concat_axis=0, axis_index_grou...  36.7 us
    pallas_call x4, Pallas kernels, call(): pl.pallas_call(kernel, out_shape=outs, in_specs=specs or [SMEM] + [VMEM]...  10.6 us
    ppermute x4, starting transfers between devices, to_upper(): return lax.ppermute(array, 'seq', links)  5.17 us
    ppermute x1, starting transfers between devices, to_core(): lax.ppermute(array, 'seq', [(device, device ^ 1) for device in range(lowe...  1.93 us
  transfers between devices with their start and end apart: 5, of which 0 were waited for; matrix products, arithmetic and copies ran while one was open for 0% of the time, Pallas kernels for 6%

profile of v8, /device:TPU:16, one launch (start us, length us, event | category | flops | bytes accessed | tf_op | source)
XLA Modules:
  0.0 55.4 jit_solution(14046511619844714142)
XLA Ops:
  0.0 3.2 %send.1 = (bf16[2,2,112,128]{3,2,1,0:T(8,128)(2,1)}, bf16[2,2,112,128]{3,2,1,0:T(8,128)(2,1)}, bf16[2,2,112,128]{3,2,1,0:T(8,128)(2,1)}, bf16[2,2,112,128]{3,2,1,0:T(8,128)(2,1)}, bf16[8,4,112,128]{3,2,1,0:T(8,128)(2,1)S(1)}) custom-call(s32[1]{0:T(128)} %bitcast.me_ref, bf16[112,16,128]{2,1,0:T(8,128)(2,1)} %q_hbm.1, bf16[112,8,128]{2,1,0:T(8,128)(2,1)} %k_hbm.1, ...), custom_call_target="tpu_custom_call" | custom-call | tf_op jit(solution)/shard_map/send/pallas_call | solution.py:291
  3.2 1.3 %collective-permute-start = (bf16[2,2,112,128]{3,2,1,0:T(8,128)(2,1)}, bf16[2,2,112,128]{3,2,1,0:T(8,128)(2,1)S(1)}, u32[]{:S(2)}, u32[]{:S(2)}) collective-permute-start(bf16[2,2,112,128]{3,2,1,0:T(8,128)(2,1)} %get-tuple-element.25), channel_id=1, source_target_pairs={{0,8},{1,9},{2,10},{3,11},{4,12},{5,13},{6,14},{7,15},{16,24},{17,... | collective-permute-start | bytes 344072 | tf_op jit(solution)/shard_map/ppermute | solution.py:303
  4.5 1.3 %collective-permute-start.1 = (bf16[2,2,112,128]{3,2,1,0:T(8,128)(2,1)}, bf16[2,2,112,128]{3,2,1,0:T(8,128)(2,1)S(1)}, u32[]{:S(2)}, u32[]{:S(2)}) collective-permute-start(bf16[2,2,112,128]{3,2,1,0:T(8,128)(2,1)} %get-tuple-element.26), channel_id=1, source_target_pairs={{0,10},{1,11},{2,8},{3,9},{4,14},{5,15},{6,12},{7,13},{16,26},{17,... | collective-permute-start | bytes 344072 | tf_op jit(solution)/shard_map/ppermute | solution.py:303
  5.8 1.3 %collective-permute-start.2 = (bf16[2,2,112,128]{3,2,1,0:T(8,128)(2,1)}, bf16[2,2,112,128]{3,2,1,0:T(8,128)(2,1)S(1)}, u32[]{:S(2)}, u32[]{:S(2)}) collective-permute-start(bf16[2,2,112,128]{3,2,1,0:T(8,128)(2,1)} %get-tuple-element.27), channel_id=1, source_target_pairs={{0,12},{1,13},{2,14},{3,15},{4,8},{5,9},{6,10},{7,11},{16,28},{17,... | collective-permute-start | bytes 344072 | tf_op jit(solution)/shard_map/ppermute | solution.py:303
  7.1 1.3 %collective-permute-start.3 = (bf16[2,2,112,128]{3,2,1,0:T(8,128)(2,1)}, bf16[2,2,112,128]{3,2,1,0:T(8,128)(2,1)S(1)}, u32[]{:S(2)}, u32[]{:S(2)}) collective-permute-start(bf16[2,2,112,128]{3,2,1,0:T(8,128)(2,1)} %get-tuple-element.28), channel_id=1, source_target_pairs={{0,14},{1,15},{2,12},{3,13},{4,10},{5,11},{6,8},{7,9},{16,30},{17,... | collective-permute-start | bytes 344072 | tf_op jit(solution)/shard_map/ppermute | solution.py:303
  8.4 23.7 %conditional.1 = (bf16[8,4,112,128]{3,2,1,0:T(8,128)(2,1)S(1)}) conditional(s32[]{:T(128)} %convert_element_type.3, () %tuple.12, bf16[8,4,112,128]{3,2,1,0:T(8,128)(2,1)S(1)} %get-tuple-element.24), branch_computations={%region_0.0_spmd, %region_1.0_spmd} | conditional | bytes 1835016 | solution.py:338
  8.4 23.7 %all_to_all.9 = bf16[8,4,112,128]{3,2,1,0:T(8,128)(2,1)S(1)} all-to-all(bf16[8,4,112,128]{3,2,1,0:T(8,128)(2,1)S(1)} %param.1), channel_id=1, replica_groups={{0,1,2,3,4,5,6,7},{8,9,10,11,12,13,14,15},{16,17,18,19,20,21,22,23},{24..., dimensions={0} | all-to-all | bytes 1835008 | tf_op jit(solution)/shard_map/cond/branch_1_fun/all_to_all | solution.py:335
  32.1 0.0 copy-start
  32.1 0.0 collective-permute-done.refs_0_
  32.1 0.0 collective-permute-done.1.refs_1_
  32.1 0.0 collective-permute-done.2.refs_2_
  32.1 0.0 collective-permute-done.3.refs_3_
  32.2 1.9 %collective-permute-start.4 = (bf16[4,2,112,128]{3,2,1,0:T(8,128)(2,1)S(1)}, bf16[4,2,112,128]{3,2,1,0:T(8,128)(2,1)S(1)}, u32[]{:S(2)}, u32[]{:S(2)}) collective-permute-start(bf16[4,2,112,128]{3,2,1,0:T(8,128)(2,1)S(1)} %get-tuple-element.35), channel_id=1, source_target_pairs={{8,9},{9,8},{10,11},{11,10},{12,13},{13,12},{14,15},{15,14},{24,25... | collective-permute-start | bytes 688136 | tf_op jit(solution)/shard_map/ppermute | solution.py:306
  34.1 0.0 copy-done
  34.1 3.4 %near.1 = (f32[1,1792]{1,0:T(1,128)S(1)}, f32[1,1792]{1,0:T(1,128)S(1)}, f32[128,1792]{1,0:T(8,128)S(1)}) custom-call(s32[1,1792]{1,0:T(1,128)S(1)} %copy-done, bf16[8,4,112,128]{3,2,1,0:T(8,128)(2,1)S(1)} %get-tuple-element.39.x_ref), custom_call_target="tpu_custom_call" | custom-call | tf_op jit(solution)/shard_map/near/pallas_call | solution.py:291
  37.5 0.0 collective-permute-done.4.neighbours_ref
  37.5 3.9 %last.1 = bf16[8,2,112,128]{3,2,1,0:T(8,128)(2,1)S(1)} custom-call(s32[1]{0:T(128)} %bitcast.me_ref, bf16[8,4,112,128]{3,2,1,0:T(8,128)(2,1)S(1)} %get-tuple-element.39.x_ref, bf16[4,2,112,128]{3,2,1,0:T(8,128)(2,1)S(1)} %get-tuple-element.34.mine_ref, bf16[4,2,112,128]{3,2,1,0:T(8,128)(2,1)S(1)} %collective-permute-done.4.neighbours_ref, ...), custom_call_target="tpu_custom_call" | custom-call | tf_op jit(solution)/shard_map/last/pallas_call | solution.py:291
  41.5 13.0 %all_to_all.10 = bf16[8,2,112,128]{3,2,1,0:T(8,128)(2,1)S(1)} all-to-all(bf16[8,2,112,128]{3,2,1,0:T(8,128)(2,1)S(1)} %last.1), channel_id=1, replica_groups={{0,1,2,3,4,5,6,7},{8,9,10,11,12,13,14,15},{16,17,18,19,20,21,22,23},{24..., dimensions={0} | all-to-all | bytes 917504 | tf_op jit(solution)/shard_map/all_to_all | solution.py:335
  54.5 0.9 %copy.10 = bf16[16,112,128]{2,0,1:T(8,128)(2,1)} copy(bf16[16,112,128]{2,1,0:T(8,128)(2,1)S(1)} %bitcast.7) | data formatting | bytes 917504 | tf_op jit(solution)/shard_map/reshape | solution.py:358
  (1 shorter events, 0.0 us)
Async XLA Ops:
  3.2 28.9 %collective-permute-start = (bf16[2,2,112,128]{3,2,1,0:T(8,128)(2,1)}, bf16[2,2,112,128]{3,2,1,0:T(8,128)(2,1)S(1)}, u32[]{:S(2)}, u32[]{:S(2)}) collective-permute-start(bf16[2,2,112,128]{3,2,1,0:T(8,128)(2,1)} %get-tuple-element.25), channel_id=1, source_target_pairs={{0,8},{1,9},{2,10},{3,11},{4,12},{5,13},{6,14},{7,15},{16,24},{17,... | collective-permute-start | bytes 344072 | tf_op jit(solution)/shard_map/ppermute | solution.py:303
  4.5 27.6 %collective-permute-start.1 = (bf16[2,2,112,128]{3,2,1,0:T(8,128)(2,1)}, bf16[2,2,112,128]{3,2,1,0:T(8,128)(2,1)S(1)}, u32[]{:S(2)}, u32[]{:S(2)}) collective-permute-start(bf16[2,2,112,128]{3,2,1,0:T(8,128)(2,1)} %get-tuple-element.26), channel_id=1, source_target_pairs={{0,10},{1,11},{2,8},{3,9},{4,14},{5,15},{6,12},{7,13},{16,26},{17,... | collective-permute-start | bytes 344072 | tf_op jit(solution)/shard_map/ppermute | solution.py:303
  5.8 26.3 %collective-permute-start.2 = (bf16[2,2,112,128]{3,2,1,0:T(8,128)(2,1)}, bf16[2,2,112,128]{3,2,1,0:T(8,128)(2,1)S(1)}, u32[]{:S(2)}, u32[]{:S(2)}) collective-permute-start(bf16[2,2,112,128]{3,2,1,0:T(8,128)(2,1)} %get-tuple-element.27), channel_id=1, source_target_pairs={{0,12},{1,13},{2,14},{3,15},{4,8},{5,9},{6,10},{7,11},{16,28},{17,... | collective-permute-start | bytes 344072 | tf_op jit(solution)/shard_map/ppermute | solution.py:303
  7.1 25.0 %collective-permute-start.3 = (bf16[2,2,112,128]{3,2,1,0:T(8,128)(2,1)}, bf16[2,2,112,128]{3,2,1,0:T(8,128)(2,1)S(1)}, u32[]{:S(2)}, u32[]{:S(2)}) collective-permute-start(bf16[2,2,112,128]{3,2,1,0:T(8,128)(2,1)} %get-tuple-element.28), channel_id=1, source_target_pairs={{0,14},{1,15},{2,12},{3,13},{4,10},{5,11},{6,8},{7,9},{16,30},{17,... | collective-permute-start | bytes 344072 | tf_op jit(solution)/shard_map/ppermute | solution.py:303
  32.1 2.0 %copy-start = (s32[1,1792]{1,0:T(1,128)S(1)}, s32[1,1792]{1,0:T(1,128)}, u32[]{:S(2)}) copy-start(s32[1,1792]{1,0:T(1,128)} %constant.13.clone.position_ref) | copy-start | bytes 21508
  32.2 5.3 %collective-permute-start.4 = (bf16[4,2,112,128]{3,2,1,0:T(8,128)(2,1)S(1)}, bf16[4,2,112,128]{3,2,1,0:T(8,128)(2,1)S(1)}, u32[]{:S(2)}, u32[]{:S(2)}) collective-permute-start(bf16[4,2,112,128]{3,2,1,0:T(8,128)(2,1)S(1)} %get-tuple-element.35), channel_id=1, source_target_pairs={{8,9},{9,8},{10,11},{11,10},{12,13},{13,12},{14,15},{15,14},{24,25... | collective-permute-start | bytes 688136 | tf_op jit(solution)/shard_map/ppermute | solution.py:306

commit v9 on v8

--- a/solution.py
+++ b/solution.py
@@ -17,8 +17,7 @@
 VMEM = pl.BlockSpec(memory_space=pltpu.VMEM)
 SMEM = pl.BlockSpec(memory_space=pltpu.SMEM)
 HBM = pl.BlockSpec(memory_space=pltpu.HBM)
-NEAR_BLOCKS = 2
-FAR_BLOCKS = 2
+TILE_BLOCKS = 2
 CONTRACT = (((1,), (1,)), ((), ()))
 
 
@@ -165,12 +164,14 @@
 
 
 def send_kernel(me_ref, q_hbm, k_hbm, v_hbm, table_hbm, query_gain_ref, key_gain_ref, *refs):
-    pairs, (near_ref, q_ref, k_ref, v_ref, table_ref, qf_ref, kf_ref, vf_ref, sems) = refs[:-9], refs[-9:]
+    (keep_ref, give_ref), fulls = refs[:2], refs[2:-8]
+    q_ref, k_ref, v_ref, table_ref, qf_ref, kf_ref, vf_ref, sems = refs[-8:]
+    steps, slots = len(fulls), keep_ref.shape[0]
     tokens, heads, width = q_ref.shape
-    kv_heads = k_ref.shape[1]
-    group = heads // kv_heads
+    kv_heads, per_chip = k_ref.shape[1], keep_ref.shape[1]
+    first, per_full = 2 * per_chip, heads // steps
     me = me_ref[0]
-    chip, core = lax.rem(me // 2, len(pairs)), lax.rem(me, 2)
+    chip, core = lax.rem(me // 2, steps), lax.rem(me, 2)
     start = pl.multiple_of(me * tokens, 8)
     copies = [
         pltpu.make_async_copy(k_hbm, k_ref, sems.at[0]),
@@ -186,20 +187,33 @@
     cosine, sine = rope_factors(table_ref[...])
     copies[2].wait()
     vf_ref[...] = v_ref[...].astype(jnp.float32).reshape(tokens * kv_heads, width)
-    for step, pair in enumerate(pairs):
-        for side in range(2):
-            head = (chip ^ step) * 2 + lax.rem(core + side, 2)
-            keys = turn(kf_ref[pl.ds(head, tokens, stride=kv_heads), :], key_gain_ref[...], cosine, sine)
-            values = vf_ref[pl.ds(head, tokens, stride=kv_heads), :].astype(jnp.bfloat16)
-            pair[side, 0] = keys
-            near_ref[head, group] = keys
-            pair[side, 1] = values
-            near_ref[head, group + 1] = values
+    for slot in range(steps):
+        step = lax.rem(core * slots + slot, steps)
+        ref = keep_ref if slot < slots else give_ref
+        for row in range(per_chip):
+            head = (chip ^ step) * per_chip + row
+            ref[slot % slots, row, 0] = turn(
+                kf_ref[pl.ds(head, tokens, stride=kv_heads), :], key_gain_ref[...], cosine, sine
+            )
+            ref[slot % slots, row, 1] = vf_ref[pl.ds(head, tokens, stride=kv_heads), :].astype(jnp.bfloat16)
+    for slot in range(slots):
+        for row in range(first):
+            part = (slot, row // 2, row % 2)
+
+            @pl.when(core == 0)
+            def _():
+                fulls[slot][row], fulls[slots + slot][row] = keep_ref[part], give_ref[part]
+
+            @pl.when(core == 1)
+            def _():
+                fulls[slot][row], fulls[slots + slot][row] = give_ref[part], keep_ref[part]
+
     copies[3].wait()
     qf_ref[...] = normalize(q_ref[...].reshape(tokens * heads, width))
-    for head in range(heads):
-        normed = qf_ref[pl.ds(head, tokens, stride=heads), :]
-        near_ref[head // group, head % group] = turn(normed, query_gain_ref[...], cosine, sine)
+    for step in range(steps):
+        for row in range(per_full):
+            normed = qf_ref[pl.ds((chip ^ step) * per_full + row, tokens, stride=heads), :]
+            fulls[step][first + row] = turn(normed, query_gain_ref[...], cosine, sine)
 
 
 def weigh(keys, values, queries, allowed, state):
@@ -221,61 +235,88 @@
     return highest, total, weighted
 
 
-def near_kernel(position_ref, x_ref, highest_ref, total_ref, weighted_ref):
-    blocks, rows, tokens, width = x_ref.shape
-    group = rows - 2
-    keys = x_ref[:, group].reshape(blocks * tokens, width)
-    values = x_ref[:, group + 1].reshape(blocks * tokens, width)
-    lanes = NEAR_BLOCKS * group * tokens
-    for first in range(0, blocks, NEAR_BLOCKS):
-        queries = x_ref[first : first + NEAR_BLOCKS, :group].reshape(lanes, width)
-        reach = (first + NEAR_BLOCKS) * tokens
-        place = slice(first * group * tokens, first * group * tokens + lanes)
-        index = lax.broadcasted_iota(jnp.int32, (reach, lanes), 0)
-        allowed = index <= position_ref[:, place]
-        results = weigh(keys[:reach], values[:reach], queries, allowed, None)
-        for ref, value in zip((highest_ref, total_ref, weighted_ref), results):
-            ref[:, place] = value
-
-
-def split_kernel(*refs):
-    for step, ref in enumerate(refs[:-2]):
-        for side in range(2):
-            refs[side - 2][step] = ref[side]
-
-
-def add_far(x_ref, pair_refs, state_refs, store):
-    blocks, rows, tokens, width = x_ref.shape
-    group = rows - 2
-    keys, values = [
-        jnp.concatenate([ref[:, i].reshape(ref.shape[0] * tokens, width) for ref in pair_refs], axis=0)
-        for i in range(2)
-    ]
-    lanes = FAR_BLOCKS * group * tokens
-    for first in range(0, blocks, FAR_BLOCKS):
-        queries = x_ref[first : first + FAR_BLOCKS, :group].reshape(lanes, width)
-        place = slice(first * group * tokens, first * group * tokens + lanes)
-        store(first, place, *weigh(keys, values, queries, None, [ref[:, place] for ref in state_refs]))
-
-
-def last_kernel(half, me_ref, x_ref, mine_ref, neighbours_ref, *refs):
-    state, out_ref = refs[:3], refs[3]
-    blocks, group, tokens, width = out_ref.shape
-
-    def store(first, place, highest, total, weighted):
+def join_kernel(keep_ref, got_ref, *outs):
+    for slot, ref in enumerate(outs):
+        ref[0], ref[1] = keep_ref[slot], got_ref[slot]
+
+
+def gather_kernel(me_ref, *refs):
+    pair_ref, query_ref = refs[-2:]
+    steps, per_chip = query_ref.shape[:2]
+    near, far = refs[:steps], refs[steps:-2]
+    chip = lax.rem(me_ref[0] // 2, steps)
+    for step in range(steps):
+        pair_ref[chip ^ step] = near[step][: 2 * per_chip].reshape(pair_ref.shape[1:])
+        query_ref[chip ^ step] = near[step][2 * per_chip :].reshape(query_ref.shape[1:])
+    for slot, ref in enumerate(far):
+        pair_ref[steps + 2 * slot : steps + 2 * slot + 2] = ref[...]
+
+
+def add_core(upper, bound, query_ref, pair_ref, state_refs, store):
+    steps, kv_heads, group, tokens, width = query_ref.shape
+    lanes = TILE_BLOCKS * group * tokens
+
+    def tiles(with_far):
+        for head in range(kv_heads):
+            for first in range(0, steps, TILE_BLOCKS):
+                count = first + TILE_BLOCKS
+                place = slice(first * group * tokens, first * group * tokens + lanes)
+                keys, values = [
+                    jnp.concatenate(
+                        [pair_ref[:count, head, i].reshape(count * tokens, width)]
+                        + ([pair_ref[steps:, head, i].reshape(steps * tokens, width)] if with_far else []),
+                        axis=0,
+                    )
+                    for i in range(2)
+                ]
+                queries = query_ref[first:count, head].reshape(lanes, width)
+                index = lax.broadcasted_iota(jnp.int32, (keys.shape[0], lanes), 0)
+                allowed = index < bound[:, place]
+                if with_far:
+                    allowed = jnp.logical_or(allowed, index >= count * tokens)
+                state = [ref[head, :, place] for ref in state_refs] if state_refs else None
+                store(head, first, place, *weigh(keys, values, queries, allowed, state))
+
+    pl.when(upper)(functools.partial(tiles, True))
+    pl.when(jnp.logical_not(upper))(functools.partial(tiles, False))
+
+
+def first_kernel(half, me_ref, bounds_ref, query_ref, pair_ref, *outs):
+    def store(head, first, place, *values):
+        for ref, value in zip(outs, values):
+            ref[head, :, place] = value
+
+    add_core(me_ref[0] >= half, bounds_ref[0:1], query_ref, pair_ref, None, store)
+
+
+def second_kernel(half, me_ref, bounds_ref, query_ref, pair_ref, *refs):
+    steps, kv_heads, group, tokens, width = query_ref.shape
+    state, outs, out_ref = refs[:3], refs[3:-1], refs[-1]
+    me = me_ref[0]
+
+    def store(head, first, place, highest, total, weighted):
         result = jnp.transpose(weighted * (1.0 / total)).astype(jnp.bfloat16)
-        out_ref[first : first + FAR_BLOCKS] = result.reshape(FAR_BLOCKS, group, tokens, width)
-
-    @pl.when(me_ref[0] >= half)
-    def _():
-        add_far(x_ref, [mine_ref, neighbours_ref], state, store)
-
-    @pl.when(me_ref[0] < half)
-    def _():
-        lanes = FAR_BLOCKS * group * tokens
-        for first in range(0, blocks, FAR_BLOCKS):
-            place = slice(first * group * tokens, first * group * tokens + lanes)
-            store(first, place, None, state[1][:, place], state[2][:, place])
+        rows = slice(head * group, (head + 1) * group)
+        out_ref[first : first + TILE_BLOCKS, rows] = result.reshape(TILE_BLOCKS, group, tokens, width)
+
+    bound = bounds_ref[1:2] + lax.rem(me, 2) * tokens
+    add_core(me >= half, bound, query_ref, pair_ref, state, store)
+    chip = lax.rem(me // 2, steps)
+    for step in range(steps):
+        outs[step][...] = out_ref[chip ^ step]
+
+
+def unpack_kernel(me_ref, *refs):
+    parts, (out_ref, floats_ref) = refs[:-2], refs[-2:]
+    tokens, heads, width = out_ref.shape
+    steps = len(parts)
+    per_chip = heads // steps
+    chip = lax.rem(me_ref[0] // 2, steps)
+    for step in range(steps):
+        for row in range(per_chip):
+            head = (chip ^ step) * per_chip + row
+            floats_ref[pl.ds(head, tokens, stride=heads), :] = parts[step][row].astype(jnp.float32)
+    out_ref[...] = floats_ref[...].reshape(tokens, heads, width).astype(jnp.bfloat16)
 
 
 def halves_plan(length, devices, query_states, key_states, value_states, query_gain, key_gain):
@@ -284,6 +325,7 @@
     group = heads // kv_heads
     half = devices // 2
     steps = half // 2
+    per_chip = kv_heads // steps
     bf16, f32 = jnp.bfloat16, jnp.float32
     me = lax.axis_index("seq")[None]
 
@@ -296,20 +338,28 @@
             scratch_shapes=scratch,
             compiler_params=pltpu.CompilerParams(vmem_limit_bytes=limit),
             name=name,
-        )(*([me] if specs is None or SMEM in specs else []), *operands)
-
-    def to_upper(step, array):
-        links = [(device, half + ((device // 2) ^ step) * 2 + device % 2) for device in range(half)]
+        )(me, *operands)
+
+    def to_upper(slot, array):
+        links = []
+        for device in range(half):
+            chip, core = device // 2, device % 2
+            links.append((device, half + (chip ^ (core * (steps // 2) + slot)) * 2 + core))
         return lax.ppermute(array, "seq", links)
 
-    def to_core(array, lowest):
-        return lax.ppermute(array, "seq", [(device, device ^ 1) for device in range(lowest, devices)])
+    def to_chip(step, array):
+        links = [(device, ((device // 2) ^ step) * 2 + device % 2) for device in range(devices)]
+        return lax.ppermute(array, "seq", links)
+
+    def to_core(array, count):
+        return lax.ppermute(array, "seq", [(device, device ^ 1) for device in range(count)])
 
     shape = jax.ShapeDtypeStruct
-    *pairs, near = call(
+    keep, give, *near = call(
         send_kernel,
         "send",
-        [shape((2, 2, tokens, width), bf16)] * steps + [shape((half, group + 2, tokens, width), bf16)],
+        [shape((steps // 2, per_chip, 2, tokens, width), bf16)] * 2
+        + [shape((per_chip * (2 + group), tokens, width), bf16)] * steps,
         query_states,
         key_states,
         value_states,
@@ -329,33 +379,47 @@
         ],
         limit=PACK_VMEM,
     )
-    groups = [list(range(half)), list(range(half, devices))]
-
-    def inside(array):
-        return lax.all_to_all(array, "seq", split_axis=0, concat_axis=0, axis_index_groups=groups, tiled=True)
-
-    far = [to_upper(step, pair) for step, pair in enumerate(pairs)]
-    arrived = lax.cond(me[0] >= 0, inside, jnp.zeros_like, near)
-    arrived, far = lax.optimization_barrier((arrived, far))
-    mine, others = call(
-        split_kernel, "split", [shape((steps, 2, tokens, width), bf16)] * 2, *far, specs=[VMEM] * steps
-    )
-    neighbours = to_core(others, half)
-    lanes = half * group * tokens
-    state = [shape((1, lanes), f32), shape((1, lanes), f32), shape((width, lanes), f32)]
-    positions = np.broadcast_to(np.arange(half * tokens, dtype=np.int32).reshape(half, 1, tokens), (half, group, tokens))
-    carried = call(near_kernel, "near", state, jnp.asarray(positions.reshape(1, lanes)), arrived, specs=[VMEM] * 2)
-
-    attended = call(
-        functools.partial(last_kernel, half),
-        "last",
-        shape((half, group, tokens, width), bf16),
-        arrived,
-        mine,
-        neighbours,
+    got = to_core(give, half)
+    joined = pl.pallas_call(
+        join_kernel,
+        out_shape=[shape((2, per_chip, 2, tokens, width), bf16)] * (steps // 2),
+        in_specs=[VMEM] * 2,
+        out_specs=[VMEM] * (steps // 2),
+        name="join",
+    )(keep, got)
+    far = [to_upper(slot, array) for slot, array in enumerate(joined)]
+    near = [near[0]] + [to_chip(step, near[step]) for step in range(1, steps)]
+    pairs, queries = call(
+        gather_kernel,
+        "gather",
+        [shape((2 * steps, per_chip, 2, tokens, width), bf16), shape((steps, per_chip, group, tokens, width), bf16)],
+        *near,
+        *far,
+    )
+    others = to_core(pairs, devices)
+    lanes = steps * group * tokens
+    state = [shape((per_chip, 1, lanes), f32), shape((per_chip, 1, lanes), f32), shape((per_chip, width, lanes), f32)]
+    block, _, token = np.indices((steps, group, tokens), dtype=np.int32)
+    bounds = np.stack([block * tokens + token + 1, block * tokens]).reshape(2, lanes)
+    carried = call(functools.partial(first_kernel, half), "first", state, jnp.asarray(bounds), queries, pairs)
+    returned = call(
+        functools.partial(second_kernel, half),
+        "second",
+        [shape((per_chip * group, tokens, width), bf16)] * steps,
+        jnp.asarray(bounds),
+        queries,
+        others,
         *carried,
-    )
-    return jnp.transpose(inside(attended).reshape(heads, tokens, width), (1, 0, 2))
+        scratch=[pltpu.VMEM((steps, per_chip * group, tokens, width), bf16)],
+    )
+    returned = [returned[0]] + [to_chip(step, returned[step]) for step in range(1, steps)]
+    return call(
+        unpack_kernel,
+        "unpack",
+        shape((tokens, heads, width), bf16),
+        *returned,
+        scratch=[pltpu.VMEM((tokens * heads, width), f32)],
+    )
 
 
 def solution(mesh):

time: 55.7 us -> 55.7 us (level)
  blocking collectives: 36.7 us -> 0 us
  waiting for transfers between devices: 0.01 us -> 22.2 us
  starting transfers between devices: 7.1 us -> 15.4 us
  Pallas kernels: 10.6 us -> 16.9 us
    all_to_all x2 -> x0, blocking collectives: 36.7 us -> none  [inside(): lax.all_to_all(array, 'seq', split_axis=0, concat_axis=0, axis_index_grou...]
    ppermute x4 -> x2, waiting for transfers between devices: 0.01 us -> 11.3 us  [to_upper(): return lax.ppermute(array, 'seq', links)]
    ppermute x1 -> x8, waiting for transfers between devices: 0.01 us -> 10.9 us  [the longest x6 10.9 us: to_chip(): return lax.ppermute(array, 'seq', links)]
    ppermute x1 -> x8, starting transfers between devices: 1.93 us -> 12.8 us  [the longest x6 10.3 us: to_chip(): return lax.ppermute(array, 'seq', links)]
    pallas_call x4 -> x5, Pallas kernels: 10.6 us -> 15 us  [call(): pl.pallas_call(kernel, out_shape=outs, in_specs=specs or [SMEM] + [VMEM]...]
    ppermute x4 -> x2, starting transfers between devices: 5.17 us -> 2.57 us  [to_upper(): return lax.ppermute(array, 'seq', links)]
    pallas_call x0 -> x1, Pallas kernels: none -> 1.89 us  [halves_plan(): pl.pallas_call(join_kernel, out_shape=[shape((2, per_chip, 2, tokens, wid...]
    reshape x1 -> x0, local copies, waits for them, and re-layouts: 0.89 us -> none  [halves_plan(): inside(attended).reshape(heads, tokens, width)]
  transfers between devices with their start and end apart: 5 -> 10, of which waited for: 0 -> 6; matrix products, arithmetic and copies ran while one was open for 0% -> 0% of each run, Pallas kernels for 6% -> 11%
where the time goes in v9:
time: 55.7 us; the launch traced here: 55.3 us
  waiting for transfers between devices  22.2 us (40%)
  Pallas kernels  16.9 us (30%)
  starting transfers between devices  15.4 us (28%)
  local copies, waits for them, and re-layouts  0.7 us (1%)
    pallas_call x5, Pallas kernels, call(): pl.pallas_call(kernel, out_shape=outs, in_specs=specs or [SMEM] + [VMEM]...  15 us
    ppermute x2, waiting for transfers between devices, to_upper(): return lax.ppermute(array, 'seq', links)  11.3 us
    ppermute x6, waiting for transfers between devices, to_chip(): return lax.ppermute(array, 'seq', links)  10.9 us
    ppermute x6, starting transfers between devices, to_chip(): return lax.ppermute(array, 'seq', links)  10.3 us
    ppermute x2, starting transfers between devices, to_upper(): return lax.ppermute(array, 'seq', links)  2.57 us
    ppermute x2, starting transfers between devices, to_core(): lax.ppermute(array, 'seq', [(device, device ^ 1) for device in range(coun...  2.51 us
    pallas_call x1, Pallas kernels, halves_plan(): pl.pallas_call(join_kernel, out_shape=[shape((2, per_chip, 2, tokens, wid...  1.89 us
  transfers between devices with their start and end apart: 10, of which 6 were waited for; matrix products, arithmetic and copies ran while one was open for 0% of the time, Pallas kernels for 11%

profile of v9, /device:TPU:16, one launch (start us, length us, event | category | flops | bytes accessed | tf_op | source)
XLA Modules:
  0.0 55.3 jit_solution(7881865670944619304)
XLA Ops:
  0.0 4.2 %send.1 = (bf16[2,2,2,112,128]{4,3,2,1,0:T(8,128)(2,1)}, bf16[2,2,2,112,128]{4,3,2,1,0:T(8,128)(2,1)}, bf16[8,112,128]{2,1,0:T(8,128)(2,1)}, bf16[8,112,128]{2,1...) custom-call(s32[1]{0:T(128)} %bitcast.me_ref, bf16[112,16,128]{2,1,0:T(8,128)(2,1)} %q_hbm.1, ...), custom_call_target="tpu_custom_call" | custom-call | tf_op jit(solution)/shard_map/send/pallas_call | solution.py:333
  4.2 0.7 %collective-permute-start.3 = (bf16[2,2,2,112,128]{4,3,2,1,0:T(8,128)(2,1)}, bf16[2,2,2,112,128]{4,3,2,1,0:T(8,128)(2,1)S(1)}, u32[]{:S(2)}, u32[]{:S(2)}) collective-permute-start(bf16[2,2,2,112,128]{4,3,2,1,0:T(8,128)(2,1)} %get-tuple-element.27), channel_id=1, source_target_pairs={{0,1},{1,0},{2,3},{3,2},{4,5},{5,4},{6,7},{7,6},{16,17},{17,16},{1... | collective-permute-start | bytes 688136 | tf_op jit(solution)/shard_map/ppermute | solution.py:355
  4.9 1.6 %collective-permute-start = (bf16[8,112,128]{2,1,0:T(8,128)(2,1)}, bf16[8,112,128]{2,1,0:T(8,128)(2,1)S(1)}, u32[]{:S(2)}, u32[]{:S(2)}) collective-permute-start(bf16[8,112,128]{2,1,0:T(8,128)(2,1)} %get-tuple-element.23), channel_id=1, source_target_pairs={{0,2},{1,3},{2,0},{3,1},{4,6},{5,7},{6,4},{7,5},{8,10},{9,11},{10,... | collective-permute-start | bytes 688136 | tf_op jit(solution)/shard_map/ppermute | solution.py:352
  6.5 1.6 %collective-permute-start.1 = (bf16[8,112,128]{2,1,0:T(8,128)(2,1)}, bf16[8,112,128]{2,1,0:T(8,128)(2,1)S(1)}, u32[]{:S(2)}, u32[]{:S(2)}) collective-permute-start(bf16[8,112,128]{2,1,0:T(8,128)(2,1)} %get-tuple-element.24), channel_id=1, source_target_pairs={{0,4},{1,5},{2,6},{3,7},{4,0},{5,1},{6,2},{7,3},{8,12},{9,13},{10,... | collective-permute-start | bytes 688136 | tf_op jit(solution)/shard_map/ppermute | solution.py:352
  8.0 0.4 collective-permute-start.2
  8.4 0.0 collective-permute-done.3.got_ref
  8.4 0.0 copy-start.2
  8.4 0.7 %copy-done.2 = bf16[2,2,2,112,128]{4,3,2,1,0:T(8,128)(2,1)} copy-done((bf16[2,2,2,112,128]{4,3,2,1,0:T(8,128)(2,1)}, bf16[2,2,2,112,128]{4,3,2,1,0:T(8,128)(2,1)S(1)}, u32[]{:S(2)}) %copy-start.2) | copy-done | bytes 229400
  9.1 0.0 copy-start
  9.1 1.9 %join.1 = (bf16[2,2,2,112,128]{4,3,2,1,0:T(8,128)(2,1)}, bf16[2,2,2,112,128]{4,3,2,1,0:T(8,128)(2,1)}) custom-call(bf16[2,2,2,112,128]{4,3,2,1,0:T(8,128)(2,1)} %get-tuple-element.26.keep_ref, bf16[2,2,2,112,128]{4,3,2,1,0:T(8,128)(2,1)} %copy-done.2), custom_call_target="tpu_custom_call" | custom-call | tf_op jit(solution)/shard_map/join/pallas_call | solution.py:383
  11.0 1.3 %collective-permute-start.4 = (bf16[2,2,2,112,128]{4,3,2,1,0:T(8,128)(2,1)}, bf16[2,2,2,112,128]{4,3,2,1,0:T(8,128)(2,1)S(1)}, u32[]{:S(2)}, u32[]{:S(2)}) collective-permute-start(bf16[2,2,2,112,128]{4,3,2,1,0:T(8,128)(2,1)} %get-tuple-element.28), channel_id=1, source_target_pairs={{0,8},{1,13},{2,10},{3,15},{4,12},{5,9},{6,14},{7,11},{16,24},{17,... | collective-permute-start | bytes 688136 | tf_op jit(solution)/shard_map/ppermute | solution.py:348
  12.3 1.3 %collective-permute-start.5 = (bf16[2,2,2,112,128]{4,3,2,1,0:T(8,128)(2,1)}, bf16[2,2,2,112,128]{4,3,2,1,0:T(8,128)(2,1)S(1)}, u32[]{:S(2)}, u32[]{:S(2)}) collective-permute-start(bf16[2,2,2,112,128]{4,3,2,1,0:T(8,128)(2,1)} %get-tuple-element.29), channel_id=1, source_target_pairs={{0,10},{1,15},{2,8},{3,13},{4,14},{5,11},{6,12},{7,9},{16,26},{17,... | collective-permute-start | bytes 688136 | tf_op jit(solution)/shard_map/ppermute | solution.py:348
  13.6 0.0 collective-permute-done.refs_1_
  13.6 1.6 %collective-permute-done.1.refs_2_ = bf16[8,112,128]{2,1,0:T(8,128)(2,1)S(1)} collective-permute-done((bf16[8,112,128]{2,1,0:T(8,128)(2,1)}, bf16[8,112,128]{2,1,0:T(8,128)(2,1)S(1)}, u32[]{:S(2)}, u32[]{:S(2)}) %collective-permute-start.1) | collective-permute-done | bytes 229408 | tf_op jit(solution)/shard_map/ppermute | solution.py:352
  15.2 3.8 %collective-permute-done.2.refs_3_ = bf16[8,112,128]{2,1,0:T(8,128)(2,1)S(1)} collective-permute-done((bf16[8,112,128]{2,1,0:T(8,128)(2,1)}, bf16[8,112,128]{2,1,0:T(8,128)(2,1)S(1)}, u32[]{:S(2)}, u32[]{:S(2)}) %collective-permute-start.2) | collective-permute-done | bytes 229408 | tf_op jit(solution)/shard_map/ppermute | solution.py:352
  19.1 7.1 %collective-permute-done.4.refs_4_ = bf16[2,2,2,112,128]{4,3,2,1,0:T(8,128)(2,1)S(1)} collective-permute-done((bf16[2,2,2,112,128]{4,3,2,1,0:T(8,128)(2,1)}, bf16[2,2,2,112,128]{4,3,2,1,0:T(8,128)(2,1)S(1)}, u32[]{:S(2)}, u32[]{:S(2)}) %collective-permute-start.4) | collective-permute-done | bytes 229408 | tf_op jit(solution)/shard_map/ppermute | solution.py:348
  26.2 4.1 %collective-permute-done.5.refs_5_ = bf16[2,2,2,112,128]{4,3,2,1,0:T(8,128)(2,1)S(1)} collective-permute-done((bf16[2,2,2,112,128]{4,3,2,1,0:T(8,128)(2,1)}, bf16[2,2,2,112,128]{4,3,2,1,0:T(8,128)(2,1)S(1)}, u32[]{:S(2)}, u32[]{:S(2)}) %collective-permute-start.5) | collective-permute-done | bytes 229408 | tf_op jit(solution)/shard_map/ppermute | solution.py:348
  30.3 0.0 copy-done
  30.3 0.0 copy-start.1
  30.3 0.1 gather.1
  30.4 1.8 %collective-permute-start.6 = (bf16[8,2,2,112,128]{4,3,2,1,0:T(8,128)(2,1)S(1)}, bf16[8,2,2,112,128]{4,3,2,1,0:T(8,128)(2,1)S(1)}, u32[]{:S(2)}, u32[]{:S(2)}) collective-permute-start(bf16[8,2,2,112,128]{4,3,2,1,0:T(8,128)(2,1)S(1)} %get-tuple-element.31.pair_ref), channel_id=1, source_target_pairs={{0,1},{1,0},{2,3},{3,2},{4,5},{5,4},{6,7},{7,6},{8,9},{9,8},{10,11... | collective-permute-start | bytes 2752520 | tf_op jit(solution)/shard_map/ppermute | solution.py:355
  32.3 0.0 copy-done.1
  32.3 4.2 %first.1 = (f32[2,1,896]{2,1,0:T(1,128)S(1)}, f32[2,1,896]{2,1,0:T(1,128)S(1)}, f32[2,128,896]{2,1,0:T(8,128)S(1)}) custom-call(s32[1]{0:T(128)} %bitcast.me_ref, s32[2,896]{1,0:T(2,128)S(1)} %copy-done.1, bf16[4,2,2,112,128]{4,3,2,1,0:T(8,128)(2,1)S(1)} %get-tuple-element.30.query_ref, bf16[8,2,2,112,128]{4,3,2,1,0:T(8,128)(2,1)S(1)} %get-tuple-element.31.pair_ref), custom_call_target="tpu_custom_call" | custom-call | tf_op jit(solution)/shard_map/first/pallas_call | solution.py:333
  36.5 0.0 collective-permute-done.6.pair_ref
  36.5 5.3 %second.1 = (bf16[4,112,128]{2,1,0:T(8,128)(2,1)S(1)}, bf16[4,112,128]{2,1,0:T(8,128)(2,1)S(1)}, bf16[4,112,128]{2,1,0:T(8,128)(2,1)S(1)}, bf16[4,112,128]{2,1,0:T(8,128)(2,1)S(1)}) custom-call(s32[1]{0:T(128)} %bitcast.me_ref, s32[2,896]{1,0:T(2,128)S(1)} %copy-done.1, bf16[4,2,2,112,128]{4,3,2,1,0:T(8,128)(2,1)S(1)} %get-tuple-element.30.query_ref, ...), custom_call_target="tpu_custom_call" | custom-call | tf_op jit(solution)/shard_map/second/pallas_call | solution.py:333
  41.8 0.6 %collective-permute-start.7 = (bf16[4,112,128]{2,1,0:T(8,128)(2,1)S(1)}, bf16[4,112,128]{2,1,0:T(8,128)(2,1)S(1)}, u32[]{:S(2)}, u32[]{:S(2)}) collective-permute-start(bf16[4,112,128]{2,1,0:T(8,128)(2,1)S(1)} %get-tuple-element.36), channel_id=1, source_target_pairs={{0,2},{1,3},{2,0},{3,1},{4,6},{5,7},{6,4},{7,5},{8,10},{9,11},{10,... | collective-permute-start | bytes 344072 | tf_op jit(solution)/shard_map/ppermute | solution.py:352
  42.4 5.2 %collective-permute-start.8 = (bf16[4,112,128]{2,1,0:T(8,128)(2,1)S(1)}, bf16[4,112,128]{2,1,0:T(8,128)(2,1)S(1)}, u32[]{:S(2)}, u32[]{:S(2)}) collective-permute-start(bf16[4,112,128]{2,1,0:T(8,128)(2,1)S(1)} %get-tuple-element.37), channel_id=1, source_target_pairs={{0,4},{1,5},{2,6},{3,7},{4,0},{5,1},{6,2},{7,3},{8,12},{9,13},{10,... | collective-permute-start | bytes 344072 | tf_op jit(solution)/shard_map/ppermute | solution.py:352
  47.6 1.0 %collective-permute-start.9 = (bf16[4,112,128]{2,1,0:T(8,128)(2,1)S(1)}, bf16[4,112,128]{2,1,0:T(8,128)(2,1)S(1)}, u32[]{:S(2)}, u32[]{:S(2)}) collective-permute-start(bf16[4,112,128]{2,1,0:T(8,128)(2,1)S(1)} %get-tuple-element.38), channel_id=1, source_target_pairs={{0,6},{1,7},{2,4},{3,5},{4,2},{5,3},{6,0},{7,1},{8,14},{9,15},{10,... | collective-permute-start | bytes 344072 | tf_op jit(solution)/shard_map/ppermute | solution.py:352
  48.5 0.0 collective-permute-done.7.refs_1_
  48.5 2.6 %collective-permute-done.8.refs_2_ = bf16[4,112,128]{2,1,0:T(8,128)(2,1)S(1)} collective-permute-done((bf16[4,112,128]{2,1,0:T(8,128)(2,1)S(1)}, bf16[4,112,128]{2,1,0:T(8,128)(2,1)S(1)}, u32[]{:S(2)}, u32[]{:S(2)}) %collective-permute-start.8) | collective-permute-done | bytes 114720 | tf_op jit(solution)/shard_map/ppermute | solution.py:352
  51.1 2.9 %collective-permute-done.9.refs_3_ = bf16[4,112,128]{2,1,0:T(8,128)(2,1)S(1)} collective-permute-done((bf16[4,112,128]{2,1,0:T(8,128)(2,1)S(1)}, bf16[4,112,128]{2,1,0:T(8,128)(2,1)S(1)}, u32[]{:S(2)}, u32[]{:S(2)}) %collective-permute-start.9) | collective-permute-done | bytes 114720 | tf_op jit(solution)/shard_map/ppermute | solution.py:352
  54.0 1.3 %unpack.1 = bf16[112,16,128]{2,1,0:T(8,128)(2,1)} custom-call(s32[1]{0:T(128)} %bitcast.me_ref, bf16[4,112,128]{2,1,0:T(8,128)(2,1)S(1)} %get-tuple-element.35.refs_0_, bf16[4,112,128]{2,1,0:T(8,128)(2,1)S(1)} %collective-permute-done.7.refs_1_, bf16[4,112,128]{2,1,0:T(8,128)(2,1)S(1)} %collective-permute-done.8.refs_2_, ...), custom_call_target="tpu_custom_call" | custom-call | tf_op jit(solution)/shard_map/unpack/pallas_call | solution.py:333
Async XLA Ops:
  4.2 4.2 %collective-permute-start.3 = (bf16[2,2,2,112,128]{4,3,2,1,0:T(8,128)(2,1)}, bf16[2,2,2,112,128]{4,3,2,1,0:T(8,128)(2,1)S(1)}, u32[]{:S(2)}, u32[]{:S(2)}) collective-permute-start(bf16[2,2,2,112,128]{4,3,2,1,0:T(8,128)(2,1)} %get-tuple-element.27), channel_id=1, source_target_pairs={{0,1},{1,0},{2,3},{3,2},{4,5},{5,4},{6,7},{7,6},{16,17},{17,16},{1... | collective-permute-start | bytes 688136 | tf_op jit(solution)/shard_map/ppermute | solution.py:355
  4.9 8.7 %collective-permute-start = (bf16[8,112,128]{2,1,0:T(8,128)(2,1)}, bf16[8,112,128]{2,1,0:T(8,128)(2,1)S(1)}, u32[]{:S(2)}, u32[]{:S(2)}) collective-permute-start(bf16[8,112,128]{2,1,0:T(8,128)(2,1)} %get-tuple-element.23), channel_id=1, source_target_pairs={{0,2},{1,3},{2,0},{3,1},{4,6},{5,7},{6,4},{7,5},{8,10},{9,11},{10,... | collective-permute-start | bytes 688136 | tf_op jit(solution)/shard_map/ppermute | solution.py:352
  6.5 8.7 %collective-permute-start.1 = (bf16[8,112,128]{2,1,0:T(8,128)(2,1)}, bf16[8,112,128]{2,1,0:T(8,128)(2,1)S(1)}, u32[]{:S(2)}, u32[]{:S(2)}) collective-permute-start(bf16[8,112,128]{2,1,0:T(8,128)(2,1)} %get-tuple-element.24), channel_id=1, source_target_pairs={{0,4},{1,5},{2,6},{3,7},{4,0},{5,1},{6,2},{7,3},{8,12},{9,13},{10,... | collective-permute-start | bytes 688136 | tf_op jit(solution)/shard_map/ppermute | solution.py:352
  8.0 11.0 %collective-permute-start.2 = (bf16[8,112,128]{2,1,0:T(8,128)(2,1)}, bf16[8,112,128]{2,1,0:T(8,128)(2,1)S(1)}, u32[]{:S(2)}, u32[]{:S(2)}) collective-permute-start(bf16[8,112,128]{2,1,0:T(8,128)(2,1)} %get-tuple-element.25), channel_id=1, source_target_pairs={{0,6},{1,7},{2,4},{3,5},{4,2},{5,3},{6,0},{7,1},{8,14},{9,15},{10,... | collective-permute-start | bytes 688136 | tf_op jit(solution)/shard_map/ppermute | solution.py:352
  8.4 0.7 %copy-start.2 = (bf16[2,2,2,112,128]{4,3,2,1,0:T(8,128)(2,1)}, bf16[2,2,2,112,128]{4,3,2,1,0:T(8,128)(2,1)S(1)}, u32[]{:S(2)}) copy-start(bf16[2,2,2,112,128]{4,3,2,1,0:T(8,128)(2,1)S(1)} %collective-permute-done.3.got_ref) | copy-start | bytes 688132
  9.1 21.2 %copy-start = (bf16[8,112,128]{2,1,0:T(8,128)(2,1)S(1)}, bf16[8,112,128]{2,1,0:T(8,128)(2,1)}, u32[]{:S(2)}) copy-start(bf16[8,112,128]{2,1,0:T(8,128)(2,1)} %get-tuple-element.22.refs_0_) | copy-start | bytes 688132
  11.0 15.2 %collective-permute-start.4 = (bf16[2,2,2,112,128]{4,3,2,1,0:T(8,128)(2,1)}, bf16[2,2,2,112,128]{4,3,2,1,0:T(8,128)(2,1)S(1)}, u32[]{:S(2)}, u32[]{:S(2)}) collective-permute-start(bf16[2,2,2,112,128]{4,3,2,1,0:T(8,128)(2,1)} %get-tuple-element.28), channel_id=1, source_target_pairs={{0,8},{1,13},{2,10},{3,15},{4,12},{5,9},{6,14},{7,11},{16,24},{17,... | collective-permute-start | bytes 688136 | tf_op jit(solution)/shard_map/ppermute | solution.py:348
  12.3 18.0 %collective-permute-start.5 = (bf16[2,2,2,112,128]{4,3,2,1,0:T(8,128)(2,1)}, bf16[2,2,2,112,128]{4,3,2,1,0:T(8,128)(2,1)S(1)}, u32[]{:S(2)}, u32[]{:S(2)}) collective-permute-start(bf16[2,2,2,112,128]{4,3,2,1,0:T(8,128)(2,1)} %get-tuple-element.29), channel_id=1, source_target_pairs={{0,10},{1,15},{2,8},{3,13},{4,14},{5,11},{6,12},{7,9},{16,26},{17,... | collective-permute-start | bytes 688136 | tf_op jit(solution)/shard_map/ppermute | solution.py:348
  30.3 1.9 %copy-start.1 = (s32[2,896]{1,0:T(2,128)S(1)}, s32[2,896]{1,0:T(2,128)}, u32[]{:S(2)}) copy-start(s32[2,896]{1,0:T(2,128)} %constant.9.clone.bounds_ref) | copy-start | bytes 21508
  30.4 6.0 %collective-permute-start.6 = (bf16[8,2,2,112,128]{4,3,2,1,0:T(8,128)(2,1)S(1)}, bf16[8,2,2,112,128]{4,3,2,1,0:T(8,128)(2,1)S(1)}, u32[]{:S(2)}, u32[]{:S(2)}) collective-permute-start(bf16[8,2,2,112,128]{4,3,2,1,0:T(8,128)(2,1)S(1)} %get-tuple-element.31.pair_ref), channel_id=1, source_target_pairs={{0,1},{1,0},{2,3},{3,2},{4,5},{5,4},{6,7},{7,6},{8,9},{9,8},{10,11... | collective-permute-start | bytes 2752520 | tf_op jit(solution)/shard_map/ppermute | solution.py:355
  41.8 6.7 %collective-permute-start.7 = (bf16[4,112,128]{2,1,0:T(8,128)(2,1)S(1)}, bf16[4,112,128]{2,1,0:T(8,128)(2,1)S(1)}, u32[]{:S(2)}, u32[]{:S(2)}) collective-permute-start(bf16[4,112,128]{2,1,0:T(8,128)(2,1)S(1)} %get-tuple-element.36), channel_id=1, source_target_pairs={{0,2},{1,3},{2,0},{3,1},{4,6},{5,7},{6,4},{7,5},{8,10},{9,11},{10,... | collective-permute-start | bytes 344072 | tf_op jit(solution)/shard_map/ppermute | solution.py:352
  42.4 8.8 %collective-permute-start.8 = (bf16[4,112,128]{2,1,0:T(8,128)(2,1)S(1)}, bf16[4,112,128]{2,1,0:T(8,128)(2,1)S(1)}, u32[]{:S(2)}, u32[]{:S(2)}) collective-permute-start(bf16[4,112,128]{2,1,0:T(8,128)(2,1)S(1)} %get-tuple-element.37), channel_id=1, source_target_pairs={{0,4},{1,5},{2,6},{3,7},{4,0},{5,1},{6,2},{7,3},{8,12},{9,13},{10,... | collective-permute-start | bytes 344072 | tf_op jit(solution)/shard_map/ppermute | solution.py:352
  47.6 6.4 %collective-permute-start.9 = (bf16[4,112,128]{2,1,0:T(8,128)(2,1)S(1)}, bf16[4,112,128]{2,1,0:T(8,128)(2,1)S(1)}, u32[]{:S(2)}, u32[]{:S(2)}) collective-permute-start(bf16[4,112,128]{2,1,0:T(8,128)(2,1)S(1)} %get-tuple-element.38), channel_id=1, source_target_pairs={{0,6},{1,7},{2,4},{3,5},{4,2},{5,3},{6,0},{7,1},{8,14},{9,15},{10,... | collective-permute-start | bytes 344072 | tf_op jit(solution)/shard_map/ppermute | solution.py:352

commit v10 on v9

--- a/solution.py
+++ b/solution.py
@@ -163,81 +163,85 @@
     return (scaled * cosine + pltpu.roll(scaled, scaled.shape[1] // 2, 1) * sine).astype(jnp.bfloat16)
 
 
-def send_kernel(me_ref, q_hbm, k_hbm, v_hbm, table_hbm, query_gain_ref, key_gain_ref, *refs):
-    (keep_ref, give_ref), fulls = refs[:2], refs[2:-8]
-    q_ref, k_ref, v_ref, table_ref, qf_ref, kf_ref, vf_ref, sems = refs[-8:]
-    steps, slots = len(fulls), keep_ref.shape[0]
+def send_kernel(me_ref, q_hbm, k_hbm, v_hbm, other_k_hbm, other_v_hbm, table_hbm, query_gain_ref, key_gain_ref, *refs):
+    outs, (q_ref, k_ref, v_ref, table_ref, qf_ref, kf_ref, vf_ref, sems) = refs[:-8], refs[-8:]
     tokens, heads, width = q_ref.shape
-    kv_heads, per_chip = k_ref.shape[1], keep_ref.shape[1]
+    slots, per_chip = (len(outs) // 3), outs[0].shape[1]
+    far, fulls = outs[:slots], outs[slots:]
+    steps, kv_heads = len(fulls), k_ref.shape[2]
     first, per_full = 2 * per_chip, heads // steps
     me = me_ref[0]
     chip, core = lax.rem(me // 2, steps), lax.rem(me, 2)
-    start = pl.multiple_of(me * tokens, 8)
-    copies = [
-        pltpu.make_async_copy(k_hbm, k_ref, sems.at[0]),
-        pltpu.make_async_copy(table_hbm.at[pl.ds(start, tokens)], table_ref, sems.at[1]),
-        pltpu.make_async_copy(v_hbm, v_ref, sems.at[2]),
-        pltpu.make_async_copy(q_hbm, q_ref, sems.at[3]),
-    ]
+    copies = []
+    for side, (k, v, device) in enumerate(((k_hbm, v_hbm, me), (other_k_hbm, other_v_hbm, me + 1 - 2 * core))):
+        rows = pl.ds(pl.multiple_of(device * tokens, 8), tokens)
+        for kind, (source, target) in enumerate(((k, k_ref), (table_hbm.at[rows], table_ref), (v, v_ref))):
+            copies.append(pltpu.make_async_copy(source, target.at[side], sems.at[3 * side + kind]))
+    copies.insert(3, pltpu.make_async_copy(q_hbm, q_ref, sems.at[6]))
     for copy in copies:
         copy.start()
-    copies[0].wait()
-    kf_ref[...] = normalize(k_ref[...].reshape(tokens * kv_heads, width))
-    copies[1].wait()
-    cosine, sine = rope_factors(table_ref[...])
-    copies[2].wait()
-    vf_ref[...] = v_ref[...].astype(jnp.float32).reshape(tokens * kv_heads, width)
-    for slot in range(steps):
-        step = lax.rem(core * slots + slot, steps)
-        ref = keep_ref if slot < slots else give_ref
+    key_gain = key_gain_ref[...]
+
+    def keys_of(head, factors):
+        return turn(kf_ref[pl.ds(head, tokens, stride=kv_heads), :], key_gain, *factors)
+
+    def values_of(head):
+        return vf_ref[pl.ds(head, tokens, stride=kv_heads), :].astype(jnp.bfloat16)
+
+    def load(side, waits):
+        for copy in waits:
+            copy.wait()
+        kf_ref[...] = normalize(k_ref[side].reshape(tokens * kv_heads, width))
+        vf_ref[...] = v_ref[side].astype(jnp.float32).reshape(tokens * kv_heads, width)
+        return rope_factors(table_ref[side])
+
+    factors = load(0, copies[:3])
+    for step in range(steps):
         for row in range(per_chip):
             head = (chip ^ step) * per_chip + row
-            ref[slot % slots, row, 0] = turn(
-                kf_ref[pl.ds(head, tokens, stride=kv_heads), :], key_gain_ref[...], cosine, sine
-            )
-            ref[slot % slots, row, 1] = vf_ref[pl.ds(head, tokens, stride=kv_heads), :].astype(jnp.bfloat16)
-    for slot in range(slots):
-        for row in range(first):
-            part = (slot, row // 2, row % 2)
-
-            @pl.when(core == 0)
-            def _():
-                fulls[slot][row], fulls[slots + slot][row] = keep_ref[part], give_ref[part]
-
-            @pl.when(core == 1)
-            def _():
-                fulls[slot][row], fulls[slots + slot][row] = give_ref[part], keep_ref[part]
-
+            fulls[step][2 * row], fulls[step][2 * row + 1] = keys_of(head, factors), values_of(head)
     copies[3].wait()
     qf_ref[...] = normalize(q_ref[...].reshape(tokens * heads, width))
     for step in range(steps):
         for row in range(per_full):
             normed = qf_ref[pl.ds((chip ^ step) * per_full + row, tokens, stride=heads), :]
-            fulls[step][first + row] = turn(normed, query_gain_ref[...], cosine, sine)
-
-
-def weigh(keys, values, queries, allowed, state):
-    scale = math.log2(math.e) / math.sqrt(keys.shape[1])
-    scores = lax.dot_general(keys, queries, CONTRACT, preferred_element_type=jnp.float32)
-    if allowed is not None:
-        scores = jnp.where(allowed, scores, MASKED)
-    highest = jnp.max(scores, axis=0, keepdims=True)
-    if state is not None:
-        highest = jnp.maximum(state[0], highest)
-    probs = jnp.exp2((scores - highest) * scale)
-    total = jnp.sum(probs, axis=0, keepdims=True)
-    weighted = lax.dot_general(
-        values, probs.astype(jnp.bfloat16), (((0,), (0,)), ((), ())), preferred_element_type=jnp.float32
-    )
+            fulls[step][first + row] = turn(normed, query_gain_ref[...], *factors)
+    for which in range(2):
+
+        @pl.when(core == which)
+        def _():
+            for slot in range(slots):
+                for row in range(first):
+                    far[slot][0, row // 2, row % 2] = fulls[which * slots + slot][row]
+
+    factors = load(1, copies[4:])
+    for slot in range(slots):
+        for row in range(per_chip):
+            head = (chip ^ (core * slots + slot)) * per_chip + row
+            far[slot][1, row, 0], far[slot][1, row, 1] = keys_of(head, factors), values_of(head)
+
+
+def weigh(segments, queries, state):
+    scale = math.log2(math.e) / math.sqrt(queries.shape[1])
+    scores = []
+    for keys, _, allowed in segments:
+        part = lax.dot_general(keys, queries, CONTRACT, preferred_element_type=jnp.float32)
+        scores.append(part if allowed is None else jnp.where(allowed, part, MASKED))
+    tops = [jnp.max(part, axis=0, keepdims=True) for part in scores] + ([] if state is None else [state[0]])
+    highest = functools.reduce(jnp.maximum, tops)
+    total = weighted = None
     if state is not None:
         factor = jnp.exp2((state[0] - highest) * scale)
-        total, weighted = state[1] * factor + total, state[2] * factor + weighted
+        total, weighted = state[1] * factor, state[2] * factor
+    for part, (_, values, _) in zip(scores, segments):
+        probs = jnp.exp2((part - highest) * scale)
+        added = jnp.sum(probs, axis=0, keepdims=True)
+        summed = lax.dot_general(
+            values, probs.astype(jnp.bfloat16), (((0,), (0,)), ((), ())), preferred_element_type=jnp.float32
+        )
+        total = added if total is None else total + added
+        weighted = summed if weighted is None else weighted + summed
     return highest, total, weighted
-
-
-def join_kernel(keep_ref, got_ref, *outs):
-    for slot, ref in enumerate(outs):
-        ref[0], ref[1] = keep_ref[slot], got_ref[slot]
 
 
 def gather_kernel(me_ref, *refs):
@@ -258,24 +262,23 @@
 
     def tiles(with_far):
         for head in range(kv_heads):
+
+            def segment(start, stop, allowed):
+                rows = (stop - start) * tokens
+                return [pair_ref[start:stop, head, i].reshape(rows, width) for i in range(2)] + [allowed]
+
             for first in range(0, steps, TILE_BLOCKS):
                 count = first + TILE_BLOCKS
                 place = slice(first * group * tokens, first * group * tokens + lanes)
-                keys, values = [
-                    jnp.concatenate(
-                        [pair_ref[:count, head, i].reshape(count * tokens, width)]
-                        + ([pair_ref[steps:, head, i].reshape(steps * tokens, width)] if with_far else []),
-                        axis=0,
-                    )
-                    for i in range(2)
-                ]
                 queries = query_ref[first:count, head].reshape(lanes, width)
-                index = lax.broadcasted_iota(jnp.int32, (keys.shape[0], lanes), 0)
-                allowed = index < bound[:, place]
+                index = first * tokens + lax.broadcasted_iota(jnp.int32, (TILE_BLOCKS * tokens, lanes), 0)
+                segments = [segment(first, count, index < bound[:, place])]
+                if first > 0:
+                    segments.append(segment(0, first, None))
                 if with_far:
-                    allowed = jnp.logical_or(allowed, index >= count * tokens)
+                    segments.append(segment(steps, 2 * steps, None))
                 state = [ref[head, :, place] for ref in state_refs] if state_refs else None
-                store(head, first, place, *weigh(keys, values, queries, allowed, state))
+                store(head, first, place, *weigh(segments, queries, state))
 
     pl.when(upper)(functools.partial(tiles, True))
     pl.when(jnp.logical_not(upper))(functools.partial(tiles, False))
@@ -355,38 +358,34 @@
         return lax.ppermute(array, "seq", [(device, device ^ 1) for device in range(count)])
 
     shape = jax.ShapeDtypeStruct
-    keep, give, *near = call(
+    slots = steps // 2
+    others = [to_core(array, half) for array in (key_states, value_states)]
+    packed = call(
         send_kernel,
         "send",
-        [shape((steps // 2, per_chip, 2, tokens, width), bf16)] * 2
+        [shape((2, per_chip, 2, tokens, width), bf16)] * slots
         + [shape((per_chip * (2 + group), tokens, width), bf16)] * steps,
         query_states,
         key_states,
         value_states,
+        *others,
         jnp.asarray(rope_table(length, width)),
         query_gain[None],
         key_gain[None],
-        specs=[SMEM, HBM, HBM, HBM, HBM, VMEM, VMEM],
+        specs=[SMEM] + [HBM] * 3 + [pl.BlockSpec(memory_space=pl.ANY)] * 2 + [HBM] + [VMEM] * 2,
         scratch=[
             pltpu.VMEM((tokens, heads, width), bf16),
-            pltpu.VMEM((tokens, kv_heads, width), bf16),
-            pltpu.VMEM((tokens, kv_heads, width), bf16),
-            pltpu.VMEM((tokens, width), f32),
+            pltpu.VMEM((2, tokens, kv_heads, width), bf16),
+            pltpu.VMEM((2, tokens, kv_heads, width), bf16),
+            pltpu.VMEM((2, tokens, width), f32),
             pltpu.VMEM((tokens * heads, width), f32),
             pltpu.VMEM((tokens * kv_heads, width), f32),
             pltpu.VMEM((tokens * kv_heads, width), f32),
-            pltpu.SemaphoreType.DMA((4,)),
+            pltpu.SemaphoreType.DMA((7,)),
         ],
         limit=PACK_VMEM,
     )
-    got = to_core(give, half)
-    joined = pl.pallas_call(
-        join_kernel,
-        out_shape=[shape((2, per_chip, 2, tokens, width), bf16)] * (steps // 2),
-        in_specs=[VMEM] * 2,
-        out_specs=[VMEM] * (steps // 2),
-        name="join",
-    )(keep, got)
+    joined, near = packed[:slots], packed[slots:]
     far = [to_upper(slot, array) for slot, array in enumerate(joined)]
     near = [near[0]] + [to_chip(step, near[step]) for step in range(1, steps)]
     pairs, queries = call(

time: 55.7 us -> 56.6 us (1.016)
  waiting for transfers between devices: 22.2 us -> 27.6 us
  Pallas kernels: 16.9 us -> 13.2 us
  starting transfers between devices: 15.4 us -> 13.4 us
  local copies, waits for them, and re-layouts: 0.7 us -> 1.68 us
    ppermute x6, waiting for transfers between devices: 10.9 us -> 14.8 us  [to_chip(): return lax.ppermute(array, 'seq', links)]
    pallas_call x1 -> x0, Pallas kernels: 1.89 us -> none  [halves_plan(): pl.pallas_call(join_kernel, out_shape=[shape((2, per_chip, 2, tokens, wid...]
    ppermute x6, starting transfers between devices: 10.3 us -> 8.44 us  [to_chip(): return lax.ppermute(array, 'seq', links)]
    pallas_call x5, Pallas kernels: 15 us -> 13.2 us  [call(): pl.pallas_call(kernel, out_shape=outs, in_specs=specs or [SMEM] + [VMEM]...]
    ppermute x2, waiting for transfers between devices: 11.3 us -> 12.8 us  [to_upper(): return lax.ppermute(array, 'seq', links)]
    unnamed x6 -> x8, local copies, waits for them, and re-layouts: 0.7 us -> 1.68 us
    ppermute x2 -> x3, starting transfers between devices: 2.51 us -> 2.44 us  [to_core(): lax.ppermute(array, 'seq', [(device, device ^ 1) for device in range(coun...]
  transfers between devices with their start and end apart: 10 -> 11, of which waited for: 6 -> 8; matrix products, arithmetic and copies ran while one was open for 0% -> 0% of each run, Pallas kernels for 11% -> 6%
where the time goes in v10:
time: 56.6 us; the launch traced here: 56.1 us
  waiting for transfers between devices  27.6 us (49%)
  starting transfers between devices  13.4 us (24%)
  Pallas kernels  13.2 us (23%)
  local copies, waits for them, and re-layouts  1.68 us (3%)
    ppermute x6, waiting for transfers between devices, to_chip(): return lax.ppermute(array, 'seq', links)  14.8 us
    pallas_call x5, Pallas kernels, call(): pl.pallas_call(kernel, out_shape=outs, in_specs=specs or [SMEM] + [VMEM]...  13.2 us
    ppermute x2, waiting for transfers between devices, to_upper(): return lax.ppermute(array, 'seq', links)  12.8 us
    ppermute x6, starting transfers between devices, to_chip(): return lax.ppermute(array, 'seq', links)  8.44 us
    ppermute x2, starting transfers between devices, to_upper(): return lax.ppermute(array, 'seq', links)  2.57 us
    ppermute x3, starting transfers between devices, to_core(): lax.ppermute(array, 'seq', [(device, device ^ 1) for device in range(coun...  2.44 us
    unnamed x8, local copies, waits for them, and re-layouts  1.68 us
  transfers between devices with their start and end apart: 11, of which 8 were waited for; matrix products, arithmetic and copies ran while one was open for 0% of the time, Pallas kernels for 6%

profile of v10, /device:TPU:16, one launch (start us, length us, event | category | flops | bytes accessed | tf_op | source)
XLA Modules:
  0.0 56.1 jit_solution(650043309036300751)
XLA Ops:
  0.0 0.7 %collective-permute-start = (bf16[112,8,128]{2,1,0:T(8,128)(2,1)}, bf16[112,8,128]{2,1,0:T(8,128)(2,1)S(1)}, u32[]{:S(2)}, u32[]{:S(2)}) collective-permute-start(bf16[112,8,128]{2,1,0:T(8,128)(2,1)} %k_hbm.1), channel_id=1, source_target_pairs={{0,1},{1,0},{2,3},{3,2},{4,5},{5,4},{6,7},{7,6},{16,17},{17,16},{1... | collective-permute-start | bytes 688136 | tf_op jit(solution)/shard_map/ppermute | solution.py:358
  0.7 0.7 %collective-permute-start.1 = (bf16[112,8,128]{2,1,0:T(8,128)(2,1)}, bf16[112,8,128]{2,1,0:T(8,128)(2,1)S(1)}, u32[]{:S(2)}, u32[]{:S(2)}) collective-permute-start(bf16[112,8,128]{2,1,0:T(8,128)(2,1)} %v_hbm.1), channel_id=1, source_target_pairs={{0,1},{1,0},{2,3},{3,2},{4,5},{5,4},{6,7},{7,6},{16,17},{17,16},{1... | collective-permute-start | bytes 688136 | tf_op jit(solution)/shard_map/ppermute | solution.py:358
  1.4 0.0 collective-permute-done.other_k_hbm
  1.4 0.0 copy-start.2
  1.4 0.0 collective-permute-done.1.other_v_hbm
  1.4 0.0 copy-start.3
  1.4 0.7 %copy-done.2 = bf16[112,8,128]{2,1,0:T(8,128)(2,1)} copy-done((bf16[112,8,128]{2,1,0:T(8,128)(2,1)}, bf16[112,8,128]{2,1,0:T(8,128)(2,1)S(1)}, u32[]{:S(2)}) %copy-start.2) | copy-done | bytes 229400
  2.1 0.1 copy-done.3
  2.1 4.9 %send.1 = (bf16[2,2,2,112,128]{4,3,2,1,0:T(8,128)(2,1)}, bf16[2,2,2,112,128]{4,3,2,1,0:T(8,128)(2,1)}, bf16[8,112,128]{2,1,0:T(8,128)(2,1)}, bf16[8,112,128]{2,1...) custom-call(s32[1]{0:T(128)} %bitcast.me_ref, bf16[112,16,128]{2,1,0:T(8,128)(2,1)} %q_hbm.1, ...), custom_call_target="tpu_custom_call" | custom-call | tf_op jit(solution)/shard_map/send/pallas_call | solution.py:336
  7.0 1.6 %collective-permute-start.2 = (bf16[8,112,128]{2,1,0:T(8,128)(2,1)}, bf16[8,112,128]{2,1,0:T(8,128)(2,1)S(1)}, u32[]{:S(2)}, u32[]{:S(2)}) collective-permute-start(bf16[8,112,128]{2,1,0:T(8,128)(2,1)} %get-tuple-element.21), channel_id=1, source_target_pairs={{0,2},{1,3},{2,0},{3,1},{4,6},{5,7},{6,4},{7,5},{8,10},{9,11},{10,... | collective-permute-start | bytes 688136 | tf_op jit(solution)/shard_map/ppermute | solution.py:355
  8.6 1.6 %collective-permute-start.3 = (bf16[8,112,128]{2,1,0:T(8,128)(2,1)}, bf16[8,112,128]{2,1,0:T(8,128)(2,1)S(1)}, u32[]{:S(2)}, u32[]{:S(2)}) collective-permute-start(bf16[8,112,128]{2,1,0:T(8,128)(2,1)} %get-tuple-element.22), channel_id=1, source_target_pairs={{0,4},{1,5},{2,6},{3,7},{4,0},{5,1},{6,2},{7,3},{8,12},{9,13},{10,... | collective-permute-start | bytes 688136 | tf_op jit(solution)/shard_map/ppermute | solution.py:355
  10.2 0.4 collective-permute-start.4
  10.6 1.3 %collective-permute-start.5 = (bf16[2,2,2,112,128]{4,3,2,1,0:T(8,128)(2,1)}, bf16[2,2,2,112,128]{4,3,2,1,0:T(8,128)(2,1)S(1)}, u32[]{:S(2)}, u32[]{:S(2)}) collective-permute-start(bf16[2,2,2,112,128]{4,3,2,1,0:T(8,128)(2,1)} %get-tuple-element.24), channel_id=1, source_target_pairs={{0,8},{1,13},{2,10},{3,15},{4,12},{5,9},{6,14},{7,11},{16,24},{17,... | collective-permute-start | bytes 688136 | tf_op jit(solution)/shard_map/ppermute | solution.py:351
  11.8 1.3 %collective-permute-start.6 = (bf16[2,2,2,112,128]{4,3,2,1,0:T(8,128)(2,1)}, bf16[2,2,2,112,128]{4,3,2,1,0:T(8,128)(2,1)S(1)}, u32[]{:S(2)}, u32[]{:S(2)}) collective-permute-start(bf16[2,2,2,112,128]{4,3,2,1,0:T(8,128)(2,1)} %get-tuple-element.25), channel_id=1, source_target_pairs={{0,10},{1,15},{2,8},{3,13},{4,14},{5,11},{6,12},{7,9},{16,26},{17,... | collective-permute-start | bytes 688136 | tf_op jit(solution)/shard_map/ppermute | solution.py:351
  13.1 1.8 %collective-permute-done.2.refs_1_ = bf16[8,112,128]{2,1,0:T(8,128)(2,1)S(1)} collective-permute-done((bf16[8,112,128]{2,1,0:T(8,128)(2,1)}, bf16[8,112,128]{2,1,0:T(8,128)(2,1)S(1)}, u32[]{:S(2)}, u32[]{:S(2)}) %collective-permute-start.2) | collective-permute-done | bytes 229408 | tf_op jit(solution)/shard_map/ppermute | solution.py:355
  14.9 2.4 %collective-permute-done.3.refs_2_ = bf16[8,112,128]{2,1,0:T(8,128)(2,1)S(1)} collective-permute-done((bf16[8,112,128]{2,1,0:T(8,128)(2,1)}, bf16[8,112,128]{2,1,0:T(8,128)(2,1)S(1)}, u32[]{:S(2)}, u32[]{:S(2)}) %collective-permute-start.3) | collective-permute-done | bytes 229408 | tf_op jit(solution)/shard_map/ppermute | solution.py:355
  17.3 5.2 %collective-permute-done.4.refs_3_ = bf16[8,112,128]{2,1,0:T(8,128)(2,1)S(1)} collective-permute-done((bf16[8,112,128]{2,1,0:T(8,128)(2,1)}, bf16[8,112,128]{2,1,0:T(8,128)(2,1)S(1)}, u32[]{:S(2)}, u32[]{:S(2)}) %collective-permute-start.4) | collective-permute-done | bytes 229408 | tf_op jit(solution)/shard_map/ppermute | solution.py:355
  22.5 8.8 %collective-permute-done.5.refs_4_ = bf16[2,2,2,112,128]{4,3,2,1,0:T(8,128)(2,1)S(1)} collective-permute-done((bf16[2,2,2,112,128]{4,3,2,1,0:T(8,128)(2,1)}, bf16[2,2,2,112,128]{4,3,2,1,0:T(8,128)(2,1)S(1)}, u32[]{:S(2)}, u32[]{:S(2)}) %collective-permute-start.5) | collective-permute-done | bytes 229408 | tf_op jit(solution)/shard_map/ppermute | solution.py:351
  31.3 4.0 %collective-permute-done.6.refs_5_ = bf16[2,2,2,112,128]{4,3,2,1,0:T(8,128)(2,1)S(1)} collective-permute-done((bf16[2,2,2,112,128]{4,3,2,1,0:T(8,128)(2,1)}, bf16[2,2,2,112,128]{4,3,2,1,0:T(8,128)(2,1)S(1)}, u32[]{:S(2)}, u32[]{:S(2)}) %collective-permute-start.6) | collective-permute-done | bytes 229408 | tf_op jit(solution)/shard_map/ppermute | solution.py:351
  35.3 0.0 copy-start
  35.3 0.9 %copy-done = bf16[8,112,128]{2,1,0:T(8,128)(2,1)S(1)} copy-done((bf16[8,112,128]{2,1,0:T(8,128)(2,1)S(1)}, bf16[8,112,128]{2,1,0:T(8,128)(2,1)}, u32[]{:S(2)}) %copy-start) | copy-done | bytes 229400
  36.2 0.0 copy-start.1
  36.2 0.1 gather.1
  36.3 1.1 %collective-permute-start.7 = (bf16[8,2,2,112,128]{4,3,2,1,0:T(8,128)(2,1)S(1)}, bf16[8,2,2,112,128]{4,3,2,1,0:T(8,128)(2,1)S(1)}, u32[]{:S(2)}, u32[]{:S(2)}) collective-permute-start(bf16[8,2,2,112,128]{4,3,2,1,0:T(8,128)(2,1)S(1)} %get-tuple-element.27.pair_ref), channel_id=1, source_target_pairs={{0,1},{1,0},{2,3},{3,2},{4,5},{5,4},{6,7},{7,6},{8,9},{9,8},{10,11... | collective-permute-start | bytes 2752520 | tf_op jit(solution)/shard_map/ppermute | solution.py:358
  37.4 0.0 copy-done.1
  37.4 3.1 %first.1 = (f32[2,1,896]{2,1,0:T(1,128)S(1)}, f32[2,1,896]{2,1,0:T(1,128)S(1)}, f32[2,128,896]{2,1,0:T(8,128)S(1)}) custom-call(s32[1]{0:T(128)} %bitcast.me_ref, s32[2,896]{1,0:T(2,128)S(1)} %copy-done.1, bf16[4,2,2,112,128]{4,3,2,1,0:T(8,128)(2,1)S(1)} %get-tuple-element.26.query_ref, bf16[8,2,2,112,128]{4,3,2,1,0:T(8,128)(2,1)S(1)} %get-tuple-element.27.pair_ref), custom_call_target="tpu_custom_call" | custom-call | tf_op jit(solution)/shard_map/first/pallas_call | solution.py:336
  40.6 0.0 collective-permute-done.7.pair_ref
  40.6 3.9 %second.1 = (bf16[4,112,128]{2,1,0:T(8,128)(2,1)S(1)}, bf16[4,112,128]{2,1,0:T(8,128)(2,1)S(1)}, bf16[4,112,128]{2,1,0:T(8,128)(2,1)S(1)}, bf16[4,112,128]{2,1,0:T(8,128)(2,1)S(1)}) custom-call(s32[1]{0:T(128)} %bitcast.me_ref, s32[2,896]{1,0:T(2,128)S(1)} %copy-done.1, bf16[4,2,2,112,128]{4,3,2,1,0:T(8,128)(2,1)S(1)} %get-tuple-element.26.query_ref, ...), custom_call_target="tpu_custom_call" | custom-call | tf_op jit(solution)/shard_map/second/pallas_call | solution.py:336
  44.5 1.1 %collective-permute-start.8 = (bf16[4,112,128]{2,1,0:T(8,128)(2,1)S(1)}, bf16[4,112,128]{2,1,0:T(8,128)(2,1)S(1)}, u32[]{:S(2)}, u32[]{:S(2)}) collective-permute-start(bf16[4,112,128]{2,1,0:T(8,128)(2,1)S(1)} %get-tuple-element.32), channel_id=1, source_target_pairs={{0,2},{1,3},{2,0},{3,1},{4,6},{5,7},{6,4},{7,5},{8,10},{9,11},{10,... | collective-permute-start | bytes 344072 | tf_op jit(solution)/shard_map/ppermute | solution.py:355
  45.5 2.9 %collective-permute-start.9 = (bf16[4,112,128]{2,1,0:T(8,128)(2,1)S(1)}, bf16[4,112,128]{2,1,0:T(8,128)(2,1)S(1)}, u32[]{:S(2)}, u32[]{:S(2)}) collective-permute-start(bf16[4,112,128]{2,1,0:T(8,128)(2,1)S(1)} %get-tuple-element.33), channel_id=1, source_target_pairs={{0,4},{1,5},{2,6},{3,7},{4,0},{5,1},{6,2},{7,3},{8,12},{9,13},{10,... | collective-permute-start | bytes 344072 | tf_op jit(solution)/shard_map/ppermute | solution.py:355
  48.4 1.0 %collective-permute-start.10 = (bf16[4,112,128]{2,1,0:T(8,128)(2,1)S(1)}, bf16[4,112,128]{2,1,0:T(8,128)(2,1)S(1)}, u32[]{:S(2)}, u32[]{:S(2)}) collective-permute-start(bf16[4,112,128]{2,1,0:T(8,128)(2,1)S(1)} %get-tuple-element.34), channel_id=1, source_target_pairs={{0,6},{1,7},{2,4},{3,5},{4,2},{5,3},{6,0},{7,1},{8,14},{9,15},{10,... | collective-permute-start | bytes 344072 | tf_op jit(solution)/shard_map/ppermute | solution.py:355
  49.4 0.7 %collective-permute-done.8.refs_1_ = bf16[4,112,128]{2,1,0:T(8,128)(2,1)S(1)} collective-permute-done((bf16[4,112,128]{2,1,0:T(8,128)(2,1)S(1)}, bf16[4,112,128]{2,1,0:T(8,128)(2,1)S(1)}, u32[]{:S(2)}, u32[]{:S(2)}) %collective-permute-start.8) | collective-permute-done | bytes 114720 | tf_op jit(solution)/shard_map/ppermute | solution.py:355
  50.1 1.8 %collective-permute-done.9.refs_2_ = bf16[4,112,128]{2,1,0:T(8,128)(2,1)S(1)} collective-permute-done((bf16[4,112,128]{2,1,0:T(8,128)(2,1)S(1)}, bf16[4,112,128]{2,1,0:T(8,128)(2,1)S(1)}, u32[]{:S(2)}, u32[]{:S(2)}) %collective-permute-start.9) | collective-permute-done | bytes 114720 | tf_op jit(solution)/shard_map/ppermute | solution.py:355
  51.9 2.9 %collective-permute-done.10.refs_3_ = bf16[4,112,128]{2,1,0:T(8,128)(2,1)S(1)} collective-permute-done((bf16[4,112,128]{2,1,0:T(8,128)(2,1)S(1)}, bf16[4,112,128]{2,1,0:T(8,128)(2,1)S(1)}, u32[]{:S(2)}, u32[]{:S(2)}) %collective-permute-start.10) | collective-permute-done | bytes 114720 | tf_op jit(solution)/shard_map/ppermute | solution.py:355
  54.8 1.3 %unpack.1 = bf16[112,16,128]{2,1,0:T(8,128)(2,1)} custom-call(s32[1]{0:T(128)} %bitcast.me_ref, bf16[4,112,128]{2,1,0:T(8,128)(2,1)S(1)} %get-tuple-element.31.refs_0_, bf16[4,112,128]{2,1,0:T(8,128)(2,1)S(1)} %collective-permute-done.8.refs_1_, bf16[4,112,128]{2,1,0:T(8,128)(2,1)S(1)} %collective-permute-done.9.refs_2_, ...), custom_call_target="tpu_custom_call" | custom-call | tf_op jit(solution)/shard_map/unpack/pallas_call | solution.py:336
Async XLA Ops:
  0.0 1.4 %collective-permute-start = (bf16[112,8,128]{2,1,0:T(8,128)(2,1)}, bf16[112,8,128]{2,1,0:T(8,128)(2,1)S(1)}, u32[]{:S(2)}, u32[]{:S(2)}) collective-permute-start(bf16[112,8,128]{2,1,0:T(8,128)(2,1)} %k_hbm.1), channel_id=1, source_target_pairs={{0,1},{1,0},{2,3},{3,2},{4,5},{5,4},{6,7},{7,6},{16,17},{17,16},{1... | collective-permute-start | bytes 688136 | tf_op jit(solution)/shard_map/ppermute | solution.py:358
  0.7 0.7 %collective-permute-start.1 = (bf16[112,8,128]{2,1,0:T(8,128)(2,1)}, bf16[112,8,128]{2,1,0:T(8,128)(2,1)S(1)}, u32[]{:S(2)}, u32[]{:S(2)}) collective-permute-start(bf16[112,8,128]{2,1,0:T(8,128)(2,1)} %v_hbm.1), channel_id=1, source_target_pairs={{0,1},{1,0},{2,3},{3,2},{4,5},{5,4},{6,7},{7,6},{16,17},{17,16},{1... | collective-permute-start | bytes 688136 | tf_op jit(solution)/shard_map/ppermute | solution.py:358
  1.4 0.7 %copy-start.2 = (bf16[112,8,128]{2,1,0:T(8,128)(2,1)}, bf16[112,8,128]{2,1,0:T(8,128)(2,1)S(1)}, u32[]{:S(2)}) copy-start(bf16[112,8,128]{2,1,0:T(8,128)(2,1)S(1)} %collective-permute-done.other_k_hbm) | copy-start | bytes 688132
  1.4 0.7 %copy-start.3 = (bf16[112,8,128]{2,1,0:T(8,128)(2,1)}, bf16[112,8,128]{2,1,0:T(8,128)(2,1)S(1)}, u32[]{:S(2)}) copy-start(bf16[112,8,128]{2,1,0:T(8,128)(2,1)S(1)} %collective-permute-done.1.other_v_hbm) | copy-start | bytes 688132
  7.0 7.9 %collective-permute-start.2 = (bf16[8,112,128]{2,1,0:T(8,128)(2,1)}, bf16[8,112,128]{2,1,0:T(8,128)(2,1)S(1)}, u32[]{:S(2)}, u32[]{:S(2)}) collective-permute-start(bf16[8,112,128]{2,1,0:T(8,128)(2,1)} %get-tuple-element.21), channel_id=1, source_target_pairs={{0,2},{1,3},{2,0},{3,1},{4,6},{5,7},{6,4},{7,5},{8,10},{9,11},{10,... | collective-permute-start | bytes 688136 | tf_op jit(solution)/shard_map/ppermute | solution.py:355
  8.6 8.7 %collective-permute-start.3 = (bf16[8,112,128]{2,1,0:T(8,128)(2,1)}, bf16[8,112,128]{2,1,0:T(8,128)(2,1)S(1)}, u32[]{:S(2)}, u32[]{:S(2)}) collective-permute-start(bf16[8,112,128]{2,1,0:T(8,128)(2,1)} %get-tuple-element.22), channel_id=1, source_target_pairs={{0,4},{1,5},{2,6},{3,7},{4,0},{5,1},{6,2},{7,3},{8,12},{9,13},{10,... | collective-permute-start | bytes 688136 | tf_op jit(solution)/shard_map/ppermute | solution.py:355
  10.2 12.3 %collective-permute-start.4 = (bf16[8,112,128]{2,1,0:T(8,128)(2,1)}, bf16[8,112,128]{2,1,0:T(8,128)(2,1)S(1)}, u32[]{:S(2)}, u32[]{:S(2)}) collective-permute-start(bf16[8,112,128]{2,1,0:T(8,128)(2,1)} %get-tuple-element.23), channel_id=1, source_target_pairs={{0,6},{1,7},{2,4},{3,5},{4,2},{5,3},{6,0},{7,1},{8,14},{9,15},{10,... | collective-permute-start | bytes 688136 | tf_op jit(solution)/shard_map/ppermute | solution.py:355
  10.6 20.7 %collective-permute-start.5 = (bf16[2,2,2,112,128]{4,3,2,1,0:T(8,128)(2,1)}, bf16[2,2,2,112,128]{4,3,2,1,0:T(8,128)(2,1)S(1)}, u32[]{:S(2)}, u32[]{:S(2)}) collective-permute-start(bf16[2,2,2,112,128]{4,3,2,1,0:T(8,128)(2,1)} %get-tuple-element.24), channel_id=1, source_target_pairs={{0,8},{1,13},{2,10},{3,15},{4,12},{5,9},{6,14},{7,11},{16,24},{17,... | collective-permute-start | bytes 688136 | tf_op jit(solution)/shard_map/ppermute | solution.py:351
  11.8 23.4 %collective-permute-start.6 = (bf16[2,2,2,112,128]{4,3,2,1,0:T(8,128)(2,1)}, bf16[2,2,2,112,128]{4,3,2,1,0:T(8,128)(2,1)S(1)}, u32[]{:S(2)}, u32[]{:S(2)}) collective-permute-start(bf16[2,2,2,112,128]{4,3,2,1,0:T(8,128)(2,1)} %get-tuple-element.25), channel_id=1, source_target_pairs={{0,10},{1,15},{2,8},{3,13},{4,14},{5,11},{6,12},{7,9},{16,26},{17,... | collective-permute-start | bytes 688136 | tf_op jit(solution)/shard_map/ppermute | solution.py:351
  35.3 0.9 %copy-start = (bf16[8,112,128]{2,1,0:T(8,128)(2,1)S(1)}, bf16[8,112,128]{2,1,0:T(8,128)(2,1)}, u32[]{:S(2)}) copy-start(bf16[8,112,128]{2,1,0:T(8,128)(2,1)} %get-tuple-element.20.refs_0_) | copy-start | bytes 688132
  36.2 1.2 %copy-start.1 = (s32[2,896]{1,0:T(2,128)S(1)}, s32[2,896]{1,0:T(2,128)}, u32[]{:S(2)}) copy-start(s32[2,896]{1,0:T(2,128)} %constant.9.clone.bounds_ref) | copy-start | bytes 21508
  36.3 4.2 %collective-permute-start.7 = (bf16[8,2,2,112,128]{4,3,2,1,0:T(8,128)(2,1)S(1)}, bf16[8,2,2,112,128]{4,3,2,1,0:T(8,128)(2,1)S(1)}, u32[]{:S(2)}, u32[]{:S(2)}) collective-permute-start(bf16[8,2,2,112,128]{4,3,2,1,0:T(8,128)(2,1)S(1)} %get-tuple-element.27.pair_ref), channel_id=1, source_target_pairs={{0,1},{1,0},{2,3},{3,2},{4,5},{5,4},{6,7},{7,6},{8,9},{9,8},{10,11... | collective-permute-start | bytes 2752520 | tf_op jit(solution)/shard_map/ppermute | solution.py:358
  44.5 5.6 %collective-permute-start.8 = (bf16[4,112,128]{2,1,0:T(8,128)(2,1)S(1)}, bf16[4,112,128]{2,1,0:T(8,128)(2,1)S(1)}, u32[]{:S(2)}, u32[]{:S(2)}) collective-permute-start(bf16[4,112,128]{2,1,0:T(8,128)(2,1)S(1)} %get-tuple-element.32), channel_id=1, source_target_pairs={{0,2},{1,3},{2,0},{3,1},{4,6},{5,7},{6,4},{7,5},{8,10},{9,11},{10,... | collective-permute-start | bytes 344072 | tf_op jit(solution)/shard_map/ppermute | solution.py:355
  45.5 6.4 %collective-permute-start.9 = (bf16[4,112,128]{2,1,0:T(8,128)(2,1)S(1)}, bf16[4,112,128]{2,1,0:T(8,128)(2,1)S(1)}, u32[]{:S(2)}, u32[]{:S(2)}) collective-permute-start(bf16[4,112,128]{2,1,0:T(8,128)(2,1)S(1)} %get-tuple-element.33), channel_id=1, source_target_pairs={{0,4},{1,5},{2,6},{3,7},{4,0},{5,1},{6,2},{7,3},{8,12},{9,13},{10,... | collective-permute-start | bytes 344072 | tf_op jit(solution)/shard_map/ppermute | solution.py:355
  48.4 6.4 %collective-permute-start.10 = (bf16[4,112,128]{2,1,0:T(8,128)(2,1)S(1)}, bf16[4,112,128]{2,1,0:T(8,128)(2,1)S(1)}, u32[]{:S(2)}, u32[]{:S(2)}) collective-permute-start(bf16[4,112,128]{2,1,0:T(8,128)(2,1)S(1)} %get-tuple-element.34), channel_id=1, source_target_pairs={{0,6},{1,7},{2,4},{3,5},{4,2},{5,3},{6,0},{7,1},{8,14},{9,15},{10,... | collective-permute-start | bytes 344072 | tf_op jit(solution)/shard_map/ppermute | solution.py:355

commit v11 on v10

--- a/solution.py
+++ b/solution.py
@@ -163,62 +163,45 @@
     return (scaled * cosine + pltpu.roll(scaled, scaled.shape[1] // 2, 1) * sine).astype(jnp.bfloat16)
 
 
-def send_kernel(me_ref, q_hbm, k_hbm, v_hbm, other_k_hbm, other_v_hbm, table_hbm, query_gain_ref, key_gain_ref, *refs):
+def send_kernel(me_ref, q_hbm, k_hbm, v_hbm, table_hbm, query_gain_ref, key_gain_ref, *refs):
     outs, (q_ref, k_ref, v_ref, table_ref, qf_ref, kf_ref, vf_ref, sems) = refs[:-8], refs[-8:]
+    steps = len(outs) // 2
+    pairs, fulls = outs[:steps], outs[steps:]
     tokens, heads, width = q_ref.shape
-    slots, per_chip = (len(outs) // 3), outs[0].shape[1]
-    far, fulls = outs[:slots], outs[slots:]
-    steps, kv_heads = len(fulls), k_ref.shape[2]
+    kv_heads, per_chip = k_ref.shape[1], pairs[0].shape[0]
     first, per_full = 2 * per_chip, heads // steps
     me = me_ref[0]
-    chip, core = lax.rem(me // 2, steps), lax.rem(me, 2)
-    copies = []
-    for side, (k, v, device) in enumerate(((k_hbm, v_hbm, me), (other_k_hbm, other_v_hbm, me + 1 - 2 * core))):
-        rows = pl.ds(pl.multiple_of(device * tokens, 8), tokens)
-        for kind, (source, target) in enumerate(((k, k_ref), (table_hbm.at[rows], table_ref), (v, v_ref))):
-            copies.append(pltpu.make_async_copy(source, target.at[side], sems.at[3 * side + kind]))
-    copies.insert(3, pltpu.make_async_copy(q_hbm, q_ref, sems.at[6]))
+    chip = lax.rem(me // 2, steps)
+    start = pl.multiple_of(me * tokens, 8)
+    copies = [
+        pltpu.make_async_copy(k_hbm, k_ref, sems.at[0]),
+        pltpu.make_async_copy(table_hbm.at[pl.ds(start, tokens)], table_ref, sems.at[1]),
+        pltpu.make_async_copy(v_hbm, v_ref, sems.at[2]),
+        pltpu.make_async_copy(q_hbm, q_ref, sems.at[3]),
+    ]
     for copy in copies:
         copy.start()
-    key_gain = key_gain_ref[...]
-
-    def keys_of(head, factors):
-        return turn(kf_ref[pl.ds(head, tokens, stride=kv_heads), :], key_gain, *factors)
-
-    def values_of(head):
-        return vf_ref[pl.ds(head, tokens, stride=kv_heads), :].astype(jnp.bfloat16)
-
-    def load(side, waits):
-        for copy in waits:
-            copy.wait()
-        kf_ref[...] = normalize(k_ref[side].reshape(tokens * kv_heads, width))
-        vf_ref[...] = v_ref[side].astype(jnp.float32).reshape(tokens * kv_heads, width)
-        return rope_factors(table_ref[side])
-
-    factors = load(0, copies[:3])
+    copies[0].wait()
+    kf_ref[...] = normalize(k_ref[...].reshape(tokens * kv_heads, width))
+    copies[1].wait()
+    cosine, sine = rope_factors(table_ref[...])
+    copies[2].wait()
+    vf_ref[...] = v_ref[...].astype(jnp.float32).reshape(tokens * kv_heads, width)
     for step in range(steps):
         for row in range(per_chip):
             head = (chip ^ step) * per_chip + row
-            fulls[step][2 * row], fulls[step][2 * row + 1] = keys_of(head, factors), values_of(head)
+            keys = turn(kf_ref[pl.ds(head, tokens, stride=kv_heads), :], key_gain_ref[...], cosine, sine)
+            values = vf_ref[pl.ds(head, tokens, stride=kv_heads), :].astype(jnp.bfloat16)
+            pairs[step][row, 0] = keys
+            fulls[step][2 * row] = keys
+            pairs[step][row, 1] = values
+            fulls[step][2 * row + 1] = values
     copies[3].wait()
     qf_ref[...] = normalize(q_ref[...].reshape(tokens * heads, width))
     for step in range(steps):
         for row in range(per_full):
             normed = qf_ref[pl.ds((chip ^ step) * per_full + row, tokens, stride=heads), :]
-            fulls[step][first + row] = turn(normed, query_gain_ref[...], *factors)
-    for which in range(2):
-
-        @pl.when(core == which)
-        def _():
-            for slot in range(slots):
-                for row in range(first):
-                    far[slot][0, row // 2, row % 2] = fulls[which * slots + slot][row]
-
-    factors = load(1, copies[4:])
-    for slot in range(slots):
-        for row in range(per_chip):
-            head = (chip ^ (core * slots + slot)) * per_chip + row
-            far[slot][1, row, 0], far[slot][1, row, 1] = keys_of(head, factors), values_of(head)
+            fulls[step][first + row] = turn(normed, query_gain_ref[...], cosine, sine)
 
 
 def weigh(segments, queries, state):
@@ -247,13 +230,12 @@
 def gather_kernel(me_ref, *refs):
     pair_ref, query_ref = refs[-2:]
     steps, per_chip = query_ref.shape[:2]
-    near, far = refs[:steps], refs[steps:-2]
+    near, far = refs[:steps], refs[steps : 2 * steps]
     chip = lax.rem(me_ref[0] // 2, steps)
     for step in range(steps):
         pair_ref[chip ^ step] = near[step][: 2 * per_chip].reshape(pair_ref.shape[1:])
         query_ref[chip ^ step] = near[step][2 * per_chip :].reshape(query_ref.shape[1:])
-    for slot, ref in enumerate(far):
-        pair_ref[steps + 2 * slot : steps + 2 * slot + 2] = ref[...]
+        pair_ref[steps + step] = far[step][...]
 
 
 def add_core(upper, bound, query_ref, pair_ref, state_refs, store):
@@ -343,51 +325,48 @@
             name=name,
         )(me, *operands)
 
-    def to_upper(slot, array):
-        links = []
-        for device in range(half):
-            chip, core = device // 2, device % 2
-            links.append((device, half + (chip ^ (core * (steps // 2) + slot)) * 2 + core))
+    def to_upper(step, array):
+        links = [(device, half + ((device // 2) ^ step) * 2 + device % 2) for device in range(half)]
         return lax.ppermute(array, "seq", links)
 
     def to_chip(step, array):
         links = [(device, ((device // 2) ^ step) * 2 + device % 2) for device in range(devices)]
         return lax.ppermute(array, "seq", links)
 
-    def to_core(array, count):
-        return lax.ppermute(array, "seq", [(device, device ^ 1) for device in range(count)])
+    def to_core(array):
+        return lax.ppermute(array, "seq", [(device, device ^ 1) for device in range(devices)])
 
     shape = jax.ShapeDtypeStruct
-    slots = steps // 2
-    others = [to_core(array, half) for array in (key_states, value_states)]
     packed = call(
         send_kernel,
         "send",
-        [shape((2, per_chip, 2, tokens, width), bf16)] * slots
+        [shape((per_chip, 2, tokens, width), bf16)] * steps
         + [shape((per_chip * (2 + group), tokens, width), bf16)] * steps,
         query_states,
         key_states,
         value_states,
-        *others,
         jnp.asarray(rope_table(length, width)),
         query_gain[None],
         key_gain[None],
-        specs=[SMEM] + [HBM] * 3 + [pl.BlockSpec(memory_space=pl.ANY)] * 2 + [HBM] + [VMEM] * 2,
+        specs=[SMEM, HBM, HBM, HBM, HBM, VMEM, VMEM],
         scratch=[
             pltpu.VMEM((tokens, heads, width), bf16),
-            pltpu.VMEM((2, tokens, kv_heads, width), bf16),
-            pltpu.VMEM((2, tokens, kv_heads, width), bf16),
-            pltpu.VMEM((2, tokens, width), f32),
+            pltpu.VMEM((tokens, kv_heads, width), bf16),
+            pltpu.VMEM((tokens, kv_heads, width), bf16),
+            pltpu.VMEM((tokens, width), f32),
             pltpu.VMEM((tokens * heads, width), f32),
             pltpu.VMEM((tokens * kv_heads, width), f32),
             pltpu.VMEM((tokens * kv_heads, width), f32),
-            pltpu.SemaphoreType.DMA((7,)),
+            pltpu.SemaphoreType.DMA((4,)),
         ],
         limit=PACK_VMEM,
     )
-    joined, near = packed[:slots], packed[slots:]
-    far = [to_upper(slot, array) for slot, array in enumerate(joined)]
-    near = [near[0]] + [to_chip(step, near[step]) for step in range(1, steps)]
+    pairs, near = packed[:steps], packed[steps:]
+    far = [to_upper(step, pair) for step, pair in enumerate(pairs)]
+    near = [near[0]] + [
+        lax.cond(me[0] >= 0, functools.partial(to_chip, step), jnp.zeros_like, near[step]) for step in range(1, steps)
+    ]
+    near, far = lax.optimization_barrier((near, far))
     pairs, queries = call(
         gather_kernel,
         "gather",
@@ -395,7 +374,7 @@
         *near,
         *far,
     )
-    others = to_core(pairs, devices)
+    others = to_core(pairs)
     lanes = steps * group * tokens
     state = [shape((per_chip, 1, lanes), f32), shape((per_chip, 1, lanes), f32), shape((per_chip, width, lanes), f32)]
     block, _, token = np.indices((steps, group, tokens), dtype=np.int32)

time: 56.6 us -> 56.7 us (level)
  local copies, waits for them, and re-layouts: 1.68 us -> 0.01 us
  waiting for transfers between devices: 27.6 us -> 28.9 us
    ppermute x6, waiting for transfers between devices: 14.8 us -> 28.9 us  [to_chip(): return lax.ppermute(array, 'seq', links)]
    ppermute x2 -> x4, waiting for transfers between devices: 12.8 us -> 0.01 us  [to_upper(): return lax.ppermute(array, 'seq', links)]
    ppermute x2 -> x4, starting transfers between devices: 2.57 us -> 5.17 us  [to_upper(): return lax.ppermute(array, 'seq', links)]
    ppermute x3 -> x1, starting transfers between devices: 2.44 us -> 0.07 us  [to_core(): lax.ppermute(array, 'seq', [(device, device ^ 1) for device in range(devi...]
    unnamed x8 -> x4, local copies, waits for them, and re-layouts: 1.68 us -> 0.01 us
  transfers between devices with their start and end apart: 11 -> 11, of which waited for: 8 -> 6; matrix products, arithmetic and copies ran while one was open for 0% -> 0% of each run, Pallas kernels for 6% -> 6%
where the time goes in v11:
time: 56.7 us; the launch traced here: 56.4 us
  waiting for transfers between devices  28.9 us (51%)
  starting transfers between devices  13.9 us (25%)
  Pallas kernels  13.5 us (24%)
    ppermute x6, waiting for transfers between devices, to_chip(): return lax.ppermute(array, 'seq', links)  28.9 us
    pallas_call x5, Pallas kernels, call(): pl.pallas_call(kernel, out_shape=outs, in_specs=specs or [SMEM] + [VMEM]...  13.5 us
    ppermute x6, starting transfers between devices, to_chip(): return lax.ppermute(array, 'seq', links)  8.67 us
    ppermute x4, starting transfers between devices, to_upper(): return lax.ppermute(array, 'seq', links)  5.17 us
  transfers between devices with their start and end apart: 11, of which 6 were waited for; matrix products, arithmetic and copies ran while one was open for 0% of the time, Pallas kernels for 6%

profile of v11, /device:TPU:16, one launch (start us, length us, event | category | flops | bytes accessed | tf_op | source)
XLA Modules:
  0.0 56.4 jit_solution(8670851509960432620)
XLA Ops:
  0.0 3.9 %send.1 = (bf16[2,2,112,128]{3,2,1,0:T(8,128)(2,1)}, bf16[2,2,112,128]{3,2,1,0:T(8,128)(2,1)}, bf16[2,2,112,128]{3,2,1,0:T(8,128)(2,1)}, bf16[2,2,112,128]{3,2,1...) custom-call(s32[1]{0:T(128)} %bitcast.me_ref, ...), custom_call_target="tpu_custom_call" | custom-call | tf_op jit(solution)/shard_map/send/pallas_call | solution.py:318
  3.9 1.3 %collective-permute-start.3 = (bf16[2,2,112,128]{3,2,1,0:T(8,128)(2,1)}, bf16[2,2,112,128]{3,2,1,0:T(8,128)(2,1)S(1)}, u32[]{:S(2)}, u32[]{:S(2)}) collective-permute-start(bf16[2,2,112,128]{3,2,1,0:T(8,128)(2,1)} %get-tuple-element.46), channel_id=1, source_target_pairs={{0,8},{1,9},{2,10},{3,11},{4,12},{5,13},{6,14},{7,15},{16,24},{17,... | collective-permute-start | bytes 344072 | tf_op jit(solution)/shard_map/ppermute | solution.py:330
  5.2 1.3 %collective-permute-start.4 = (bf16[2,2,112,128]{3,2,1,0:T(8,128)(2,1)}, bf16[2,2,112,128]{3,2,1,0:T(8,128)(2,1)S(1)}, u32[]{:S(2)}, u32[]{:S(2)}) collective-permute-start(bf16[2,2,112,128]{3,2,1,0:T(8,128)(2,1)} %get-tuple-element.47), channel_id=1, source_target_pairs={{0,10},{1,11},{2,8},{3,9},{4,14},{5,15},{6,12},{7,13},{16,26},{17,... | collective-permute-start | bytes 344072 | tf_op jit(solution)/shard_map/ppermute | solution.py:330
  6.5 1.3 %collective-permute-start.5 = (bf16[2,2,112,128]{3,2,1,0:T(8,128)(2,1)}, bf16[2,2,112,128]{3,2,1,0:T(8,128)(2,1)S(1)}, u32[]{:S(2)}, u32[]{:S(2)}) collective-permute-start(bf16[2,2,112,128]{3,2,1,0:T(8,128)(2,1)} %get-tuple-element.48), channel_id=1, source_target_pairs={{0,12},{1,13},{2,14},{3,15},{4,8},{5,9},{6,10},{7,11},{16,28},{17,... | collective-permute-start | bytes 344072 | tf_op jit(solution)/shard_map/ppermute | solution.py:330
  7.8 1.3 %collective-permute-start.6 = (bf16[2,2,112,128]{3,2,1,0:T(8,128)(2,1)}, bf16[2,2,112,128]{3,2,1,0:T(8,128)(2,1)S(1)}, u32[]{:S(2)}, u32[]{:S(2)}) collective-permute-start(bf16[2,2,112,128]{3,2,1,0:T(8,128)(2,1)} %get-tuple-element.49), channel_id=1, source_target_pairs={{0,14},{1,15},{2,12},{3,13},{4,10},{5,11},{6,8},{7,9},{16,30},{17,... | collective-permute-start | bytes 344072 | tf_op jit(solution)/shard_map/ppermute | solution.py:330
  9.1 10.0 %conditional.3 = (bf16[8,112,128]{2,1,0:T(8,128)(2,1)}) conditional(s32[]{:T(128)} %convert_element_type.2, () %tuple.24, bf16[8,112,128]{2,1,0:T(8,128)(2,1)S(1)} %get-tuple-element.43), branch_computations={%region_0.0_spmd, %region_1.0_spmd} | conditional | bytes 917552 | solution.py:367
  9.1 1.6 %collective-permute-start = (bf16[8,112,128]{2,1,0:T(8,128)(2,1)S(1)}, bf16[8,112,128]{2,1,0:T(8,128)(2,1)}, u32[]{:S(2)}, u32[]{:S(2)}) collective-permute-start(bf16[8,112,128]{2,1,0:T(8,128)(2,1)S(1)} %param.1), channel_id=1, source_target_pairs={{0,2},{1,3},{2,0},{3,1},{4,6},{5,7},{6,4},{7,5},{8,10},{9,11},{10,... | collective-permute-start | bytes 688136 | tf_op jit(solution)/shard_map/cond/branch_1_fun/ppermute | solution.py:334
  10.7 8.4 %collective-permute-done = bf16[8,112,128]{2,1,0:T(8,128)(2,1)} collective-permute-done((bf16[8,112,128]{2,1,0:T(8,128)(2,1)S(1)}, bf16[8,112,128]{2,1,0:T(8,128)(2,1)}, u32[]{:S(2)}, u32[]{:S(2)}) %collective-permute-start) | collective-permute-done | bytes 229408 | tf_op jit(solution)/shard_map/cond/branch_1_fun/ppermute | solution.py:334
  19.1 0.0 copy-start
  19.1 8.9 %conditional.4 = (bf16[8,112,128]{2,1,0:T(8,128)(2,1)}) conditional(s32[]{:T(128)} %convert_element_type.2, () %tuple.25, bf16[8,112,128]{2,1,0:T(8,128)(2,1)S(1)} %get-tuple-element.44), branch_computations={%region_2.0_spmd, %region_3.0_spmd} | conditional | bytes 917552 | solution.py:367
  19.1 0.0 collective-permute-start.1
  19.1 8.9 %collective-permute-done.1 = bf16[8,112,128]{2,1,0:T(8,128)(2,1)} collective-permute-done((bf16[8,112,128]{2,1,0:T(8,128)(2,1)S(1)}, bf16[8,112,128]{2,1,0:T(8,128)(2,1)}, u32[]{:S(2)}, u32[]{:S(2)}) %collective-permute-start.1) | collective-permute-done | bytes 229408 | tf_op jit(solution)/shard_map/cond/branch_1_fun/ppermute | solution.py:334
  28.0 9.4 %conditional.5 = (bf16[8,112,128]{2,1,0:T(8,128)(2,1)}) conditional(s32[]{:T(128)} %convert_element_type.2, () %tuple.26, bf16[8,112,128]{2,1,0:T(8,128)(2,1)S(1)} %get-tuple-element.45), branch_computations={%region_4.0_spmd, %region_5.0_spmd} | conditional | bytes 917552 | solution.py:367
  28.0 3.5 %collective-permute-start.2 = (bf16[8,112,128]{2,1,0:T(8,128)(2,1)S(1)}, bf16[8,112,128]{2,1,0:T(8,128)(2,1)}, u32[]{:S(2)}, u32[]{:S(2)}) collective-permute-start(bf16[8,112,128]{2,1,0:T(8,128)(2,1)S(1)} %param.5), channel_id=1, source_target_pairs={{0,6},{1,7},{2,4},{3,5},{4,2},{5,3},{6,0},{7,1},{8,14},{9,15},{10,... | collective-permute-start | bytes 688136 | tf_op jit(solution)/shard_map/cond/branch_1_fun/ppermute | solution.py:334
  31.5 5.9 %collective-permute-done.2 = bf16[8,112,128]{2,1,0:T(8,128)(2,1)} collective-permute-done((bf16[8,112,128]{2,1,0:T(8,128)(2,1)S(1)}, bf16[8,112,128]{2,1,0:T(8,128)(2,1)}, u32[]{:S(2)}, u32[]{:S(2)}) %collective-permute-start.2) | collective-permute-done | bytes 229408 | tf_op jit(solution)/shard_map/cond/branch_1_fun/ppermute | solution.py:334
  37.4 0.0 collective-permute-done.3.refs_4_
  37.4 0.0 collective-permute-done.4.refs_5_
  37.4 0.0 collective-permute-done.5.refs_6_
  37.5 0.0 collective-permute-done.6.refs_7_
  37.5 0.0 copy-done
  37.5 0.0 copy-start.1
  37.5 1.3 %gather.1 = (bf16[8,2,2,112,128]{4,3,2,1,0:T(8,128)(2,1)S(1)}, bf16[4,2,2,112,128]{4,3,2,1,0:T(8,128)(2,1)S(1)}) custom-call(s32[1]{0:T(128)} %bitcast.me_ref, bf16[8,112,128]{2,1,0:T(8,128)(2,1)S(1)} %copy-done, bf16[8,112,128]{2,1,0:T(8,128)(2,1)} %get-tuple-element.67.refs_1_, bf16[8,112,128]{2,1,0:T(8,128)(2,1)} %get-tuple-element.68.refs_2_, ...), custom_call_target="tpu_custom_call" | custom-call | tf_op jit(solution)/shard_map/gather/pallas_call | solution.py:318
  38.7 0.1 collective-permute-start.7
  38.8 0.0 copy-done.1
  38.8 3.1 %first.1 = (f32[2,1,896]{2,1,0:T(1,128)S(1)}, f32[2,1,896]{2,1,0:T(1,128)S(1)}, f32[2,128,896]{2,1,0:T(8,128)S(1)}) custom-call(s32[1]{0:T(128)} %bitcast.me_ref, s32[2,896]{1,0:T(2,128)S(1)} %copy-done.1, bf16[4,2,2,112,128]{4,3,2,1,0:T(8,128)(2,1)S(1)} %get-tuple-element.58.query_ref, bf16[8,2,2,112,128]{4,3,2,1,0:T(8,128)(2,1)S(1)} %get-tuple-element.59.pair_ref), custom_call_target="tpu_custom_call" | custom-call | tf_op jit(solution)/shard_map/first/pallas_call | solution.py:318
  42.0 0.0 collective-permute-done.7.pair_ref
  42.0 3.9 %second.1 = (bf16[4,112,128]{2,1,0:T(8,128)(2,1)S(1)}, bf16[4,112,128]{2,1,0:T(8,128)(2,1)S(1)}, bf16[4,112,128]{2,1,0:T(8,128)(2,1)S(1)}, bf16[4,112,128]{2,1,0:T(8,128)(2,1)S(1)}) custom-call(s32[1]{0:T(128)} %bitcast.me_ref, s32[2,896]{1,0:T(2,128)S(1)} %copy-done.1, bf16[4,2,2,112,128]{4,3,2,1,0:T(8,128)(2,1)S(1)} %get-tuple-element.58.query_ref, ...), custom_call_target="tpu_custom_call" | custom-call | tf_op jit(solution)/shard_map/second/pallas_call | solution.py:318
  45.9 0.7 %collective-permute-start.8 = (bf16[4,112,128]{2,1,0:T(8,128)(2,1)S(1)}, bf16[4,112,128]{2,1,0:T(8,128)(2,1)S(1)}, u32[]{:S(2)}, u32[]{:S(2)}) collective-permute-start(bf16[4,112,128]{2,1,0:T(8,128)(2,1)S(1)} %get-tuple-element.64), channel_id=1, source_target_pairs={{0,2},{1,3},{2,0},{3,1},{4,6},{5,7},{6,4},{7,5},{8,10},{9,11},{10,... | collective-permute-start | bytes 344072 | tf_op jit(solution)/shard_map/ppermute | solution.py:334
  46.6 2.6 %collective-permute-start.9 = (bf16[4,112,128]{2,1,0:T(8,128)(2,1)S(1)}, bf16[4,112,128]{2,1,0:T(8,128)(2,1)S(1)}, u32[]{:S(2)}, u32[]{:S(2)}) collective-permute-start(bf16[4,112,128]{2,1,0:T(8,128)(2,1)S(1)} %get-tuple-element.65), channel_id=1, source_target_pairs={{0,4},{1,5},{2,6},{3,7},{4,0},{5,1},{6,2},{7,3},{8,12},{9,13},{10,... | collective-permute-start | bytes 344072 | tf_op jit(solution)/shard_map/ppermute | solution.py:334
  49.2 0.3 collective-permute-start.10
  49.4 2.0 %collective-permute-done.8.refs_1_ = bf16[4,112,128]{2,1,0:T(8,128)(2,1)S(1)} collective-permute-done((bf16[4,112,128]{2,1,0:T(8,128)(2,1)S(1)}, bf16[4,112,128]{2,1,0:T(8,128)(2,1)S(1)}, u32[]{:S(2)}, u32[]{:S(2)}) %collective-permute-start.8) | collective-permute-done | bytes 114720 | tf_op jit(solution)/shard_map/ppermute | solution.py:334
  51.5 1.6 %collective-permute-done.9.refs_2_ = bf16[4,112,128]{2,1,0:T(8,128)(2,1)S(1)} collective-permute-done((bf16[4,112,128]{2,1,0:T(8,128)(2,1)S(1)}, bf16[4,112,128]{2,1,0:T(8,128)(2,1)S(1)}, u32[]{:S(2)}, u32[]{:S(2)}) %collective-permute-start.9) | collective-permute-done | bytes 114720 | tf_op jit(solution)/shard_map/ppermute | solution.py:334
  53.1 2.1 %collective-permute-done.10.refs_3_ = bf16[4,112,128]{2,1,0:T(8,128)(2,1)S(1)} collective-permute-done((bf16[4,112,128]{2,1,0:T(8,128)(2,1)S(1)}, bf16[4,112,128]{2,1,0:T(8,128)(2,1)S(1)}, u32[]{:S(2)}, u32[]{:S(2)}) %collective-permute-start.10) | collective-permute-done | bytes 114720 | tf_op jit(solution)/shard_map/ppermute | solution.py:334
  55.1 1.3 %unpack.1 = bf16[112,16,128]{2,1,0:T(8,128)(2,1)} custom-call(s32[1]{0:T(128)} %bitcast.me_ref, bf16[4,112,128]{2,1,0:T(8,128)(2,1)S(1)} %get-tuple-element.63.refs_0_, bf16[4,112,128]{2,1,0:T(8,128)(2,1)S(1)} %collective-permute-done.8.refs_1_, bf16[4,112,128]{2,1,0:T(8,128)(2,1)S(1)} %collective-permute-done.9.refs_2_, ...), custom_call_target="tpu_custom_call" | custom-call | tf_op jit(solution)/shard_map/unpack/pallas_call | solution.py:318
Async XLA Ops:
  3.9 33.5 %collective-permute-start.3 = (bf16[2,2,112,128]{3,2,1,0:T(8,128)(2,1)}, bf16[2,2,112,128]{3,2,1,0:T(8,128)(2,1)S(1)}, u32[]{:S(2)}, u32[]{:S(2)}) collective-permute-start(bf16[2,2,112,128]{3,2,1,0:T(8,128)(2,1)} %get-tuple-element.46), channel_id=1, source_target_pairs={{0,8},{1,9},{2,10},{3,11},{4,12},{5,13},{6,14},{7,15},{16,24},{17,... | collective-permute-start | bytes 344072 | tf_op jit(solution)/shard_map/ppermute | solution.py:330
  5.2 32.2 %collective-permute-start.4 = (bf16[2,2,112,128]{3,2,1,0:T(8,128)(2,1)}, bf16[2,2,112,128]{3,2,1,0:T(8,128)(2,1)S(1)}, u32[]{:S(2)}, u32[]{:S(2)}) collective-permute-start(bf16[2,2,112,128]{3,2,1,0:T(8,128)(2,1)} %get-tuple-element.47), channel_id=1, source_target_pairs={{0,10},{1,11},{2,8},{3,9},{4,14},{5,15},{6,12},{7,13},{16,26},{17,... | collective-permute-start | bytes 344072 | tf_op jit(solution)/shard_map/ppermute | solution.py:330
  6.5 30.9 %collective-permute-start.5 = (bf16[2,2,112,128]{3,2,1,0:T(8,128)(2,1)}, bf16[2,2,112,128]{3,2,1,0:T(8,128)(2,1)S(1)}, u32[]{:S(2)}, u32[]{:S(2)}) collective-permute-start(bf16[2,2,112,128]{3,2,1,0:T(8,128)(2,1)} %get-tuple-element.48), channel_id=1, source_target_pairs={{0,12},{1,13},{2,14},{3,15},{4,8},{5,9},{6,10},{7,11},{16,28},{17,... | collective-permute-start | bytes 344072 | tf_op jit(solution)/shard_map/ppermute | solution.py:330
  7.8 29.6 %collective-permute-start.6 = (bf16[2,2,112,128]{3,2,1,0:T(8,128)(2,1)}, bf16[2,2,112,128]{3,2,1,0:T(8,128)(2,1)S(1)}, u32[]{:S(2)}, u32[]{:S(2)}) collective-permute-start(bf16[2,2,112,128]{3,2,1,0:T(8,128)(2,1)} %get-tuple-element.49), channel_id=1, source_target_pairs={{0,14},{1,15},{2,12},{3,13},{4,10},{5,11},{6,8},{7,9},{16,30},{17,... | collective-permute-start | bytes 344072 | tf_op jit(solution)/shard_map/ppermute | solution.py:330
  9.1 10.0 %collective-permute-start = (bf16[8,112,128]{2,1,0:T(8,128)(2,1)S(1)}, bf16[8,112,128]{2,1,0:T(8,128)(2,1)}, u32[]{:S(2)}, u32[]{:S(2)}) collective-permute-start(bf16[8,112,128]{2,1,0:T(8,128)(2,1)S(1)} %param.1), channel_id=1, source_target_pairs={{0,2},{1,3},{2,0},{3,1},{4,6},{5,7},{6,4},{7,5},{8,10},{9,11},{10,... | collective-permute-start | bytes 688136 | tf_op jit(solution)/shard_map/cond/branch_1_fun/ppermute | solution.py:334
  19.1 18.4 %copy-start = (bf16[8,112,128]{2,1,0:T(8,128)(2,1)S(1)}, bf16[8,112,128]{2,1,0:T(8,128)(2,1)}, u32[]{:S(2)}) copy-start(bf16[8,112,128]{2,1,0:T(8,128)(2,1)} %get-tuple-element.50.refs_0_) | copy-start | bytes 688132
  19.1 8.9 %collective-permute-start.1 = (bf16[8,112,128]{2,1,0:T(8,128)(2,1)S(1)}, bf16[8,112,128]{2,1,0:T(8,128)(2,1)}, u32[]{:S(2)}, u32[]{:S(2)}) collective-permute-start(bf16[8,112,128]{2,1,0:T(8,128)(2,1)S(1)} %param.3), channel_id=1, source_target_pairs={{0,4},{1,5},{2,6},{3,7},{4,0},{5,1},{6,2},{7,3},{8,12},{9,13},{10,... | collective-permute-start | bytes 688136 | tf_op jit(solution)/shard_map/cond/branch_1_fun/ppermute | solution.py:334
  28.0 9.4 %collective-permute-start.2 = (bf16[8,112,128]{2,1,0:T(8,128)(2,1)S(1)}, bf16[8,112,128]{2,1,0:T(8,128)(2,1)}, u32[]{:S(2)}, u32[]{:S(2)}) collective-permute-start(bf16[8,112,128]{2,1,0:T(8,128)(2,1)S(1)} %param.5), channel_id=1, source_target_pairs={{0,6},{1,7},{2,4},{3,5},{4,2},{5,3},{6,0},{7,1},{8,14},{9,15},{10,... | collective-permute-start | bytes 688136 | tf_op jit(solution)/shard_map/cond/branch_1_fun/ppermute | solution.py:334
  37.5 1.4 %copy-start.1 = (s32[2,896]{1,0:T(2,128)S(1)}, s32[2,896]{1,0:T(2,128)}, u32[]{:S(2)}) copy-start(s32[2,896]{1,0:T(2,128)} %constant.17.clone.bounds_ref) | copy-start | bytes 21508
  38.7 3.2 %collective-permute-start.7 = (bf16[8,2,2,112,128]{4,3,2,1,0:T(8,128)(2,1)S(1)}, bf16[8,2,2,112,128]{4,3,2,1,0:T(8,128)(2,1)S(1)}, u32[]{:S(2)}, u32[]{:S(2)}) collective-permute-start(bf16[8,2,2,112,128]{4,3,2,1,0:T(8,128)(2,1)S(1)} %get-tuple-element.59.pair_ref), channel_id=1, source_target_pairs={{0,1},{1,0},{2,3},{3,2},{4,5},{5,4},{6,7},{7,6},{8,9},{9,8},{10,11... | collective-permute-start | bytes 2752520 | tf_op jit(solution)/shard_map/ppermute | solution.py:337
  45.9 5.6 %collective-permute-start.8 = (bf16[4,112,128]{2,1,0:T(8,128)(2,1)S(1)}, bf16[4,112,128]{2,1,0:T(8,128)(2,1)S(1)}, u32[]{:S(2)}, u32[]{:S(2)}) collective-permute-start(bf16[4,112,128]{2,1,0:T(8,128)(2,1)S(1)} %get-tuple-element.64), channel_id=1, source_target_pairs={{0,2},{1,3},{2,0},{3,1},{4,6},{5,7},{6,4},{7,5},{8,10},{9,11},{10,... | collective-permute-start | bytes 344072 | tf_op jit(solution)/shard_map/ppermute | solution.py:334
  46.6 6.5 %collective-permute-start.9 = (bf16[4,112,128]{2,1,0:T(8,128)(2,1)S(1)}, bf16[4,112,128]{2,1,0:T(8,128)(2,1)S(1)}, u32[]{:S(2)}, u32[]{:S(2)}) collective-permute-start(bf16[4,112,128]{2,1,0:T(8,128)(2,1)S(1)} %get-tuple-element.65), channel_id=1, source_target_pairs={{0,4},{1,5},{2,6},{3,7},{4,0},{5,1},{6,2},{7,3},{8,12},{9,13},{10,... | collective-permute-start | bytes 344072 | tf_op jit(solution)/shard_map/ppermute | solution.py:334
  49.2 6.0 %collective-permute-start.10 = (bf16[4,112,128]{2,1,0:T(8,128)(2,1)S(1)}, bf16[4,112,128]{2,1,0:T(8,128)(2,1)S(1)}, u32[]{:S(2)}, u32[]{:S(2)}) collective-permute-start(bf16[4,112,128]{2,1,0:T(8,128)(2,1)S(1)} %get-tuple-element.66), channel_id=1, source_target_pairs={{0,6},{1,7},{2,4},{3,5},{4,2},{5,3},{6,0},{7,1},{8,14},{9,15},{10,... | collective-permute-start | bytes 344072 | tf_op jit(solution)/shard_map/ppermute | solution.py:334

commit v12 on v8

--- a/solution.py
+++ b/solution.py
@@ -202,22 +202,26 @@
         near_ref[head // group, head % group] = turn(normed, query_gain_ref[...], cosine, sine)
 
 
-def weigh(keys, values, queries, allowed, state):
-    scale = math.log2(math.e) / math.sqrt(keys.shape[1])
-    scores = lax.dot_general(keys, queries, CONTRACT, preferred_element_type=jnp.float32)
-    if allowed is not None:
-        scores = jnp.where(allowed, scores, MASKED)
-    highest = jnp.max(scores, axis=0, keepdims=True)
-    if state is not None:
-        highest = jnp.maximum(state[0], highest)
-    probs = jnp.exp2((scores - highest) * scale)
-    total = jnp.sum(probs, axis=0, keepdims=True)
-    weighted = lax.dot_general(
-        values, probs.astype(jnp.bfloat16), (((0,), (0,)), ((), ())), preferred_element_type=jnp.float32
-    )
+def weigh(segments, queries, state):
+    scale = math.log2(math.e) / math.sqrt(queries.shape[1])
+    scores = []
+    for keys, _, allowed in segments:
+        part = lax.dot_general(keys, queries, CONTRACT, preferred_element_type=jnp.float32)
+        scores.append(part if allowed is None else jnp.where(allowed, part, MASKED))
+    tops = [jnp.max(part, axis=0, keepdims=True) for part in scores] + ([] if state is None else [state[0]])
+    highest = functools.reduce(jnp.maximum, tops)
+    total = weighted = None
     if state is not None:
         factor = jnp.exp2((state[0] - highest) * scale)
-        total, weighted = state[1] * factor + total, state[2] * factor + weighted
+        total, weighted = state[1] * factor, state[2] * factor
+    for part, (_, values, _) in zip(scores, segments):
+        probs = jnp.exp2((part - highest) * scale)
+        added = jnp.sum(probs, axis=0, keepdims=True)
+        summed = lax.dot_general(
+            values, probs.astype(jnp.bfloat16), (((0,), (0,)), ((), ())), preferred_element_type=jnp.float32
+        )
+        total = added if total is None else total + added
+        weighted = summed if weighted is None else weighted + summed
     return highest, total, weighted
 
 
@@ -228,13 +232,15 @@
     values = x_ref[:, group + 1].reshape(blocks * tokens, width)
     lanes = NEAR_BLOCKS * group * tokens
     for first in range(0, blocks, NEAR_BLOCKS):
-        queries = x_ref[first : first + NEAR_BLOCKS, :group].reshape(lanes, width)
-        reach = (first + NEAR_BLOCKS) * tokens
+        count = first + NEAR_BLOCKS
+        queries = x_ref[first:count, :group].reshape(lanes, width)
         place = slice(first * group * tokens, first * group * tokens + lanes)
-        index = lax.broadcasted_iota(jnp.int32, (reach, lanes), 0)
-        allowed = index <= position_ref[:, place]
-        results = weigh(keys[:reach], values[:reach], queries, allowed, None)
-        for ref, value in zip((highest_ref, total_ref, weighted_ref), results):
+        start, stop = first * tokens, count * tokens
+        index = start + lax.broadcasted_iota(jnp.int32, (stop - start, lanes), 0)
+        segments = [(keys[start:stop], values[start:stop], index <= position_ref[:, place])]
+        if first > 0:
+            segments.append((keys[:start], values[:start], None))
+        for ref, value in zip((highest_ref, total_ref, weighted_ref), weigh(segments, queries, None)):
             ref[:, place] = value
 
 
@@ -247,15 +253,12 @@
 def add_far(x_ref, pair_refs, state_refs, store):
     blocks, rows, tokens, width = x_ref.shape
     group = rows - 2
-    keys, values = [
-        jnp.concatenate([ref[:, i].reshape(ref.shape[0] * tokens, width) for ref in pair_refs], axis=0)
-        for i in range(2)
-    ]
+    segments = [[ref[:, i].reshape(ref.shape[0] * tokens, width) for i in range(2)] + [None] for ref in pair_refs]
     lanes = FAR_BLOCKS * group * tokens
     for first in range(0, blocks, FAR_BLOCKS):
         queries = x_ref[first : first + FAR_BLOCKS, :group].reshape(lanes, width)
         place = slice(first * group * tokens, first * group * tokens + lanes)
-        store(first, place, *weigh(keys, values, queries, None, [ref[:, place] for ref in state_refs]))
+        store(first, place, *weigh(segments, queries, [ref[:, place] for ref in state_refs]))
 
 
 def last_kernel(half, me_ref, x_ref, mine_ref, neighbours_ref, *refs):
@@ -335,17 +338,17 @@
         return lax.all_to_all(array, "seq", split_axis=0, concat_axis=0, axis_index_groups=groups, tiled=True)
 
     far = [to_upper(step, pair) for step, pair in enumerate(pairs)]
-    arrived = lax.cond(me[0] >= 0, inside, jnp.zeros_like, near)
-    arrived, far = lax.optimization_barrier((arrived, far))
-    mine, others = call(
-        split_kernel, "split", [shape((steps, 2, tokens, width), bf16)] * 2, *far, specs=[VMEM] * steps
-    )
-    neighbours = to_core(others, half)
+    arrived = inside(near)
     lanes = half * group * tokens
     state = [shape((1, lanes), f32), shape((1, lanes), f32), shape((width, lanes), f32)]
     positions = np.broadcast_to(np.arange(half * tokens, dtype=np.int32).reshape(half, 1, tokens), (half, group, tokens))
     carried = call(near_kernel, "near", state, jnp.asarray(positions.reshape(1, lanes)), arrived, specs=[VMEM] * 2)
 
+    carried, far = lax.optimization_barrier((carried, far))
+    mine, others = call(
+        split_kernel, "split", [shape((steps, 2, tokens, width), bf16)] * 2, *far, specs=[VMEM] * steps
+    )
+    neighbours = to_core(others, half)
     attended = call(
         functools.partial(last_kernel, half),
         "last",

time: 55.7 us -> 54.2 us (0.973)
  blocking collectives: 36.7 us -> 10.9 us
  waiting for transfers between devices: 0.01 us -> 20.4 us
  starting transfers between devices: 7.1 us -> 11 us
    all_to_all x2 -> x1, blocking collectives: 36.7 us -> 10.9 us  [inside(): lax.all_to_all(array, 'seq', split_axis=0, concat_axis=0, axis_index_grou...]
    all_to_all x0 -> x1, waiting for transfers between devices: none -> 11 us  [inside(): lax.all_to_all(array, 'seq', split_axis=0, concat_axis=0, axis_index_grou...]
    ppermute x4, waiting for transfers between devices: 0.01 us -> 7.89 us  [to_upper(): return lax.ppermute(array, 'seq', links)]
    all_to_all x0 -> x1, starting transfers between devices: none -> 3.95 us  [inside(): lax.all_to_all(array, 'seq', split_axis=0, concat_axis=0, axis_index_grou...]
    ppermute x1, waiting for transfers between devices: 0.01 us -> 1.45 us  [to_core(): lax.ppermute(array, 'seq', [(device, device ^ 1) for device in range(lowe...]
  transfers between devices with their start and end apart: 5 -> 6, of which waited for: 0 -> 4; matrix products, arithmetic and copies ran while one was open for 0% -> 0% of each run, Pallas kernels for 6% -> 5%
where the time goes in v12:
time: 54.2 us; the launch traced here: 53.8 us
  waiting for transfers between devices  20.4 us (38%)
  starting transfers between devices  11 us (20%)
  blocking collectives  10.9 us (20%)
  Pallas kernels  10.4 us (19%)
  local copies, waits for them, and re-layouts  0.91 us (2%)
    all_to_all x1, waiting for transfers between devices, inside(): lax.all_to_all(array, 'seq', split_axis=0, concat_axis=0, axis_index_grou...  11 us
    all_to_all x1, blocking collectives, inside(): lax.all_to_all(array, 'seq', split_axis=0, concat_axis=0, axis_index_grou...  10.9 us
    pallas_call x4, Pallas kernels, call(): pl.pallas_call(kernel, out_shape=outs, in_specs=specs or [SMEM] + [VMEM]...  10.4 us
    ppermute x4, waiting for transfers between devices, to_upper(): return lax.ppermute(array, 'seq', links)  7.89 us
    ppermute x4, starting transfers between devices, to_upper(): return lax.ppermute(array, 'seq', links)  5.17 us
    all_to_all x1, starting transfers between devices, inside(): lax.all_to_all(array, 'seq', split_axis=0, concat_axis=0, axis_index_grou...  3.95 us
    ppermute x1, starting transfers between devices, to_core(): lax.ppermute(array, 'seq', [(device, device ^ 1) for device in range(lowe...  1.92 us
    ppermute x1, waiting for transfers between devices, to_core(): lax.ppermute(array, 'seq', [(device, device ^ 1) for device in range(lowe...  1.45 us
  transfers between devices with their start and end apart: 6, of which 4 were waited for; matrix products, arithmetic and copies ran while one was open for 0% of the time, Pallas kernels for 5%

profile of v12, /device:TPU:16, one launch (start us, length us, event | category | flops | bytes accessed | tf_op | source)
XLA Modules:
  0.0 53.8 jit_solution(11712603652083190622)
XLA Ops:
  0.0 4.2 %send.1 = (bf16[2,2,112,128]{3,2,1,0:T(8,128)(2,1)}, bf16[2,2,112,128]{3,2,1,0:T(8,128)(2,1)}, bf16[2,2,112,128]{3,2,1,0:T(8,128)(2,1)}, bf16[2,2,112,128]{3,2,1,0:T(8,128)(2,1)}, bf16[8,4,112,128]{3,2,1,0:T(8,128)(2,1)}) custom-call(s32[1]{0:T(128)} %bitcast.me_ref, bf16[112,16,128]{2,1,0:T(8,128)(2,1)} %q_hbm.1, bf16[112,8,128]{2,1,0:T(8,128)(2,1)} %k_hbm.1, ...), custom_call_target="tpu_custom_call" | custom-call | tf_op jit(solution)/shard_map/send/pallas_call | solution.py:294
  4.2 0.0 copy-start.4
  4.2 0.0 copy-start.3
  4.2 0.0 copy-start.2
  4.2 0.0 copy-start.1
  4.2 4.0 %all-to-all-start = ((bf16[8,4,112,128]{3,2,1,0:T(8,128)(2,1)}), bf16[8,4,112,128]{3,2,1,0:T(8,128)(2,1)S(1)}, u32[]{:S(2)}, u32[]{:S(2)}) async-start(bf16[8,4,112,128]{3,2,1,0:T(8,128)(2,1)} %get-tuple-element.22), calls=%async_computation | async-start | bytes 1835008 | tf_op jit(solution)/shard_map/all_to_all | solution.py:338
  8.2 0.0 copy-start
  8.2 0.0 copy-done.4
  8.2 1.3 %collective-permute-start = (bf16[2,2,112,128]{3,2,1,0:T(8,128)(2,1)S(1)}, bf16[2,2,112,128]{3,2,1,0:T(8,128)(2,1)S(1)}, u32[]{:S(2)}, u32[]{:S(2)}) collective-permute-start(bf16[2,2,112,128]{3,2,1,0:T(8,128)(2,1)S(1)} %copy-done.4), channel_id=1, source_target_pairs={{0,8},{1,9},{2,10},{3,11},{4,12},{5,13},{6,14},{7,15},{16,24},{17,... | collective-permute-start | bytes 344072 | tf_op jit(solution)/shard_map/ppermute | solution.py:306
  9.5 0.0 copy-done.3
  9.5 1.3 %collective-permute-start.1 = (bf16[2,2,112,128]{3,2,1,0:T(8,128)(2,1)S(1)}, bf16[2,2,112,128]{3,2,1,0:T(8,128)(2,1)S(1)}, u32[]{:S(2)}, u32[]{:S(2)}) collective-permute-start(bf16[2,2,112,128]{3,2,1,0:T(8,128)(2,1)S(1)} %copy-done.3), channel_id=1, source_target_pairs={{0,10},{1,11},{2,8},{3,9},{4,14},{5,15},{6,12},{7,13},{16,26},{17,... | collective-permute-start | bytes 344072 | tf_op jit(solution)/shard_map/ppermute | solution.py:306
  10.8 0.0 copy-done.2
  10.8 1.3 %collective-permute-start.2 = (bf16[2,2,112,128]{3,2,1,0:T(8,128)(2,1)S(1)}, bf16[2,2,112,128]{3,2,1,0:T(8,128)(2,1)S(1)}, u32[]{:S(2)}, u32[]{:S(2)}) collective-permute-start(bf16[2,2,112,128]{3,2,1,0:T(8,128)(2,1)S(1)} %copy-done.2), channel_id=1, source_target_pairs={{0,12},{1,13},{2,14},{3,15},{4,8},{5,9},{6,10},{7,11},{16,28},{17,... | collective-permute-start | bytes 344072 | tf_op jit(solution)/shard_map/ppermute | solution.py:306
  12.1 0.0 copy-done.1
  12.1 1.3 %collective-permute-start.3 = (bf16[2,2,112,128]{3,2,1,0:T(8,128)(2,1)S(1)}, bf16[2,2,112,128]{3,2,1,0:T(8,128)(2,1)S(1)}, u32[]{:S(2)}, u32[]{:S(2)}) collective-permute-start(bf16[2,2,112,128]{3,2,1,0:T(8,128)(2,1)S(1)} %copy-done.1), channel_id=1, source_target_pairs={{0,14},{1,15},{2,12},{3,13},{4,10},{5,11},{6,8},{7,9},{16,30},{17,... | collective-permute-start | bytes 344072 | tf_op jit(solution)/shard_map/ppermute | solution.py:306
  13.4 11.0 %all-to-all-done.x_ref = bf16[8,4,112,128]{3,2,1,0:T(8,128)(2,1)S(1)} async-done(((bf16[8,4,112,128]{3,2,1,0:T(8,128)(2,1)}), bf16[8,4,112,128]{3,2,1,0:T(8,128)(2,1)S(1)}, u32[]{:S(2)}, u32[]{:S(2)}) %all-to-all-start) | async-done | bytes 917536 | tf_op jit(solution)/shard_map/all_to_all | solution.py:338
  24.4 0.0 copy-done
  24.4 2.7 %near.1 = (f32[1,1792]{1,0:T(1,128)S(1)}, f32[1,1792]{1,0:T(1,128)S(1)}, f32[128,1792]{1,0:T(8,128)S(1)}) custom-call(s32[1,1792]{1,0:T(1,128)S(1)} %copy-done, bf16[8,4,112,128]{3,2,1,0:T(8,128)(2,1)S(1)} %all-to-all-done.x_ref), custom_call_target="tpu_custom_call" | custom-call | tf_op jit(solution)/shard_map/near/pallas_call | solution.py:294
  27.1 0.0 collective-permute-done.refs_0_
  27.1 0.0 collective-permute-done.1.refs_1_
  27.1 5.0 %collective-permute-done.2.refs_2_ = bf16[2,2,112,128]{3,2,1,0:T(8,128)(2,1)S(1)} collective-permute-done((bf16[2,2,112,128]{3,2,1,0:T(8,128)(2,1)S(1)}, bf16[2,2,112,128]{3,2,1,0:T(8,128)(2,1)S(1)}, u32[]{:S(2)}, u32[]{:S(2)}) %collective-permute-start.2) | collective-permute-done | bytes 114720 | tf_op jit(solution)/shard_map/ppermute | solution.py:306
  32.1 2.9 %collective-permute-done.3.refs_3_ = bf16[2,2,112,128]{3,2,1,0:T(8,128)(2,1)S(1)} collective-permute-done((bf16[2,2,112,128]{3,2,1,0:T(8,128)(2,1)S(1)}, bf16[2,2,112,128]{3,2,1,0:T(8,128)(2,1)S(1)}, u32[]{:S(2)}, u32[]{:S(2)}) %collective-permute-start.3) | collective-permute-done | bytes 114720 | tf_op jit(solution)/shard_map/ppermute | solution.py:306
  35.0 1.9 %collective-permute-start.4 = (bf16[4,2,112,128]{3,2,1,0:T(8,128)(2,1)S(1)}, bf16[4,2,112,128]{3,2,1,0:T(8,128)(2,1)S(1)}, u32[]{:S(2)}, u32[]{:S(2)}) collective-permute-start(bf16[4,2,112,128]{3,2,1,0:T(8,128)(2,1)S(1)} %get-tuple-element.35), channel_id=1, source_target_pairs={{8,9},{9,8},{10,11},{11,10},{12,13},{13,12},{14,15},{15,14},{24,25... | collective-permute-start | bytes 688136 | tf_op jit(solution)/shard_map/ppermute | solution.py:309
  37.0 1.5 %collective-permute-done.4.neighbours_ref = bf16[4,2,112,128]{3,2,1,0:T(8,128)(2,1)S(1)} collective-permute-done((bf16[4,2,112,128]{3,2,1,0:T(8,128)(2,1)S(1)}, bf16[4,2,112,128]{3,2,1,0:T(8,128)(2,1)S(1)}, u32[]{:S(2)}, u32[]{:S(2)}) %collective-permute-start.4) | collective-permute-done | bytes 229408 | tf_op jit(solution)/shard_map/ppermute | solution.py:309
  38.4 3.6 %last.1 = bf16[8,2,112,128]{3,2,1,0:T(8,128)(2,1)S(1)} custom-call(s32[1]{0:T(128)} %bitcast.me_ref, bf16[8,4,112,128]{3,2,1,0:T(8,128)(2,1)S(1)} %all-to-all-done.x_ref, bf16[4,2,112,128]{3,2,1,0:T(8,128)(2,1)S(1)} %get-tuple-element.34.mine_ref, bf16[4,2,112,128]{3,2,1,0:T(8,128)(2,1)S(1)} %collective-permute-done.4.neighbours_ref, ...), custom_call_target="tpu_custom_call" | custom-call | tf_op jit(solution)/shard_map/last/pallas_call | solution.py:294
  42.0 10.9 %all_to_all.10 = bf16[8,2,112,128]{3,2,1,0:T(8,128)(2,1)S(1)} all-to-all(bf16[8,2,112,128]{3,2,1,0:T(8,128)(2,1)S(1)} %last.1), channel_id=1, replica_groups={{0,1,2,3,4,5,6,7},{8,9,10,11,12,13,14,15},{16,17,18,19,20,21,22,23},{24..., dimensions={0} | all-to-all | bytes 917504 | tf_op jit(solution)/shard_map/all_to_all | solution.py:338
  52.9 0.9 %copy.10 = bf16[16,112,128]{2,0,1:T(8,128)(2,1)} copy(bf16[16,112,128]{2,1,0:T(8,128)(2,1)S(1)} %bitcast.7) | data formatting | bytes 917504 | tf_op jit(solution)/shard_map/reshape | solution.py:361
  (1 shorter events, 0.0 us)
Async XLA Ops:
  4.2 4.0 %copy-start.4 = (bf16[2,2,112,128]{3,2,1,0:T(8,128)(2,1)S(1)}, bf16[2,2,112,128]{3,2,1,0:T(8,128)(2,1)}, u32[]{:S(2)}) copy-start(bf16[2,2,112,128]{3,2,1,0:T(8,128)(2,1)} %get-tuple-element.26) | copy-start | bytes 344068
  4.2 5.3 %copy-start.3 = (bf16[2,2,112,128]{3,2,1,0:T(8,128)(2,1)S(1)}, bf16[2,2,112,128]{3,2,1,0:T(8,128)(2,1)}, u32[]{:S(2)}) copy-start(bf16[2,2,112,128]{3,2,1,0:T(8,128)(2,1)} %get-tuple-element.27) | copy-start | bytes 344068
  4.2 6.6 %copy-start.2 = (bf16[2,2,112,128]{3,2,1,0:T(8,128)(2,1)S(1)}, bf16[2,2,112,128]{3,2,1,0:T(8,128)(2,1)}, u32[]{:S(2)}) copy-start(bf16[2,2,112,128]{3,2,1,0:T(8,128)(2,1)} %get-tuple-element.28) | copy-start | bytes 344068
  4.2 7.9 %copy-start.1 = (bf16[2,2,112,128]{3,2,1,0:T(8,128)(2,1)S(1)}, bf16[2,2,112,128]{3,2,1,0:T(8,128)(2,1)}, u32[]{:S(2)}) copy-start(bf16[2,2,112,128]{3,2,1,0:T(8,128)(2,1)} %get-tuple-element.29) | copy-start | bytes 344068
  4.2 20.2 %all-to-all-start = ((bf16[8,4,112,128]{3,2,1,0:T(8,128)(2,1)}), bf16[8,4,112,128]{3,2,1,0:T(8,128)(2,1)S(1)}, u32[]{:S(2)}, u32[]{:S(2)}) async-start(bf16[8,4,112,128]{3,2,1,0:T(8,128)(2,1)} %get-tuple-element.22), calls=%async_computation | async-start | bytes 1835008 | tf_op jit(solution)/shard_map/all_to_all | solution.py:338
  8.2 16.3 %copy-start = (s32[1,1792]{1,0:T(1,128)S(1)}, s32[1,1792]{1,0:T(1,128)}, u32[]{:S(2)}) copy-start(s32[1,1792]{1,0:T(1,128)} %constant.9.clone.position_ref) | copy-start | bytes 21508
  8.2 18.9 %collective-permute-start = (bf16[2,2,112,128]{3,2,1,0:T(8,128)(2,1)S(1)}, bf16[2,2,112,128]{3,2,1,0:T(8,128)(2,1)S(1)}, u32[]{:S(2)}, u32[]{:S(2)}) collective-permute-start(bf16[2,2,112,128]{3,2,1,0:T(8,128)(2,1)S(1)} %copy-done.4), channel_id=1, source_target_pairs={{0,8},{1,9},{2,10},{3,11},{4,12},{5,13},{6,14},{7,15},{16,24},{17,... | collective-permute-start | bytes 344072 | tf_op jit(solution)/shard_map/ppermute | solution.py:306
  9.5 17.6 %collective-permute-start.1 = (bf16[2,2,112,128]{3,2,1,0:T(8,128)(2,1)S(1)}, bf16[2,2,112,128]{3,2,1,0:T(8,128)(2,1)S(1)}, u32[]{:S(2)}, u32[]{:S(2)}) collective-permute-start(bf16[2,2,112,128]{3,2,1,0:T(8,128)(2,1)S(1)} %copy-done.3), channel_id=1, source_target_pairs={{0,10},{1,11},{2,8},{3,9},{4,14},{5,15},{6,12},{7,13},{16,26},{17,... | collective-permute-start | bytes 344072 | tf_op jit(solution)/shard_map/ppermute | solution.py:306
  10.8 21.3 %collective-permute-start.2 = (bf16[2,2,112,128]{3,2,1,0:T(8,128)(2,1)S(1)}, bf16[2,2,112,128]{3,2,1,0:T(8,128)(2,1)S(1)}, u32[]{:S(2)}, u32[]{:S(2)}) collective-permute-start(bf16[2,2,112,128]{3,2,1,0:T(8,128)(2,1)S(1)} %copy-done.2), channel_id=1, source_target_pairs={{0,12},{1,13},{2,14},{3,15},{4,8},{5,9},{6,10},{7,11},{16,28},{17,... | collective-permute-start | bytes 344072 | tf_op jit(solution)/shard_map/ppermute | solution.py:306
  12.1 22.9 %collective-permute-start.3 = (bf16[2,2,112,128]{3,2,1,0:T(8,128)(2,1)S(1)}, bf16[2,2,112,128]{3,2,1,0:T(8,128)(2,1)S(1)}, u32[]{:S(2)}, u32[]{:S(2)}) collective-permute-start(bf16[2,2,112,128]{3,2,1,0:T(8,128)(2,1)S(1)} %copy-done.1), channel_id=1, source_target_pairs={{0,14},{1,15},{2,12},{3,13},{4,10},{5,11},{6,8},{7,9},{16,30},{17,... | collective-permute-start | bytes 344072 | tf_op jit(solution)/shard_map/ppermute | solution.py:306
  35.0 3.4 %collective-permute-start.4 = (bf16[4,2,112,128]{3,2,1,0:T(8,128)(2,1)S(1)}, bf16[4,2,112,128]{3,2,1,0:T(8,128)(2,1)S(1)}, u32[]{:S(2)}, u32[]{:S(2)}) collective-permute-start(bf16[4,2,112,128]{3,2,1,0:T(8,128)(2,1)S(1)} %get-tuple-element.35), channel_id=1, source_target_pairs={{8,9},{9,8},{10,11},{11,10},{12,13},{13,12},{14,15},{15,14},{24,25... | collective-permute-start | bytes 688136 | tf_op jit(solution)/shard_map/ppermute | solution.py:309

commit v13 on v12

--- a/solution.py
+++ b/solution.py
@@ -250,10 +250,10 @@
             refs[side - 2][step] = ref[side]
 
 
-def add_far(x_ref, pair_refs, state_refs, store):
+def add_far(x_ref, pairs_ref, state_refs, store):
     blocks, rows, tokens, width = x_ref.shape
     group = rows - 2
-    segments = [[ref[:, i].reshape(ref.shape[0] * tokens, width) for i in range(2)] + [None] for ref in pair_refs]
+    segments = [[pairs_ref[:, i].reshape(pairs_ref.shape[0] * tokens, width) for i in range(2)] + [None]]
     lanes = FAR_BLOCKS * group * tokens
     for first in range(0, blocks, FAR_BLOCKS):
         queries = x_ref[first : first + FAR_BLOCKS, :group].reshape(lanes, width)
@@ -261,7 +261,24 @@
         store(first, place, *weigh(segments, queries, [ref[:, place] for ref in state_refs]))
 
 
-def last_kernel(half, me_ref, x_ref, mine_ref, neighbours_ref, *refs):
+def far_kernel(half, me_ref, x_ref, pairs_ref, *refs):
+    state, outs = refs[:3], refs[3:]
+
+    def store(first, place, *values):
+        for ref, value in zip(outs, values):
+            ref[:, place] = value
+
+    @pl.when(me_ref[0] >= half)
+    def _():
+        add_far(x_ref, pairs_ref, state, store)
+
+    @pl.when(me_ref[0] < half)
+    def _():
+        for ref, before in zip(outs, state):
+            ref[...] = before[...]
+
+
+def last_kernel(half, me_ref, x_ref, pairs_ref, *refs):
     state, out_ref = refs[:3], refs[3]
     blocks, group, tokens, width = out_ref.shape
 
@@ -271,7 +288,7 @@
 
     @pl.when(me_ref[0] >= half)
     def _():
-        add_far(x_ref, [mine_ref, neighbours_ref], state, store)
+        add_far(x_ref, pairs_ref, state, store)
 
     @pl.when(me_ref[0] < half)
     def _():
@@ -348,13 +365,13 @@
     mine, others = call(
         split_kernel, "split", [shape((steps, 2, tokens, width), bf16)] * 2, *far, specs=[VMEM] * steps
     )
-    neighbours = to_core(others, half)
+    neighbours = to_core(others, 0)
+    carried = call(functools.partial(far_kernel, half), "far", state, arrived, mine, *carried)
     attended = call(
         functools.partial(last_kernel, half),
         "last",
         shape((half, group, tokens, width), bf16),
         arrived,
-        mine,
         neighbours,
         *carried,
     )

time: 54.2 us -> 51.6 us (0.952)
  starting transfers between devices: 11 us -> 9.19 us
  waiting for transfers between devices: 20.4 us -> 18.9 us
  Pallas kernels: 10.4 us -> 11.2 us
    ppermute x1, starting transfers between devices: 1.92 us -> 0.07 us  [to_core(): lax.ppermute(array, 'seq', [(device, device ^ 1) for device in range(lowe...]
    ppermute x1, waiting for transfers between devices: 1.45 us -> 0.01 us  [to_core(): lax.ppermute(array, 'seq', [(device, device ^ 1) for device in range(lowe...]
    pallas_call x4 -> x5, Pallas kernels: 10.4 us -> 11.2 us  [call(): pl.pallas_call(kernel, out_shape=outs, in_specs=specs or [SMEM] + [VMEM]...]
  transfers between devices with their start and end apart: 6 -> 6, of which waited for: 4 -> 3; matrix products, arithmetic and copies ran while one was open for 0% -> 0% of each run, Pallas kernels for 5% -> 9%
where the time goes in v13:
time: 51.6 us; the launch traced here: 51.3 us
  waiting for transfers between devices  18.9 us (37%)
  Pallas kernels  11.2 us (22%)
  blocking collectives  10.9 us (21%)
  starting transfers between devices  9.19 us (18%)
  local copies, waits for them, and re-layouts  0.91 us (2%)
    pallas_call x5, Pallas kernels, call(): pl.pallas_call(kernel, out_shape=outs, in_specs=specs or [SMEM] + [VMEM]...  11.2 us
    all_to_all x1, waiting for transfers between devices, inside(): lax.all_to_all(array, 'seq', split_axis=0, concat_axis=0, axis_index_grou...  11 us
    all_to_all x1, blocking collectives, inside(): lax.all_to_all(array, 'seq', split_axis=0, concat_axis=0, axis_index_grou...  10.9 us
    ppermute x4, waiting for transfers between devices, to_upper(): return lax.ppermute(array, 'seq', links)  7.89 us
    ppermute x4, starting transfers between devices, to_upper(): return lax.ppermute(array, 'seq', links)  5.17 us
    all_to_all x1, starting transfers between devices, inside(): lax.all_to_all(array, 'seq', split_axis=0, concat_axis=0, axis_index_grou...  3.95 us
  transfers between devices with their start and end apart: 6, of which 3 were waited for; matrix products, arithmetic and copies ran while one was open for 0% of the time, Pallas kernels for 9%

profile of v13, /device:TPU:16, one launch (start us, length us, event | category | flops | bytes accessed | tf_op | source)
XLA Modules:
  0.0 51.3 jit_solution(1097088025552921231)
XLA Ops:
  0.0 4.1 %send.1 = (bf16[2,2,112,128]{3,2,1,0:T(8,128)(2,1)}, bf16[2,2,112,128]{3,2,1,0:T(8,128)(2,1)}, bf16[2,2,112,128]{3,2,1,0:T(8,128)(2,1)}, bf16[2,2,112,128]{3,2,1,0:T(8,128)(2,1)}, bf16[8,4,112,128]{3,2,1,0:T(8,128)(2,1)}) custom-call(s32[1]{0:T(128)} %bitcast.me_ref, bf16[112,16,128]{2,1,0:T(8,128)(2,1)} %q_hbm.1, bf16[112,8,128]{2,1,0:T(8,128)(2,1)} %k_hbm.1, ...), custom_call_target="tpu_custom_call" | custom-call | tf_op jit(solution)/shard_map/send/pallas_call | solution.py:311
  4.2 0.0 copy-start.4
  4.2 0.0 copy-start.3
  4.2 0.0 copy-start.2
  4.2 0.0 copy-start.1
  4.2 4.0 %all-to-all-start = ((bf16[8,4,112,128]{3,2,1,0:T(8,128)(2,1)}), bf16[8,4,112,128]{3,2,1,0:T(8,128)(2,1)S(1)}, u32[]{:S(2)}, u32[]{:S(2)}) async-start(bf16[8,4,112,128]{3,2,1,0:T(8,128)(2,1)} %get-tuple-element.25), calls=%async_computation | async-start | bytes 1835008 | tf_op jit(solution)/shard_map/all_to_all | solution.py:355
  8.2 0.0 copy-start
  8.2 0.0 copy-done.4
  8.2 1.3 %collective-permute-start = (bf16[2,2,112,128]{3,2,1,0:T(8,128)(2,1)S(1)}, bf16[2,2,112,128]{3,2,1,0:T(8,128)(2,1)S(1)}, u32[]{:S(2)}, u32[]{:S(2)}) collective-permute-start(bf16[2,2,112,128]{3,2,1,0:T(8,128)(2,1)S(1)} %copy-done.4), channel_id=1, source_target_pairs={{0,8},{1,9},{2,10},{3,11},{4,12},{5,13},{6,14},{7,15},{16,24},{17,... | collective-permute-start | bytes 344072 | tf_op jit(solution)/shard_map/ppermute | solution.py:323
  9.5 0.0 copy-done.3
  9.5 1.3 %collective-permute-start.1 = (bf16[2,2,112,128]{3,2,1,0:T(8,128)(2,1)S(1)}, bf16[2,2,112,128]{3,2,1,0:T(8,128)(2,1)S(1)}, u32[]{:S(2)}, u32[]{:S(2)}) collective-permute-start(bf16[2,2,112,128]{3,2,1,0:T(8,128)(2,1)S(1)} %copy-done.3), channel_id=1, source_target_pairs={{0,10},{1,11},{2,8},{3,9},{4,14},{5,15},{6,12},{7,13},{16,26},{17,... | collective-permute-start | bytes 344072 | tf_op jit(solution)/shard_map/ppermute | solution.py:323
  10.8 0.0 copy-done.2
  10.8 1.3 %collective-permute-start.2 = (bf16[2,2,112,128]{3,2,1,0:T(8,128)(2,1)S(1)}, bf16[2,2,112,128]{3,2,1,0:T(8,128)(2,1)S(1)}, u32[]{:S(2)}, u32[]{:S(2)}) collective-permute-start(bf16[2,2,112,128]{3,2,1,0:T(8,128)(2,1)S(1)} %copy-done.2), channel_id=1, source_target_pairs={{0,12},{1,13},{2,14},{3,15},{4,8},{5,9},{6,10},{7,11},{16,28},{17,... | collective-permute-start | bytes 344072 | tf_op jit(solution)/shard_map/ppermute | solution.py:323
  12.1 0.0 copy-done.1
  12.1 1.3 %collective-permute-start.3 = (bf16[2,2,112,128]{3,2,1,0:T(8,128)(2,1)S(1)}, bf16[2,2,112,128]{3,2,1,0:T(8,128)(2,1)S(1)}, u32[]{:S(2)}, u32[]{:S(2)}) collective-permute-start(bf16[2,2,112,128]{3,2,1,0:T(8,128)(2,1)S(1)} %copy-done.1), channel_id=1, source_target_pairs={{0,14},{1,15},{2,12},{3,13},{4,10},{5,11},{6,8},{7,9},{16,30},{17,... | collective-permute-start | bytes 344072 | tf_op jit(solution)/shard_map/ppermute | solution.py:323
  13.4 11.0 %all-to-all-done.x_ref = bf16[8,4,112,128]{3,2,1,0:T(8,128)(2,1)S(1)} async-done(((bf16[8,4,112,128]{3,2,1,0:T(8,128)(2,1)}), bf16[8,4,112,128]{3,2,1,0:T(8,128)(2,1)S(1)}, u32[]{:S(2)}, u32[]{:S(2)}) %all-to-all-start) | async-done | bytes 917536 | tf_op jit(solution)/shard_map/all_to_all | solution.py:355
  24.4 0.0 copy-done
  24.4 2.7 %near.1 = (f32[1,1792]{1,0:T(1,128)S(1)}, f32[1,1792]{1,0:T(1,128)S(1)}, f32[128,1792]{1,0:T(8,128)S(1)}) custom-call(s32[1,1792]{1,0:T(1,128)S(1)} %copy-done, bf16[8,4,112,128]{3,2,1,0:T(8,128)(2,1)S(1)} %all-to-all-done.x_ref), custom_call_target="tpu_custom_call" | custom-call | tf_op jit(solution)/shard_map/near/pallas_call | solution.py:311
  27.1 0.0 collective-permute-done.refs_0_
  27.1 0.0 collective-permute-done.1.refs_1_
  27.1 5.0 %collective-permute-done.2.refs_2_ = bf16[2,2,112,128]{3,2,1,0:T(8,128)(2,1)S(1)} collective-permute-done((bf16[2,2,112,128]{3,2,1,0:T(8,128)(2,1)S(1)}, bf16[2,2,112,128]{3,2,1,0:T(8,128)(2,1)S(1)}, u32[]{:S(2)}, u32[]{:S(2)}) %collective-permute-start.2) | collective-permute-done | bytes 114720 | tf_op jit(solution)/shard_map/ppermute | solution.py:323
  32.1 2.9 %collective-permute-done.3.refs_3_ = bf16[2,2,112,128]{3,2,1,0:T(8,128)(2,1)S(1)} collective-permute-done((bf16[2,2,112,128]{3,2,1,0:T(8,128)(2,1)S(1)}, bf16[2,2,112,128]{3,2,1,0:T(8,128)(2,1)S(1)}, u32[]{:S(2)}, u32[]{:S(2)}) %collective-permute-start.3) | collective-permute-done | bytes 114720 | tf_op jit(solution)/shard_map/ppermute | solution.py:323
  35.0 0.1 collective-permute-start.4
  35.1 2.1 %far.1 = (f32[1,1792]{1,0:T(1,128)S(1)}, f32[1,1792]{1,0:T(1,128)S(1)}, f32[128,1792]{1,0:T(8,128)S(1)}) custom-call(s32[1]{0:T(128)} %bitcast.me_ref, bf16[8,4,112,128]{3,2,1,0:T(8,128)(2,1)S(1)} %all-to-all-done.x_ref, bf16[4,2,112,128]{3,2,1,0:T(8,128)(2,1)S(1)} %get-tuple-element.38.pairs_ref, f32[1,1792]{1,0:T(1,128)S(1)} %get-tuple-element.39.refs_0_, ...), custom_call_target="tpu_custom_call" | custom-call | tf_op jit(solution)/shard_map/far/pallas_call | solution.py:311
  37.2 0.0 collective-permute-done.4.pairs_ref
  37.2 2.3 %last.1 = bf16[8,2,112,128]{3,2,1,0:T(8,128)(2,1)S(1)} custom-call(s32[1]{0:T(128)} %bitcast.me_ref, bf16[8,4,112,128]{3,2,1,0:T(8,128)(2,1)S(1)} %all-to-all-done.x_ref, bf16[4,2,112,128]{3,2,1,0:T(8,128)(2,1)S(1)} %collective-permute-done.4.pairs_ref, f32[1,1792]{1,0:T(1,128)S(1)} %get-tuple-element.42.refs_0_, f32[1,1792]{1,0:T(1,128)S(1)} %get-tuple-element.43.refs_1_, ...), custom_call_target="tpu_custom_call" | custom-call | tf_op jit(solution)/shard_map/last/pallas_call | solution.py:311
  39.5 10.9 %all_to_all.10 = bf16[8,2,112,128]{3,2,1,0:T(8,128)(2,1)S(1)} all-to-all(bf16[8,2,112,128]{3,2,1,0:T(8,128)(2,1)S(1)} %last.1), channel_id=1, replica_groups={{0,1,2,3,4,5,6,7},{8,9,10,11,12,13,14,15},{16,17,18,19,20,21,22,23},{24..., dimensions={0} | all-to-all | bytes 917504 | tf_op jit(solution)/shard_map/all_to_all | solution.py:355
  50.4 0.9 %copy.10 = bf16[16,112,128]{2,0,1:T(8,128)(2,1)} copy(bf16[16,112,128]{2,1,0:T(8,128)(2,1)S(1)} %bitcast.7) | data formatting | bytes 917504 | tf_op jit(solution)/shard_map/reshape | solution.py:378
  (1 shorter events, 0.0 us)
Async XLA Ops:
  4.2 4.0 %copy-start.4 = (bf16[2,2,112,128]{3,2,1,0:T(8,128)(2,1)S(1)}, bf16[2,2,112,128]{3,2,1,0:T(8,128)(2,1)}, u32[]{:S(2)}) copy-start(bf16[2,2,112,128]{3,2,1,0:T(8,128)(2,1)} %get-tuple-element.29) | copy-start | bytes 344068
  4.2 5.3 %copy-start.3 = (bf16[2,2,112,128]{3,2,1,0:T(8,128)(2,1)S(1)}, bf16[2,2,112,128]{3,2,1,0:T(8,128)(2,1)}, u32[]{:S(2)}) copy-start(bf16[2,2,112,128]{3,2,1,0:T(8,128)(2,1)} %get-tuple-element.30) | copy-start | bytes 344068
  4.2 6.6 %copy-start.2 = (bf16[2,2,112,128]{3,2,1,0:T(8,128)(2,1)S(1)}, bf16[2,2,112,128]{3,2,1,0:T(8,128)(2,1)}, u32[]{:S(2)}) copy-start(bf16[2,2,112,128]{3,2,1,0:T(8,128)(2,1)} %get-tuple-element.31) | copy-start | bytes 344068
  4.2 7.9 %copy-start.1 = (bf16[2,2,112,128]{3,2,1,0:T(8,128)(2,1)S(1)}, bf16[2,2,112,128]{3,2,1,0:T(8,128)(2,1)}, u32[]{:S(2)}) copy-start(bf16[2,2,112,128]{3,2,1,0:T(8,128)(2,1)} %get-tuple-element.32) | copy-start | bytes 344068
  4.2 20.2 %all-to-all-start = ((bf16[8,4,112,128]{3,2,1,0:T(8,128)(2,1)}), bf16[8,4,112,128]{3,2,1,0:T(8,128)(2,1)S(1)}, u32[]{:S(2)}, u32[]{:S(2)}) async-start(bf16[8,4,112,128]{3,2,1,0:T(8,128)(2,1)} %get-tuple-element.25), calls=%async_computation | async-start | bytes 1835008 | tf_op jit(solution)/shard_map/all_to_all | solution.py:355
  8.2 16.3 %copy-start = (s32[1,1792]{1,0:T(1,128)S(1)}, s32[1,1792]{1,0:T(1,128)}, u32[]{:S(2)}) copy-start(s32[1,1792]{1,0:T(1,128)} %constant.9.clone.position_ref) | copy-start | bytes 21508
  8.2 18.9 %collective-permute-start = (bf16[2,2,112,128]{3,2,1,0:T(8,128)(2,1)S(1)}, bf16[2,2,112,128]{3,2,1,0:T(8,128)(2,1)S(1)}, u32[]{:S(2)}, u32[]{:S(2)}) collective-permute-start(bf16[2,2,112,128]{3,2,1,0:T(8,128)(2,1)S(1)} %copy-done.4), channel_id=1, source_target_pairs={{0,8},{1,9},{2,10},{3,11},{4,12},{5,13},{6,14},{7,15},{16,24},{17,... | collective-permute-start | bytes 344072 | tf_op jit(solution)/shard_map/ppermute | solution.py:323
  9.5 17.6 %collective-permute-start.1 = (bf16[2,2,112,128]{3,2,1,0:T(8,128)(2,1)S(1)}, bf16[2,2,112,128]{3,2,1,0:T(8,128)(2,1)S(1)}, u32[]{:S(2)}, u32[]{:S(2)}) collective-permute-start(bf16[2,2,112,128]{3,2,1,0:T(8,128)(2,1)S(1)} %copy-done.3), channel_id=1, source_target_pairs={{0,10},{1,11},{2,8},{3,9},{4,14},{5,15},{6,12},{7,13},{16,26},{17,... | collective-permute-start | bytes 344072 | tf_op jit(solution)/shard_map/ppermute | solution.py:323
  10.8 21.3 %collective-permute-start.2 = (bf16[2,2,112,128]{3,2,1,0:T(8,128)(2,1)S(1)}, bf16[2,2,112,128]{3,2,1,0:T(8,128)(2,1)S(1)}, u32[]{:S(2)}, u32[]{:S(2)}) collective-permute-start(bf16[2,2,112,128]{3,2,1,0:T(8,128)(2,1)S(1)} %copy-done.2), channel_id=1, source_target_pairs={{0,12},{1,13},{2,14},{3,15},{4,8},{5,9},{6,10},{7,11},{16,28},{17,... | collective-permute-start | bytes 344072 | tf_op jit(solution)/shard_map/ppermute | solution.py:323
  12.1 22.9 %collective-permute-start.3 = (bf16[2,2,112,128]{3,2,1,0:T(8,128)(2,1)S(1)}, bf16[2,2,112,128]{3,2,1,0:T(8,128)(2,1)S(1)}, u32[]{:S(2)}, u32[]{:S(2)}) collective-permute-start(bf16[2,2,112,128]{3,2,1,0:T(8,128)(2,1)S(1)} %copy-done.1), channel_id=1, source_target_pairs={{0,14},{1,15},{2,12},{3,13},{4,10},{5,11},{6,8},{7,9},{16,30},{17,... | collective-permute-start | bytes 344072 | tf_op jit(solution)/shard_map/ppermute | solution.py:323
  35.0 2.2 %collective-permute-start.4 = (bf16[4,2,112,128]{3,2,1,0:T(8,128)(2,1)S(1)}, bf16[4,2,112,128]{3,2,1,0:T(8,128)(2,1)S(1)}, u32[]{:S(2)}, u32[]{:S(2)}) collective-permute-start(bf16[4,2,112,128]{3,2,1,0:T(8,128)(2,1)S(1)} %get-tuple-element.37), channel_id=1, source_target_pairs={{0,1},{1,0},{2,3},{3,2},{4,5},{5,4},{6,7},{7,6},{8,9},{9,8},{10,11... | collective-permute-start | bytes 688136 | tf_op jit(solution)/shard_map/ppermute | solution.py:326

commit v14 on v13

--- a/solution.py
+++ b/solution.py
@@ -319,7 +319,7 @@
         )(*([me] if specs is None or SMEM in specs else []), *operands)
 
     def to_upper(step, array):
-        links = [(device, half + ((device // 2) ^ step) * 2 + device % 2) for device in range(half)]
+        links = [(device, ((device // 2) ^ (steps + step)) * 2 + device % 2) for device in range(devices)]
         return lax.ppermute(array, "seq", links)
 
     def to_core(array, lowest):

time: 51.6 us -> 50.6 us (0.981)
  waiting for transfers between devices: 18.9 us -> 16.3 us
  blocking collectives: 10.9 us -> 11.9 us
  starting transfers between devices: 9.19 us -> 9.94 us
    ppermute x4, waiting for transfers between devices: 7.89 us -> 6.05 us  [to_upper(): return lax.ppermute(array, 'seq', links)]
    all_to_all x1, blocking collectives: 10.9 us -> 11.9 us  [inside(): lax.all_to_all(array, 'seq', split_axis=0, concat_axis=0, axis_index_grou...]
    all_to_all x1, waiting for transfers between devices: 11 us -> 10.2 us  [inside(): lax.all_to_all(array, 'seq', split_axis=0, concat_axis=0, axis_index_grou...]
    ppermute x4, starting transfers between devices: 5.17 us -> 5.91 us  [to_upper(): return lax.ppermute(array, 'seq', links)]
where the time goes in v14:
time: 50.6 us; the launch traced here: 50.3 us
  waiting for transfers between devices  16.3 us (32%)
  blocking collectives  11.9 us (24%)
  Pallas kernels  11.2 us (22%)
  starting transfers between devices  9.94 us (20%)
  local copies, waits for them, and re-layouts  0.91 us (2%)
    all_to_all x1, blocking collectives, inside(): lax.all_to_all(array, 'seq', split_axis=0, concat_axis=0, axis_index_grou...  11.9 us
    pallas_call x5, Pallas kernels, call(): pl.pallas_call(kernel, out_shape=outs, in_specs=specs or [SMEM] + [VMEM]...  11.2 us
    all_to_all x1, waiting for transfers between devices, inside(): lax.all_to_all(array, 'seq', split_axis=0, concat_axis=0, axis_index_grou...  10.2 us
    ppermute x4, waiting for transfers between devices, to_upper(): return lax.ppermute(array, 'seq', links)  6.05 us
    ppermute x4, starting transfers between devices, to_upper(): return lax.ppermute(array, 'seq', links)  5.91 us
    all_to_all x1, starting transfers between devices, inside(): lax.all_to_all(array, 'seq', split_axis=0, concat_axis=0, axis_index_grou...  3.95 us
  transfers between devices with their start and end apart: 6, of which 3 were waited for; matrix products, arithmetic and copies ran while one was open for 0% of the time, Pallas kernels for 9%

profile of v14, /device:TPU:16, one launch (start us, length us, event | category | flops | bytes accessed | tf_op | source)
XLA Modules:
  0.0 50.3 jit_solution(2933360954418378603)
XLA Ops:
  0.0 4.1 %send.1 = (bf16[2,2,112,128]{3,2,1,0:T(8,128)(2,1)}, bf16[2,2,112,128]{3,2,1,0:T(8,128)(2,1)}, bf16[2,2,112,128]{3,2,1,0:T(8,128)(2,1)}, bf16[2,2,112,128]{3,2,1,0:T(8,128)(2,1)}, bf16[8,4,112,128]{3,2,1,0:T(8,128)(2,1)}) custom-call(s32[1]{0:T(128)} %bitcast.me_ref, bf16[112,16,128]{2,1,0:T(8,128)(2,1)} %q_hbm.1, bf16[112,8,128]{2,1,0:T(8,128)(2,1)} %k_hbm.1, ...), custom_call_target="tpu_custom_call" | custom-call | tf_op jit(solution)/shard_map/send/pallas_call | solution.py:311
  4.2 0.0 copy-start.4
  4.2 0.0 copy-start.3
  4.2 0.0 copy-start.2
  4.2 0.0 copy-start.1
  4.2 4.0 %all-to-all-start = ((bf16[8,4,112,128]{3,2,1,0:T(8,128)(2,1)}), bf16[8,4,112,128]{3,2,1,0:T(8,128)(2,1)S(1)}, u32[]{:S(2)}, u32[]{:S(2)}) async-start(bf16[8,4,112,128]{3,2,1,0:T(8,128)(2,1)} %get-tuple-element.25), calls=%async_computation | async-start | bytes 1835008 | tf_op jit(solution)/shard_map/all_to_all | solution.py:355
  8.2 0.0 copy-start
  8.2 0.0 copy-done.4
  8.2 0.4 collective-permute-start
  8.6 0.0 copy-done.3
  8.6 4.0 %collective-permute-start.1 = (bf16[2,2,112,128]{3,2,1,0:T(8,128)(2,1)S(1)}, bf16[2,2,112,128]{3,2,1,0:T(8,128)(2,1)S(1)}, u32[]{:S(2)}, u32[]{:S(2)}) collective-permute-start(bf16[2,2,112,128]{3,2,1,0:T(8,128)(2,1)S(1)} %copy-done.3), channel_id=1, source_target_pairs={{0,10},{1,11},{2,8},{3,9},{4,14},{5,15},{6,12},{7,13},{8,2},{9,3},... | collective-permute-start | bytes 344072 | tf_op jit(solution)/shard_map/ppermute | solution.py:323
  12.6 0.0 copy-done.2
  12.6 0.3 collective-permute-start.2
  12.9 0.0 copy-done.1
  12.9 1.1 %collective-permute-start.3 = (bf16[2,2,112,128]{3,2,1,0:T(8,128)(2,1)S(1)}, bf16[2,2,112,128]{3,2,1,0:T(8,128)(2,1)S(1)}, u32[]{:S(2)}, u32[]{:S(2)}) collective-permute-start(bf16[2,2,112,128]{3,2,1,0:T(8,128)(2,1)S(1)} %copy-done.1), channel_id=1, source_target_pairs={{0,14},{1,15},{2,12},{3,13},{4,10},{5,11},{6,8},{7,9},{8,6},{9,7},... | collective-permute-start | bytes 344072 | tf_op jit(solution)/shard_map/ppermute | solution.py:323
  14.1 10.2 %all-to-all-done.x_ref = bf16[8,4,112,128]{3,2,1,0:T(8,128)(2,1)S(1)} async-done(((bf16[8,4,112,128]{3,2,1,0:T(8,128)(2,1)}), bf16[8,4,112,128]{3,2,1,0:T(8,128)(2,1)S(1)}, u32[]{:S(2)}, u32[]{:S(2)}) %all-to-all-start) | async-done | bytes 917536 | tf_op jit(solution)/shard_map/all_to_all | solution.py:355
  24.3 0.0 copy-done
  24.3 2.7 %near.1 = (f32[1,1792]{1,0:T(1,128)S(1)}, f32[1,1792]{1,0:T(1,128)S(1)}, f32[128,1792]{1,0:T(8,128)S(1)}) custom-call(s32[1,1792]{1,0:T(1,128)S(1)} %copy-done, bf16[8,4,112,128]{3,2,1,0:T(8,128)(2,1)S(1)} %all-to-all-done.x_ref), custom_call_target="tpu_custom_call" | custom-call | tf_op jit(solution)/shard_map/near/pallas_call | solution.py:311
  27.0 0.0 collective-permute-done.refs_0_
  27.0 0.0 collective-permute-done.1.refs_1_
  27.0 3.5 %collective-permute-done.2.refs_2_ = bf16[2,2,112,128]{3,2,1,0:T(8,128)(2,1)S(1)} collective-permute-done((bf16[2,2,112,128]{3,2,1,0:T(8,128)(2,1)S(1)}, bf16[2,2,112,128]{3,2,1,0:T(8,128)(2,1)S(1)}, u32[]{:S(2)}, u32[]{:S(2)}) %collective-permute-start.2) | collective-permute-done | bytes 114720 | tf_op jit(solution)/shard_map/ppermute | solution.py:323
  30.5 2.6 %collective-permute-done.3.refs_3_ = bf16[2,2,112,128]{3,2,1,0:T(8,128)(2,1)S(1)} collective-permute-done((bf16[2,2,112,128]{3,2,1,0:T(8,128)(2,1)S(1)}, bf16[2,2,112,128]{3,2,1,0:T(8,128)(2,1)S(1)}, u32[]{:S(2)}, u32[]{:S(2)}) %collective-permute-start.3) | collective-permute-done | bytes 114720 | tf_op jit(solution)/shard_map/ppermute | solution.py:323
  33.1 0.1 collective-permute-start.4
  33.1 2.1 %far.1 = (f32[1,1792]{1,0:T(1,128)S(1)}, f32[1,1792]{1,0:T(1,128)S(1)}, f32[128,1792]{1,0:T(8,128)S(1)}) custom-call(s32[1]{0:T(128)} %bitcast.me_ref, bf16[8,4,112,128]{3,2,1,0:T(8,128)(2,1)S(1)} %all-to-all-done.x_ref, bf16[4,2,112,128]{3,2,1,0:T(8,128)(2,1)S(1)} %get-tuple-element.38.pairs_ref, f32[1,1792]{1,0:T(1,128)S(1)} %get-tuple-element.39.refs_0_, ...), custom_call_target="tpu_custom_call" | custom-call | tf_op jit(solution)/shard_map/far/pallas_call | solution.py:311
  35.2 0.0 collective-permute-done.4.pairs_ref
  35.3 2.3 %last.1 = bf16[8,2,112,128]{3,2,1,0:T(8,128)(2,1)S(1)} custom-call(s32[1]{0:T(128)} %bitcast.me_ref, bf16[8,4,112,128]{3,2,1,0:T(8,128)(2,1)S(1)} %all-to-all-done.x_ref, bf16[4,2,112,128]{3,2,1,0:T(8,128)(2,1)S(1)} %collective-permute-done.4.pairs_ref, f32[1,1792]{1,0:T(1,128)S(1)} %get-tuple-element.42.refs_0_, f32[1,1792]{1,0:T(1,128)S(1)} %get-tuple-element.43.refs_1_, ...), custom_call_target="tpu_custom_call" | custom-call | tf_op jit(solution)/shard_map/last/pallas_call | solution.py:311
  37.5 11.9 %all_to_all.10 = bf16[8,2,112,128]{3,2,1,0:T(8,128)(2,1)S(1)} all-to-all(bf16[8,2,112,128]{3,2,1,0:T(8,128)(2,1)S(1)} %last.1), channel_id=1, replica_groups={{0,1,2,3,4,5,6,7},{8,9,10,11,12,13,14,15},{16,17,18,19,20,21,22,23},{24..., dimensions={0} | all-to-all | bytes 917504 | tf_op jit(solution)/shard_map/all_to_all | solution.py:355
  49.4 0.9 %copy.10 = bf16[16,112,128]{2,0,1:T(8,128)(2,1)} copy(bf16[16,112,128]{2,1,0:T(8,128)(2,1)S(1)} %bitcast.7) | data formatting | bytes 917504 | tf_op jit(solution)/shard_map/reshape | solution.py:378
  (1 shorter events, 0.0 us)
Async XLA Ops:
  4.2 4.0 %copy-start.4 = (bf16[2,2,112,128]{3,2,1,0:T(8,128)(2,1)S(1)}, bf16[2,2,112,128]{3,2,1,0:T(8,128)(2,1)}, u32[]{:S(2)}) copy-start(bf16[2,2,112,128]{3,2,1,0:T(8,128)(2,1)} %get-tuple-element.29) | copy-start | bytes 344068
  4.2 4.4 %copy-start.3 = (bf16[2,2,112,128]{3,2,1,0:T(8,128)(2,1)S(1)}, bf16[2,2,112,128]{3,2,1,0:T(8,128)(2,1)}, u32[]{:S(2)}) copy-start(bf16[2,2,112,128]{3,2,1,0:T(8,128)(2,1)} %get-tuple-element.30) | copy-start | bytes 344068
  4.2 8.4 %copy-start.2 = (bf16[2,2,112,128]{3,2,1,0:T(8,128)(2,1)S(1)}, bf16[2,2,112,128]{3,2,1,0:T(8,128)(2,1)}, u32[]{:S(2)}) copy-start(bf16[2,2,112,128]{3,2,1,0:T(8,128)(2,1)} %get-tuple-element.31) | copy-start | bytes 344068
  4.2 8.8 %copy-start.1 = (bf16[2,2,112,128]{3,2,1,0:T(8,128)(2,1)S(1)}, bf16[2,2,112,128]{3,2,1,0:T(8,128)(2,1)}, u32[]{:S(2)}) copy-start(bf16[2,2,112,128]{3,2,1,0:T(8,128)(2,1)} %get-tuple-element.32) | copy-start | bytes 344068
  4.2 20.1 %all-to-all-start = ((bf16[8,4,112,128]{3,2,1,0:T(8,128)(2,1)}), bf16[8,4,112,128]{3,2,1,0:T(8,128)(2,1)S(1)}, u32[]{:S(2)}, u32[]{:S(2)}) async-start(bf16[8,4,112,128]{3,2,1,0:T(8,128)(2,1)} %get-tuple-element.25), calls=%async_computation | async-start | bytes 1835008 | tf_op jit(solution)/shard_map/all_to_all | solution.py:355
  8.2 16.1 %copy-start = (s32[1,1792]{1,0:T(1,128)S(1)}, s32[1,1792]{1,0:T(1,128)}, u32[]{:S(2)}) copy-start(s32[1,1792]{1,0:T(1,128)} %constant.9.clone.position_ref) | copy-start | bytes 21508
  8.2 18.8 %collective-permute-start = (bf16[2,2,112,128]{3,2,1,0:T(8,128)(2,1)S(1)}, bf16[2,2,112,128]{3,2,1,0:T(8,128)(2,1)S(1)}, u32[]{:S(2)}, u32[]{:S(2)}) collective-permute-start(bf16[2,2,112,128]{3,2,1,0:T(8,128)(2,1)S(1)} %copy-done.4), channel_id=1, source_target_pairs={{0,8},{1,9},{2,10},{3,11},{4,12},{5,13},{6,14},{7,15},{8,0},{9,1},... | collective-permute-start | bytes 344072 | tf_op jit(solution)/shard_map/ppermute | solution.py:323
  8.6 18.4 %collective-permute-start.1 = (bf16[2,2,112,128]{3,2,1,0:T(8,128)(2,1)S(1)}, bf16[2,2,112,128]{3,2,1,0:T(8,128)(2,1)S(1)}, u32[]{:S(2)}, u32[]{:S(2)}) collective-permute-start(bf16[2,2,112,128]{3,2,1,0:T(8,128)(2,1)S(1)} %copy-done.3), channel_id=1, source_target_pairs={{0,10},{1,11},{2,8},{3,9},{4,14},{5,15},{6,12},{7,13},{8,2},{9,3},... | collective-permute-start | bytes 344072 | tf_op jit(solution)/shard_map/ppermute | solution.py:323
  12.6 17.9 %collective-permute-start.2 = (bf16[2,2,112,128]{3,2,1,0:T(8,128)(2,1)S(1)}, bf16[2,2,112,128]{3,2,1,0:T(8,128)(2,1)S(1)}, u32[]{:S(2)}, u32[]{:S(2)}) collective-permute-start(bf16[2,2,112,128]{3,2,1,0:T(8,128)(2,1)S(1)} %copy-done.2), channel_id=1, source_target_pairs={{0,12},{1,13},{2,14},{3,15},{4,8},{5,9},{6,10},{7,11},{8,4},{9,5},... | collective-permute-start | bytes 344072 | tf_op jit(solution)/shard_map/ppermute | solution.py:323
  12.9 20.1 %collective-permute-start.3 = (bf16[2,2,112,128]{3,2,1,0:T(8,128)(2,1)S(1)}, bf16[2,2,112,128]{3,2,1,0:T(8,128)(2,1)S(1)}, u32[]{:S(2)}, u32[]{:S(2)}) collective-permute-start(bf16[2,2,112,128]{3,2,1,0:T(8,128)(2,1)S(1)} %copy-done.1), channel_id=1, source_target_pairs={{0,14},{1,15},{2,12},{3,13},{4,10},{5,11},{6,8},{7,9},{8,6},{9,7},... | collective-permute-start | bytes 344072 | tf_op jit(solution)/shard_map/ppermute | solution.py:323
  33.1 2.2 %collective-permute-start.4 = (bf16[4,2,112,128]{3,2,1,0:T(8,128)(2,1)S(1)}, bf16[4,2,112,128]{3,2,1,0:T(8,128)(2,1)S(1)}, u32[]{:S(2)}, u32[]{:S(2)}) collective-permute-start(bf16[4,2,112,128]{3,2,1,0:T(8,128)(2,1)S(1)} %get-tuple-element.37), channel_id=1, source_target_pairs={{0,1},{1,0},{2,3},{3,2},{4,5},{5,4},{6,7},{7,6},{8,9},{9,8},{10,11... | collective-permute-start | bytes 688136 | tf_op jit(solution)/shard_map/ppermute | solution.py:326

commit v15 on v12

--- a/solution.py
+++ b/solution.py
@@ -302,7 +302,7 @@
         )(*([me] if specs is None or SMEM in specs else []), *operands)
 
     def to_upper(step, array):
-        links = [(device, half + ((device // 2) ^ step) * 2 + device % 2) for device in range(half)]
+        links = [(device, ((device // 2) ^ (steps + step)) * 2 + device % 2) for device in range(devices)]
         return lax.ppermute(array, "seq", links)
 
     def to_core(array, lowest):
@@ -338,17 +338,17 @@
         return lax.all_to_all(array, "seq", split_axis=0, concat_axis=0, axis_index_groups=groups, tiled=True)
 
     far = [to_upper(step, pair) for step, pair in enumerate(pairs)]
-    arrived = inside(near)
+    arrived = lax.cond(me[0] >= 0, inside, jnp.zeros_like, near)
+    arrived, far = lax.optimization_barrier((arrived, far))
+    mine, others = call(
+        split_kernel, "split", [shape((steps, 2, tokens, width), bf16)] * 2, *far, specs=[VMEM] * steps
+    )
+    neighbours = to_core(others, 0)
     lanes = half * group * tokens
     state = [shape((1, lanes), f32), shape((1, lanes), f32), shape((width, lanes), f32)]
     positions = np.broadcast_to(np.arange(half * tokens, dtype=np.int32).reshape(half, 1, tokens), (half, group, tokens))
     carried = call(near_kernel, "near", state, jnp.asarray(positions.reshape(1, lanes)), arrived, specs=[VMEM] * 2)
 
-    carried, far = lax.optimization_barrier((carried, far))
-    mine, others = call(
-        split_kernel, "split", [shape((steps, 2, tokens, width), bf16)] * 2, *far, specs=[VMEM] * steps
-    )
-    neighbours = to_core(others, half)
     attended = call(
         functools.partial(last_kernel, half),
         "last",

time: 54.2 us -> 51.6 us (0.952)
  blocking collectives: 10.9 us -> 34.3 us
  waiting for transfers between devices: 20.4 us -> 0.01 us
  starting transfers between devices: 11 us -> 6.06 us
  Pallas kernels: 10.4 us -> 9.55 us
    all_to_all x1 -> x2, blocking collectives: 10.9 us -> 34.3 us  [inside(): lax.all_to_all(array, 'seq', split_axis=0, concat_axis=0, axis_index_grou...]
    all_to_all x1 -> x0, waiting for transfers between devices: 11 us -> none  [inside(): lax.all_to_all(array, 'seq', split_axis=0, concat_axis=0, axis_index_grou...]
    ppermute x4, waiting for transfers between devices: 7.89 us -> 0.01 us  [to_upper(): return lax.ppermute(array, 'seq', links)]
    all_to_all x1 -> x0, starting transfers between devices: 3.95 us -> none  [inside(): lax.all_to_all(array, 'seq', split_axis=0, concat_axis=0, axis_index_grou...]
    ppermute x1, starting transfers between devices: 1.92 us -> 0.15 us  [to_core(): lax.ppermute(array, 'seq', [(device, device ^ 1) for device in range(lowe...]
    ppermute x1, waiting for transfers between devices: 1.45 us -> 0.01 us  [to_core(): lax.ppermute(array, 'seq', [(device, device ^ 1) for device in range(lowe...]
    pallas_call x4, Pallas kernels: 10.4 us -> 9.55 us  [call(): pl.pallas_call(kernel, out_shape=outs, in_specs=specs or [SMEM] + [VMEM]...]
    ppermute x4, starting transfers between devices: 5.17 us -> 5.91 us  [to_upper(): return lax.ppermute(array, 'seq', links)]
  transfers between devices with their start and end apart: 6 -> 5, of which waited for: 4 -> 0; matrix products, arithmetic and copies ran while one was open for 0% -> 0% of each run, Pallas kernels for 5% -> 5%
where the time goes in v15:
time: 51.6 us; the launch traced here: 51.4 us
  blocking collectives  34.3 us (66%)
  Pallas kernels  9.55 us (19%)
  starting transfers between devices  6.06 us (12%)
  local copies, waits for them, and re-layouts  1.35 us (3%)
    all_to_all x2, blocking collectives, inside(): lax.all_to_all(array, 'seq', split_axis=0, concat_axis=0, axis_index_grou...  34.3 us
    pallas_call x4, Pallas kernels, call(): pl.pallas_call(kernel, out_shape=outs, in_specs=specs or [SMEM] + [VMEM]...  9.55 us
    ppermute x4, starting transfers between devices, to_upper(): return lax.ppermute(array, 'seq', links)  5.91 us
  transfers between devices with their start and end apart: 5, of which 0 were waited for; matrix products, arithmetic and copies ran while one was open for 0% of the time, Pallas kernels for 5%

profile of v15, /device:TPU:16, one launch (start us, length us, event | category | flops | bytes accessed | tf_op | source)
XLA Modules:
  0.0 51.4 jit_solution(2324309934523822669)
XLA Ops:
  0.0 3.2 %send.1 = (bf16[2,2,112,128]{3,2,1,0:T(8,128)(2,1)}, bf16[2,2,112,128]{3,2,1,0:T(8,128)(2,1)}, bf16[2,2,112,128]{3,2,1,0:T(8,128)(2,1)}, bf16[2,2,112,128]{3,2,1,0:T(8,128)(2,1)}, bf16[8,4,112,128]{3,2,1,0:T(8,128)(2,1)S(1)}) custom-call(s32[1]{0:T(128)} %bitcast.me_ref, bf16[112,16,128]{2,1,0:T(8,128)(2,1)} %q_hbm.1, bf16[112,8,128]{2,1,0:T(8,128)(2,1)} %k_hbm.1, ...), custom_call_target="tpu_custom_call" | custom-call | tf_op jit(solution)/shard_map/send/pallas_call | solution.py:294
  3.2 0.1 collective-permute-start
  3.3 3.9 %collective-permute-start.1 = (bf16[2,2,112,128]{3,2,1,0:T(8,128)(2,1)}, bf16[2,2,112,128]{3,2,1,0:T(8,128)(2,1)S(1)}, u32[]{:S(2)}, u32[]{:S(2)}) collective-permute-start(bf16[2,2,112,128]{3,2,1,0:T(8,128)(2,1)} %get-tuple-element.26), channel_id=1, source_target_pairs={{0,10},{1,11},{2,8},{3,9},{4,14},{5,15},{6,12},{7,13},{8,2},{9,3},... | collective-permute-start | bytes 344072 | tf_op jit(solution)/shard_map/ppermute | solution.py:306
  7.2 0.4 collective-permute-start.2
  7.6 1.5 %collective-permute-start.3 = (bf16[2,2,112,128]{3,2,1,0:T(8,128)(2,1)}, bf16[2,2,112,128]{3,2,1,0:T(8,128)(2,1)S(1)}, u32[]{:S(2)}, u32[]{:S(2)}) collective-permute-start(bf16[2,2,112,128]{3,2,1,0:T(8,128)(2,1)} %get-tuple-element.28), channel_id=1, source_target_pairs={{0,14},{1,15},{2,12},{3,13},{4,10},{5,11},{6,8},{7,9},{8,6},{9,7},... | collective-permute-start | bytes 344072 | tf_op jit(solution)/shard_map/ppermute | solution.py:306
  9.2 21.3 %conditional.1 = (bf16[8,4,112,128]{3,2,1,0:T(8,128)(2,1)S(1)}) conditional(s32[]{:T(128)} %convert_element_type.3, () %tuple.12, bf16[8,4,112,128]{3,2,1,0:T(8,128)(2,1)S(1)} %get-tuple-element.24), branch_computations={%region_0.0_spmd, %region_1.0_spmd} | conditional | bytes 1835016 | solution.py:341
  9.2 21.3 %all_to_all.9 = bf16[8,4,112,128]{3,2,1,0:T(8,128)(2,1)S(1)} all-to-all(bf16[8,4,112,128]{3,2,1,0:T(8,128)(2,1)S(1)} %param.1), channel_id=1, replica_groups={{0,1,2,3,4,5,6,7},{8,9,10,11,12,13,14,15},{16,17,18,19,20,21,22,23},{24..., dimensions={0} | all-to-all | bytes 1835008 | tf_op jit(solution)/shard_map/cond/branch_1_fun/all_to_all | solution.py:338
  30.4 0.0 copy-start
  30.5 0.0 collective-permute-done.refs_0_
  30.5 0.0 collective-permute-done.1.refs_1_
  30.5 0.0 collective-permute-done.2.refs_2_
  30.5 0.0 collective-permute-done.3.refs_3_
  30.5 0.2 collective-permute-start.4
  30.7 0.5 copy-done
  31.1 2.7 %near.1 = (f32[1,1792]{1,0:T(1,128)S(1)}, f32[1,1792]{1,0:T(1,128)S(1)}, f32[128,1792]{1,0:T(8,128)S(1)}) custom-call(s32[1,1792]{1,0:T(1,128)S(1)} %copy-done, bf16[8,4,112,128]{3,2,1,0:T(8,128)(2,1)S(1)} %get-tuple-element.39.x_ref), custom_call_target="tpu_custom_call" | custom-call | tf_op jit(solution)/shard_map/near/pallas_call | solution.py:294
  33.8 0.0 collective-permute-done.4.neighbours_ref
  33.8 3.6 %last.1 = bf16[8,2,112,128]{3,2,1,0:T(8,128)(2,1)S(1)} custom-call(s32[1]{0:T(128)} %bitcast.me_ref, bf16[8,4,112,128]{3,2,1,0:T(8,128)(2,1)S(1)} %get-tuple-element.39.x_ref, bf16[4,2,112,128]{3,2,1,0:T(8,128)(2,1)S(1)} %get-tuple-element.34.mine_ref, bf16[4,2,112,128]{3,2,1,0:T(8,128)(2,1)S(1)} %collective-permute-done.4.neighbours_ref, ...), custom_call_target="tpu_custom_call" | custom-call | tf_op jit(solution)/shard_map/last/pallas_call | solution.py:294
  37.5 13.0 %all_to_all.10 = bf16[8,2,112,128]{3,2,1,0:T(8,128)(2,1)S(1)} all-to-all(bf16[8,2,112,128]{3,2,1,0:T(8,128)(2,1)S(1)} %last.1), channel_id=1, replica_groups={{0,1,2,3,4,5,6,7},{8,9,10,11,12,13,14,15},{16,17,18,19,20,21,22,23},{24..., dimensions={0} | all-to-all | bytes 917504 | tf_op jit(solution)/shard_map/all_to_all | solution.py:338
  50.5 0.9 %copy.10 = bf16[16,112,128]{2,0,1:T(8,128)(2,1)} copy(bf16[16,112,128]{2,1,0:T(8,128)(2,1)S(1)} %bitcast.7) | data formatting | bytes 917504 | tf_op jit(solution)/shard_map/reshape | solution.py:361
  (1 shorter events, 0.0 us)
Async XLA Ops:
  3.2 27.2 %collective-permute-start = (bf16[2,2,112,128]{3,2,1,0:T(8,128)(2,1)}, bf16[2,2,112,128]{3,2,1,0:T(8,128)(2,1)S(1)}, u32[]{:S(2)}, u32[]{:S(2)}) collective-permute-start(bf16[2,2,112,128]{3,2,1,0:T(8,128)(2,1)} %get-tuple-element.25), channel_id=1, source_target_pairs={{0,8},{1,9},{2,10},{3,11},{4,12},{5,13},{6,14},{7,15},{8,0},{9,1},... | collective-permute-start | bytes 344072 | tf_op jit(solution)/shard_map/ppermute | solution.py:306
  3.3 27.1 %collective-permute-start.1 = (bf16[2,2,112,128]{3,2,1,0:T(8,128)(2,1)}, bf16[2,2,112,128]{3,2,1,0:T(8,128)(2,1)S(1)}, u32[]{:S(2)}, u32[]{:S(2)}) collective-permute-start(bf16[2,2,112,128]{3,2,1,0:T(8,128)(2,1)} %get-tuple-element.26), channel_id=1, source_target_pairs={{0,10},{1,11},{2,8},{3,9},{4,14},{5,15},{6,12},{7,13},{8,2},{9,3},... | collective-permute-start | bytes 344072 | tf_op jit(solution)/shard_map/ppermute | solution.py:306
  7.2 23.3 %collective-permute-start.2 = (bf16[2,2,112,128]{3,2,1,0:T(8,128)(2,1)}, bf16[2,2,112,128]{3,2,1,0:T(8,128)(2,1)S(1)}, u32[]{:S(2)}, u32[]{:S(2)}) collective-permute-start(bf16[2,2,112,128]{3,2,1,0:T(8,128)(2,1)} %get-tuple-element.27), channel_id=1, source_target_pairs={{0,12},{1,13},{2,14},{3,15},{4,8},{5,9},{6,10},{7,11},{8,4},{9,5},... | collective-permute-start | bytes 344072 | tf_op jit(solution)/shard_map/ppermute | solution.py:306
  7.6 22.8 %collective-permute-start.3 = (bf16[2,2,112,128]{3,2,1,0:T(8,128)(2,1)}, bf16[2,2,112,128]{3,2,1,0:T(8,128)(2,1)S(1)}, u32[]{:S(2)}, u32[]{:S(2)}) collective-permute-start(bf16[2,2,112,128]{3,2,1,0:T(8,128)(2,1)} %get-tuple-element.28), channel_id=1, source_target_pairs={{0,14},{1,15},{2,12},{3,13},{4,10},{5,11},{6,8},{7,9},{8,6},{9,7},... | collective-permute-start | bytes 344072 | tf_op jit(solution)/shard_map/ppermute | solution.py:306
  30.4 0.7 %copy-start = (s32[1,1792]{1,0:T(1,128)S(1)}, s32[1,1792]{1,0:T(1,128)}, u32[]{:S(2)}) copy-start(s32[1,1792]{1,0:T(1,128)} %constant.13.clone.position_ref) | copy-start | bytes 21508
  30.5 3.3 %collective-permute-start.4 = (bf16[4,2,112,128]{3,2,1,0:T(8,128)(2,1)S(1)}, bf16[4,2,112,128]{3,2,1,0:T(8,128)(2,1)S(1)}, u32[]{:S(2)}, u32[]{:S(2)}) collective-permute-start(bf16[4,2,112,128]{3,2,1,0:T(8,128)(2,1)S(1)} %get-tuple-element.35), channel_id=1, source_target_pairs={{0,1},{1,0},{2,3},{3,2},{4,5},{5,4},{6,7},{7,6},{8,9},{9,8},{10,11... | collective-permute-start | bytes 688136 | tf_op jit(solution)/shard_map/ppermute | solution.py:309
